TPU v7x, 32 devices: a whole 2x2x4 slice. The times are simulated.
32 devices in a mesh: wide: 16 (over z, x, core), narrow: 2 (over y).
Axes of the slice: x: 2, y: 2, z: 4, core: 2. Of those that a mesh axis runs over, the one named last changes fastest.
Arguments:
- states: bfloat16 [768, 128, 1024], P('wide', None, 'narrow'), may hold values from -6 to 6
- proj_weight: bfloat16 [1024, 128], P('narrow'), may hold values from -0.1875 to 0.1875
- lengths: int32 [768], replicated, may hold values from 64 to 128
- query_block: int32 [192], P('wide'), may hold values from 0 to 3
- cand_block: int32 [192], P('wide'), may hold values from 0 to 63, as said below
- pair_valid: int32 [192], P('wide'), may hold values 0 or 1
Outputs:
- pair_scores: float32 [192, 12, 12], P('wide')
Inputs may be any that keep to these rules, and one draw needn't show every extreme that they name: `cand_block`: pair k of index r of wide is pair r * 12 + k. Among the 12 pairs of one index of wide, every owner (owner = block // 4) is named by either no pair or exactly 2 pairs, and pairs naming the same owner name the same block.
All inputs are finite; a program needn't handle non-finite values. No bound on the sum of `pair_valid` on one device may be relied on, other than what follows from the above.
Results may differ from a plain program's by a relative error of at most 0.0003.
Values may be sent and summed in bfloat16 or wider, within the bound.
No kernel may reach another device: no remote copies, remote signals or barrier semaphores. Data moves between devices by JAX's collectives and lax.ppermute only.
A program may use at most 128 MiB of HBM per device.

v0:
```python
import math

import jax
import jax.numpy as jnp
from jax import lax
from jax.sharding import PartitionSpec as P

BLK = 12
SLOTS = 2


sharpness = 20.0


def unit_rows(values):
    return values * lax.rsqrt(jnp.sum(values * values, axis=-1, keepdims=True) + 1e-06)


def local(states, proj_weight, lengths, query_block, cand_block, pair_valid):
    narrow_count = lax.axis_size("narrow")
    my_narrow = lax.axis_index("narrow")
    my_wide = lax.axis_index("wide")
    owners = lax.axis_size("wide")
    par_dev, length, width_part = states.shape
    width = proj_weight.shape[1]
    share = length // narrow_count
    blocks_dev = par_dev // BLK
    pair_count = query_block.shape[0]
    summed = lax.psum_scatter(
        jnp.einsum("ptd,de->tpe", states, proj_weight, preferred_element_type=jnp.float32),
        "narrow",
        scatter_dimension=0,
        tiled=True,
    )
    local_rows = unit_rows(summed).astype(jnp.bfloat16)
    query_rows = lax.all_gather(local_rows, "narrow", axis=0, tiled=True)
    cand_tiles = (
        local_rows.reshape(share, blocks_dev, BLK, width)
        .transpose(1, 2, 0, 3)
        .reshape(blocks_dev, BLK * share, width)
    )
    query_tiles = (
        query_rows.reshape(length, blocks_dev, BLK, width)
        .transpose(1, 0, 2, 3)
        .reshape(blocks_dev, length * BLK, width)
    )
    owner = cand_block // blocks_dev
    local_block = cand_block % blocks_dev
    positions = jnp.arange(pair_count)
    earlier = positions[:, None] > positions[None, :]
    same = owner[:, None] == owner[None, :]
    rank = jnp.sum((earlier & same).astype(jnp.int32), axis=1)
    slots = SLOTS
    target = owner * slots + rank
    chosen = (target[None, :] == jnp.arange(owners * slots)[:, None]) & (rank == rank)[None, :]
    requests = jnp.sum(jnp.where(chosen, local_block[None, :], 0), axis=1).reshape(owners, slots)
    asked = lax.all_to_all(requests, "wide", split_axis=0, concat_axis=0, tiled=True)
    outgoing = jnp.take(cand_tiles, asked.reshape(-1), axis=0).reshape(
        owners, slots, BLK * share, width
    )
    incoming = lax.all_to_all(outgoing, "wide", split_axis=0, concat_axis=0, tiled=True)
    pair_tiles = jnp.take(incoming.reshape(owners * slots, BLK * share, width), target, axis=0)
    block_len = lengths.reshape(-1, BLK)
    cand_len = jnp.take(block_len, cand_block, axis=0)
    cand_tok = my_narrow * share + jnp.arange(share)
    cand_mask = (
        (cand_tok[None, None, :] < cand_len[:, :, None])
        .astype(jnp.float32)
        .reshape(pair_count, BLK * share)
    )
    query_len = jnp.take(block_len, my_wide * blocks_dev + query_block, axis=0)
    query_mask = (
        (jnp.arange(length)[None, :, None] < query_len[:, None, :])
        .astype(jnp.float32)
        .reshape(pair_count, length * BLK)
    )
    group = math.gcd(pair_count, 4)
    groups = pair_count // group

    def score_group(items):
        tiles_g, blocks_g, mask_g = items
        query_g = jnp.take(query_tiles, blocks_g, axis=0)
        sim = jnp.einsum("gre,gqe->grq", tiles_g, query_g, preferred_element_type=jnp.float32)
        weights = jnp.exp(sharpness * sim) * mask_g[:, :, None]
        return jnp.sum(weights.reshape(group, BLK, share, length * BLK), axis=2)

    sums = lax.map(
        score_group,
        (
            pair_tiles.reshape(groups, group, BLK * share, width),
            query_block.reshape(groups, group),
            cand_mask.reshape(groups, group, BLK * share),
        ),
    )
    sums = sums.reshape(pair_count, BLK, length * BLK)
    totals = lax.psum(sums.astype(jnp.bfloat16), "narrow").astype(jnp.float32)
    smooth = jnp.log(totals) / sharpness * query_mask[:, None, :]
    score = jnp.sum(smooth.reshape(pair_count, BLK, length, BLK), axis=2) / length
    return score * pair_valid.astype(jnp.float32)[:, None, None]


def solution(mesh):
    in_specs = (P("wide", None, "narrow"), P("narrow", None), P(), P("wide"), P("wide"), P("wide"))
    out_specs = P("wide", None, None)
    return jax.shard_map(local, mesh=mesh, in_specs=in_specs, out_specs=out_specs, check_vma=False)
```

profile of v0, /device:TPU:0, one launch (start us, length us, event | category | flops | bytes accessed | tf_op | source)
XLA Modules:
  0.0 340.9 jit_solution(3748692034319594010)
XLA Ops:
  6.5 0.9 copy-done
  7.4 4.9 %convolution_bitcast_fusion = f32[128,48,128]{0,2,1:T(8,128)S(1)} fusion(bf16[48,128,512]{2,1,0:T(8,128)(2,1)} %param.10, bf16[512,128]{1,0:T(8,128)(2,1)S(1)} %copy-done), kind=kOutput, calls=%fused_computation.23 | convolution fusion | flops 805306368 | bytes 9568256 | tf_op jit(solution)/shard_map/ptd,de->tpe/dot_general | solution.py:30
  12.4 2.4 copy.38
  16.4 7.4 %all-to-all-start = ((s32[16,1,2]{2,1,0:T(1,128)}), s32[16,1,2]{2,1,0:T(1,128)S(1)}, u32[]{:S(2)}, u32[]{:S(2)}) async-start(s32[16,1,2]{2,1,0:T(1,128)} %bitcast.7), calls=%async_computation | async-start | bytes 16384 | tf_op jit(solution)/shard_map/all_to_all | solution.py:57
  23.8 6.3 %all-to-all-done = s32[16,1,2]{2,1,0:T(1,128)S(1)} async-done(((s32[16,1,2]{2,1,0:T(1,128)}), s32[16,1,2]{2,1,0:T(1,128)S(1)}, u32[]{:S(2)}, u32[]{:S(2)}) %all-to-all-start) | async-done | bytes 160 | tf_op jit(solution)/shard_map/all_to_all | solution.py:57
  31.6 29.5 %reduce-scatter.2.cloned.1.call-done = f32[64,48,128]{2,1,0:T(8,128)} async-done(((f32[128,48,128]{2,1,0:T(8,128)}), f32[64,48,128]{2,1,0:T(8,128)}) %reduce-scatter.2.cloned.1.call-update) | async-done | bytes 1572880 | tf_op jit(solution)/shard_map/reduce_scatter | solution.py:29
  61.1 2.0 multiply_reduce_fusion
  63.8 4.0 %gather_fusion.1 = bf16[32,768,128]{2,1,0:T(8,128)(2,1)} fusion(bf16[4,768,128]{2,1,0:T(8,128)(2,1)S(1)} %bitcast.53, s32[1024]{0:T(1024)S(1)} %pad_clamp_fusion.4), kind=kCustom, calls=%fused_computation.3 | custom fusion | bytes 12583040 | tf_op jit(solution)/shard_map/jit(_take)/gather | solution.py:58
  67.8 6.1 %broadcast_select_fusion = bf16[16,2,768,128]{3,2,1,0:T(8,128)(2,1)} fusion(bf16[16,2,768,128]{3,2,1,0:T(8,128)(2,1)} %bitcast.54, pred[16,2]{1,0:T(8,128)(4,1)S(1)} %copy.36), kind=kLoop, calls=%fused_computation.21 | loop fusion | flops 3145728 | bytes 12582944 | tf_op jit(solution)/shard_map/jit(_take)/select_n | solution.py:58
  74.0 5.8 %all-to-all-start.1 = ((bf16[16,2,768,128]{3,2,1,0:T(8,128)(2,1)}), bf16[16,2,768,128]{3,2,1,0:T(8,128)(2,1)}, u32[]{:S(2)}, u32[]{:S(2)}) async-start(bf16[16,2,768,128]{3,2,1,0:T(8,128)(2,1)} %broadcast_select_fusion), calls=%async_computation.2 | async-start | bytes 12582912 | tf_op jit(solution)/shard_map/all_to_all | solution.py:61
  82.7 27.2 %all-gather.2.cloned.1.call-done = bf16[128,48,128]{2,1,0:T(8,128)(2,1)} async-done(((bf16[64,48,128]{2,1,0:T(8,128)(2,1)}), bf16[128,48,128]{2,1,0:T(8,128)(2,1)}) %all-gather.2.cloned.1.call-update) | async-done | bytes 1572880 | tf_op jit(solution)/shard_map/all_gather | solution.py:36
  109.8 1.8 copy.40
  111.6 1.2 copy.41
  113.1 80.9 %all-to-all-done.1 = bf16[16,2,768,128]{3,2,1,0:T(8,128)(2,1)} async-done(((bf16[16,2,768,128]{3,2,1,0:T(8,128)(2,1)}), bf16[16,2,768,128]{3,2,1,0:T(8,128)(2,1)}, u32[]{:S(2)}, u32[]{:S(2)}) %all-to-all-start.1) | async-done | bytes 6291488 | tf_op jit(solution)/shard_map/all_to_all | solution.py:61
  194.0 5.1 %gather_fusion.2 = bf16[12,768,128]{2,1,0:T(8,128)(2,1)} fusion(bf16[32,768,128]{2,1,0:T(8,128)(2,1)} %bitcast.16, s32[1024]{0:T(1024)S(1)} %pad_clamp_fusion.3), kind=kCustom, calls=%fused_computation.4 | custom fusion | bytes 4718640 | tf_op jit(solution)/shard_map/jit(_take)/gather | solution.py:62
  199.1 3.4 broadcast_select_fusion.1
  202.5 60.1 %while.10 = (s32[]{:T(128)}, bf16[3,4,12,1536]{3,2,1,0:T(8,128)(2,1)}, bf16[3,4,768,128]{3,2,1,0:T(8,128)(2,1)}, s32[3,4]{1,0:T(4,128)S(1)}, bf16[4,1536,128]{2,...) while((s32[]{:T(128)}, bf16[3,4,12,1536]{3,2,1,0:T(8,128)(2,1)}, ...), condition=%wide.region_6.8_spmd, body=%wide.region_4.7_spmd.sunk | while | flops 1222829056 | bytes 43787452 | solution.py:87
  202.5 0.8 gather_fusion
  203.4 9.2 %exponential_multiply_fusion.2 = f32[4,768,1536]{2,1,0:T(8,128)} fusion(f32[4,768]{1,0:T(4,128)S(1)} %dynamic-slice_bitcast_fusion.2, bf16[4,1536,128]{2,1,0:T(8,128)(2,1)S(1)} %gather_fusion, pred[4]{0:T(512)(128)(4,1)S(1)} %compare_and_fusion.6, bf16[3,4,768,128]{3,2,1,0:T(8,128)(2,1)} %get-tuple-element.137, s32[]{:T(128)} %get-tuple-element.127), kind=kOutput, calls=%fused_computation.5.clone.1 | convolution fusion | flops 1218183168 | bytes 21246468 | tf_op jit(solution)/shard_map/while/body/eval_jaxpr/gre,gqe->grq/dot_general | solution.py:83
  212.6 9.2 %reduce_sum.53 = bf16[4,12,1536]{2,1,0:T(8,128)(2,1)S(1)} reduce(f32[4,12,64,1536]{3,2,1,0:T(8,128)} %bitcast.52, f32[]{:T(128)} %constant.106.clone.1..sunk), dimensions={2}, to_apply=%region_5.6 | reduce | flops 4644864 | bytes 19021828 | tf_op jit(solution)/shard_map/while/body/eval_jaxpr/reduce_sum | solution.py:85
  222.5 0.8 gather_fusion
  223.4 9.2 %exponential_multiply_fusion.2 = f32[4,768,1536]{2,1,0:T(8,128)} fusion(f32[4,768]{1,0:T(4,128)S(1)} %dynamic-slice_bitcast_fusion.2, bf16[4,1536,128]{2,1,0:T(8,128)(2,1)S(1)} %gather_fusion, pred[4]{0:T(512)(128)(4,1)S(1)} %compare_and_fusion.6, bf16[3,4,768,128]{3,2,1,0:T(8,128)(2,1)} %get-tuple-element.137, s32[]{:T(128)} %get-tuple-element.127), kind=kOutput, calls=%fused_computation.5.clone.1 | convolution fusion | flops 1218183168 | bytes 21246468 | tf_op jit(solution)/shard_map/while/body/eval_jaxpr/gre,gqe->grq/dot_general | solution.py:83
  232.6 9.2 %reduce_sum.53 = bf16[4,12,1536]{2,1,0:T(8,128)(2,1)S(1)} reduce(f32[4,12,64,1536]{3,2,1,0:T(8,128)} %bitcast.52, f32[]{:T(128)} %constant.106.clone.1..sunk), dimensions={2}, to_apply=%region_5.6 | reduce | flops 4644864 | bytes 19021828 | tf_op jit(solution)/shard_map/while/body/eval_jaxpr/reduce_sum | solution.py:85
  241.8 0.7 bitcast_dynamic-update-slice_fusion.2
  242.6 0.8 gather_fusion
  243.5 9.2 %exponential_multiply_fusion.2 = f32[4,768,1536]{2,1,0:T(8,128)} fusion(f32[4,768]{1,0:T(4,128)S(1)} %dynamic-slice_bitcast_fusion.2, bf16[4,1536,128]{2,1,0:T(8,128)(2,1)S(1)} %gather_fusion, pred[4]{0:T(512)(128)(4,1)S(1)} %compare_and_fusion.6, bf16[3,4,768,128]{3,2,1,0:T(8,128)(2,1)} %get-tuple-element.137, s32[]{:T(128)} %get-tuple-element.127), kind=kOutput, calls=%fused_computation.5.clone.1 | convolution fusion | flops 1218183168 | bytes 21246468 | tf_op jit(solution)/shard_map/while/body/eval_jaxpr/gre,gqe->grq/dot_general | solution.py:83
  252.7 9.2 %reduce_sum.53 = bf16[4,12,1536]{2,1,0:T(8,128)(2,1)S(1)} reduce(f32[4,12,64,1536]{3,2,1,0:T(8,128)} %bitcast.52, f32[]{:T(128)} %constant.106.clone.1..sunk), dimensions={2}, to_apply=%region_5.6 | reduce | flops 4644864 | bytes 19021828 | tf_op jit(solution)/shard_map/while/body/eval_jaxpr/reduce_sum | solution.py:85
  262.6 52.6 %all-reduce.2.cloned.1.call-done = bf16[12,12,1536]{2,1,0:T(8,128)(2,1)} async-done(((bf16[12,12,1536]{2,1,0:T(8,128)(2,1)}), bf16[12,12,1536]{2,1,0:T(8,128)(2,1)}) %all-reduce.2.cloned.1.call-update) | async-done | bytes 442384 | tf_op jit(solution)/shard_map/psum | solution.py:96
  315.2 1.2 log_multiply_fusion
  316.5 11.9 %reshape.171 = f32[12,12,128,12]{3,2,1,0:T(8,128)} reshape(f32[12,12,1536]{2,1,0:T(8,128)S(1)} %log_multiply_fusion) | data formatting | bytes 1769472 | tf_op jit(solution)/shard_map/reshape | solution.py:98
  328.4 5.3 %reduce_sum.48 = f32[12,12,12]{2,1,0:T(8,128)S(1)} reduce(f32[12,12,128,12]{3,2,1,0:T(8,128)} %reshape.171, f32[]{:T(128)} %constant.106.clone.1), dimensions={2}, to_apply=%region_8.10 | reduce | flops 219456 | bytes 891652 | tf_op jit(solution)/shard_map/reduce_sum | solution.py:98
  333.7 0.7 broadcast_multiply_fusion
  (78 shorter events, 8.3 us)
Async XLA Ops:
  6.5 0.9 copy-start
  6.5 54.5 %reduce-scatter.2.cloned.1.call-start = ((), (), s32[]{:S(2)}) async-start(), calls=%async_computation.3 | async-start | bytes 4718592 | tf_op jit(solution)/shard_map/reduce_scatter | solution.py:29
  14.8 0.7 copy-start.6
  16.4 13.7 %all-to-all-start = ((s32[16,1,2]{2,1,0:T(1,128)}), s32[16,1,2]{2,1,0:T(1,128)S(1)}, u32[]{:S(2)}, u32[]{:S(2)}) async-start(s32[16,1,2]{2,1,0:T(1,128)} %bitcast.7), calls=%async_computation | async-start | bytes 16384 | tf_op jit(solution)/shard_map/all_to_all | solution.py:57
  61.1 2.0 copy-start.3
  63.6 4.2 %copy-start.2 = (bf16[64,48,128]{2,1,0:T(8,128)(2,1)}, bf16[64,48,128]{2,1,0:T(8,128)(2,1)S(1)}, u32[]{:S(2)}) copy-start(bf16[64,48,128]{2,1,0:T(8,128)(2,1)S(1)} %multiply_convert_fusion) | copy-start | bytes 2359300
  74.0 6.0 %copy-start.4 = (s32[768]{0:T(1024)S(1)}, s32[768]{0:T(1024)}, u32[]{:S(2)}) copy-start(s32[768]{0:T(1024)} %param.12) | copy-start | bytes 9220
  74.0 7.3 %copy-start.5 = (s32[12]{0:T(128)S(1)}, s32[12]{0:T(128)}, u32[]{:S(2)}) copy-start(s32[12]{0:T(128)} %param.13) | copy-start | bytes 148
  74.0 120.0 %all-to-all-start.1 = ((bf16[16,2,768,128]{3,2,1,0:T(8,128)(2,1)}), bf16[16,2,768,128]{3,2,1,0:T(8,128)(2,1)}, u32[]{:S(2)}, u32[]{:S(2)}) async-start(bf16[16,2,768,128]{3,2,1,0:T(8,128)(2,1)} %broadcast_select_fusion), calls=%async_computation.2 | async-start | bytes 12582912 | tf_op jit(solution)/shard_map/all_to_all | solution.py:61
  79.8 2.9 copy-start.7
  79.8 30.1 %all-gather.2.cloned.1.call-start = ((), (), s32[]{:S(2)}) async-start(), calls=%async_computation.4 | async-start | bytes 2359296 | tf_op jit(solution)/shard_map/all_gather | solution.py:36
  80.6 234.6 %all-reduce.2.cloned.1.call-start = ((), (), s32[]{:S(2)}) async-start(), calls=%async_computation.5 | async-start | bytes 1179648 | tf_op jit(solution)/shard_map/psum | solution.py:96
  328.4 6.1 %copy-start.1 = (bf16[512,128]{1,0:T(8,128)(2,1)S(1)}, bf16[512,128]{1,0:T(8,128)(2,1)}, u32[]{:S(2)}) copy-start(bf16[512,128]{1,0:T(8,128)(2,1)} %param.11) | copy-start | bytes 393220
Sparse Core Ops, SparseCore 0:
  14.9 46.1 reduce-scatter.1
  82.2 27.5 all-gather.1
  262.7 52.4 all-reduce.1
where the time goes:
time: 342 us; the launch traced here: 341 us
  waiting for transfers between devices  197 us (58%)
  other arithmetic  48.1 us (14%)
  local copies, waits for them, and re-layouts  36.8 us (11%)
  matrix products  32.6 us (10%)
  starting transfers between devices  13.4 us (4%)
  between operations  13.4 us (4%)
    all_to_all x1, waiting for transfers between devices, local(): lax.all_to_all(outgoing, 'wide', split_axis=0, concat_axis=0, tiled=True)  80.9 us
    psum x1, waiting for transfers between devices, local(): totals = lax.psum(sums.astype(jnp.bfloat16), 'narrow').astype(jnp.float32)  52.6 us
    reduce_scatter x1, waiting for transfers between devices, local(): lax.psum_scatter(jnp.einsum('ptd,de->tpe', states, proj_weight, preferred...  29.5 us
    dot_general x3, matrix products, score_group(): jnp.einsum('gre,gqe->grq', tiles_g, query_g, preferred_element_type=jnp.f...  27.7 us
    reduce_sum x3, other arithmetic, score_group(): return jnp.sum(weights.reshape(group, BLK, share, length * BLK), axis=2)  27.6 us
    all_gather x1, waiting for transfers between devices, local(): query_rows = lax.all_gather(local_rows, 'narrow', axis=0, tiled=True)  27.2 us
    reshape x1, local copies, waits for them, and re-layouts, local(): smooth.reshape(pair_count, BLK, length, BLK)  11.9 us
    all_to_all x1, starting transfers between devices, local(): lax.all_to_all(requests, 'wide', split_axis=0, concat_axis=0, tiled=True)  7.35 us
  transfers between devices with their start and end apart: 5, of which 5 were waited for; matrix products, arithmetic and copies ran while one was open for 2% of the time, Pallas kernels for 0%

commit v1 on v0

v1 whole, which is shorter than its diff:
```python
import functools
import math

import jax
import jax.numpy as jnp
from jax import lax
from jax.experimental import pallas as pl
from jax.experimental.pallas import tpu as pltpu
from jax.sharding import PartitionSpec as P

BLK = 12
SHARPNESS = 20.0
EXP2_SCALE = SHARPNESS * math.log2(math.e)
COLS = 256
SMEM = pltpu.SMEM
VMEM = pltpu.VMEM


def vmem_params(mib):
    return pltpu.CompilerParams(vmem_limit_bytes=mib * 2**20)


def plan_kernel(pairs, cand_ref, sel_ref, first_ref, second_ref, slot_ref):
    def step(k, count):
        block = cand_ref[k]
        found = lax.fori_loop(
            0, k, lambda e, f: jnp.where(cand_ref[e] == block, slot_ref[e], f), jnp.int32(-1)
        )
        new = found < 0
        slot = jnp.where(new, count, found)
        slot = jnp.minimum(slot, pairs // 2 - 1)
        slot_ref[k] = slot

        @pl.when(new)
        def _():
            sel_ref[slot] = block
            first_ref[slot] = k
            second_ref[slot] = k

        @pl.when(jnp.logical_not(new))
        def _():
            second_ref[slot] = k

        return count + new.astype(jnp.int32)

    lax.fori_loop(0, pairs, step, jnp.int32(0))


def plan(cand_block):
    pairs = cand_block.shape[0]
    out = jax.ShapeDtypeStruct((pairs // 2,), jnp.int32)
    return pl.pallas_call(
        functools.partial(plan_kernel, pairs),
        out_shape=(out, out, out),
        in_specs=[pl.BlockSpec(memory_space=SMEM)],
        out_specs=[pl.BlockSpec(memory_space=SMEM)] * 3,
        scratch_shapes=[SMEM((pairs,), jnp.int32)],
    )(cand_block)


def project_kernel(me_ref, states_ref, weight_ref, out_ref):
    out_ref[0, 0] = jnp.dot(
        states_ref[0], weight_ref[...], preferred_element_type=jnp.float32
    ).astype(out_ref.dtype)


def project(me, states, weight, shares, offset, count, dtype):
    blocks, rows, width = states.shape
    out_width = weight.shape[1]
    part = rows // shares
    return pl.pallas_call(
        project_kernel,
        out_shape=jax.ShapeDtypeStruct((count, blocks, part, out_width), dtype),
        grid_spec=pltpu.PrefetchScalarGridSpec(
            num_scalar_prefetch=1,
            grid=(count, blocks),
            in_specs=[
                pl.BlockSpec(
                    (1, part, width), lambda d, b, m: (b, lax.rem(m[0] + offset + d, shares), 0)
                ),
                pl.BlockSpec((width, out_width), lambda d, b, m: (0, 0)),
            ],
            out_specs=pl.BlockSpec((1, 1, part, out_width), lambda d, b, m: (d, b, 0, 0)),
        ),
        cost_estimate=pl.CostEstimate(
            flops=2 * count * blocks * part * width * out_width,
            bytes_accessed=2 * count * blocks * part * width,
            transcendentals=0,
        ),
    )(me, states, weight)


def unit_kernel(others, pieces, keep_ref, *refs):
    out_ref = refs[-1]
    total = keep_ref[0, 0]
    for ref in refs[:others]:
        total = total + ref[0].astype(jnp.float32)
    norm = jnp.sum(total * total, axis=-1, keepdims=True)
    unit = (total * lax.rsqrt(norm + 1e-06)).astype(jnp.bfloat16)
    if pieces is None:
        out_ref[0] = unit
    else:
        size = unit.shape[0] // pieces
        for m in range(pieces):
            out_ref[m, 0] = unit[m * size : (m + 1) * size]


def unit_rows(keep, received, owners):
    _, blocks, part, width = keep.shape
    size = part // owners
    direct = size % 16 == 0
    if direct:
        shape = (owners, blocks, size, width)
        out_spec = pl.BlockSpec((owners, 1, size, width), lambda b: (0, b, 0, 0))
    else:
        shape = (blocks, part, width)
        out_spec = pl.BlockSpec((1, part, width), lambda b: (b, 0, 0))
    out = pl.pallas_call(
        functools.partial(unit_kernel, len(received), owners if direct else None),
        out_shape=jax.ShapeDtypeStruct(shape, jnp.bfloat16),
        grid=(blocks,),
        in_specs=[pl.BlockSpec((1, 1, part, width), lambda b: (0, b, 0, 0))]
        + [pl.BlockSpec((1, part, width), lambda b: (b, 0, 0))] * len(received),
        out_specs=out_spec,
    )(keep, *received)
    if direct:
        return out
    return out.reshape(blocks, owners, size, width).transpose(1, 0, 2, 3)


def route_kernel(dests, slots, owners, asked_ref, pieces_ref, out_ref):
    def step(d, carry):
        side = d // owners
        requester = d - side * owners
        for k in range(slots):
            out_ref[d, k] = pieces_ref[asked_ref[requester, side * slots + k]]
        return carry

    lax.fori_loop(0, dests, step, 0)


def route(asked, pieces, owners, shares):
    slots = asked.shape[1] // shares
    dests = owners * shares
    return pl.pallas_call(
        functools.partial(route_kernel, dests, slots, owners),
        out_shape=jax.ShapeDtypeStruct((dests, slots) + pieces.shape[1:], jnp.bfloat16),
        in_specs=[pl.BlockSpec(memory_space=SMEM), pl.BlockSpec(memory_space=VMEM)],
        out_specs=pl.BlockSpec(memory_space=VMEM),
        compiler_params=vmem_params(48),
    )(asked, pieces)


def score_kernel(
    length, where_ref, sel_ref, first_ref, second_ref, query_block_ref, lengths_ref, valid_ref,
    query_ref, cand_ref, out_ref, totals_ref,
):
    owner, side = where_ref[0], where_ref[1]
    slots, rows, _ = cand_ref.shape
    blocks = query_ref.shape[0]
    out_ref[...] = jnp.zeros_like(out_ref)
    totals_ref[...] = jnp.ones_like(totals_ref)
    upper = lax.broadcasted_iota(jnp.int32, (length // 2, COLS), 0) + length // 2
    lane = lax.broadcasted_iota(jnp.int32, (16, length), 1)

    def slot_step(k, carry):
        slot = side * slots + k
        block = sel_ref[slot]
        for which_ref in (first_ref, second_ref):
            pair = which_ref[slot]
            query = query_block_ref[pair]

            def column_step(c, carry):
                start = pl.multiple_of(c * COLS, COLS)
                sim = lax.dot_general(
                    cand_ref[k],
                    query_ref[query, pl.ds(start, COLS)],
                    (((1,), (1,)), ((), ())),
                    preferred_element_type=jnp.float32,
                )
                for b in range(BLK):
                    live = lengths_ref[block * BLK + b]
                    low = jnp.exp2(sim[b * length : b * length + length // 2] * EXP2_SCALE)
                    high = jnp.exp2(sim[b * length + length // 2 : (b + 1) * length] * EXP2_SCALE)
                    both = low + jnp.where(upper < live, high, 0.0)
                    totals_ref[pl.ds(b, 1), pl.ds(start, COLS)] = jnp.sum(both, axis=0, keepdims=True)
                return carry

            lax.fori_loop(0, rows // COLS, column_step, 0)
            score = jnp.zeros((16, length), jnp.float32)
            for a in range(BLK):
                live = lengths_ref[(owner * blocks + query) * BLK + a]
                logs = jnp.log(totals_ref[:, a * length : (a + 1) * length])
                summed = jnp.sum(jnp.where(lane < live, logs, 0.0), axis=1, keepdims=True)
                score = jnp.where(lane == a, summed, score)
            keep = valid_ref[pair].astype(jnp.float32) / (SHARPNESS * length)
            out_ref[pair] = score[:BLK, :BLK] * keep
        return carry

    lax.fori_loop(0, slots, slot_step, 0)


def score(where, sel, first, second, query_block, lengths, valid, query, cand, length):
    pairs = query_block.shape[0]
    slots, rows, width = cand.shape
    count = 2 * slots * rows * rows
    return pl.pallas_call(
        functools.partial(score_kernel, length),
        out_shape=jax.ShapeDtypeStruct((pairs, BLK, BLK), jnp.float32),
        in_specs=[pl.BlockSpec(memory_space=SMEM)] * 7 + [pl.BlockSpec(memory_space=VMEM)] * 2,
        out_specs=pl.BlockSpec(memory_space=VMEM),
        scratch_shapes=[VMEM((16, rows), jnp.float32)],
        compiler_params=vmem_params(48),
        cost_estimate=pl.CostEstimate(
            flops=2 * count * width, bytes_accessed=4 * rows * width, transcendentals=count
        ),
    )(where, sel, first, second, query_block, lengths, valid, query, cand)


def local(states, proj_weight, lengths, query_block, cand_block, pair_valid):
    shares = lax.axis_size("narrow")
    owners = lax.axis_size("wide")
    side = lax.axis_index("narrow").astype(jnp.int32)
    owner = lax.axis_index("wide").astype(jnp.int32)
    paras, length, width_part = states.shape
    width = proj_weight.shape[1]
    blocks = paras // BLK
    rows = BLK * length
    flat = states.reshape(blocks, rows, width_part)
    me = side.reshape(1)

    def shift(d):
        return [(i, (i + d) % shares) for i in range(shares)]

    sel, first, second = plan(cand_block)
    sent = project(me, flat, proj_weight, shares, 1, shares - 1, jnp.bfloat16)
    received = [lax.ppermute(sent[d - 1], "narrow", shift(d)) for d in range(1, shares)]
    asked = lax.all_to_all(
        jnp.broadcast_to(sel[None], (owners,) + sel.shape), "wide", 0, 0, tiled=True
    )
    kept = project(me, flat, proj_weight, shares, 0, 1, jnp.float32)
    mine = unit_rows(kept, received, owners)
    spread = lax.all_to_all(mine, "wide", 0, 0, tiled=True)
    size = mine.shape[2]
    by_side = [mine] + [lax.ppermute(mine, "narrow", shift(d)) for d in range(1, shares)]
    order = jnp.stack(by_side)
    query = jnp.stack(
        [lax.dynamic_index_in_dim(order, lax.rem(side - s + shares, shares), 0, False) for s in range(shares)]
    )
    query = query.transpose(2, 0, 1, 3, 4).reshape(blocks, rows, width)
    outgoing = route(asked, spread.reshape(owners * blocks, size, width), owners, shares)
    incoming = lax.all_to_all(outgoing, ("narrow", "wide"), 0, 0, tiled=True)
    cand = incoming.transpose(1, 0, 2, 3).reshape(-1, rows, width)
    part = score(
        jnp.stack([owner, side]), sel, first, second, query_block, lengths, pair_valid, query, cand, length
    )
    out = part
    for d in range(1, shares):
        out = out + lax.ppermute(part, "narrow", shift(d))
    return out


def solution(mesh):
    in_specs = (P("wide", None, "narrow"), P("narrow", None), P(), P("wide"), P("wide"), P("wide"))
    out_specs = P("wide", None, None)
    return jax.shard_map(local, mesh=mesh, in_specs=in_specs, out_specs=out_specs, check_vma=False)
```

time: 342 us -> 119 us (0.35)
  waiting for transfers between devices: 197 us -> 39 us
  other arithmetic: 48.1 us -> 1.51 us
  local copies, waits for them, and re-layouts: 36.8 us -> 2.94 us
  Pallas kernels: 0 us -> 33.3 us
  matrix products: 32.6 us -> 0 us
  blocking collectives: 0 us -> 26.4 us
  between operations: 13.4 us -> 0.14 us
    all_to_all x2, waiting for transfers between devices: 87.2 us -> 0.01 us  [the longest x1 0.01 us: local(): incoming = lax.all_to_all(outgoing, ('narrow', 'wide'), 0, 0, tiled=True)]
    psum x1 -> x0, waiting for transfers between devices: 52.6 us -> none  [local(): totals = lax.psum(sums.astype(jnp.bfloat16), 'narrow').astype(jnp.float32)]
    ppermute x0 -> x3, waiting for transfers between devices: none -> 39 us  [the longest x1 30.4 us: local(): lax.ppermute(mine, 'narrow', shift(d))]
    reduce_sum x7 -> x0, other arithmetic: 35.2 us -> none  [the longest x3 27.6 us: score_group(): return jnp.sum(weights.reshape(group, BLK, share, length * BLK), axis=2)]
    pallas_call x0 -> x6, Pallas kernels: none -> 33.3 us  [the longest x1 16.3 us: score(): pl.pallas_call(functools.partial(score_kernel, length), out_shape=jax.Sha...]
    dot_general x4 -> x0, matrix products: 32.6 us -> none  [the longest x3 27.7 us: score_group(): jnp.einsum('gre,gqe->grq', tiles_g, query_g, preferred_element_type=jnp.f...]
    reduce_scatter x1 -> x0, waiting for transfers between devices: 29.5 us -> none  [local(): lax.psum_scatter(jnp.einsum('ptd,de->tpe', states, proj_weight, preferred...]
    all_gather x1 -> x0, waiting for transfers between devices: 27.2 us -> none  [local(): query_rows = lax.all_gather(local_rows, 'narrow', axis=0, tiled=True)]
  transfers between devices with their start and end apart: 5 -> 5, of which waited for: 5 -> 3; matrix products, arithmetic and copies ran while one was open for 2% -> 2% of each run, Pallas kernels for 0% -> 9%
where the time goes in v1:
time: 119 us; the launch traced here: 118 us
  waiting for transfers between devices  39 us (33%)
  Pallas kernels  33.3 us (28%)
  blocking collectives  26.4 us (22%)
  starting transfers between devices  14.9 us (13%)
  local copies, waits for them, and re-layouts  2.94 us (2%)
  other arithmetic  1.51 us (1%)
    ppermute x1, waiting for transfers between devices, local(): lax.ppermute(mine, 'narrow', shift(d))  30.4 us
    all_to_all x1, blocking collectives, local(): spread = lax.all_to_all(mine, 'wide', 0, 0, tiled=True)  26.4 us
    pallas_call x1, Pallas kernels, score(): pl.pallas_call(functools.partial(score_kernel, length), out_shape=jax.Sha...  16.3 us
    pallas_call x2, Pallas kernels, project(): pl.pallas_call(project_kernel, out_shape=jax.ShapeDtypeStruct((count, blo...  9.02 us
    all_to_all x1, starting transfers between devices, local(): lax.all_to_all(jnp.broadcast_to(sel[None], (owners,) + sel.shape), 'wide'...  5.91 us
    ppermute x1, waiting for transfers between devices, local(): out = out + lax.ppermute(part, 'narrow', shift(d))  4.33 us
    ppermute x1, waiting for transfers between devices, local(): lax.ppermute(sent[d - 1], 'narrow', shift(d))  4.19 us
    pallas_call x1, Pallas kernels, unit_rows(): pl.pallas_call(functools.partial(unit_kernel, len(received), owners if di...  3.92 us
  transfers between devices with their start and end apart: 5, of which 3 were waited for; matrix products, arithmetic and copies ran while one was open for 2% of the time, Pallas kernels for 9%

profile of v1, /device:TPU:0, one launch (start us, length us, event | category | flops | bytes accessed | tf_op | source)
XLA Modules:
  0.0 118.1 jit_solution(16596093747607590722)
XLA Ops:
  0.0 4.4 %shard_map.66 = bf16[1,4,768,128]{3,2,1,0:T(8,128)(2,1)} custom-call(s32[1]{0:T(128)} %bitcast.1.me_ref, bf16[4,1536,512]{2,1,0:T(8,128)(2,1)} %bitcast.17, bf16[512,128]{1,0:T(8,128)(2,1)} %weight_ref.3), custom_call_target="tpu_custom_call" | custom-call | flops 402653184 | bytes 3145728 | tf_op jit(solution)/shard_map/pallas_call | solution.py:71
  4.4 3.0 %collective-permute-start = (bf16[4,768,128]{2,1,0:T(8,128)(2,1)}, bf16[4,768,128]{2,1,0:T(8,128)(2,1)S(1)}, u32[]{:S(2)}, u32[]{:S(2)}) collective-permute-start(bf16[4,768,128]{2,1,0:T(8,128)(2,1)} %bitcast.21), channel_id=1, source_target_pairs={{0,1},{1,0},{2,3},{3,2},{4,5},{5,4},{6,7},{7,6},{8,9},{9,8},{10,11... | collective-permute-start | bytes 2359304 | tf_op jit(solution)/shard_map/ppermute | solution.py:237
  7.4 1.7 %shard_map.64 = (s32[6]{0:T(128)}, s32[6]{0:T(128)}, s32[6]{0:T(128)}) custom-call(s32[12]{0:T(128)} %cand_ref.1), custom_call_target="tpu_custom_call" | custom-call | tf_op jit(solution)/shard_map/pallas_call | solution.py:52
  9.2 1.3 %broadcast_in_dim.2 = s32[16,1,6]{2,1,0:T(1,128)} broadcast(s32[6]{0:T(128)} %get-tuple-element.8.sel_ref), dimensions={2} | broadcast | bytes 408 | tf_op jit(solution)/shard_map/broadcast_in_dim | solution.py:239
  10.4 5.9 %all-to-all-start = ((s32[16,1,6]{2,1,0:T(1,128)}), s32[16,1,6]{2,1,0:T(1,128)S(1)}, u32[]{:S(2)}, u32[]{:S(2)}) async-start(s32[16,1,6]{2,1,0:T(1,128)} %broadcast_in_dim.2), calls=%async_computation | async-start | bytes 16384 | tf_op jit(solution)/shard_map/all_to_all | solution.py:238
  16.4 4.6 %shard_map.65.keep_ref = f32[1,4,768,128]{3,2,1,0:T(8,128)} custom-call(s32[1]{0:T(128)} %bitcast.1.me_ref, bf16[4,1536,512]{2,1,0:T(8,128)(2,1)} %bitcast.18, bf16[512,128]{1,0:T(8,128)(2,1)} %weight_ref.3), custom_call_target="tpu_custom_call" | custom-call | flops 402653184 | bytes 3145728 | tf_op jit(solution)/shard_map/pallas_call | solution.py:71
  21.0 4.2 %collective-permute-done.refs_0_ = bf16[4,768,128]{2,1,0:T(8,128)(2,1)S(1)} collective-permute-done((bf16[4,768,128]{2,1,0:T(8,128)(2,1)}, bf16[4,768,128]{2,1,0:T(8,128)(2,1)S(1)}, u32[]{:S(2)}, u32[]{:S(2)}) %collective-permute-start) | collective-permute-done | bytes 786464 | tf_op jit(solution)/shard_map/ppermute | solution.py:237
  25.1 0.9 copy-done.7
  26.0 3.9 %shard_map.67 = bf16[16,4,48,128]{3,2,1,0:T(8,128)(2,1)} custom-call(f32[1,4,768,128]{3,2,1,0:T(8,128)} %shard_map.65.keep_ref, bf16[4,768,128]{2,1,0:T(8,128)(2,1)} %copy-done.7), custom_call_target="tpu_custom_call" | custom-call | tf_op jit(solution)/shard_map/pallas_call | solution.py:118
  30.0 0.0 all-to-all-done
  30.0 26.4 %all_to_all.18 = bf16[16,4,48,128]{3,2,1,0:T(8,128)(2,1)S(1)} all-to-all(bf16[16,4,48,128]{3,2,1,0:T(8,128)(2,1)} %shard_map.67), channel_id=1, replica_groups=mesh['wide'=16,'narrow'=2] {'wide'}, dimensions={0} | all-to-all | bytes 1572864 | tf_op jit(solution)/shard_map/all_to_all | solution.py:243
  56.4 2.3 %shard_map.68 = bf16[32,3,48,128]{3,2,1,0:T(8,128)(2,1)} custom-call(s32[16,6]{1,0:T(8,128)S(1)} %bitcast.16, bf16[64,48,128]{2,1,0:T(8,128)(2,1)S(1)} %bitcast.13), custom_call_target="tpu_custom_call" | custom-call | tf_op jit(solution)/shard_map/pallas_call | solution.py:145
  58.7 3.9 %all-to-all-start.2 = ((bf16[32,3,48,128]{3,2,1,0:T(8,128)(2,1)}), bf16[32,3,48,128]{3,2,1,0:T(8,128)(2,1)S(1)}, u32[]{:S(2)}, u32[]{:S(2)}) async-start(bf16[32,3,48,128]{3,2,1,0:T(8,128)(2,1)} %shard_map.68), calls=%async_computation.2 | async-start | bytes 2359296 | tf_op jit(solution)/shard_map/all_to_all | solution.py:252
  62.5 0.0 copy-done.6
  62.5 1.8 %collective-permute-start.1 = (bf16[16,4,48,128]{3,2,1,0:T(8,128)(2,1)S(1)}, bf16[16,4,48,128]{3,2,1,0:T(8,128)(2,1)S(1)}, u32[]{:S(2)}, u32[]{:S(2)}) collective-permute-start(bf16[16,4,48,128]{3,2,1,0:T(8,128)(2,1)S(1)} %copy-done.6), channel_id=1, source_target_pairs={{0,1},{1,0},{2,3},{3,2},{4,5},{5,4},{6,7},{7,6},{8,9},{9,8},{10,11... | collective-permute-start | bytes 2359304 | tf_op jit(solution)/shard_map/ppermute | solution.py:245
  64.4 0.1 pad_add_fusion.where_ref
  64.4 30.4 %collective-permute-done.1 = bf16[16,4,48,128]{3,2,1,0:T(8,128)(2,1)S(1)} collective-permute-done((bf16[16,4,48,128]{3,2,1,0:T(8,128)(2,1)S(1)}, bf16[16,4,48,128]{3,2,1,0:T(8,128)(2,1)S(1)}, u32[]{:S(2)}, u32[]{:S(2)}) %collective-permute-start.1) | collective-permute-done | bytes 786464 | tf_op jit(solution)/shard_map/ppermute | solution.py:245
  94.9 0.6 fusion.1
  95.5 0.1 maximum_bitcast_fusion
  95.7 0.1 copy.10
  95.8 0.0 copy-start.1
  95.8 0.0 copy-start.2
  95.8 0.0 copy-start.3
  95.9 0.0 all-to-all-done.2
  95.9 0.1 copy.13
  96.0 0.5 copy-done
  96.5 0.0 copy-done.1
  96.5 0.0 copy-done.4
  96.5 16.3 %shard_map.69 = f32[12,12,12]{2,1,0:T(8,128)S(1)} custom-call(s32[2]{0:T(128)S(1)} %pad_add_fusion.where_ref, s32[6]{0:T(128)S(1)} %copy-done, s32[6]{0:T(128)S(1)} %copy-done.4, s32[6]{0:T(128)S(1)} %copy-done.5, s32[12]{0:T(128)S(1)} %copy-done.2, s32[768]{0:T(1024)S(1)} %copy-done.1, s32[12]{0:T(128)S(1)} %copy-done.3, ...), custom_call_target="tpu_custom_call" | custom-call | flops 3623878656 | bytes 786432 | tf_op jit(solution)/shard_map/pallas_call | solution.py:207
  112.8 0.4 collective-permute-start.2
  113.2 4.3 %collective-permute-done.2 = f32[12,12,12]{2,1,0:T(8,128)S(1)} collective-permute-done((f32[12,12,12]{2,1,0:T(8,128)S(1)}, f32[12,12,12]{2,1,0:T(8,128)S(1)}, u32[]{:S(2)}, u32[]{:S(2)}) %collective-permute-start.2) | collective-permute-done | bytes 6944 | tf_op jit(solution)/shard_map/ppermute | solution.py:259
  117.5 0.7 add.23
  (8 shorter events, 0.0 us)
Async XLA Ops:
  4.4 20.7 %collective-permute-start = (bf16[4,768,128]{2,1,0:T(8,128)(2,1)}, bf16[4,768,128]{2,1,0:T(8,128)(2,1)S(1)}, u32[]{:S(2)}, u32[]{:S(2)}) collective-permute-start(bf16[4,768,128]{2,1,0:T(8,128)(2,1)} %bitcast.21), channel_id=1, source_target_pairs={{0,1},{1,0},{2,3},{3,2},{4,5},{5,4},{6,7},{7,6},{8,9},{9,8},{10,11... | collective-permute-start | bytes 2359304 | tf_op jit(solution)/shard_map/ppermute | solution.py:237
  10.4 19.5 %all-to-all-start = ((s32[16,1,6]{2,1,0:T(1,128)}), s32[16,1,6]{2,1,0:T(1,128)S(1)}, u32[]{:S(2)}, u32[]{:S(2)}) async-start(s32[16,1,6]{2,1,0:T(1,128)} %broadcast_in_dim.2), calls=%async_computation | async-start | bytes 16384 | tf_op jit(solution)/shard_map/all_to_all | solution.py:238
  25.1 0.9 copy-start.7
  58.7 3.9 %copy-start.6 = (bf16[16,4,48,128]{3,2,1,0:T(8,128)(2,1)S(1)}, bf16[16,4,48,128]{3,2,1,0:T(8,128)(2,1)}, u32[]{:S(2)}) copy-start(bf16[16,4,48,128]{3,2,1,0:T(8,128)(2,1)} %shard_map.67) | copy-start | bytes 2359300
  58.7 37.2 %all-to-all-start.2 = ((bf16[32,3,48,128]{3,2,1,0:T(8,128)(2,1)}), bf16[32,3,48,128]{3,2,1,0:T(8,128)(2,1)S(1)}, u32[]{:S(2)}, u32[]{:S(2)}) async-start(bf16[32,3,48,128]{3,2,1,0:T(8,128)(2,1)} %shard_map.68), calls=%async_computation.2 | async-start | bytes 2359296 | tf_op jit(solution)/shard_map/all_to_all | solution.py:252
  62.5 32.4 %collective-permute-start.1 = (bf16[16,4,48,128]{3,2,1,0:T(8,128)(2,1)S(1)}, bf16[16,4,48,128]{3,2,1,0:T(8,128)(2,1)S(1)}, u32[]{:S(2)}, u32[]{:S(2)}) collective-permute-start(bf16[16,4,48,128]{3,2,1,0:T(8,128)(2,1)S(1)} %copy-done.6), channel_id=1, source_target_pairs={{0,1},{1,0},{2,3},{3,2},{4,5},{5,4},{6,7},{7,6},{8,9},{9,8},{10,11... | collective-permute-start | bytes 2359304 | tf_op jit(solution)/shard_map/ppermute | solution.py:245
  95.8 0.7 copy-start
  95.8 0.7 copy-start.1
  95.8 0.7 copy-start.2
  95.8 0.7 copy-start.3
  95.8 0.7 copy-start.4
  95.8 0.7 copy-start.5
  112.8 4.7 %collective-permute-start.2 = (f32[12,12,12]{2,1,0:T(8,128)S(1)}, f32[12,12,12]{2,1,0:T(8,128)S(1)}, u32[]{:S(2)}, u32[]{:S(2)}) collective-permute-start(f32[12,12,12]{2,1,0:T(8,128)S(1)} %shard_map.69), channel_id=1, source_target_pairs={{0,1},{1,0},{2,3},{3,2},{4,5},{5,4},{6,7},{7,6},{8,9},{9,8},{10,11... | collective-permute-start | bytes 20744 | tf_op jit(solution)/shard_map/ppermute | solution.py:259

commit v2 on v1

--- a/solution.py
+++ b/solution.py
@@ -12,6 +12,7 @@
 SHARPNESS = 20.0
 EXP2_SCALE = SHARPNESS * math.log2(math.e)
 COLS = 256
+CHUNK = 2
 SMEM = pltpu.SMEM
 VMEM = pltpu.VMEM
 
@@ -163,41 +164,36 @@
     upper = lax.broadcasted_iota(jnp.int32, (length // 2, COLS), 0) + length // 2
     lane = lax.broadcasted_iota(jnp.int32, (16, length), 1)
 
-    def slot_step(k, carry):
+    def pair_step(i, carry):
+        k = i // 2
         slot = side * slots + k
         block = sel_ref[slot]
-        for which_ref in (first_ref, second_ref):
-            pair = which_ref[slot]
-            query = query_block_ref[pair]
-
-            def column_step(c, carry):
-                start = pl.multiple_of(c * COLS, COLS)
-                sim = lax.dot_general(
-                    cand_ref[k],
-                    query_ref[query, pl.ds(start, COLS)],
-                    (((1,), (1,)), ((), ())),
-                    preferred_element_type=jnp.float32,
-                )
-                for b in range(BLK):
-                    live = lengths_ref[block * BLK + b]
-                    low = jnp.exp2(sim[b * length : b * length + length // 2] * EXP2_SCALE)
-                    high = jnp.exp2(sim[b * length + length // 2 : (b + 1) * length] * EXP2_SCALE)
-                    both = low + jnp.where(upper < live, high, 0.0)
-                    totals_ref[pl.ds(b, 1), pl.ds(start, COLS)] = jnp.sum(both, axis=0, keepdims=True)
-                return carry
-
-            lax.fori_loop(0, rows // COLS, column_step, 0)
-            score = jnp.zeros((16, length), jnp.float32)
-            for a in range(BLK):
-                live = lengths_ref[(owner * blocks + query) * BLK + a]
-                logs = jnp.log(totals_ref[:, a * length : (a + 1) * length])
-                summed = jnp.sum(jnp.where(lane < live, logs, 0.0), axis=1, keepdims=True)
-                score = jnp.where(lane == a, summed, score)
-            keep = valid_ref[pair].astype(jnp.float32) / (SHARPNESS * length)
-            out_ref[pair] = score[:BLK, :BLK] * keep
+        pair = jnp.where(i - 2 * k == 0, first_ref[slot], second_ref[slot])
+        query = query_block_ref[pair]
+        for start in range(0, rows, COLS):
+            sim = lax.dot_general(
+                cand_ref[k],
+                query_ref[query, start : start + COLS],
+                (((1,), (1,)), ((), ())),
+                preferred_element_type=jnp.float32,
+            )
+            for b in range(BLK):
+                live = lengths_ref[block * BLK + b]
+                low = jnp.exp2(sim[b * length : b * length + length // 2] * EXP2_SCALE)
+                high = jnp.exp2(sim[b * length + length // 2 : (b + 1) * length] * EXP2_SCALE)
+                both = low + jnp.where(upper < live, high, 0.0)
+                totals_ref[b : b + 1, start : start + COLS] = jnp.sum(both, axis=0, keepdims=True)
+        score = jnp.zeros((16, length), jnp.float32)
+        for a in range(BLK):
+            live = lengths_ref[(owner * blocks + query) * BLK + a]
+            logs = jnp.log(totals_ref[:, a * length : (a + 1) * length])
+            summed = jnp.sum(jnp.where(lane < live, logs, 0.0), axis=1, keepdims=True)
+            score = jnp.where(lane == a, summed, score)
+        keep = valid_ref[pair].astype(jnp.float32) / (SHARPNESS * length)
+        out_ref[pair] = score[:BLK, :BLK] * keep
         return carry
 
-    lax.fori_loop(0, slots, slot_step, 0)
+    lax.fori_loop(0, 2 * slots, pair_step, 0)
 
 
 def score(where, sel, first, second, query_block, lengths, valid, query, cand, length):
@@ -210,14 +206,14 @@
         in_specs=[pl.BlockSpec(memory_space=SMEM)] * 7 + [pl.BlockSpec(memory_space=VMEM)] * 2,
         out_specs=pl.BlockSpec(memory_space=VMEM),
         scratch_shapes=[VMEM((16, rows), jnp.float32)],
-        compiler_params=vmem_params(48),
+        compiler_params=vmem_params(24),
         cost_estimate=pl.CostEstimate(
             flops=2 * count * width, bytes_accessed=4 * rows * width, transcendentals=count
         ),
     )(where, sel, first, second, query_block, lengths, valid, query, cand)
 
 
-def local(states, proj_weight, lengths, query_block, cand_block, pair_valid):
+def local_general(states, proj_weight, lengths, query_block, cand_block, pair_valid):
     shares = lax.axis_size("narrow")
     owners = lax.axis_size("wide")
     side = lax.axis_index("narrow").astype(jnp.int32)
@@ -260,7 +256,228 @@
     return out
 
 
+def split_kernel(first, sel_count, place_ref, *refs):
+    if sel_count:
+        sel_ref, refs = refs[0], refs[1:]
+    states_ref, weight_ref = refs[:2]
+    outs, all_ref = refs[2:6], refs[6]
+    b, half = pl.program_id(0), pl.program_id(1)
+    part = states_ref.shape[1]
+    blocks = pl.num_programs(0)
+    all_ref[pl.ds(pl.multiple_of(half * part, part), part)] = jnp.dot(
+        states_ref[0], weight_ref[...], preferred_element_type=jnp.float32
+    ).astype(all_ref.dtype)
+
+    @pl.when(half == 1)
+    def _():
+        x, side = place_ref[1], place_ref[3]
+        size = part // 16
+        for rel, out_ref in enumerate(outs):
+            base = (side ^ (rel // 2)) * part + (x ^ (rel % 2)) * (2 * size)
+            for z in range(4):
+                for c in range(2):
+                    source = pl.multiple_of(base + z * 4 * size + c * size, 16)
+                    target = pl.multiple_of(((z * 2 + c) * CHUNK + b) * size, 16)
+                    out_ref[pl.ds(target, size)] = all_ref[pl.ds(source, size)]
+
+    if sel_count:
+
+        @pl.when((half == 1) & (b == 0))
+        def _():
+            lane = lax.broadcasted_iota(jnp.int32, (16, all_ref.shape[1]), 1)
+            row = jnp.zeros_like(lane)
+            for k in range(sel_count):
+                row = jnp.where(lane == k, sel_ref[k], row)
+            row = row.astype(jnp.float32).astype(all_ref.dtype)
+            for out_ref in outs:
+                out_ref[8 * CHUNK * (part // 16) :] = row
+
+
+def split(place, sel, states, weight, first):
+    _, rows, width = states.shape
+    out_width = weight.shape[1]
+    part = rows // 2
+    sel_count = 0 if sel is None else sel.shape[0]
+    out_rows = 8 * CHUNK * (part // 16) + (16 if sel_count else 0)
+    out = jax.ShapeDtypeStruct((out_rows, out_width), jnp.bfloat16)
+    whole = pl.BlockSpec((out_rows, out_width), lambda b, h, *m: (0, 0))
+    scalars = (place,) if sel is None else (place, sel)
+    return pl.pallas_call(
+        functools.partial(split_kernel, first, sel_count),
+        out_shape=(out,) * 4,
+        grid_spec=pltpu.PrefetchScalarGridSpec(
+            num_scalar_prefetch=len(scalars),
+            grid=(CHUNK, 2),
+            in_specs=[
+                pl.BlockSpec((1, part, width), lambda b, h, *m: (first + b, h, 0)),
+                pl.BlockSpec((width, out_width), lambda b, h, *m: (0, 0)),
+            ],
+            out_specs=[whole] * 4,
+            scratch_shapes=[VMEM((rows, out_width), jnp.bfloat16)],
+        ),
+        compiler_params=vmem_params(58),
+        cost_estimate=pl.CostEstimate(
+            flops=2 * CHUNK * rows * width * out_width,
+            bytes_accessed=2 * CHUNK * rows * width,
+            transcendentals=0,
+        ),
+    )(*scalars, states, weight)
+
+
+def gather_unit_kernel(size, place_ref, own_ref, x_ref, y_ref, xy_ref, *outs):
+    z, c = place_ref[0], place_ref[2]
+    sends, queries = outs[:8], outs[8:]
+    span = CHUNK * size
+    for rel, send_ref in enumerate(sends):
+        source = pl.multiple_of(((z ^ (rel // 2)) * 2 + (c ^ (rel % 2))) * span, 16)
+        for dx, (one_ref, two_ref) in enumerate(((own_ref, y_ref), (x_ref, xy_ref))):
+            total = one_ref[pl.ds(source, span)].astype(jnp.float32)
+            total = total + two_ref[pl.ds(source, span)].astype(jnp.float32)
+            norm = jnp.sum(total * total, axis=-1, keepdims=True)
+            unit = (total * lax.rsqrt(norm + 1e-06)).astype(jnp.bfloat16)
+            send_ref[dx * span : (dx + 1) * span] = unit
+            queries[dx][pl.ds(source, span)] = unit
+        if send_ref.shape[0] > 2 * span:
+            row = lax.broadcasted_iota(jnp.int32, (16, own_ref.shape[1]), 0)
+            send_ref[2 * span :] = jnp.where(
+                row == 0,
+                own_ref[8 * span :].astype(jnp.float32),
+                x_ref[8 * span :].astype(jnp.float32),
+            ).astype(jnp.bfloat16)
+
+
+def gather_unit(place, own, x, y, xy, size):
+    width = own.shape[1]
+    span = CHUNK * size
+    extra = own.shape[0] - 8 * span
+    send = jax.ShapeDtypeStruct((2 * span + extra, width), jnp.bfloat16)
+    query = jax.ShapeDtypeStruct((8 * span, width), jnp.bfloat16)
+    return pl.pallas_call(
+        functools.partial(gather_unit_kernel, size),
+        out_shape=(send,) * 8 + (query,) * 2,
+        in_specs=[pl.BlockSpec(memory_space=SMEM)] + [pl.BlockSpec(memory_space=VMEM)] * 4,
+        out_specs=[pl.BlockSpec(memory_space=VMEM)] * 10,
+        compiler_params=vmem_params(16),
+    )(place, own, x, y, xy)
+
+
+def cube_route_kernel(size, slots, parts, place_ref, *refs):
+    spread, out_ref, pieces_ref, rows_ref, asked_ref, sem = refs[:parts], *refs[parts:]
+    z, x, c = place_ref[0], place_ref[1], place_ref[2]
+    blocks = pieces_ref.shape[0] // 16
+    span = CHUNK * size
+    for i, ref in enumerate(spread):
+        first, rel = i // 8 * CHUNK, i % 8
+        for dx in range(2):
+            owner = (z ^ (rel // 2)) * 4 + (x ^ dx) * 2 + (c ^ (rel % 2))
+            for b in range(CHUNK):
+                begin = dx * span + b * size
+                pieces_ref[owner * blocks + first + b] = ref[begin : begin + size]
+            if ref.shape[0] > 2 * span:
+                row = ref[2 * span :].astype(jnp.float32)[dx : dx + 1]
+                rows_ref[pl.ds(owner, 1)] = row.astype(jnp.int32)
+    copy = pltpu.make_async_copy(rows_ref, asked_ref, sem)
+    copy.start()
+    copy.wait()
+
+    def step(d, carry):
+        side = d // 16
+        for k in range(slots):
+            out_ref[d, k] = pieces_ref[asked_ref[d - side * 16, side * slots + k]]
+        return carry
+
+    lax.fori_loop(0, 32, step, 0, unroll=4)
+
+
+def cube_route(place, spread, size, slots, blocks):
+    width = spread[0].shape[1]
+    return pl.pallas_call(
+        functools.partial(cube_route_kernel, size, slots, len(spread)),
+        out_shape=jax.ShapeDtypeStruct((32, slots, size, width), jnp.bfloat16),
+        in_specs=[pl.BlockSpec(memory_space=SMEM)]
+        + [pl.BlockSpec(memory_space=VMEM)] * len(spread),
+        out_specs=pl.BlockSpec(memory_space=VMEM),
+        scratch_shapes=[
+            VMEM((16 * blocks, size, width), jnp.bfloat16),
+            VMEM((16, width), jnp.int32),
+            SMEM((16, width), jnp.int32),
+            pltpu.SemaphoreType.DMA,
+        ],
+        compiler_params=vmem_params(16),
+    )(place, *spread)
+
+
+def queries_kernel(size, place_ref, *refs):
+    parts, out_ref = refs[:-1], refs[-1]
+    x, side = place_ref[1], place_ref[3]
+    for i, ref in enumerate(parts):
+        first, rel = i // 4 * CHUNK, i % 4
+        base = (side ^ (rel // 2)) * (16 * size) + (x ^ (rel % 2)) * (2 * size)
+        for z in range(4):
+            for c in range(2):
+                target = pl.multiple_of(base + z * 4 * size + c * size, 16)
+                for b in range(CHUNK):
+                    begin = ((z * 2 + c) * CHUNK + b) * size
+                    out_ref[first + b, pl.ds(target, size)] = ref[begin : begin + size]
+
+
+def queries(place, parts, size, blocks):
+    width = parts[0].shape[1]
+    return pl.pallas_call(
+        functools.partial(queries_kernel, size),
+        out_shape=jax.ShapeDtypeStruct((blocks, 32 * size, width), jnp.bfloat16),
+        in_specs=[pl.BlockSpec(memory_space=SMEM)] + [pl.BlockSpec(memory_space=VMEM)] * len(parts),
+        out_specs=pl.BlockSpec(memory_space=VMEM),
+        compiler_params=vmem_params(16),
+    )(place, *parts)
+
+
+def local_cube(states, proj_weight, lengths, query_block, cand_block, pair_valid):
+    side = lax.axis_index("narrow").astype(jnp.int32)
+    owner = lax.axis_index("wide").astype(jnp.int32)
+    place = jnp.stack([owner // 4, owner // 2 % 2, owner % 2, side])
+    paras, length, width_part = states.shape
+    width = proj_weight.shape[1]
+    blocks = paras // BLK
+    rows = BLK * length
+    size = rows // 32
+    slots = cand_block.shape[0] // 4
+    flat = states.reshape(blocks, rows, width_part)
+
+    def near(array, rel):
+        flip = rel % 2 * 4 + rel // 2
+        return lax.ppermute(array, ("wide", "narrow"), [(i, i ^ flip) for i in range(32)])
+
+    def along(array, rel):
+        flip = rel // 2 * 4 + rel % 2
+        return lax.ppermute(array, "wide", [(i, i ^ flip) for i in range(16)])
+
+    sel, first, second = plan(cand_block)
+    spread, query_parts = [], []
+    for c in range(0, blocks, CHUNK):
+        last = c + CHUNK == blocks
+        parts = split(place, sel if last else None, flat, proj_weight, c)
+        parts = [parts[0]] + [near(parts[rel], rel) for rel in (1, 2, 3)]
+        *sends, own, other = gather_unit(place, *parts, size)
+        spread += [sends[0]] + [along(sends[rel], rel) for rel in range(1, 8)]
+        query_parts.append((own, other))
+    outgoing = cube_route(place, spread, size, slots, blocks)
+    outgoing, query_parts = lax.optimization_barrier((outgoing, query_parts))
+    incoming = lax.all_to_all(outgoing, ("narrow", "wide"), 0, 0, tiled=True)
+    gathered = []
+    for own, other in query_parts:
+        gathered += [own, near(other, 1), near(own, 2), near(other, 3)]
+    query = queries(place, gathered, size, blocks)
+    cand = incoming.transpose(1, 0, 2, 3).reshape(-1, rows, width)
+    part = score(
+        jnp.stack([owner, side]), sel, first, second, query_block, lengths, pair_valid, query, cand, length
+    )
+    return part + lax.ppermute(part, "narrow", [(0, 1), (1, 0)])
+
+
 def solution(mesh):
     in_specs = (P("wide", None, "narrow"), P("narrow", None), P(), P("wide"), P("wide"), P("wide"))
     out_specs = P("wide", None, None)
+    cube = mesh.shape["wide"] == 16 and mesh.shape["narrow"] == 2
+    local = local_cube if cube else local_general
     return jax.shard_map(local, mesh=mesh, in_specs=in_specs, out_specs=out_specs, check_vma=False)

time: 119 us -> 122 us (1.025)
  starting transfers between devices: 14.9 us -> 45 us
  blocking collectives: 26.4 us -> 0 us
  waiting for transfers between devices: 39 us -> 44.6 us
  Pallas kernels: 33.3 us -> 28.7 us
  local copies, waits for them, and re-layouts: 2.94 us -> 1.63 us
    ppermute x3 -> x27, starting transfers between devices: 5.15 us -> 39.9 us  [the longest x12 21.8 us: near(): lax.ppermute(array, ('wide', 'narrow'), [(i, i ^ flip) for i in range(32)])]
    all_to_all x1 -> x0, blocking collectives: 26.4 us -> none  [local(): spread = lax.all_to_all(mine, 'wide', 0, 0, tiled=True)]
    ppermute x3 -> x27, waiting for transfers between devices: 39 us -> 44.6 us  [the longest x12 33.2 us: near(): lax.ppermute(array, ('wide', 'narrow'), [(i, i ^ flip) for i in range(32)])]
    pallas_call x1, Pallas kernels: 16.3 us -> 11.3 us  [score(): pl.pallas_call(functools.partial(score_kernel, length), out_shape=jax.Sha...]
    all_to_all x2 -> x1, starting transfers between devices: 9.76 us -> 5.13 us  [local_cube(): incoming = lax.all_to_all(outgoing, ('narrow', 'wide'), 0, 0, tiled=True)]
    broadcast_in_dim x1 -> x0, local copies, waits for them, and re-layouts: 1.29 us -> none  [local(): jnp.broadcast_to(sel[None], (owners,) + sel.shape)]
    pallas_call x4 -> x6, Pallas kernels: 15.2 us -> 15.7 us  [the longest x2 10.6 us: split(): pl.pallas_call(functools.partial(split_kernel, first, sel_count), out_sha...]
  transfers between devices with their start and end apart: 5 -> 28, of which waited for: 3 -> 8; matrix products, arithmetic and copies ran while one was open for 2% -> 0% of each run, Pallas kernels for 9% -> 8%
where the time goes in v2:
time: 122 us
  starting transfers between devices  45 us (37%)
  waiting for transfers between devices  44.6 us (37%)
  Pallas kernels  28.7 us (24%)
  local copies, waits for them, and re-layouts  1.63 us (1%)
  other arithmetic  1.3 us (1%)
    ppermute x12, waiting for transfers between devices, near(): lax.ppermute(array, ('wide', 'narrow'), [(i, i ^ flip) for i in range(32)])  33.2 us
    ppermute x12, starting transfers between devices, near(): lax.ppermute(array, ('wide', 'narrow'), [(i, i ^ flip) for i in range(32)])  21.8 us
    ppermute x14, starting transfers between devices, along(): return lax.ppermute(array, 'wide', [(i, i ^ flip) for i in range(16)])  16.6 us
    pallas_call x1, Pallas kernels, score(): pl.pallas_call(functools.partial(score_kernel, length), out_shape=jax.Sha...  11.3 us
    pallas_call x2, Pallas kernels, split(): pl.pallas_call(functools.partial(split_kernel, first, sel_count), out_sha...  10.6 us
    ppermute x14, waiting for transfers between devices, along(): return lax.ppermute(array, 'wide', [(i, i ^ flip) for i in range(16)])  8.26 us
    all_to_all x1, starting transfers between devices, local_cube(): incoming = lax.all_to_all(outgoing, ('narrow', 'wide'), 0, 0, tiled=True)  5.13 us
    ppermute x1, waiting for transfers between devices, local_cube(): return part + lax.ppermute(part, 'narrow', [(0, 1), (1, 0)])  3.17 us
  transfers between devices with their start and end apart: 28, of which 8 were waited for; matrix products, arithmetic and copies ran while one was open for 0% of the time, Pallas kernels for 8%

profile of v2, /device:TPU:0, one launch (start us, length us, event | category | flops | bytes accessed | tf_op | source)
XLA Modules:
  0.0 121.5 jit_solution(9658213315613158560)
XLA Ops:
  0.6 5.2 %shard_map.65 = (bf16[768,128]{1,0:T(8,128)(2,1)}, bf16[768,128]{1,0:T(8,128)(2,1)}, bf16[768,128]{1,0:T(8,128)(2,1)}, bf16[768,128]{1,0:T(8,128)(2,1)}) custom-call(s32[4]{0:T(128)} %pad_add_fusion.1.place_ref, bf16[4,1536,512]{2,1,0:T(8,128)(2,1)} %bitcast.9, bf16[512,128]{1,0:T(8,128)(2,1)} %refs_2_.1), custom_call_target="tpu_custom_call" | custom-call | flops 402653184 | bytes 3145728 | tf_op jit(solution)/shard_map/pallas_call | solution.py:305
  5.8 2.9 %collective-permute-start = (bf16[768,128]{1,0:T(8,128)(2,1)}, bf16[768,128]{1,0:T(8,128)(2,1)S(1)}, u32[]{:S(2)}, u32[]{:S(2)}) collective-permute-start(bf16[768,128]{1,0:T(8,128)(2,1)} %get-tuple-element.45), channel_id=1, source_target_pairs={{0,4},{1,5},{2,6},{3,7},{4,0},{5,1},{6,2},{7,3},{8,12},{9,13},{10,... | collective-permute-start | bytes 589832 | tf_op jit(solution)/shard_map/ppermute | solution.py:449
  8.7 1.7 %shard_map.64 = (s32[6]{0:T(128)}, s32[6]{0:T(128)}, s32[6]{0:T(128)}) custom-call(s32[12]{0:T(128)} %cand_ref.1), custom_call_target="tpu_custom_call" | custom-call | tf_op jit(solution)/shard_map/pallas_call | solution.py:53
  10.5 5.4 %shard_map.67 = (bf16[784,128]{1,0:T(8,128)(2,1)}, bf16[784,128]{1,0:T(8,128)(2,1)}, bf16[784,128]{1,0:T(8,128)(2,1)}, bf16[784,128]{1,0:T(8,128)(2,1)}) custom-call(s32[4]{0:T(128)} %pad_add_fusion.1.place_ref, s32[6]{0:T(128)} %get-tuple-element.41.refs_0_.sel_ref, bf16[4,1536,512]{2,1,0:T(8,128)(2,1)} %bitcast.10, bf16[512,128]{1,0:T(8,128)(2,1)} %refs_2_.1), custom_call_target="tpu_custom_call" | custom-call | flops 402653184 | bytes 3145728 | tf_op jit(solution)/shard_map/pallas_call | solution.py:305
  15.9 2.1 %collective-permute-start.11 = (bf16[784,128]{1,0:T(8,128)(2,1)}, bf16[784,128]{1,0:T(8,128)(2,1)S(1)}, u32[]{:S(2)}, u32[]{:S(2)}) collective-permute-start(bf16[784,128]{1,0:T(8,128)(2,1)} %get-tuple-element.58), channel_id=1, source_target_pairs={{0,1},{1,0},{2,3},{3,2},{4,5},{5,4},{6,7},{7,6},{8,9},{9,8},{10,11... | collective-permute-start | bytes 602120 | tf_op jit(solution)/shard_map/ppermute | solution.py:449
  18.0 2.9 %collective-permute-start.2 = (bf16[768,128]{1,0:T(8,128)(2,1)S(1)}, bf16[768,128]{1,0:T(8,128)(2,1)S(1)}, u32[]{:S(2)}, u32[]{:S(2)}) collective-permute-start(bf16[768,128]{1,0:T(8,128)(2,1)S(1)} %copy-done.9), channel_id=1, source_target_pairs={{0,5},{1,4},{2,7},{3,6},{4,1},{5,0},{6,3},{7,2},{8,13},{9,12},{10,... | collective-permute-start | bytes 589832 | tf_op jit(solution)/shard_map/ppermute | solution.py:449
  21.0 14.3 %collective-permute-done.1.y_ref = bf16[768,128]{1,0:T(8,128)(2,1)S(1)} collective-permute-done((bf16[768,128]{1,0:T(8,128)(2,1)S(1)}, bf16[768,128]{1,0:T(8,128)(2,1)S(1)}, u32[]{:S(2)}, u32[]{:S(2)}) %collective-permute-start.1) | collective-permute-done | bytes 196640 | tf_op jit(solution)/shard_map/ppermute | solution.py:449
  35.3 0.8 shard_map.66
  36.2 1.9 %collective-permute-start.4 = (bf16[192,128]{1,0:T(8,128)(2,1)S(1)}, bf16[192,128]{1,0:T(8,128)(2,1)S(1)}, u32[]{:S(2)}, u32[]{:S(2)}) collective-permute-start(bf16[192,128]{1,0:T(8,128)(2,1)S(1)} %get-tuple-element.50), channel_id=1, source_target_pairs={{0,8},{2,10},{4,12},{6,14},{8,0},{10,2},{12,4},{14,6},{16,24},{18,... | collective-permute-start | bytes 147464 | tf_op jit(solution)/shard_map/ppermute | solution.py:453
  38.2 2.8 %collective-permute-start.6 = (bf16[192,128]{1,0:T(8,128)(2,1)S(1)}, bf16[192,128]{1,0:T(8,128)(2,1)S(1)}, u32[]{:S(2)}, u32[]{:S(2)}) collective-permute-start(bf16[192,128]{1,0:T(8,128)(2,1)S(1)} %get-tuple-element.52), channel_id=1, source_target_pairs={{0,16},{2,18},{4,20},{6,22},{8,24},{10,26},{12,28},{14,30},{16,0},... | collective-permute-start | bytes 147464 | tf_op jit(solution)/shard_map/ppermute | solution.py:453
  40.9 0.9 copy-done
  41.9 0.8 shard_map.68
  42.8 1.6 %collective-permute-start.14 = (bf16[208,128]{1,0:T(8,128)(2,1)S(1)}, bf16[208,128]{1,0:T(8,128)(2,1)S(1)}, u32[]{:S(2)}, u32[]{:S(2)}) collective-permute-start(bf16[208,128]{1,0:T(8,128)(2,1)S(1)} %get-tuple-element.62), channel_id=1, source_target_pairs={{0,8},{2,10},{4,12},{6,14},{8,0},{10,2},{12,4},{14,6},{16,24},{18,... | collective-permute-start | bytes 159752 | tf_op jit(solution)/shard_map/ppermute | solution.py:453
  44.5 2.5 %collective-permute-start.8 = (bf16[192,128]{1,0:T(8,128)(2,1)S(1)}, bf16[192,128]{1,0:T(8,128)(2,1)S(1)}, u32[]{:S(2)}, u32[]{:S(2)}) collective-permute-start(bf16[192,128]{1,0:T(8,128)(2,1)S(1)} %get-tuple-element.54), channel_id=1, source_target_pairs={{0,24},{2,26},{4,28},{6,30},{8,16},{10,18},{12,20},{14,22},{16,8},... | collective-permute-start | bytes 147464 | tf_op jit(solution)/shard_map/ppermute | solution.py:453
  47.0 1.0 collective-permute-start.9
  48.0 3.3 %collective-permute-done.7.refs_5_ = bf16[192,128]{1,0:T(8,128)(2,1)S(1)} collective-permute-done((bf16[192,128]{1,0:T(8,128)(2,1)S(1)}, bf16[192,128]{1,0:T(8,128)(2,1)S(1)}, u32[]{:S(2)}, u32[]{:S(2)}) %collective-permute-start.7) | collective-permute-done | bytes 49184 | tf_op jit(solution)/shard_map/ppermute | solution.py:453
  51.4 2.5 %collective-permute-start.16 = (bf16[208,128]{1,0:T(8,128)(2,1)S(1)}, bf16[208,128]{1,0:T(8,128)(2,1)S(1)}, u32[]{:S(2)}, u32[]{:S(2)}) collective-permute-start(bf16[208,128]{1,0:T(8,128)(2,1)S(1)} %get-tuple-element.64), channel_id=1, source_target_pairs={{0,16},{2,18},{4,20},{6,22},{8,24},{10,26},{12,28},{14,30},{16,0},... | collective-permute-start | bytes 159752 | tf_op jit(solution)/shard_map/ppermute | solution.py:453
  54.5 2.7 %collective-permute-start.18 = (bf16[208,128]{1,0:T(8,128)(2,1)S(1)}, bf16[208,128]{1,0:T(8,128)(2,1)S(1)}, u32[]{:S(2)}, u32[]{:S(2)}) collective-permute-start(bf16[208,128]{1,0:T(8,128)(2,1)S(1)} %get-tuple-element.66), channel_id=1, source_target_pairs={{0,24},{2,26},{4,28},{6,30},{8,16},{10,18},{12,20},{14,22},{16,8},... | collective-permute-start | bytes 159752 | tf_op jit(solution)/shard_map/ppermute | solution.py:453
  57.9 3.8 %collective-permute-done.17.refs_13_ = bf16[208,128]{1,0:T(8,128)(2,1)S(1)} collective-permute-done((bf16[208,128]{1,0:T(8,128)(2,1)S(1)}, bf16[208,128]{1,0:T(8,128)(2,1)S(1)}, u32[]{:S(2)}, u32[]{:S(2)}) %collective-permute-start.17) | collective-permute-done | bytes 53280 | tf_op jit(solution)/shard_map/ppermute | solution.py:453
  61.7 1.1 collective-permute-done.19.refs_15_
  62.9 2.8 %shard_map.69 = bf16[32,3,48,128]{3,2,1,0:T(8,128)(2,1)} custom-call(s32[4]{0:T(128)S(1)} %copy-done.2, bf16[192,128]{1,0:T(8,128)(2,1)S(1)} %get-tuple-element.48.refs_0_, bf16[192,128]{1,0:T(8,128)(2,1)S(1)} %collective-permute-done.3.refs_1_, bf16[192,128]{1,0:T(8,128)(2,1)S(1)} %collective-permute-done.4.refs_2_, ...), custom_call_target="tpu_custom_call" | custom-call | tf_op jit(solution)/shard_map/pallas_call | solution.py:394
  65.6 5.1 %all-to-all-start = ((bf16[32,3,48,128]{3,2,1,0:T(8,128)(2,1)}), bf16[32,3,48,128]{3,2,1,0:T(8,128)(2,1)S(1)}, u32[]{:S(2)}, u32[]{:S(2)}) async-start(bf16[32,3,48,128]{3,2,1,0:T(8,128)(2,1)} %shard_map.69), calls=%async_computation | async-start | bytes 2359296 | tf_op jit(solution)/shard_map/all_to_all | solution.py:466
  70.8 1.8 %collective-permute-start.21 = (bf16[768,128]{1,0:T(8,128)(2,1)S(1)}, bf16[768,128]{1,0:T(8,128)(2,1)S(1)}, u32[]{:S(2)}, u32[]{:S(2)}) collective-permute-start(bf16[768,128]{1,0:T(8,128)(2,1)S(1)} %get-tuple-element.72.refs_0_), channel_id=1, source_target_pairs={{0,1},{1,0},{2,3},{3,2},{4,5},{5,4},{6,7},{7,6},{8,9},{9,8},{10,11... | collective-permute-start | bytes 589832 | tf_op jit(solution)/shard_map/ppermute | solution.py:449
  72.6 1.5 %collective-permute-start.22 = (bf16[768,128]{1,0:T(8,128)(2,1)S(1)}, bf16[768,128]{1,0:T(8,128)(2,1)S(1)}, u32[]{:S(2)}, u32[]{:S(2)}) collective-permute-start(bf16[768,128]{1,0:T(8,128)(2,1)S(1)} %get-tuple-element.73), channel_id=1, source_target_pairs={{0,5},{1,4},{2,7},{3,6},{4,1},{5,0},{6,3},{7,2},{8,13},{9,12},{10,... | collective-permute-start | bytes 589832 | tf_op jit(solution)/shard_map/ppermute | solution.py:449
  74.3 1.8 %collective-permute-start.24 = (bf16[768,128]{1,0:T(8,128)(2,1)S(1)}, bf16[768,128]{1,0:T(8,128)(2,1)S(1)}, u32[]{:S(2)}, u32[]{:S(2)}) collective-permute-start(bf16[768,128]{1,0:T(8,128)(2,1)S(1)} %get-tuple-element.74.refs_4_), channel_id=1, source_target_pairs={{0,1},{1,0},{2,3},{3,2},{4,5},{5,4},{6,7},{7,6},{8,9},{9,8},{10,11... | collective-permute-start | bytes 589832 | tf_op jit(solution)/shard_map/ppermute | solution.py:449
  76.1 1.5 %collective-permute-start.25 = (bf16[768,128]{1,0:T(8,128)(2,1)S(1)}, bf16[768,128]{1,0:T(8,128)(2,1)S(1)}, u32[]{:S(2)}, u32[]{:S(2)}) collective-permute-start(bf16[768,128]{1,0:T(8,128)(2,1)S(1)} %get-tuple-element.75), channel_id=1, source_target_pairs={{0,5},{1,4},{2,7},{3,6},{4,1},{5,0},{6,3},{7,2},{8,13},{9,12},{10,... | collective-permute-start | bytes 589832 | tf_op jit(solution)/shard_map/ppermute | solution.py:449
  77.5 15.0 %collective-permute-done.21.refs_2_ = bf16[768,128]{1,0:T(8,128)(2,1)S(1)} collective-permute-done((bf16[768,128]{1,0:T(8,128)(2,1)S(1)}, bf16[768,128]{1,0:T(8,128)(2,1)S(1)}, u32[]{:S(2)}, u32[]{:S(2)}) %collective-permute-start.21) | collective-permute-done | bytes 196640 | tf_op jit(solution)/shard_map/ppermute | solution.py:449
  92.5 7.0 %collective-permute-start.23 = (bf16[768,128]{1,0:T(8,128)(2,1)S(1)}, bf16[768,128]{1,0:T(8,128)(2,1)S(1)}, u32[]{:S(2)}, u32[]{:S(2)}) collective-permute-start(bf16[768,128]{1,0:T(8,128)(2,1)S(1)} %get-tuple-element.75), channel_id=1, source_target_pairs={{0,4},{1,5},{2,6},{3,7},{4,0},{5,1},{6,2},{7,3},{8,12},{9,13},{10,... | collective-permute-start | bytes 589832 | tf_op jit(solution)/shard_map/ppermute | solution.py:449
  99.6 3.5 %collective-permute-done.24.refs_6_ = bf16[768,128]{1,0:T(8,128)(2,1)S(1)} collective-permute-done((bf16[768,128]{1,0:T(8,128)(2,1)S(1)}, bf16[768,128]{1,0:T(8,128)(2,1)S(1)}, u32[]{:S(2)}, u32[]{:S(2)}) %collective-permute-start.24) | collective-permute-done | bytes 196640 | tf_op jit(solution)/shard_map/ppermute | solution.py:449
  104.9 11.3 %shard_map.71 = f32[12,12,12]{2,1,0:T(8,128)S(1)} custom-call(s32[2]{0:T(128)S(1)} %pad_add_fusion.where_ref, s32[6]{0:T(128)S(1)} %copy-done.3, s32[6]{0:T(128)S(1)} %copy-done.7, s32[6]{0:T(128)S(1)} %copy-done.8, s32[12]{0:T(128)S(1)} %copy-done.5, s32[768]{0:T(1024)S(1)} %copy-done.4, s32[12]{0:T(128)S(1)} %copy-done.6, ...), custom_call_target="tpu_custom_call" | custom-call | flops 3623878656 | bytes 786432 | tf_op jit(solution)/shard_map/pallas_call | solution.py:203
  116.2 1.5 %collective-permute-start.26 = (f32[12,12,12]{2,1,0:T(8,128)S(1)}, f32[12,12,12]{2,1,0:T(8,128)S(1)}, u32[]{:S(2)}, u32[]{:S(2)}) collective-permute-start(f32[12,12,12]{2,1,0:T(8,128)S(1)} %shard_map.71), channel_id=1, source_target_pairs={{0,1},{1,0},{2,3},{3,2},{4,5},{5,4},{6,7},{7,6},{8,9},{9,8},{10,11... | collective-permute-start | bytes 20744 | tf_op jit(solution)/shard_map/ppermute | solution.py:475
  117.7 3.2 %collective-permute-done.26 = f32[12,12,12]{2,1,0:T(8,128)S(1)} collective-permute-done((f32[12,12,12]{2,1,0:T(8,128)S(1)}, f32[12,12,12]{2,1,0:T(8,128)S(1)}, u32[]{:S(2)}, u32[]{:S(2)}) %collective-permute-start.26) | collective-permute-done | bytes 6944 | tf_op jit(solution)/shard_map/ppermute | solution.py:475
  (58 shorter events, 5.2 us)
Async XLA Ops:
  5.8 15.1 %collective-permute-start = (bf16[768,128]{1,0:T(8,128)(2,1)}, bf16[768,128]{1,0:T(8,128)(2,1)S(1)}, u32[]{:S(2)}, u32[]{:S(2)}) collective-permute-start(bf16[768,128]{1,0:T(8,128)(2,1)} %get-tuple-element.45), channel_id=1, source_target_pairs={{0,4},{1,5},{2,6},{3,7},{4,0},{5,1},{6,2},{7,3},{8,12},{9,13},{10,... | collective-permute-start | bytes 589832 | tf_op jit(solution)/shard_map/ppermute | solution.py:449
  10.5 7.5 %copy-start.10 = (bf16[768,128]{1,0:T(8,128)(2,1)S(1)}, bf16[768,128]{1,0:T(8,128)(2,1)}, u32[]{:S(2)}) copy-start(bf16[768,128]{1,0:T(8,128)(2,1)} %get-tuple-element.46) | copy-start | bytes 589828
  10.5 7.5 %copy-start.9 = (bf16[768,128]{1,0:T(8,128)(2,1)S(1)}, bf16[768,128]{1,0:T(8,128)(2,1)}, u32[]{:S(2)}) copy-start(bf16[768,128]{1,0:T(8,128)(2,1)} %get-tuple-element.47) | copy-start | bytes 589828
  10.5 24.8 %copy-start.1 = (bf16[768,128]{1,0:T(8,128)(2,1)S(1)}, bf16[768,128]{1,0:T(8,128)(2,1)}, u32[]{:S(2)}) copy-start(bf16[768,128]{1,0:T(8,128)(2,1)} %get-tuple-element.44.own_ref) | copy-start | bytes 589828
  10.5 24.8 %copy-start.2 = (s32[4]{0:T(128)S(1)}, s32[4]{0:T(128)}, u32[]{:S(2)}) copy-start(s32[4]{0:T(128)} %pad_add_fusion.1.place_ref) | copy-start | bytes 52
  15.9 22.2 %collective-permute-start.10 = (bf16[784,128]{1,0:T(8,128)(2,1)}, bf16[784,128]{1,0:T(8,128)(2,1)S(1)}, u32[]{:S(2)}, u32[]{:S(2)}) collective-permute-start(bf16[784,128]{1,0:T(8,128)(2,1)} %get-tuple-element.57), channel_id=1, source_target_pairs={{0,4},{1,5},{2,6},{3,7},{4,0},{5,1},{6,2},{7,3},{8,12},{9,13},{10,... | collective-permute-start | bytes 602120 | tf_op jit(solution)/shard_map/ppermute | solution.py:449
  15.9 22.3 %collective-permute-start.11 = (bf16[784,128]{1,0:T(8,128)(2,1)}, bf16[784,128]{1,0:T(8,128)(2,1)S(1)}, u32[]{:S(2)}, u32[]{:S(2)}) collective-permute-start(bf16[784,128]{1,0:T(8,128)(2,1)} %get-tuple-element.58), channel_id=1, source_target_pairs={{0,1},{1,0},{2,3},{3,2},{4,5},{5,4},{6,7},{7,6},{8,9},{9,8},{10,11... | collective-permute-start | bytes 602120 | tf_op jit(solution)/shard_map/ppermute | solution.py:449
  18.0 17.3 %collective-permute-start.1 = (bf16[768,128]{1,0:T(8,128)(2,1)S(1)}, bf16[768,128]{1,0:T(8,128)(2,1)S(1)}, u32[]{:S(2)}, u32[]{:S(2)}) collective-permute-start(bf16[768,128]{1,0:T(8,128)(2,1)S(1)} %copy-done.10), channel_id=1, source_target_pairs={{0,1},{1,0},{2,3},{3,2},{4,5},{5,4},{6,7},{7,6},{8,9},{9,8},{10,11... | collective-permute-start | bytes 589832 | tf_op jit(solution)/shard_map/ppermute | solution.py:449
  18.0 17.3 %collective-permute-start.2 = (bf16[768,128]{1,0:T(8,128)(2,1)S(1)}, bf16[768,128]{1,0:T(8,128)(2,1)S(1)}, u32[]{:S(2)}, u32[]{:S(2)}) collective-permute-start(bf16[768,128]{1,0:T(8,128)(2,1)S(1)} %copy-done.9), channel_id=1, source_target_pairs={{0,5},{1,4},{2,7},{3,6},{4,1},{5,0},{6,3},{7,2},{8,13},{9,12},{10,... | collective-permute-start | bytes 589832 | tf_op jit(solution)/shard_map/ppermute | solution.py:449
  20.9 20.0 %collective-permute-start.12 = (bf16[784,128]{1,0:T(8,128)(2,1)}, bf16[784,128]{1,0:T(8,128)(2,1)S(1)}, u32[]{:S(2)}, u32[]{:S(2)}) collective-permute-start(bf16[784,128]{1,0:T(8,128)(2,1)} %get-tuple-element.59), channel_id=1, source_target_pairs={{0,5},{1,4},{2,7},{3,6},{4,1},{5,0},{6,3},{7,2},{8,13},{9,12},{10,... | collective-permute-start | bytes 602120 | tf_op jit(solution)/shard_map/ppermute | solution.py:449
  36.2 6.7 %collective-permute-start.3 = (bf16[192,128]{1,0:T(8,128)(2,1)S(1)}, bf16[192,128]{1,0:T(8,128)(2,1)S(1)}, u32[]{:S(2)}, u32[]{:S(2)}) collective-permute-start(bf16[192,128]{1,0:T(8,128)(2,1)S(1)} %get-tuple-element.49), channel_id=1, source_target_pairs={{0,2},{2,0},{4,6},{6,4},{8,10},{10,8},{12,14},{14,12},{16,18},{18,... | collective-permute-start | bytes 147464 | tf_op jit(solution)/shard_map/ppermute | solution.py:453
  36.2 8.2 %collective-permute-start.4 = (bf16[192,128]{1,0:T(8,128)(2,1)S(1)}, bf16[192,128]{1,0:T(8,128)(2,1)S(1)}, u32[]{:S(2)}, u32[]{:S(2)}) collective-permute-start(bf16[192,128]{1,0:T(8,128)(2,1)S(1)} %get-tuple-element.50), channel_id=1, source_target_pairs={{0,8},{2,10},{4,12},{6,14},{8,0},{10,2},{12,4},{14,6},{16,24},{18,... | collective-permute-start | bytes 147464 | tf_op jit(solution)/shard_map/ppermute | solution.py:453
  38.1 6.4 %collective-permute-start.5 = (bf16[192,128]{1,0:T(8,128)(2,1)S(1)}, bf16[192,128]{1,0:T(8,128)(2,1)S(1)}, u32[]{:S(2)}, u32[]{:S(2)}) collective-permute-start(bf16[192,128]{1,0:T(8,128)(2,1)S(1)} %get-tuple-element.51), channel_id=1, source_target_pairs={{0,10},{2,8},{4,14},{6,12},{8,2},{10,0},{12,6},{14,4},{16,26},{18,... | collective-permute-start | bytes 147464 | tf_op jit(solution)/shard_map/ppermute | solution.py:453
  38.2 8.8 %collective-permute-start.6 = (bf16[192,128]{1,0:T(8,128)(2,1)S(1)}, bf16[192,128]{1,0:T(8,128)(2,1)S(1)}, u32[]{:S(2)}, u32[]{:S(2)}) collective-permute-start(bf16[192,128]{1,0:T(8,128)(2,1)S(1)} %get-tuple-element.52), channel_id=1, source_target_pairs={{0,16},{2,18},{4,20},{6,22},{8,24},{10,26},{12,28},{14,30},{16,0},... | collective-permute-start | bytes 147464 | tf_op jit(solution)/shard_map/ppermute | solution.py:453
  42.7 11.8 %collective-permute-start.13 = (bf16[208,128]{1,0:T(8,128)(2,1)S(1)}, bf16[208,128]{1,0:T(8,128)(2,1)S(1)}, u32[]{:S(2)}, u32[]{:S(2)}) collective-permute-start(bf16[208,128]{1,0:T(8,128)(2,1)S(1)} %get-tuple-element.61), channel_id=1, source_target_pairs={{0,2},{2,0},{4,6},{6,4},{8,10},{10,8},{12,14},{14,12},{16,18},{18,... | collective-permute-start | bytes 159752 | tf_op jit(solution)/shard_map/ppermute | solution.py:453
  42.8 14.3 %collective-permute-start.14 = (bf16[208,128]{1,0:T(8,128)(2,1)S(1)}, bf16[208,128]{1,0:T(8,128)(2,1)S(1)}, u32[]{:S(2)}, u32[]{:S(2)}) collective-permute-start(bf16[208,128]{1,0:T(8,128)(2,1)S(1)} %get-tuple-element.62), channel_id=1, source_target_pairs={{0,8},{2,10},{4,12},{6,14},{8,0},{10,2},{12,4},{14,6},{16,24},{18,... | collective-permute-start | bytes 159752 | tf_op jit(solution)/shard_map/ppermute | solution.py:453
  44.4 6.9 %collective-permute-start.7 = (bf16[192,128]{1,0:T(8,128)(2,1)S(1)}, bf16[192,128]{1,0:T(8,128)(2,1)S(1)}, u32[]{:S(2)}, u32[]{:S(2)}) collective-permute-start(bf16[192,128]{1,0:T(8,128)(2,1)S(1)} %get-tuple-element.53), channel_id=1, source_target_pairs={{0,18},{2,16},{4,22},{6,20},{8,26},{10,24},{12,30},{14,28},{16,2},... | collective-permute-start | bytes 147464 | tf_op jit(solution)/shard_map/ppermute | solution.py:453
  44.5 6.8 %collective-permute-start.8 = (bf16[192,128]{1,0:T(8,128)(2,1)S(1)}, bf16[192,128]{1,0:T(8,128)(2,1)S(1)}, u32[]{:S(2)}, u32[]{:S(2)}) collective-permute-start(bf16[192,128]{1,0:T(8,128)(2,1)S(1)} %get-tuple-element.54), channel_id=1, source_target_pairs={{0,24},{2,26},{4,28},{6,30},{8,16},{10,18},{12,20},{14,22},{16,8},... | collective-permute-start | bytes 147464 | tf_op jit(solution)/shard_map/ppermute | solution.py:453
  47.0 6.8 %collective-permute-start.9 = (bf16[192,128]{1,0:T(8,128)(2,1)S(1)}, bf16[192,128]{1,0:T(8,128)(2,1)S(1)}, u32[]{:S(2)}, u32[]{:S(2)}) collective-permute-start(bf16[192,128]{1,0:T(8,128)(2,1)S(1)} %get-tuple-element.55), channel_id=1, source_target_pairs={{0,26},{2,24},{4,30},{6,28},{8,18},{10,16},{12,22},{14,20},{16,10}... | collective-permute-start | bytes 147464 | tf_op jit(solution)/shard_map/ppermute | solution.py:453
  51.3 6.6 %collective-permute-start.15 = (bf16[208,128]{1,0:T(8,128)(2,1)S(1)}, bf16[208,128]{1,0:T(8,128)(2,1)S(1)}, u32[]{:S(2)}, u32[]{:S(2)}) collective-permute-start(bf16[208,128]{1,0:T(8,128)(2,1)S(1)} %get-tuple-element.63), channel_id=1, source_target_pairs={{0,10},{2,8},{4,14},{6,12},{8,2},{10,0},{12,6},{14,4},{16,26},{18,... | collective-permute-start | bytes 159752 | tf_op jit(solution)/shard_map/ppermute | solution.py:453
  51.4 6.6 %collective-permute-start.16 = (bf16[208,128]{1,0:T(8,128)(2,1)S(1)}, bf16[208,128]{1,0:T(8,128)(2,1)S(1)}, u32[]{:S(2)}, u32[]{:S(2)}) collective-permute-start(bf16[208,128]{1,0:T(8,128)(2,1)S(1)} %get-tuple-element.64), channel_id=1, source_target_pairs={{0,16},{2,18},{4,20},{6,22},{8,24},{10,26},{12,28},{14,30},{16,0},... | collective-permute-start | bytes 159752 | tf_op jit(solution)/shard_map/ppermute | solution.py:453
  53.9 7.9 %collective-permute-start.17 = (bf16[208,128]{1,0:T(8,128)(2,1)S(1)}, bf16[208,128]{1,0:T(8,128)(2,1)S(1)}, u32[]{:S(2)}, u32[]{:S(2)}) collective-permute-start(bf16[208,128]{1,0:T(8,128)(2,1)S(1)} %get-tuple-element.65), channel_id=1, source_target_pairs={{0,18},{2,16},{4,22},{6,20},{8,26},{10,24},{12,30},{14,28},{16,2},... | collective-permute-start | bytes 159752 | tf_op jit(solution)/shard_map/ppermute | solution.py:453
  54.5 7.2 %collective-permute-start.18 = (bf16[208,128]{1,0:T(8,128)(2,1)S(1)}, bf16[208,128]{1,0:T(8,128)(2,1)S(1)}, u32[]{:S(2)}, u32[]{:S(2)}) collective-permute-start(bf16[208,128]{1,0:T(8,128)(2,1)S(1)} %get-tuple-element.66), channel_id=1, source_target_pairs={{0,24},{2,26},{4,28},{6,30},{8,16},{10,18},{12,20},{14,22},{16,8},... | collective-permute-start | bytes 159752 | tf_op jit(solution)/shard_map/ppermute | solution.py:453
  57.2 5.7 %collective-permute-start.19 = (bf16[208,128]{1,0:T(8,128)(2,1)S(1)}, bf16[208,128]{1,0:T(8,128)(2,1)S(1)}, u32[]{:S(2)}, u32[]{:S(2)}) collective-permute-start(bf16[208,128]{1,0:T(8,128)(2,1)S(1)} %get-tuple-element.67), channel_id=1, source_target_pairs={{0,26},{2,24},{4,30},{6,28},{8,18},{10,16},{12,22},{14,20},{16,10}... | collective-permute-start | bytes 159752 | tf_op jit(solution)/shard_map/ppermute | solution.py:453
  65.6 38.6 %all-to-all-start = ((bf16[32,3,48,128]{3,2,1,0:T(8,128)(2,1)}), bf16[32,3,48,128]{3,2,1,0:T(8,128)(2,1)S(1)}, u32[]{:S(2)}, u32[]{:S(2)}) async-start(bf16[32,3,48,128]{3,2,1,0:T(8,128)(2,1)} %shard_map.69), calls=%async_computation | async-start | bytes 2359296 | tf_op jit(solution)/shard_map/all_to_all | solution.py:466
  70.8 21.8 %collective-permute-start.21 = (bf16[768,128]{1,0:T(8,128)(2,1)S(1)}, bf16[768,128]{1,0:T(8,128)(2,1)S(1)}, u32[]{:S(2)}, u32[]{:S(2)}) collective-permute-start(bf16[768,128]{1,0:T(8,128)(2,1)S(1)} %get-tuple-element.72.refs_0_), channel_id=1, source_target_pairs={{0,1},{1,0},{2,3},{3,2},{4,5},{5,4},{6,7},{7,6},{8,9},{9,8},{10,11... | collective-permute-start | bytes 589832 | tf_op jit(solution)/shard_map/ppermute | solution.py:449
  72.6 27.0 %collective-permute-start.22 = (bf16[768,128]{1,0:T(8,128)(2,1)S(1)}, bf16[768,128]{1,0:T(8,128)(2,1)S(1)}, u32[]{:S(2)}, u32[]{:S(2)}) collective-permute-start(bf16[768,128]{1,0:T(8,128)(2,1)S(1)} %get-tuple-element.73), channel_id=1, source_target_pairs={{0,5},{1,4},{2,7},{3,6},{4,1},{5,0},{6,3},{7,2},{8,13},{9,12},{10,... | collective-permute-start | bytes 589832 | tf_op jit(solution)/shard_map/ppermute | solution.py:449
  74.1 25.5 %collective-permute-start.20 = (bf16[768,128]{1,0:T(8,128)(2,1)S(1)}, bf16[768,128]{1,0:T(8,128)(2,1)S(1)}, u32[]{:S(2)}, u32[]{:S(2)}) collective-permute-start(bf16[768,128]{1,0:T(8,128)(2,1)S(1)} %get-tuple-element.73), channel_id=1, source_target_pairs={{0,4},{1,5},{2,6},{3,7},{4,0},{5,1},{6,2},{7,3},{8,12},{9,13},{10,... | collective-permute-start | bytes 589832 | tf_op jit(solution)/shard_map/ppermute | solution.py:449
  74.3 28.8 %collective-permute-start.24 = (bf16[768,128]{1,0:T(8,128)(2,1)S(1)}, bf16[768,128]{1,0:T(8,128)(2,1)S(1)}, u32[]{:S(2)}, u32[]{:S(2)}) collective-permute-start(bf16[768,128]{1,0:T(8,128)(2,1)S(1)} %get-tuple-element.74.refs_4_), channel_id=1, source_target_pairs={{0,1},{1,0},{2,3},{3,2},{4,5},{5,4},{6,7},{7,6},{8,9},{9,8},{10,11... | collective-permute-start | bytes 589832 | tf_op jit(solution)/shard_map/ppermute | solution.py:449
  76.1 27.0 %collective-permute-start.25 = (bf16[768,128]{1,0:T(8,128)(2,1)S(1)}, bf16[768,128]{1,0:T(8,128)(2,1)S(1)}, u32[]{:S(2)}, u32[]{:S(2)}) collective-permute-start(bf16[768,128]{1,0:T(8,128)(2,1)S(1)} %get-tuple-element.75), channel_id=1, source_target_pairs={{0,5},{1,4},{2,7},{3,6},{4,1},{5,0},{6,3},{7,2},{8,13},{9,12},{10,... | collective-permute-start | bytes 589832 | tf_op jit(solution)/shard_map/ppermute | solution.py:449
  92.5 11.0 %collective-permute-start.23 = (bf16[768,128]{1,0:T(8,128)(2,1)S(1)}, bf16[768,128]{1,0:T(8,128)(2,1)S(1)}, u32[]{:S(2)}, u32[]{:S(2)}) collective-permute-start(bf16[768,128]{1,0:T(8,128)(2,1)S(1)} %get-tuple-element.75), channel_id=1, source_target_pairs={{0,4},{1,5},{2,6},{3,7},{4,0},{5,1},{6,2},{7,3},{8,12},{9,13},{10,... | collective-permute-start | bytes 589832 | tf_op jit(solution)/shard_map/ppermute | solution.py:449
  116.2 4.6 %collective-permute-start.26 = (f32[12,12,12]{2,1,0:T(8,128)S(1)}, f32[12,12,12]{2,1,0:T(8,128)S(1)}, u32[]{:S(2)}, u32[]{:S(2)}) collective-permute-start(f32[12,12,12]{2,1,0:T(8,128)S(1)} %shard_map.71), channel_id=1, source_target_pairs={{0,1},{1,0},{2,3},{3,2},{4,5},{5,4},{6,7},{7,6},{8,9},{9,8},{10,11... | collective-permute-start | bytes 20744 | tf_op jit(solution)/shard_map/ppermute | solution.py:475
  (7 other events, 5.0 us)

commit v3 on v2

--- a/solution.py
+++ b/solution.py
@@ -256,78 +256,84 @@
     return out
 
 
-def split_kernel(first, sel_count, place_ref, *refs):
+def place():
+    owner = lax.axis_index("wide")
+    return owner // 4, owner // 2 % 2, owner % 2, lax.axis_index("narrow")
+
+
+def split_kernel(first, over, sel_count, *refs):
     if sel_count:
         sel_ref, refs = refs[0], refs[1:]
-    states_ref, weight_ref = refs[:2]
-    outs, all_ref = refs[2:6], refs[6]
-    b, half = pl.program_id(0), pl.program_id(1)
-    part = states_ref.shape[1]
-    blocks = pl.num_programs(0)
-    all_ref[pl.ds(pl.multiple_of(half * part, part), part)] = jnp.dot(
-        states_ref[0], weight_ref[...], preferred_element_type=jnp.float32
-    ).astype(all_ref.dtype)
-
-    @pl.when(half == 1)
-    def _():
-        x, side = place_ref[1], place_ref[3]
-        size = part // 16
-        for rel, out_ref in enumerate(outs):
-            base = (side ^ (rel // 2)) * part + (x ^ (rel % 2)) * (2 * size)
-            for z in range(4):
+    states_ref, weight_ref, *outs, rows_ref, sems = refs
+    _, x, _, side = place()
+    blocks, part, _ = rows_ref.shape
+    size = part // 16
+    start = pl.multiple_of((side ^ over) * part, part)
+
+    def load(b):
+        return pltpu.make_async_copy(
+            states_ref.at[first + b, pl.ds(start, part)], rows_ref.at[b], sems.at[b]
+        )
+
+    for b in range(blocks):
+        load(b).start()
+    for b in range(blocks):
+        load(b).wait()
+        for z in range(4):
+            for dx in range(2):
+                source = pl.multiple_of((x ^ dx) * (2 * size) + z * 4 * size, 16)
+                both = jnp.dot(
+                    rows_ref[b, pl.ds(source, 2 * size)],
+                    weight_ref[...],
+                    preferred_element_type=jnp.float32,
+                ).astype(jnp.bfloat16)
                 for c in range(2):
-                    source = pl.multiple_of(base + z * 4 * size + c * size, 16)
-                    target = pl.multiple_of(((z * 2 + c) * CHUNK + b) * size, 16)
-                    out_ref[pl.ds(target, size)] = all_ref[pl.ds(source, size)]
-
+                    target = ((z * 2 + c) * blocks + b) * size
+                    outs[dx][target : target + size] = both[c * size : (c + 1) * size]
     if sel_count:
-
-        @pl.when((half == 1) & (b == 0))
-        def _():
-            lane = lax.broadcasted_iota(jnp.int32, (16, all_ref.shape[1]), 1)
-            row = jnp.zeros_like(lane)
-            for k in range(sel_count):
-                row = jnp.where(lane == k, sel_ref[k], row)
-            row = row.astype(jnp.float32).astype(all_ref.dtype)
-            for out_ref in outs:
-                out_ref[8 * CHUNK * (part // 16) :] = row
-
-
-def split(place, sel, states, weight, first):
+        lane = lax.broadcasted_iota(jnp.int32, (16, outs[0].shape[1]), 1)
+        row = jnp.zeros_like(lane)
+        for k in range(sel_count):
+            row = jnp.where(lane == k, sel_ref[k], row)
+        row = row.astype(jnp.float32).astype(jnp.bfloat16)
+        for out_ref in outs:
+            out_ref[8 * blocks * size :] = row
+
+
+def split(over, sel, states, weight, first):
     _, rows, width = states.shape
     out_width = weight.shape[1]
     part = rows // 2
     sel_count = 0 if sel is None else sel.shape[0]
     out_rows = 8 * CHUNK * (part // 16) + (16 if sel_count else 0)
-    out = jax.ShapeDtypeStruct((out_rows, out_width), jnp.bfloat16)
-    whole = pl.BlockSpec((out_rows, out_width), lambda b, h, *m: (0, 0))
-    scalars = (place,) if sel is None else (place, sel)
-    return pl.pallas_call(
-        functools.partial(split_kernel, first, sel_count),
-        out_shape=(out,) * 4,
-        grid_spec=pltpu.PrefetchScalarGridSpec(
-            num_scalar_prefetch=len(scalars),
-            grid=(CHUNK, 2),
-            in_specs=[
-                pl.BlockSpec((1, part, width), lambda b, h, *m: (first + b, h, 0)),
-                pl.BlockSpec((width, out_width), lambda b, h, *m: (0, 0)),
-            ],
-            out_specs=[whole] * 4,
-            scratch_shapes=[VMEM((rows, out_width), jnp.bfloat16)],
-        ),
-        compiler_params=vmem_params(58),
+    scalars = () if sel is None else (sel,)
+    return pl.pallas_call(
+        functools.partial(split_kernel, first, over, sel_count),
+        out_shape=(jax.ShapeDtypeStruct((out_rows, out_width), jnp.bfloat16),) * 2,
+        in_specs=[pl.BlockSpec(memory_space=SMEM)] * len(scalars)
+        + [pl.BlockSpec(memory_space=pltpu.HBM), pl.BlockSpec(memory_space=VMEM)],
+        out_specs=[pl.BlockSpec(memory_space=VMEM)] * 2,
+        scratch_shapes=[
+            VMEM((CHUNK, part, width), jnp.bfloat16),
+            pltpu.SemaphoreType.DMA((CHUNK,)),
+        ],
+        compiler_params=vmem_params(50),
         cost_estimate=pl.CostEstimate(
-            flops=2 * CHUNK * rows * width * out_width,
-            bytes_accessed=2 * CHUNK * rows * width,
+            flops=2 * CHUNK * part * width * out_width,
+            bytes_accessed=2 * CHUNK * part * width,
             transcendentals=0,
         ),
     )(*scalars, states, weight)
 
 
-def gather_unit_kernel(size, place_ref, own_ref, x_ref, y_ref, xy_ref, *outs):
-    z, c = place_ref[0], place_ref[2]
-    sends, queries = outs[:8], outs[8:]
+def gather_unit_kernel(size, before, own_ref, x_ref, y_ref, xy_ref, *refs):
+    z, _, c, _ = place()
+    earlier, sends, query = refs[:before], refs[before : before + 8], refs[before + 8 :]
     span = CHUNK * size
+    base = 0
+    for ref, out_ref in zip(earlier, query):
+        base = ref.shape[0]
+        out_ref[:base] = ref[...]
     for rel, send_ref in enumerate(sends):
         source = pl.multiple_of(((z ^ (rel // 2)) * 2 + (c ^ (rel % 2))) * span, 16)
         for dx, (one_ref, two_ref) in enumerate(((own_ref, y_ref), (x_ref, xy_ref))):
@@ -336,7 +342,7 @@
             norm = jnp.sum(total * total, axis=-1, keepdims=True)
             unit = (total * lax.rsqrt(norm + 1e-06)).astype(jnp.bfloat16)
             send_ref[dx * span : (dx + 1) * span] = unit
-            queries[dx][pl.ds(source, span)] = unit
+            query[dx][pl.ds(pl.multiple_of(base + source, 16), span)] = unit
         if send_ref.shape[0] > 2 * span:
             row = lax.broadcasted_iota(jnp.int32, (16, own_ref.shape[1]), 0)
             send_ref[2 * span :] = jnp.where(
@@ -346,24 +352,25 @@
             ).astype(jnp.bfloat16)
 
 
-def gather_unit(place, own, x, y, xy, size):
+def gather_unit(own, x, y, xy, earlier, size):
     width = own.shape[1]
     span = CHUNK * size
     extra = own.shape[0] - 8 * span
+    base = earlier[0].shape[0] if earlier else 0
     send = jax.ShapeDtypeStruct((2 * span + extra, width), jnp.bfloat16)
-    query = jax.ShapeDtypeStruct((8 * span, width), jnp.bfloat16)
-    return pl.pallas_call(
-        functools.partial(gather_unit_kernel, size),
+    query = jax.ShapeDtypeStruct((base + 8 * span, width), jnp.bfloat16)
+    return pl.pallas_call(
+        functools.partial(gather_unit_kernel, size, len(earlier)),
         out_shape=(send,) * 8 + (query,) * 2,
-        in_specs=[pl.BlockSpec(memory_space=SMEM)] + [pl.BlockSpec(memory_space=VMEM)] * 4,
+        in_specs=[pl.BlockSpec(memory_space=VMEM)] * (4 + len(earlier)),
         out_specs=[pl.BlockSpec(memory_space=VMEM)] * 10,
-        compiler_params=vmem_params(16),
-    )(place, own, x, y, xy)
-
-
-def cube_route_kernel(size, slots, parts, place_ref, *refs):
+        compiler_params=vmem_params(12),
+    )(own, x, y, xy, *earlier)
+
+
+def cube_route_kernel(size, slots, parts, *refs):
     spread, out_ref, pieces_ref, rows_ref, asked_ref, sem = refs[:parts], *refs[parts:]
-    z, x, c = place_ref[0], place_ref[1], place_ref[2]
+    z, x, c, _ = place()
     blocks = pieces_ref.shape[0] // 16
     span = CHUNK * size
     for i, ref in enumerate(spread):
@@ -389,13 +396,12 @@
     lax.fori_loop(0, 32, step, 0, unroll=4)
 
 
-def cube_route(place, spread, size, slots, blocks):
+def cube_route(spread, size, slots, blocks):
     width = spread[0].shape[1]
     return pl.pallas_call(
         functools.partial(cube_route_kernel, size, slots, len(spread)),
         out_shape=jax.ShapeDtypeStruct((32, slots, size, width), jnp.bfloat16),
-        in_specs=[pl.BlockSpec(memory_space=SMEM)]
-        + [pl.BlockSpec(memory_space=VMEM)] * len(spread),
+        in_specs=[pl.BlockSpec(memory_space=VMEM)] * len(spread),
         out_specs=pl.BlockSpec(memory_space=VMEM),
         scratch_shapes=[
             VMEM((16 * blocks, size, width), jnp.bfloat16),
@@ -404,38 +410,37 @@
             pltpu.SemaphoreType.DMA,
         ],
         compiler_params=vmem_params(16),
-    )(place, *spread)
-
-
-def queries_kernel(size, place_ref, *refs):
+    )(*spread)
+
+
+def queries_kernel(size, *refs):
     parts, out_ref = refs[:-1], refs[-1]
-    x, side = place_ref[1], place_ref[3]
-    for i, ref in enumerate(parts):
-        first, rel = i // 4 * CHUNK, i % 4
+    _, x, _, side = place()
+    for rel, ref in enumerate(parts):
         base = (side ^ (rel // 2)) * (16 * size) + (x ^ (rel % 2)) * (2 * size)
-        for z in range(4):
-            for c in range(2):
-                target = pl.multiple_of(base + z * 4 * size + c * size, 16)
-                for b in range(CHUNK):
-                    begin = ((z * 2 + c) * CHUNK + b) * size
-                    out_ref[first + b, pl.ds(target, size)] = ref[begin : begin + size]
-
-
-def queries(place, parts, size, blocks):
+        for first in range(0, out_ref.shape[0], CHUNK):
+            for z in range(4):
+                for c in range(2):
+                    target = pl.multiple_of(base + z * 4 * size + c * size, 16)
+                    for b in range(CHUNK):
+                        begin = (8 * first + (z * 2 + c) * CHUNK + b) * size
+                        out_ref[first + b, pl.ds(target, size)] = ref[begin : begin + size]
+
+
+def queries(parts, size, blocks):
     width = parts[0].shape[1]
     return pl.pallas_call(
         functools.partial(queries_kernel, size),
         out_shape=jax.ShapeDtypeStruct((blocks, 32 * size, width), jnp.bfloat16),
-        in_specs=[pl.BlockSpec(memory_space=SMEM)] + [pl.BlockSpec(memory_space=VMEM)] * len(parts),
+        in_specs=[pl.BlockSpec(memory_space=VMEM)] * len(parts),
         out_specs=pl.BlockSpec(memory_space=VMEM),
-        compiler_params=vmem_params(16),
-    )(place, *parts)
+        compiler_params=vmem_params(12),
+    )(*parts)
 
 
 def local_cube(states, proj_weight, lengths, query_block, cand_block, pair_valid):
     side = lax.axis_index("narrow").astype(jnp.int32)
     owner = lax.axis_index("wide").astype(jnp.int32)
-    place = jnp.stack([owner // 4, owner // 2 % 2, owner % 2, side])
     paras, length, width_part = states.shape
     width = proj_weight.shape[1]
     blocks = paras // BLK
@@ -453,21 +458,23 @@
         return lax.ppermute(array, "wide", [(i, i ^ flip) for i in range(16)])
 
     sel, first, second = plan(cand_block)
-    spread, query_parts = [], []
+    spread, query_parts = [], ()
     for c in range(0, blocks, CHUNK):
-        last = c + CHUNK == blocks
-        parts = split(place, sel if last else None, flat, proj_weight, c)
-        parts = [parts[0]] + [near(parts[rel], rel) for rel in (1, 2, 3)]
-        *sends, own, other = gather_unit(place, *parts, size)
-        spread += [sends[0]] + [along(sends[rel], rel) for rel in range(1, 8)]
-        query_parts.append((own, other))
-    outgoing = cube_route(place, spread, size, slots, blocks)
-    outgoing, query_parts = lax.optimization_barrier((outgoing, query_parts))
+        ids = sel if c + CHUNK == blocks else None
+        far = split(1, ids, flat, proj_weight, c)
+        own, aside = split(0, ids, flat, proj_weight, c)
+        if c:
+            far, aside, y, xy, x = lax.optimization_barrier((far, aside, y, xy, x))
+        y, xy, x = near(far[0], 2), near(far[1], 3), near(aside, 1)
+        *sends, own, other = gather_unit(own, x, y, xy, query_parts, size)
+        moved = {rel: along(sends[rel], rel) for rel in (4, 5, 6, 7, 2, 3, 1)}
+        spread += [sends[0]] + [moved[rel] for rel in range(1, 8)]
+        query_parts = (own, other)
+    outgoing = cube_route(spread, size, slots, blocks)
+    outgoing, (own, other) = lax.optimization_barrier((outgoing, query_parts))
     incoming = lax.all_to_all(outgoing, ("narrow", "wide"), 0, 0, tiled=True)
-    gathered = []
-    for own, other in query_parts:
-        gathered += [own, near(other, 1), near(own, 2), near(other, 3)]
-    query = queries(place, gathered, size, blocks)
+    gathered = {2: near(own, 2), 3: near(other, 3), 1: near(other, 1)}
+    query = queries([own] + [gathered[rel] for rel in (1, 2, 3)], size, blocks)
     cand = incoming.transpose(1, 0, 2, 3).reshape(-1, rows, width)
     part = score(
         jnp.stack([owner, side]), sel, first, second, query_block, lengths, pair_valid, query, cand, length

time: 122 us -> 111 us (0.910)
  starting transfers between devices: 45 us -> 36.2 us
  Pallas kernels: 28.7 us -> 24.6 us
  waiting for transfers between devices: 44.6 us -> 46.5 us
  local copies, waits for them, and re-layouts: 1.63 us -> 2.88 us
    ppermute x12 -> x9, starting transfers between devices: 21.8 us -> 11.7 us  [near(): lax.ppermute(array, ('wide', 'narrow'), [(i, i ^ flip) for i in range(32)])]
    pallas_call x4 -> x6, Pallas kernels: 12.3 us -> 9.24 us  [the longest x4 8.63 us: split(): pl.pallas_call(functools.partial(split_kernel, first, over, sel_count), o...]
    ppermute x12 -> x9, waiting for transfers between devices: 33.2 us -> 35.7 us  [near(): lax.ppermute(array, ('wide', 'narrow'), [(i, i ^ flip) for i in range(32)])]
    ppermute x14, waiting for transfers between devices: 8.26 us -> 6.73 us  [along(): return lax.ppermute(array, 'wide', [(i, i ^ flip) for i in range(16)])]
    transpose x1, local copies, waits for them, and re-layouts: 0.08 us -> 1.35 us  [local_cube(): cand = incoming.transpose(1, 0, 2, 3).reshape(-1, rows, width)]
  transfers between devices with their start and end apart: 28 -> 25, of which waited for: 8 -> 10; matrix products, arithmetic and copies ran while one was open for 0% -> 0% of each run, Pallas kernels for 8% -> 8%
where the time goes in v3:
time: 111 us
  waiting for transfers between devices  46.5 us (42%)
  starting transfers between devices  36.2 us (33%)
  Pallas kernels  24.6 us (22%)
  local copies, waits for them, and re-layouts  2.88 us (3%)
    ppermute x9, waiting for transfers between devices, near(): lax.ppermute(array, ('wide', 'narrow'), [(i, i ^ flip) for i in range(32)])  35.7 us
    ppermute x14, starting transfers between devices, along(): return lax.ppermute(array, 'wide', [(i, i ^ flip) for i in range(16)])  17.6 us
    ppermute x9, starting transfers between devices, near(): lax.ppermute(array, ('wide', 'narrow'), [(i, i ^ flip) for i in range(32)])  11.7 us
    pallas_call x1, Pallas kernels, score(): pl.pallas_call(functools.partial(score_kernel, length), out_shape=jax.Sha...  11.3 us
    pallas_call x4, Pallas kernels, split(): pl.pallas_call(functools.partial(split_kernel, first, over, sel_count), o...  8.63 us
    ppermute x14, waiting for transfers between devices, along(): return lax.ppermute(array, 'wide', [(i, i ^ flip) for i in range(16)])  6.73 us
    all_to_all x1, starting transfers between devices, local_cube(): incoming = lax.all_to_all(outgoing, ('narrow', 'wide'), 0, 0, tiled=True)  6.25 us
    ppermute x1, waiting for transfers between devices, local_cube(): return part + lax.ppermute(part, 'narrow', [(0, 1), (1, 0)])  4.01 us
  transfers between devices with their start and end apart: 25, of which 10 were waited for; matrix products, arithmetic and copies ran while one was open for 0% of the time, Pallas kernels for 8%

profile of v3, /device:TPU:0, one launch (start us, length us, event | category | flops | bytes accessed | tf_op | source)
XLA Modules:
  0.0 111.1 jit_solution(11621567373695369589)
XLA Ops:
  0.9 1.9 %shard_map.65 = (bf16[768,128]{1,0:T(8,128)(2,1)S(1)}, bf16[768,128]{1,0:T(8,128)(2,1)S(1)}) custom-call(bf16[4,1536,512]{2,1,0:T(8,128)(2,1)} %bitcast.6, bf16[512,128]{1,0:T(8,128)(2,1)S(1)} %copy-done), custom_call_target="tpu_custom_call" | custom-call | flops 201326592 | bytes 1572864 | tf_op jit(solution)/shard_map/pallas_call | solution.py:310
  2.8 3.0 %collective-permute-start = (bf16[768,128]{1,0:T(8,128)(2,1)S(1)}, bf16[768,128]{1,0:T(8,128)(2,1)S(1)}, u32[]{:S(2)}, u32[]{:S(2)}) collective-permute-start(bf16[768,128]{1,0:T(8,128)(2,1)S(1)} %get-tuple-element.46), channel_id=1, source_target_pairs={{0,4},{1,5},{2,6},{3,7},{4,0},{5,1},{6,2},{7,3},{8,12},{9,13},{10,... | collective-permute-start | bytes 589832 | tf_op jit(solution)/shard_map/ppermute | solution.py:454
  5.8 1.9 %shard_map.66 = (bf16[768,128]{1,0:T(8,128)(2,1)S(1)}, bf16[768,128]{1,0:T(8,128)(2,1)S(1)}) custom-call(bf16[4,1536,512]{2,1,0:T(8,128)(2,1)} %bitcast.7, bf16[512,128]{1,0:T(8,128)(2,1)S(1)} %copy-done), custom_call_target="tpu_custom_call" | custom-call | flops 201326592 | bytes 1572864 | tf_op jit(solution)/shard_map/pallas_call | solution.py:310
  7.7 1.6 %collective-permute-start.1 = (bf16[768,128]{1,0:T(8,128)(2,1)S(1)}, bf16[768,128]{1,0:T(8,128)(2,1)S(1)}, u32[]{:S(2)}, u32[]{:S(2)}) collective-permute-start(bf16[768,128]{1,0:T(8,128)(2,1)S(1)} %get-tuple-element.47), channel_id=1, source_target_pairs={{0,1},{1,0},{2,3},{3,2},{4,5},{5,4},{6,7},{7,6},{8,9},{9,8},{10,11... | collective-permute-start | bytes 589832 | tf_op jit(solution)/shard_map/ppermute | solution.py:454
  9.3 1.7 %shard_map.64 = (s32[6]{0:T(128)}, s32[6]{0:T(128)}, s32[6]{0:T(128)}) custom-call(s32[12]{0:T(128)} %cand_ref.1), custom_call_target="tpu_custom_call" | custom-call | tf_op jit(solution)/shard_map/pallas_call | solution.py:53
  11.7 2.4 %shard_map.69 = (bf16[784,128]{1,0:T(8,128)(2,1)S(1)}, bf16[784,128]{1,0:T(8,128)(2,1)S(1)}) custom-call(s32[6]{0:T(128)S(1)} %copy-done.2, bf16[4,1536,512]{2,1,0:T(8,128)(2,1)} %bitcast.8, bf16[512,128]{1,0:T(8,128)(2,1)S(1)} %copy-done.1), custom_call_target="tpu_custom_call" | custom-call | flops 201326592 | bytes 1572864 | tf_op jit(solution)/shard_map/pallas_call | solution.py:310
  14.1 2.4 %shard_map.68 = (bf16[784,128]{1,0:T(8,128)(2,1)S(1)}, bf16[784,128]{1,0:T(8,128)(2,1)S(1)}) custom-call(s32[6]{0:T(128)S(1)} %copy-done.2, bf16[4,1536,512]{2,1,0:T(8,128)(2,1)} %bitcast.9, bf16[512,128]{1,0:T(8,128)(2,1)S(1)} %copy-done.1), custom_call_target="tpu_custom_call" | custom-call | flops 201326592 | bytes 1572864 | tf_op jit(solution)/shard_map/pallas_call | solution.py:310
  16.6 1.7 %collective-permute-done.1.y_ref = bf16[768,128]{1,0:T(8,128)(2,1)S(1)} collective-permute-done((bf16[768,128]{1,0:T(8,128)(2,1)S(1)}, bf16[768,128]{1,0:T(8,128)(2,1)S(1)}, u32[]{:S(2)}, u32[]{:S(2)}) %collective-permute-start.1) | collective-permute-done | bytes 196640 | tf_op jit(solution)/shard_map/ppermute | solution.py:454
  18.7 1.7 %collective-permute-start.11 = (bf16[784,128]{1,0:T(8,128)(2,1)S(1)}, bf16[784,128]{1,0:T(8,128)(2,1)S(1)}, u32[]{:S(2)}, u32[]{:S(2)}) collective-permute-start(bf16[784,128]{1,0:T(8,128)(2,1)S(1)} %get-tuple-element.62), channel_id=1, source_target_pairs={{0,1},{1,0},{2,3},{3,2},{4,5},{5,4},{6,7},{7,6},{8,9},{9,8},{10,11... | collective-permute-start | bytes 602120 | tf_op jit(solution)/shard_map/ppermute | solution.py:454
  20.4 1.4 %collective-permute-start.12 = (bf16[784,128]{1,0:T(8,128)(2,1)S(1)}, bf16[784,128]{1,0:T(8,128)(2,1)S(1)}, u32[]{:S(2)}, u32[]{:S(2)}) collective-permute-start(bf16[784,128]{1,0:T(8,128)(2,1)S(1)} %get-tuple-element.63), channel_id=1, source_target_pairs={{0,5},{1,4},{2,7},{3,6},{4,1},{5,0},{6,3},{7,2},{8,13},{9,12},{10,... | collective-permute-start | bytes 602120 | tf_op jit(solution)/shard_map/ppermute | solution.py:454
  22.2 1.6 %collective-permute-start.4 = (bf16[192,128]{1,0:T(8,128)(2,1)S(1)}, bf16[192,128]{1,0:T(8,128)(2,1)S(1)}, u32[]{:S(2)}, u32[]{:S(2)}) collective-permute-start(bf16[192,128]{1,0:T(8,128)(2,1)S(1)} %get-tuple-element.51), channel_id=1, source_target_pairs={{0,8},{2,10},{4,12},{6,14},{8,0},{10,2},{12,4},{14,6},{16,24},{18,... | collective-permute-start | bytes 147464 | tf_op jit(solution)/shard_map/ppermute | solution.py:458
  23.8 2.2 %collective-permute-done.10.x_ref = bf16[784,128]{1,0:T(8,128)(2,1)S(1)} collective-permute-done((bf16[784,128]{1,0:T(8,128)(2,1)S(1)}, bf16[784,128]{1,0:T(8,128)(2,1)S(1)}, u32[]{:S(2)}, u32[]{:S(2)}) %collective-permute-start.10) | collective-permute-done | bytes 200736 | tf_op jit(solution)/shard_map/ppermute | solution.py:454
  26.0 1.7 %collective-permute-done.11.y_ref = bf16[784,128]{1,0:T(8,128)(2,1)S(1)} collective-permute-done((bf16[784,128]{1,0:T(8,128)(2,1)S(1)}, bf16[784,128]{1,0:T(8,128)(2,1)S(1)}, u32[]{:S(2)}, u32[]{:S(2)}) %collective-permute-start.11) | collective-permute-done | bytes 200736 | tf_op jit(solution)/shard_map/ppermute | solution.py:454
  27.7 2.5 %collective-permute-start.6 = (bf16[192,128]{1,0:T(8,128)(2,1)S(1)}, bf16[192,128]{1,0:T(8,128)(2,1)S(1)}, u32[]{:S(2)}, u32[]{:S(2)}) collective-permute-start(bf16[192,128]{1,0:T(8,128)(2,1)S(1)} %get-tuple-element.53), channel_id=1, source_target_pairs={{0,16},{2,18},{4,20},{6,22},{8,24},{10,26},{12,28},{14,30},{16,0},... | collective-permute-start | bytes 147464 | tf_op jit(solution)/shard_map/ppermute | solution.py:458
  30.6 1.6 %collective-permute-start.14 = (bf16[208,128]{1,0:T(8,128)(2,1)S(1)}, bf16[208,128]{1,0:T(8,128)(2,1)S(1)}, u32[]{:S(2)}, u32[]{:S(2)}) collective-permute-start(bf16[208,128]{1,0:T(8,128)(2,1)S(1)} %get-tuple-element.68), channel_id=1, source_target_pairs={{0,8},{2,10},{4,12},{6,14},{8,0},{10,2},{12,4},{14,6},{16,24},{18,... | collective-permute-start | bytes 159752 | tf_op jit(solution)/shard_map/ppermute | solution.py:458
  32.3 1.5 %collective-permute-start.7 = (bf16[192,128]{1,0:T(8,128)(2,1)S(1)}, bf16[192,128]{1,0:T(8,128)(2,1)S(1)}, u32[]{:S(2)}, u32[]{:S(2)}) collective-permute-start(bf16[192,128]{1,0:T(8,128)(2,1)S(1)} %get-tuple-element.54), channel_id=1, source_target_pairs={{0,18},{2,16},{4,22},{6,20},{8,26},{10,24},{12,30},{14,28},{16,2},... | collective-permute-start | bytes 147464 | tf_op jit(solution)/shard_map/ppermute | solution.py:458
  34.9 2.4 %collective-permute-start.9 = (bf16[192,128]{1,0:T(8,128)(2,1)S(1)}, bf16[192,128]{1,0:T(8,128)(2,1)S(1)}, u32[]{:S(2)}, u32[]{:S(2)}) collective-permute-start(bf16[192,128]{1,0:T(8,128)(2,1)S(1)} %get-tuple-element.56), channel_id=1, source_target_pairs={{0,26},{2,24},{4,30},{6,28},{8,18},{10,16},{12,22},{14,20},{16,10}... | collective-permute-start | bytes 147464 | tf_op jit(solution)/shard_map/ppermute | solution.py:458
  38.1 1.6 %collective-permute-done.8.refs_6_ = bf16[192,128]{1,0:T(8,128)(2,1)S(1)} collective-permute-done((bf16[192,128]{1,0:T(8,128)(2,1)S(1)}, bf16[192,128]{1,0:T(8,128)(2,1)S(1)}, u32[]{:S(2)}, u32[]{:S(2)}) %collective-permute-start.8) | collective-permute-done | bytes 49184 | tf_op jit(solution)/shard_map/ppermute | solution.py:458
  39.7 1.4 %collective-permute-start.16 = (bf16[208,128]{1,0:T(8,128)(2,1)S(1)}, bf16[208,128]{1,0:T(8,128)(2,1)S(1)}, u32[]{:S(2)}, u32[]{:S(2)}) collective-permute-start(bf16[208,128]{1,0:T(8,128)(2,1)S(1)} %get-tuple-element.70), channel_id=1, source_target_pairs={{0,16},{2,18},{4,20},{6,22},{8,24},{10,26},{12,28},{14,30},{16,0},... | collective-permute-start | bytes 159752 | tf_op jit(solution)/shard_map/ppermute | solution.py:458
  41.1 1.7 %collective-permute-start.17 = (bf16[208,128]{1,0:T(8,128)(2,1)S(1)}, bf16[208,128]{1,0:T(8,128)(2,1)S(1)}, u32[]{:S(2)}, u32[]{:S(2)}) collective-permute-start(bf16[208,128]{1,0:T(8,128)(2,1)S(1)} %get-tuple-element.71), channel_id=1, source_target_pairs={{0,18},{2,16},{4,22},{6,20},{8,26},{10,24},{12,30},{14,28},{16,2},... | collective-permute-start | bytes 159752 | tf_op jit(solution)/shard_map/ppermute | solution.py:458
  42.8 2.2 %collective-permute-start.18 = (bf16[208,128]{1,0:T(8,128)(2,1)S(1)}, bf16[208,128]{1,0:T(8,128)(2,1)S(1)}, u32[]{:S(2)}, u32[]{:S(2)}) collective-permute-start(bf16[208,128]{1,0:T(8,128)(2,1)S(1)} %get-tuple-element.72), channel_id=1, source_target_pairs={{0,24},{2,26},{4,28},{6,30},{8,16},{10,18},{12,20},{14,22},{16,8},... | collective-permute-start | bytes 159752 | tf_op jit(solution)/shard_map/ppermute | solution.py:458
  45.0 1.4 %collective-permute-start.19 = (bf16[208,128]{1,0:T(8,128)(2,1)S(1)}, bf16[208,128]{1,0:T(8,128)(2,1)S(1)}, u32[]{:S(2)}, u32[]{:S(2)}) collective-permute-start(bf16[208,128]{1,0:T(8,128)(2,1)S(1)} %get-tuple-element.73), channel_id=1, source_target_pairs={{0,26},{2,24},{4,30},{6,28},{8,18},{10,16},{12,22},{14,20},{16,10}... | collective-permute-start | bytes 159752 | tf_op jit(solution)/shard_map/ppermute | solution.py:458
  46.4 3.0 %collective-permute-done.17.refs_13_ = bf16[208,128]{1,0:T(8,128)(2,1)S(1)} collective-permute-done((bf16[208,128]{1,0:T(8,128)(2,1)S(1)}, bf16[208,128]{1,0:T(8,128)(2,1)S(1)}, u32[]{:S(2)}, u32[]{:S(2)}) %collective-permute-start.17) | collective-permute-done | bytes 53280 | tf_op jit(solution)/shard_map/ppermute | solution.py:458
  50.7 2.2 %shard_map.71 = bf16[32,3,48,128]{3,2,1,0:T(8,128)(2,1)} custom-call(bf16[192,128]{1,0:T(8,128)(2,1)S(1)} %get-tuple-element.49.refs_0_, bf16[192,128]{1,0:T(8,128)(2,1)S(1)} %collective-permute-done.3.refs_1_, bf16[192,128]{1,0:T(8,128)(2,1)S(1)} %collective-permute-done.4.refs_2_, bf16[192,128]{1,0:T(8,128)(2,1)S(1)} %collective-permute-done.5.refs_3_, ...), custom_call_target="tpu_custom_call" | custom-call | tf_op jit(solution)/shard_map/pallas_call | solution.py:401
  52.9 6.3 %all-to-all-start = ((bf16[32,3,48,128]{3,2,1,0:T(8,128)(2,1)}), bf16[32,3,48,128]{3,2,1,0:T(8,128)(2,1)}, u32[]{:S(2)}, u32[]{:S(2)}) async-start(bf16[32,3,48,128]{3,2,1,0:T(8,128)(2,1)} %shard_map.71), calls=%async_computation | async-start | bytes 2359296 | tf_op jit(solution)/shard_map/all_to_all | solution.py:475
  59.2 1.8 %collective-permute-start.20 = (bf16[1536,128]{1,0:T(8,128)(2,1)S(1)}, bf16[1536,128]{1,0:T(8,128)(2,1)S(1)}, u32[]{:S(2)}, u32[]{:S(2)}) collective-permute-start(bf16[1536,128]{1,0:T(8,128)(2,1)S(1)} %get-tuple-element.77), channel_id=1, source_target_pairs={{0,4},{1,5},{2,6},{3,7},{4,0},{5,1},{6,2},{7,3},{8,12},{9,13},{10,... | collective-permute-start | bytes 1179656 | tf_op jit(solution)/shard_map/ppermute | solution.py:454
  60.9 1.5 %collective-permute-start.21 = (bf16[1536,128]{1,0:T(8,128)(2,1)S(1)}, bf16[1536,128]{1,0:T(8,128)(2,1)S(1)}, u32[]{:S(2)}, u32[]{:S(2)}) collective-permute-start(bf16[1536,128]{1,0:T(8,128)(2,1)S(1)} %get-tuple-element.76.refs_0_), channel_id=1, source_target_pairs={{0,1},{1,0},{2,3},{3,2},{4,5},{5,4},{6,7},{7,6},{8,9},{9,8},{10,11... | collective-permute-start | bytes 1179656 | tf_op jit(solution)/shard_map/ppermute | solution.py:454
  62.8 18.7 %collective-permute-done.20.refs_1_ = bf16[1536,128]{1,0:T(8,128)(2,1)S(1)} collective-permute-done((bf16[1536,128]{1,0:T(8,128)(2,1)S(1)}, bf16[1536,128]{1,0:T(8,128)(2,1)S(1)}, u32[]{:S(2)}, u32[]{:S(2)}) %collective-permute-start.20) | collective-permute-done | bytes 393248 | tf_op jit(solution)/shard_map/ppermute | solution.py:454
  81.5 11.4 %collective-permute-done.22.refs_3_ = bf16[1536,128]{1,0:T(8,128)(2,1)S(1)} collective-permute-done((bf16[1536,128]{1,0:T(8,128)(2,1)S(1)}, bf16[1536,128]{1,0:T(8,128)(2,1)S(1)}, u32[]{:S(2)}, u32[]{:S(2)}) %collective-permute-start.22) | collective-permute-done | bytes 393248 | tf_op jit(solution)/shard_map/ppermute | solution.py:454
  93.1 1.3 %copy.7 = bf16[3,32,48,128]{3,2,1,0:T(8,128)(2,1)S(1)} copy(bf16[3,32,48,128]{3,2,0,1:T(8,128)(2,1)} %bitcast.3) | data formatting | bytes 2359296 | tf_op jit(solution)/shard_map/transpose | solution.py:478
  94.6 11.3 %shard_map.73 = f32[12,12,12]{2,1,0:T(8,128)S(1)} custom-call(s32[2]{0:T(128)S(1)} %pad_add_fusion.where_ref, s32[6]{0:T(128)S(1)} %copy-done.3, s32[6]{0:T(128)S(1)} %copy-done.7, s32[6]{0:T(128)S(1)} %copy-done.8, s32[12]{0:T(128)S(1)} %copy-done.5, s32[768]{0:T(1024)S(1)} %copy-done.4, s32[12]{0:T(128)S(1)} %copy-done.6, ...), custom_call_target="tpu_custom_call" | custom-call | flops 3623878656 | bytes 786432 | tf_op jit(solution)/shard_map/pallas_call | solution.py:203
  106.5 4.0 %collective-permute-done.23 = f32[12,12,12]{2,1,0:T(8,128)S(1)} collective-permute-done((f32[12,12,12]{2,1,0:T(8,128)S(1)}, f32[12,12,12]{2,1,0:T(8,128)S(1)}, u32[]{:S(2)}, u32[]{:S(2)}) %collective-permute-start.23) | collective-permute-done | bytes 6944 | tf_op jit(solution)/shard_map/ppermute | solution.py:482
  (49 shorter events, 7.7 us)
Async XLA Ops:
  2.8 8.3 %copy-start.1 = (bf16[512,128]{1,0:T(8,128)(2,1)S(1)}, bf16[512,128]{1,0:T(8,128)(2,1)}, u32[]{:S(2)}) copy-start(bf16[512,128]{1,0:T(8,128)(2,1)} %refs_2_.3) | copy-start | bytes 393220
  2.8 13.8 %collective-permute-start = (bf16[768,128]{1,0:T(8,128)(2,1)S(1)}, bf16[768,128]{1,0:T(8,128)(2,1)S(1)}, u32[]{:S(2)}, u32[]{:S(2)}) collective-permute-start(bf16[768,128]{1,0:T(8,128)(2,1)S(1)} %get-tuple-element.46), channel_id=1, source_target_pairs={{0,4},{1,5},{2,6},{3,7},{4,0},{5,1},{6,2},{7,3},{8,12},{9,13},{10,... | collective-permute-start | bytes 589832 | tf_op jit(solution)/shard_map/ppermute | solution.py:454
  7.7 10.6 %collective-permute-start.1 = (bf16[768,128]{1,0:T(8,128)(2,1)S(1)}, bf16[768,128]{1,0:T(8,128)(2,1)S(1)}, u32[]{:S(2)}, u32[]{:S(2)}) collective-permute-start(bf16[768,128]{1,0:T(8,128)(2,1)S(1)} %get-tuple-element.47), channel_id=1, source_target_pairs={{0,1},{1,0},{2,3},{3,2},{4,5},{5,4},{6,7},{7,6},{8,9},{9,8},{10,11... | collective-permute-start | bytes 589832 | tf_op jit(solution)/shard_map/ppermute | solution.py:454
  9.3 9.1 %collective-permute-start.2 = (bf16[768,128]{1,0:T(8,128)(2,1)S(1)}, bf16[768,128]{1,0:T(8,128)(2,1)S(1)}, u32[]{:S(2)}, u32[]{:S(2)}) collective-permute-start(bf16[768,128]{1,0:T(8,128)(2,1)S(1)} %get-tuple-element.48), channel_id=1, source_target_pairs={{0,5},{1,4},{2,7},{3,6},{4,1},{5,0},{6,3},{7,2},{8,13},{9,12},{10,... | collective-permute-start | bytes 589832 | tf_op jit(solution)/shard_map/ppermute | solution.py:454
  18.3 7.7 %collective-permute-start.10 = (bf16[784,128]{1,0:T(8,128)(2,1)S(1)}, bf16[784,128]{1,0:T(8,128)(2,1)S(1)}, u32[]{:S(2)}, u32[]{:S(2)}) collective-permute-start(bf16[784,128]{1,0:T(8,128)(2,1)S(1)} %get-tuple-element.61), channel_id=1, source_target_pairs={{0,4},{1,5},{2,6},{3,7},{4,0},{5,1},{6,2},{7,3},{8,12},{9,13},{10,... | collective-permute-start | bytes 602120 | tf_op jit(solution)/shard_map/ppermute | solution.py:454
  18.7 9.0 %collective-permute-start.11 = (bf16[784,128]{1,0:T(8,128)(2,1)S(1)}, bf16[784,128]{1,0:T(8,128)(2,1)S(1)}, u32[]{:S(2)}, u32[]{:S(2)}) collective-permute-start(bf16[784,128]{1,0:T(8,128)(2,1)S(1)} %get-tuple-element.62), channel_id=1, source_target_pairs={{0,1},{1,0},{2,3},{3,2},{4,5},{5,4},{6,7},{7,6},{8,9},{9,8},{10,11... | collective-permute-start | bytes 602120 | tf_op jit(solution)/shard_map/ppermute | solution.py:454
  20.4 9.8 %collective-permute-start.12 = (bf16[784,128]{1,0:T(8,128)(2,1)S(1)}, bf16[784,128]{1,0:T(8,128)(2,1)S(1)}, u32[]{:S(2)}, u32[]{:S(2)}) collective-permute-start(bf16[784,128]{1,0:T(8,128)(2,1)S(1)} %get-tuple-element.63), channel_id=1, source_target_pairs={{0,5},{1,4},{2,7},{3,6},{4,1},{5,0},{6,3},{7,2},{8,13},{9,12},{10,... | collective-permute-start | bytes 602120 | tf_op jit(solution)/shard_map/ppermute | solution.py:454
  22.1 8.5 %collective-permute-start.3 = (bf16[192,128]{1,0:T(8,128)(2,1)S(1)}, bf16[192,128]{1,0:T(8,128)(2,1)S(1)}, u32[]{:S(2)}, u32[]{:S(2)}) collective-permute-start(bf16[192,128]{1,0:T(8,128)(2,1)S(1)} %get-tuple-element.50), channel_id=1, source_target_pairs={{0,2},{2,0},{4,6},{6,4},{8,10},{10,8},{12,14},{14,12},{16,18},{18,... | collective-permute-start | bytes 147464 | tf_op jit(solution)/shard_map/ppermute | solution.py:458
  22.2 10.1 %collective-permute-start.4 = (bf16[192,128]{1,0:T(8,128)(2,1)S(1)}, bf16[192,128]{1,0:T(8,128)(2,1)S(1)}, u32[]{:S(2)}, u32[]{:S(2)}) collective-permute-start(bf16[192,128]{1,0:T(8,128)(2,1)S(1)} %get-tuple-element.51), channel_id=1, source_target_pairs={{0,8},{2,10},{4,12},{6,14},{8,0},{10,2},{12,4},{14,6},{16,24},{18,... | collective-permute-start | bytes 147464 | tf_op jit(solution)/shard_map/ppermute | solution.py:458
  26.0 7.7 %collective-permute-start.5 = (bf16[192,128]{1,0:T(8,128)(2,1)S(1)}, bf16[192,128]{1,0:T(8,128)(2,1)S(1)}, u32[]{:S(2)}, u32[]{:S(2)}) collective-permute-start(bf16[192,128]{1,0:T(8,128)(2,1)S(1)} %get-tuple-element.52), channel_id=1, source_target_pairs={{0,10},{2,8},{4,14},{6,12},{8,2},{10,0},{12,6},{14,4},{16,26},{18,... | collective-permute-start | bytes 147464 | tf_op jit(solution)/shard_map/ppermute | solution.py:458
  27.7 7.2 %collective-permute-start.6 = (bf16[192,128]{1,0:T(8,128)(2,1)S(1)}, bf16[192,128]{1,0:T(8,128)(2,1)S(1)}, u32[]{:S(2)}, u32[]{:S(2)}) collective-permute-start(bf16[192,128]{1,0:T(8,128)(2,1)S(1)} %get-tuple-element.53), channel_id=1, source_target_pairs={{0,16},{2,18},{4,20},{6,22},{8,24},{10,26},{12,28},{14,30},{16,0},... | collective-permute-start | bytes 147464 | tf_op jit(solution)/shard_map/ppermute | solution.py:458
  30.5 12.3 %collective-permute-start.13 = (bf16[208,128]{1,0:T(8,128)(2,1)S(1)}, bf16[208,128]{1,0:T(8,128)(2,1)S(1)}, u32[]{:S(2)}, u32[]{:S(2)}) collective-permute-start(bf16[208,128]{1,0:T(8,128)(2,1)S(1)} %get-tuple-element.67), channel_id=1, source_target_pairs={{0,2},{2,0},{4,6},{6,4},{8,10},{10,8},{12,14},{14,12},{16,18},{18,... | collective-permute-start | bytes 159752 | tf_op jit(solution)/shard_map/ppermute | solution.py:458
  30.6 14.4 %collective-permute-start.14 = (bf16[208,128]{1,0:T(8,128)(2,1)S(1)}, bf16[208,128]{1,0:T(8,128)(2,1)S(1)}, u32[]{:S(2)}, u32[]{:S(2)}) collective-permute-start(bf16[208,128]{1,0:T(8,128)(2,1)S(1)} %get-tuple-element.68), channel_id=1, source_target_pairs={{0,8},{2,10},{4,12},{6,14},{8,0},{10,2},{12,4},{14,6},{16,24},{18,... | collective-permute-start | bytes 159752 | tf_op jit(solution)/shard_map/ppermute | solution.py:458
  32.3 5.8 %collective-permute-start.7 = (bf16[192,128]{1,0:T(8,128)(2,1)S(1)}, bf16[192,128]{1,0:T(8,128)(2,1)S(1)}, u32[]{:S(2)}, u32[]{:S(2)}) collective-permute-start(bf16[192,128]{1,0:T(8,128)(2,1)S(1)} %get-tuple-element.54), channel_id=1, source_target_pairs={{0,18},{2,16},{4,22},{6,20},{8,26},{10,24},{12,30},{14,28},{16,2},... | collective-permute-start | bytes 147464 | tf_op jit(solution)/shard_map/ppermute | solution.py:458
  33.7 5.9 %collective-permute-start.8 = (bf16[192,128]{1,0:T(8,128)(2,1)S(1)}, bf16[192,128]{1,0:T(8,128)(2,1)S(1)}, u32[]{:S(2)}, u32[]{:S(2)}) collective-permute-start(bf16[192,128]{1,0:T(8,128)(2,1)S(1)} %get-tuple-element.55), channel_id=1, source_target_pairs={{0,24},{2,26},{4,28},{6,30},{8,16},{10,18},{12,20},{14,22},{16,8},... | collective-permute-start | bytes 147464 | tf_op jit(solution)/shard_map/ppermute | solution.py:458
  34.9 6.3 %collective-permute-start.9 = (bf16[192,128]{1,0:T(8,128)(2,1)S(1)}, bf16[192,128]{1,0:T(8,128)(2,1)S(1)}, u32[]{:S(2)}, u32[]{:S(2)}) collective-permute-start(bf16[192,128]{1,0:T(8,128)(2,1)S(1)} %get-tuple-element.56), channel_id=1, source_target_pairs={{0,26},{2,24},{4,30},{6,28},{8,18},{10,16},{12,22},{14,20},{16,10}... | collective-permute-start | bytes 147464 | tf_op jit(solution)/shard_map/ppermute | solution.py:458
  38.1 8.3 %collective-permute-start.15 = (bf16[208,128]{1,0:T(8,128)(2,1)S(1)}, bf16[208,128]{1,0:T(8,128)(2,1)S(1)}, u32[]{:S(2)}, u32[]{:S(2)}) collective-permute-start(bf16[208,128]{1,0:T(8,128)(2,1)S(1)} %get-tuple-element.69), channel_id=1, source_target_pairs={{0,10},{2,8},{4,14},{6,12},{8,2},{10,0},{12,6},{14,4},{16,26},{18,... | collective-permute-start | bytes 159752 | tf_op jit(solution)/shard_map/ppermute | solution.py:458
  39.7 6.7 %collective-permute-start.16 = (bf16[208,128]{1,0:T(8,128)(2,1)S(1)}, bf16[208,128]{1,0:T(8,128)(2,1)S(1)}, u32[]{:S(2)}, u32[]{:S(2)}) collective-permute-start(bf16[208,128]{1,0:T(8,128)(2,1)S(1)} %get-tuple-element.70), channel_id=1, source_target_pairs={{0,16},{2,18},{4,20},{6,22},{8,24},{10,26},{12,28},{14,30},{16,0},... | collective-permute-start | bytes 159752 | tf_op jit(solution)/shard_map/ppermute | solution.py:458
  41.1 8.3 %collective-permute-start.17 = (bf16[208,128]{1,0:T(8,128)(2,1)S(1)}, bf16[208,128]{1,0:T(8,128)(2,1)S(1)}, u32[]{:S(2)}, u32[]{:S(2)}) collective-permute-start(bf16[208,128]{1,0:T(8,128)(2,1)S(1)} %get-tuple-element.71), channel_id=1, source_target_pairs={{0,18},{2,16},{4,22},{6,20},{8,26},{10,24},{12,30},{14,28},{16,2},... | collective-permute-start | bytes 159752 | tf_op jit(solution)/shard_map/ppermute | solution.py:458
  42.8 6.6 %collective-permute-start.18 = (bf16[208,128]{1,0:T(8,128)(2,1)S(1)}, bf16[208,128]{1,0:T(8,128)(2,1)S(1)}, u32[]{:S(2)}, u32[]{:S(2)}) collective-permute-start(bf16[208,128]{1,0:T(8,128)(2,1)S(1)} %get-tuple-element.72), channel_id=1, source_target_pairs={{0,24},{2,26},{4,28},{6,30},{8,16},{10,18},{12,20},{14,22},{16,8},... | collective-permute-start | bytes 159752 | tf_op jit(solution)/shard_map/ppermute | solution.py:458
  45.0 5.7 %collective-permute-start.19 = (bf16[208,128]{1,0:T(8,128)(2,1)S(1)}, bf16[208,128]{1,0:T(8,128)(2,1)S(1)}, u32[]{:S(2)}, u32[]{:S(2)}) collective-permute-start(bf16[208,128]{1,0:T(8,128)(2,1)S(1)} %get-tuple-element.73), channel_id=1, source_target_pairs={{0,26},{2,24},{4,30},{6,28},{8,18},{10,16},{12,22},{14,20},{16,10}... | collective-permute-start | bytes 159752 | tf_op jit(solution)/shard_map/ppermute | solution.py:458
  52.9 40.2 %all-to-all-start = ((bf16[32,3,48,128]{3,2,1,0:T(8,128)(2,1)}), bf16[32,3,48,128]{3,2,1,0:T(8,128)(2,1)}, u32[]{:S(2)}, u32[]{:S(2)}) async-start(bf16[32,3,48,128]{3,2,1,0:T(8,128)(2,1)} %shard_map.71), calls=%async_computation | async-start | bytes 2359296 | tf_op jit(solution)/shard_map/all_to_all | solution.py:475
  59.2 22.3 %collective-permute-start.20 = (bf16[1536,128]{1,0:T(8,128)(2,1)S(1)}, bf16[1536,128]{1,0:T(8,128)(2,1)S(1)}, u32[]{:S(2)}, u32[]{:S(2)}) collective-permute-start(bf16[1536,128]{1,0:T(8,128)(2,1)S(1)} %get-tuple-element.77), channel_id=1, source_target_pairs={{0,4},{1,5},{2,6},{3,7},{4,0},{5,1},{6,2},{7,3},{8,12},{9,13},{10,... | collective-permute-start | bytes 1179656 | tf_op jit(solution)/shard_map/ppermute | solution.py:454
  60.9 20.6 %collective-permute-start.21 = (bf16[1536,128]{1,0:T(8,128)(2,1)S(1)}, bf16[1536,128]{1,0:T(8,128)(2,1)S(1)}, u32[]{:S(2)}, u32[]{:S(2)}) collective-permute-start(bf16[1536,128]{1,0:T(8,128)(2,1)S(1)} %get-tuple-element.76.refs_0_), channel_id=1, source_target_pairs={{0,1},{1,0},{2,3},{3,2},{4,5},{5,4},{6,7},{7,6},{8,9},{9,8},{10,11... | collective-permute-start | bytes 1179656 | tf_op jit(solution)/shard_map/ppermute | solution.py:454
  62.4 30.5 %collective-permute-start.22 = (bf16[1536,128]{1,0:T(8,128)(2,1)S(1)}, bf16[1536,128]{1,0:T(8,128)(2,1)S(1)}, u32[]{:S(2)}, u32[]{:S(2)}) collective-permute-start(bf16[1536,128]{1,0:T(8,128)(2,1)S(1)} %get-tuple-element.77), channel_id=1, source_target_pairs={{0,5},{1,4},{2,7},{3,6},{4,1},{5,0},{6,3},{7,2},{8,13},{9,12},{10,... | collective-permute-start | bytes 1179656 | tf_op jit(solution)/shard_map/ppermute | solution.py:454
  93.1 1.4 %copy-start.3 = (s32[6]{0:T(128)S(1)}, s32[6]{0:T(128)}, u32[]{:S(2)}) copy-start(s32[6]{0:T(128)} %get-tuple-element.42.refs_0_.sel_ref) | copy-start | bytes 76
  93.1 1.4 %copy-start.4 = (s32[768]{0:T(1024)S(1)}, s32[768]{0:T(1024)}, u32[]{:S(2)}) copy-start(s32[768]{0:T(1024)} %lengths_ref.1) | copy-start | bytes 9220
  93.1 1.4 %copy-start.5 = (s32[12]{0:T(128)S(1)}, s32[12]{0:T(128)}, u32[]{:S(2)}) copy-start(s32[12]{0:T(128)} %query_block_ref.1) | copy-start | bytes 148
  93.1 1.4 %copy-start.6 = (s32[12]{0:T(128)S(1)}, s32[12]{0:T(128)}, u32[]{:S(2)}) copy-start(s32[12]{0:T(128)} %valid_ref.1) | copy-start | bytes 148
  93.1 1.4 %copy-start.7 = (s32[6]{0:T(128)S(1)}, s32[6]{0:T(128)}, u32[]{:S(2)}) copy-start(s32[6]{0:T(128)} %get-tuple-element.43.first_ref) | copy-start | bytes 76
  93.1 1.4 %copy-start.8 = (s32[6]{0:T(128)S(1)}, s32[6]{0:T(128)}, u32[]{:S(2)}) copy-start(s32[6]{0:T(128)} %get-tuple-element.44.second_ref) | copy-start | bytes 76
  105.9 4.6 %collective-permute-start.23 = (f32[12,12,12]{2,1,0:T(8,128)S(1)}, f32[12,12,12]{2,1,0:T(8,128)S(1)}, u32[]{:S(2)}, u32[]{:S(2)}) collective-permute-start(f32[12,12,12]{2,1,0:T(8,128)S(1)} %shard_map.73), channel_id=1, source_target_pairs={{0,1},{1,0},{2,3},{3,2},{4,5},{5,4},{6,7},{7,6},{8,9},{9,8},{10,11... | collective-permute-start | bytes 20744 | tf_op jit(solution)/shard_map/ppermute | solution.py:482
  (2 other events, 1.5 us)

commit v4 on v3

--- a/solution.py
+++ b/solution.py
@@ -12,7 +12,7 @@
 SHARPNESS = 20.0
 EXP2_SCALE = SHARPNESS * math.log2(math.e)
 COLS = 256
-CHUNK = 2
+CHUNK = 4
 SMEM = pltpu.SMEM
 VMEM = pltpu.VMEM
 
@@ -154,10 +154,11 @@
 
 def score_kernel(
     length, where_ref, sel_ref, first_ref, second_ref, query_block_ref, lengths_ref, valid_ref,
-    query_ref, cand_ref, out_ref, totals_ref,
+    query_ref, cand_ref, out_ref, totals_ref, *block_refs,
 ):
     owner, side = where_ref[0], where_ref[1]
-    slots, rows, _ = cand_ref.shape
+    rows = query_ref.shape[1]
+    slots = cand_ref.shape[-3]
     blocks = query_ref.shape[0]
     out_ref[...] = jnp.zeros_like(out_ref)
     totals_ref[...] = jnp.ones_like(totals_ref)
@@ -170,9 +171,13 @@
         block = sel_ref[slot]
         pair = jnp.where(i - 2 * k == 0, first_ref[slot], second_ref[slot])
         query = query_block_ref[pair]
+        if block_refs:
+            pieces, _, size, _ = cand_ref.shape
+            for piece in range(pieces):
+                block_refs[0][piece * size : (piece + 1) * size] = cand_ref[piece, k]
         for start in range(0, rows, COLS):
             sim = lax.dot_general(
-                cand_ref[k],
+                block_refs[0][...] if block_refs else cand_ref[k],
                 query_ref[query, start : start + COLS],
                 (((1,), (1,)), ((), ())),
                 preferred_element_type=jnp.float32,
@@ -198,14 +203,16 @@
 
 def score(where, sel, first, second, query_block, lengths, valid, query, cand, length):
     pairs = query_block.shape[0]
-    slots, rows, width = cand.shape
+    slots, width = cand.shape[-3], cand.shape[-1]
+    rows = query.shape[1]
     count = 2 * slots * rows * rows
+    block = [VMEM((rows, width), jnp.bfloat16)] if cand.ndim == 4 else []
     return pl.pallas_call(
         functools.partial(score_kernel, length),
         out_shape=jax.ShapeDtypeStruct((pairs, BLK, BLK), jnp.float32),
         in_specs=[pl.BlockSpec(memory_space=SMEM)] * 7 + [pl.BlockSpec(memory_space=VMEM)] * 2,
         out_specs=pl.BlockSpec(memory_space=VMEM),
-        scratch_shapes=[VMEM((16, rows), jnp.float32)],
+        scratch_shapes=[VMEM((16, rows), jnp.float32)] + block,
         compiler_params=vmem_params(24),
         cost_estimate=pl.CostEstimate(
             flops=2 * count * width, bytes_accessed=4 * rows * width, transcendentals=count
@@ -261,10 +268,8 @@
     return owner // 4, owner // 2 % 2, owner % 2, lax.axis_index("narrow")
 
 
-def split_kernel(first, over, sel_count, *refs):
-    if sel_count:
-        sel_ref, refs = refs[0], refs[1:]
-    states_ref, weight_ref, *outs, rows_ref, sems = refs
+def split_kernel(first, over, states_ref, weight_ref, *refs):
+    *outs, rows_ref, sems = refs
     _, x, _, side = place()
     blocks, part, _ = rows_ref.shape
     size = part // 16
@@ -290,28 +295,17 @@
                 for c in range(2):
                     target = ((z * 2 + c) * blocks + b) * size
                     outs[dx][target : target + size] = both[c * size : (c + 1) * size]
-    if sel_count:
-        lane = lax.broadcasted_iota(jnp.int32, (16, outs[0].shape[1]), 1)
-        row = jnp.zeros_like(lane)
-        for k in range(sel_count):
-            row = jnp.where(lane == k, sel_ref[k], row)
-        row = row.astype(jnp.float32).astype(jnp.bfloat16)
-        for out_ref in outs:
-            out_ref[8 * blocks * size :] = row
-
-
-def split(over, sel, states, weight, first):
+
+
+def split(over, states, weight, first):
     _, rows, width = states.shape
     out_width = weight.shape[1]
     part = rows // 2
-    sel_count = 0 if sel is None else sel.shape[0]
-    out_rows = 8 * CHUNK * (part // 16) + (16 if sel_count else 0)
-    scalars = () if sel is None else (sel,)
-    return pl.pallas_call(
-        functools.partial(split_kernel, first, over, sel_count),
+    out_rows = 8 * CHUNK * (part // 16)
+    return pl.pallas_call(
+        functools.partial(split_kernel, first, over),
         out_shape=(jax.ShapeDtypeStruct((out_rows, out_width), jnp.bfloat16),) * 2,
-        in_specs=[pl.BlockSpec(memory_space=SMEM)] * len(scalars)
-        + [pl.BlockSpec(memory_space=pltpu.HBM), pl.BlockSpec(memory_space=VMEM)],
+        in_specs=[pl.BlockSpec(memory_space=pltpu.HBM), pl.BlockSpec(memory_space=VMEM)],
         out_specs=[pl.BlockSpec(memory_space=VMEM)] * 2,
         scratch_shapes=[
             VMEM((CHUNK, part, width), jnp.bfloat16),
@@ -323,17 +317,20 @@
             bytes_accessed=2 * CHUNK * part * width,
             transcendentals=0,
         ),
-    )(*scalars, states, weight)
-
-
-def gather_unit_kernel(size, before, own_ref, x_ref, y_ref, xy_ref, *refs):
+    )(states, weight)
+
+
+def gather_unit_kernel(size, sel_ref, sel_x_ref, own_ref, x_ref, y_ref, xy_ref, *outs):
     z, _, c, _ = place()
-    earlier, sends, query = refs[:before], refs[before : before + 8], refs[before + 8 :]
+    sends, query = outs[:8], outs[8:]
     span = CHUNK * size
-    base = 0
-    for ref, out_ref in zip(earlier, query):
-        base = ref.shape[0]
-        out_ref[:base] = ref[...]
+    shape = (16, own_ref.shape[1])
+    row, lane = (lax.broadcasted_iota(jnp.int32, shape, axis) for axis in range(2))
+    asked = jnp.zeros(shape, jnp.int32)
+    for dx, ids_ref in enumerate((sel_ref, sel_x_ref)):
+        for k in range(ids_ref.shape[0]):
+            asked = jnp.where((row == dx) & (lane == k), ids_ref[k], asked)
+    asked = asked.astype(jnp.float32).astype(jnp.bfloat16)
     for rel, send_ref in enumerate(sends):
         source = pl.multiple_of(((z ^ (rel // 2)) * 2 + (c ^ (rel % 2))) * span, 16)
         for dx, (one_ref, two_ref) in enumerate(((own_ref, y_ref), (x_ref, xy_ref))):
@@ -342,30 +339,21 @@
             norm = jnp.sum(total * total, axis=-1, keepdims=True)
             unit = (total * lax.rsqrt(norm + 1e-06)).astype(jnp.bfloat16)
             send_ref[dx * span : (dx + 1) * span] = unit
-            query[dx][pl.ds(pl.multiple_of(base + source, 16), span)] = unit
-        if send_ref.shape[0] > 2 * span:
-            row = lax.broadcasted_iota(jnp.int32, (16, own_ref.shape[1]), 0)
-            send_ref[2 * span :] = jnp.where(
-                row == 0,
-                own_ref[8 * span :].astype(jnp.float32),
-                x_ref[8 * span :].astype(jnp.float32),
-            ).astype(jnp.bfloat16)
-
-
-def gather_unit(own, x, y, xy, earlier, size):
-    width = own.shape[1]
-    span = CHUNK * size
-    extra = own.shape[0] - 8 * span
-    base = earlier[0].shape[0] if earlier else 0
-    send = jax.ShapeDtypeStruct((2 * span + extra, width), jnp.bfloat16)
-    query = jax.ShapeDtypeStruct((base + 8 * span, width), jnp.bfloat16)
-    return pl.pallas_call(
-        functools.partial(gather_unit_kernel, size, len(earlier)),
+            query[dx][pl.ds(source, span)] = unit
+        send_ref[2 * span :] = asked
+
+
+def gather_unit(sel, sel_x, own, x, y, xy, size):
+    rows, width = own.shape
+    send = jax.ShapeDtypeStruct((2 * CHUNK * size + 16, width), jnp.bfloat16)
+    query = jax.ShapeDtypeStruct((rows, width), jnp.bfloat16)
+    return pl.pallas_call(
+        functools.partial(gather_unit_kernel, size),
         out_shape=(send,) * 8 + (query,) * 2,
-        in_specs=[pl.BlockSpec(memory_space=VMEM)] * (4 + len(earlier)),
+        in_specs=[pl.BlockSpec(memory_space=SMEM)] * 2 + [pl.BlockSpec(memory_space=VMEM)] * 4,
         out_specs=[pl.BlockSpec(memory_space=VMEM)] * 10,
         compiler_params=vmem_params(12),
-    )(own, x, y, xy, *earlier)
+    )(sel, sel_x, own, x, y, xy)
 
 
 def cube_route_kernel(size, slots, parts, *refs):
@@ -458,26 +446,22 @@
         return lax.ppermute(array, "wide", [(i, i ^ flip) for i in range(16)])
 
     sel, first, second = plan(cand_block)
-    spread, query_parts = [], ()
-    for c in range(0, blocks, CHUNK):
-        ids = sel if c + CHUNK == blocks else None
-        far = split(1, ids, flat, proj_weight, c)
-        own, aside = split(0, ids, flat, proj_weight, c)
-        if c:
-            far, aside, y, xy, x = lax.optimization_barrier((far, aside, y, xy, x))
-        y, xy, x = near(far[0], 2), near(far[1], 3), near(aside, 1)
-        *sends, own, other = gather_unit(own, x, y, xy, query_parts, size)
-        moved = {rel: along(sends[rel], rel) for rel in (4, 5, 6, 7, 2, 3, 1)}
-        spread += [sends[0]] + [moved[rel] for rel in range(1, 8)]
-        query_parts = (own, other)
+    sel_x = near(sel, 1)
+    far = split(1, flat, proj_weight, 0)
+    weight, *far = lax.optimization_barrier((proj_weight, *far))
+    y, xy = near(far[0], 2), near(far[1], 3)
+    own, aside = split(0, flat, weight, 0)
+    x = near(aside, 1)
+    *sends, own, other = gather_unit(sel, sel_x, own, x, y, xy, size)
+    moved = {rel: along(sends[rel], rel) for rel in (4, 5, 6, 7, 2, 3, 1)}
+    other = near(other, 1)
+    spread = [sends[0]] + [moved[rel] for rel in range(1, 8)]
     outgoing = cube_route(spread, size, slots, blocks)
-    outgoing, (own, other) = lax.optimization_barrier((outgoing, query_parts))
+    outgoing, own, other = lax.optimization_barrier((outgoing, own, other))
     incoming = lax.all_to_all(outgoing, ("narrow", "wide"), 0, 0, tiled=True)
-    gathered = {2: near(own, 2), 3: near(other, 3), 1: near(other, 1)}
-    query = queries([own] + [gathered[rel] for rel in (1, 2, 3)], size, blocks)
-    cand = incoming.transpose(1, 0, 2, 3).reshape(-1, rows, width)
+    query = queries([own, other, near(own, 2), near(other, 2)], size, blocks)
     part = score(
-        jnp.stack([owner, side]), sel, first, second, query_block, lengths, pair_valid, query, cand, length
+        jnp.stack([owner, side]), sel, first, second, query_block, lengths, pair_valid, query, incoming, length
     )
     return part + lax.ppermute(part, "narrow", [(0, 1), (1, 0)])
 

time: 111 us -> 115 us (1.036)
  waiting for transfers between devices: 46.5 us -> 58 us
  starting transfers between devices: 36.2 us -> 25.8 us
  local copies, waits for them, and re-layouts: 2.88 us -> 7.38 us
  Pallas kernels: 24.6 us -> 21.7 us
    ppermute x14 -> x7, starting transfers between devices: 17.6 us -> 9.79 us  [along(): return lax.ppermute(array, 'wide', [(i, i ^ flip) for i in range(16)])]
    ppermute x9 -> x7, waiting for transfers between devices: 35.7 us -> 42.6 us  [near(): lax.ppermute(array, ('wide', 'narrow'), [(i, i ^ flip) for i in range(32)])]
    unnamed x18 -> x26, local copies, waits for them, and re-layouts: 1.53 us -> 7.38 us
    ppermute x14 -> x7, waiting for transfers between devices: 6.73 us -> 11.1 us  [along(): return lax.ppermute(array, 'wide', [(i, i ^ flip) for i in range(16)])]
    pallas_call x6 -> x3, Pallas kernels: 9.24 us -> 6.33 us  [the longest x2 5.28 us: split(): pl.pallas_call(functools.partial(split_kernel, first, over), out_shape=(j...]
    ppermute x9 -> x7, starting transfers between devices: 11.7 us -> 9.95 us  [near(): lax.ppermute(array, ('wide', 'narrow'), [(i, i ^ flip) for i in range(32)])]
    transpose x1 -> x0, local copies, waits for them, and re-layouts: 1.35 us -> none  [local_cube(): cand = incoming.transpose(1, 0, 2, 3).reshape(-1, rows, width)]
  transfers between devices with their start and end apart: 25 -> 16, of which waited for: 10 -> 10; matrix products, arithmetic and copies ran while one was open for 0% -> 1% of each run, Pallas kernels for 8% -> 4%
where the time goes in v4:
time: 115 us; the launch traced here: 114 us
  waiting for transfers between devices  58 us (50%)
  starting transfers between devices  25.8 us (22%)
  Pallas kernels  21.7 us (19%)
  local copies, waits for them, and re-layouts  7.38 us (6%)
  other arithmetic  1.25 us (1%)
    ppermute x7, waiting for transfers between devices, near(): lax.ppermute(array, ('wide', 'narrow'), [(i, i ^ flip) for i in range(32)])  42.6 us
    pallas_call x1, Pallas kernels, score(): pl.pallas_call(functools.partial(score_kernel, length), out_shape=jax.Sha...  11.3 us
    ppermute x7, waiting for transfers between devices, along(): return lax.ppermute(array, 'wide', [(i, i ^ flip) for i in range(16)])  11.1 us
    ppermute x7, starting transfers between devices, near(): lax.ppermute(array, ('wide', 'narrow'), [(i, i ^ flip) for i in range(32)])  9.95 us
    ppermute x7, starting transfers between devices, along(): return lax.ppermute(array, 'wide', [(i, i ^ flip) for i in range(16)])  9.79 us
    unnamed x26, local copies, waits for them, and re-layouts  7.38 us
    all_to_all x1, starting transfers between devices, local_cube(): incoming = lax.all_to_all(outgoing, ('narrow', 'wide'), 0, 0, tiled=True)  5.68 us
    pallas_call x2, Pallas kernels, split(): pl.pallas_call(functools.partial(split_kernel, first, over), out_shape=(j...  5.28 us
  transfers between devices with their start and end apart: 16, of which 10 were waited for; matrix products, arithmetic and copies ran while one was open for 1% of the time, Pallas kernels for 4%

profile of v4, /device:TPU:0, one launch (start us, length us, event | category | flops | bytes accessed | tf_op | source)
XLA Modules:
  0.0 114.3 jit_solution(16924038849200781894)
XLA Ops:
  0.0 0.9 copy-done
  0.9 2.6 %shard_map.65 = (bf16[1536,128]{1,0:T(8,128)(2,1)S(1)}, bf16[1536,128]{1,0:T(8,128)(2,1)S(1)}) custom-call(bf16[4,1536,512]{2,1,0:T(8,128)(2,1)} %bitcast.3, bf16[512,128]{1,0:T(8,128)(2,1)S(1)} %copy-done), custom_call_target="tpu_custom_call" | custom-call | flops 402653184 | bytes 3145728 | tf_op jit(solution)/shard_map/pallas_call | solution.py:305
  3.5 2.6 %shard_map.66 = (bf16[1536,128]{1,0:T(8,128)(2,1)S(1)}, bf16[1536,128]{1,0:T(8,128)(2,1)S(1)}) custom-call(bf16[4,1536,512]{2,1,0:T(8,128)(2,1)} %bitcast.4, bf16[512,128]{1,0:T(8,128)(2,1)S(1)} %copy-done), custom_call_target="tpu_custom_call" | custom-call | flops 402653184 | bytes 3145728 | tf_op jit(solution)/shard_map/pallas_call | solution.py:305
  6.2 3.0 %collective-permute-start.1 = (bf16[1536,128]{1,0:T(8,128)(2,1)S(1)}, bf16[1536,128]{1,0:T(8,128)(2,1)S(1)}, u32[]{:S(2)}, u32[]{:S(2)}) collective-permute-start(bf16[1536,128]{1,0:T(8,128)(2,1)S(1)} %get-tuple-element.35), channel_id=1, source_target_pairs={{0,4},{1,5},{2,6},{3,7},{4,0},{5,1},{6,2},{7,3},{8,12},{9,13},{10,... | collective-permute-start | bytes 1179656 | tf_op jit(solution)/shard_map/ppermute | solution.py:442
  9.2 1.5 %collective-permute-start.2 = (bf16[1536,128]{1,0:T(8,128)(2,1)S(1)}, bf16[1536,128]{1,0:T(8,128)(2,1)S(1)}, u32[]{:S(2)}, u32[]{:S(2)}) collective-permute-start(bf16[1536,128]{1,0:T(8,128)(2,1)S(1)} %get-tuple-element.36), channel_id=1, source_target_pairs={{0,1},{1,0},{2,3},{3,2},{4,5},{5,4},{6,7},{7,6},{8,9},{9,8},{10,11... | collective-permute-start | bytes 1179656 | tf_op jit(solution)/shard_map/ppermute | solution.py:442
  10.7 1.7 %shard_map.64 = (s32[6]{0:T(128)}, s32[6]{0:T(128)}, s32[6]{0:T(128)}) custom-call(s32[12]{0:T(128)} %cand_ref.1), custom_call_target="tpu_custom_call" | custom-call | tf_op jit(solution)/shard_map/pallas_call | solution.py:53
  12.5 2.0 %collective-permute-start = (s32[6]{0:T(128)}, s32[6]{0:T(128)S(1)}, u32[]{:S(2)}, u32[]{:S(2)}) collective-permute-start(s32[6]{0:T(128)} %get-tuple-element.28.sel_ref), channel_id=1, source_target_pairs={{0,4},{1,5},{2,6},{3,7},{4,0},{5,1},{6,2},{7,3},{8,12},{9,13},{10,... | collective-permute-start | bytes 80 | tf_op jit(solution)/shard_map/ppermute | solution.py:442
  14.5 12.3 %collective-permute-done.sel_x_ref = s32[6]{0:T(128)S(1)} collective-permute-done((s32[6]{0:T(128)}, s32[6]{0:T(128)S(1)}, u32[]{:S(2)}, u32[]{:S(2)}) %collective-permute-start) | collective-permute-done | bytes 56 | tf_op jit(solution)/shard_map/ppermute | solution.py:442
  26.8 1.4 %collective-permute-done.2.y_ref = bf16[1536,128]{1,0:T(8,128)(2,1)S(1)} collective-permute-done((bf16[1536,128]{1,0:T(8,128)(2,1)S(1)}, bf16[1536,128]{1,0:T(8,128)(2,1)S(1)}, u32[]{:S(2)}, u32[]{:S(2)}) %collective-permute-start.2) | collective-permute-done | bytes 393248 | tf_op jit(solution)/shard_map/ppermute | solution.py:442
  28.8 1.0 shard_map.67
  29.9 1.3 %collective-permute-start.11 = (bf16[1536,128]{1,0:T(8,128)(2,1)S(1)}, bf16[1536,128]{1,0:T(8,128)(2,1)S(1)}, u32[]{:S(2)}, u32[]{:S(2)}) collective-permute-start(bf16[1536,128]{1,0:T(8,128)(2,1)S(1)} %get-tuple-element.47), channel_id=1, source_target_pairs={{0,4},{1,5},{2,6},{3,7},{4,0},{5,1},{6,2},{7,3},{8,12},{9,13},{10,... | collective-permute-start | bytes 1179656 | tf_op jit(solution)/shard_map/ppermute | solution.py:442
  31.2 1.9 %collective-permute-start.10 = (bf16[400,128]{1,0:T(8,128)(2,1)S(1)}, bf16[400,128]{1,0:T(8,128)(2,1)S(1)}, u32[]{:S(2)}, u32[]{:S(2)}) collective-permute-start(bf16[400,128]{1,0:T(8,128)(2,1)S(1)} %get-tuple-element.45), channel_id=1, source_target_pairs={{0,26},{2,24},{4,30},{6,28},{8,18},{10,16},{12,22},{14,20},{16,10}... | collective-permute-start | bytes 307208 | tf_op jit(solution)/shard_map/ppermute | solution.py:446
  33.1 1.8 %collective-permute-start.4 = (bf16[400,128]{1,0:T(8,128)(2,1)S(1)}, bf16[400,128]{1,0:T(8,128)(2,1)S(1)}, u32[]{:S(2)}, u32[]{:S(2)}) collective-permute-start(bf16[400,128]{1,0:T(8,128)(2,1)S(1)} %get-tuple-element.39), channel_id=1, source_target_pairs={{0,2},{2,0},{4,6},{6,4},{8,10},{10,8},{12,14},{14,12},{16,18},{18,... | collective-permute-start | bytes 307208 | tf_op jit(solution)/shard_map/ppermute | solution.py:446
  34.9 1.4 %collective-permute-start.6 = (bf16[400,128]{1,0:T(8,128)(2,1)S(1)}, bf16[400,128]{1,0:T(8,128)(2,1)S(1)}, u32[]{:S(2)}, u32[]{:S(2)}) collective-permute-start(bf16[400,128]{1,0:T(8,128)(2,1)S(1)} %get-tuple-element.41), channel_id=1, source_target_pairs={{0,10},{2,8},{4,14},{6,12},{8,2},{10,0},{12,6},{14,4},{16,26},{18,... | collective-permute-start | bytes 307208 | tf_op jit(solution)/shard_map/ppermute | solution.py:446
  36.3 1.8 %collective-permute-done.10.refs_7_ = bf16[400,128]{1,0:T(8,128)(2,1)S(1)} collective-permute-done((bf16[400,128]{1,0:T(8,128)(2,1)S(1)}, bf16[400,128]{1,0:T(8,128)(2,1)S(1)}, u32[]{:S(2)}, u32[]{:S(2)}) %collective-permute-start.10) | collective-permute-done | bytes 102432 | tf_op jit(solution)/shard_map/ppermute | solution.py:446
  38.1 2.0 %collective-permute-start.7 = (bf16[400,128]{1,0:T(8,128)(2,1)S(1)}, bf16[400,128]{1,0:T(8,128)(2,1)S(1)}, u32[]{:S(2)}, u32[]{:S(2)}) collective-permute-start(bf16[400,128]{1,0:T(8,128)(2,1)S(1)} %get-tuple-element.42), channel_id=1, source_target_pairs={{0,16},{2,18},{4,20},{6,22},{8,24},{10,26},{12,28},{14,30},{16,0},... | collective-permute-start | bytes 307208 | tf_op jit(solution)/shard_map/ppermute | solution.py:446
  40.7 2.2 %collective-permute-start.9 = (bf16[400,128]{1,0:T(8,128)(2,1)S(1)}, bf16[400,128]{1,0:T(8,128)(2,1)S(1)}, u32[]{:S(2)}, u32[]{:S(2)}) collective-permute-start(bf16[400,128]{1,0:T(8,128)(2,1)S(1)} %get-tuple-element.44), channel_id=1, source_target_pairs={{0,24},{2,26},{4,28},{6,30},{8,16},{10,18},{12,20},{14,22},{16,8},... | collective-permute-start | bytes 307208 | tf_op jit(solution)/shard_map/ppermute | solution.py:446
  42.9 1.0 collective-permute-done.6.refs_3_
  43.9 7.4 %collective-permute-done.7.refs_4_ = bf16[400,128]{1,0:T(8,128)(2,1)S(1)} collective-permute-done((bf16[400,128]{1,0:T(8,128)(2,1)S(1)}, bf16[400,128]{1,0:T(8,128)(2,1)S(1)}, u32[]{:S(2)}, u32[]{:S(2)}) %collective-permute-start.7) | collective-permute-done | bytes 102432 | tf_op jit(solution)/shard_map/ppermute | solution.py:446
  51.3 0.8 collective-permute-done.8.refs_5_
  52.1 2.2 %shard_map.68 = bf16[32,3,48,128]{3,2,1,0:T(8,128)(2,1)} custom-call(bf16[400,128]{1,0:T(8,128)(2,1)S(1)} %get-tuple-element.38.refs_0_, bf16[400,128]{1,0:T(8,128)(2,1)S(1)} %collective-permute-done.4.refs_1_, bf16[400,128]{1,0:T(8,128)(2,1)S(1)} %collective-permute-done.5.refs_2_, bf16[400,128]{1,0:T(8,128)(2,1)S(1)} %collective-permute-done.6.refs_3_, ...), custom_call_target="tpu_custom_call" | custom-call | tf_op jit(solution)/shard_map/pallas_call | solution.py:389
  54.3 5.7 %all-to-all-start = ((bf16[32,3,48,128]{3,2,1,0:T(8,128)(2,1)}), bf16[32,3,48,128]{3,2,1,0:T(8,128)(2,1)S(1)}, u32[]{:S(2)}, u32[]{:S(2)}) async-start(bf16[32,3,48,128]{3,2,1,0:T(8,128)(2,1)} %shard_map.68), calls=%async_computation | async-start | bytes 2359296 | tf_op jit(solution)/shard_map/all_to_all | solution.py:461
  60.0 1.8 %collective-permute-start.12 = (bf16[1536,128]{1,0:T(8,128)(2,1)S(1)}, bf16[1536,128]{1,0:T(8,128)(2,1)S(1)}, u32[]{:S(2)}, u32[]{:S(2)}) collective-permute-start(bf16[1536,128]{1,0:T(8,128)(2,1)S(1)} %get-tuple-element.48.refs_0_), channel_id=1, source_target_pairs={{0,1},{1,0},{2,3},{3,2},{4,5},{5,4},{6,7},{7,6},{8,9},{9,8},{10,11... | collective-permute-start | bytes 1179656 | tf_op jit(solution)/shard_map/ppermute | solution.py:442
  62.7 19.1 %collective-permute-done.12.refs_2_ = bf16[1536,128]{1,0:T(8,128)(2,1)S(1)} collective-permute-done((bf16[1536,128]{1,0:T(8,128)(2,1)S(1)}, bf16[1536,128]{1,0:T(8,128)(2,1)S(1)}, u32[]{:S(2)}, u32[]{:S(2)}) %collective-permute-start.12) | collective-permute-done | bytes 393248 | tf_op jit(solution)/shard_map/ppermute | solution.py:442
  81.8 0.7 copy-done.1
  82.5 9.9 %collective-permute-done.13.refs_3_ = bf16[1536,128]{1,0:T(8,128)(2,1)S(1)} collective-permute-done((bf16[1536,128]{1,0:T(8,128)(2,1)S(1)}, bf16[1536,128]{1,0:T(8,128)(2,1)S(1)}, u32[]{:S(2)}, u32[]{:S(2)}) %collective-permute-start.13) | collective-permute-done | bytes 393248 | tf_op jit(solution)/shard_map/ppermute | solution.py:442
  92.4 0.8 copy-done.3
  93.2 1.0 copy-done.2
  94.1 1.0 copy-done.4
  97.7 11.3 %shard_map.70 = f32[12,12,12]{2,1,0:T(8,128)S(1)} custom-call(s32[2]{0:T(128)S(1)} %copy-done.10, s32[6]{0:T(128)S(1)} %copy-done.6, s32[6]{0:T(128)S(1)} %copy-done.11, s32[6]{0:T(128)S(1)} %copy-done.12, s32[12]{0:T(128)S(1)} %copy-done.8, s32[768]{0:T(1024)S(1)} %copy-done.7, s32[12]{0:T(128)S(1)} %copy-done.9, ...), custom_call_target="tpu_custom_call" | custom-call | flops 3623878656 | bytes 786432 | tf_op jit(solution)/shard_map/pallas_call | solution.py:210
  109.3 4.3 %collective-permute-done.14 = f32[12,12,12]{2,1,0:T(8,128)S(1)} collective-permute-done((f32[12,12,12]{2,1,0:T(8,128)S(1)}, f32[12,12,12]{2,1,0:T(8,128)S(1)}, u32[]{:S(2)}, u32[]{:S(2)}) %collective-permute-start.14) | collective-permute-done | bytes 6944 | tf_op jit(solution)/shard_map/ppermute | solution.py:466
  113.6 0.7 add.3
  (35 shorter events, 5.0 us)
Async XLA Ops:
  0.0 0.9 copy-start
  6.2 20.6 %collective-permute-start.1 = (bf16[1536,128]{1,0:T(8,128)(2,1)S(1)}, bf16[1536,128]{1,0:T(8,128)(2,1)S(1)}, u32[]{:S(2)}, u32[]{:S(2)}) collective-permute-start(bf16[1536,128]{1,0:T(8,128)(2,1)S(1)} %get-tuple-element.35), channel_id=1, source_target_pairs={{0,4},{1,5},{2,6},{3,7},{4,0},{5,1},{6,2},{7,3},{8,12},{9,13},{10,... | collective-permute-start | bytes 1179656 | tf_op jit(solution)/shard_map/ppermute | solution.py:442
  9.2 19.0 %collective-permute-start.2 = (bf16[1536,128]{1,0:T(8,128)(2,1)S(1)}, bf16[1536,128]{1,0:T(8,128)(2,1)S(1)}, u32[]{:S(2)}, u32[]{:S(2)}) collective-permute-start(bf16[1536,128]{1,0:T(8,128)(2,1)S(1)} %get-tuple-element.36), channel_id=1, source_target_pairs={{0,1},{1,0},{2,3},{3,2},{4,5},{5,4},{6,7},{7,6},{8,9},{9,8},{10,11... | collective-permute-start | bytes 1179656 | tf_op jit(solution)/shard_map/ppermute | solution.py:442
  10.7 17.5 %collective-permute-start.3 = (bf16[1536,128]{1,0:T(8,128)(2,1)S(1)}, bf16[1536,128]{1,0:T(8,128)(2,1)S(1)}, u32[]{:S(2)}, u32[]{:S(2)}) collective-permute-start(bf16[1536,128]{1,0:T(8,128)(2,1)S(1)} %get-tuple-element.37), channel_id=1, source_target_pairs={{0,5},{1,4},{2,7},{3,6},{4,1},{5,0},{6,3},{7,2},{8,13},{9,12},{10,... | collective-permute-start | bytes 1179656 | tf_op jit(solution)/shard_map/ppermute | solution.py:442
  12.5 14.3 %collective-permute-start = (s32[6]{0:T(128)}, s32[6]{0:T(128)S(1)}, u32[]{:S(2)}, u32[]{:S(2)}) collective-permute-start(s32[6]{0:T(128)} %get-tuple-element.28.sel_ref), channel_id=1, source_target_pairs={{0,4},{1,5},{2,6},{3,7},{4,0},{5,1},{6,2},{7,3},{8,12},{9,13},{10,... | collective-permute-start | bytes 80 | tf_op jit(solution)/shard_map/ppermute | solution.py:442
  28.2 0.6 copy-start.5
  29.9 24.4 %collective-permute-start.11 = (bf16[1536,128]{1,0:T(8,128)(2,1)S(1)}, bf16[1536,128]{1,0:T(8,128)(2,1)S(1)}, u32[]{:S(2)}, u32[]{:S(2)}) collective-permute-start(bf16[1536,128]{1,0:T(8,128)(2,1)S(1)} %get-tuple-element.47), channel_id=1, source_target_pairs={{0,4},{1,5},{2,6},{3,7},{4,0},{5,1},{6,2},{7,3},{8,12},{9,13},{10,... | collective-permute-start | bytes 1179656 | tf_op jit(solution)/shard_map/ppermute | solution.py:442
  31.2 6.9 %collective-permute-start.10 = (bf16[400,128]{1,0:T(8,128)(2,1)S(1)}, bf16[400,128]{1,0:T(8,128)(2,1)S(1)}, u32[]{:S(2)}, u32[]{:S(2)}) collective-permute-start(bf16[400,128]{1,0:T(8,128)(2,1)S(1)} %get-tuple-element.45), channel_id=1, source_target_pairs={{0,26},{2,24},{4,30},{6,28},{8,18},{10,16},{12,22},{14,20},{16,10}... | collective-permute-start | bytes 307208 | tf_op jit(solution)/shard_map/ppermute | solution.py:446
  33.1 7.0 %collective-permute-start.4 = (bf16[400,128]{1,0:T(8,128)(2,1)S(1)}, bf16[400,128]{1,0:T(8,128)(2,1)S(1)}, u32[]{:S(2)}, u32[]{:S(2)}) collective-permute-start(bf16[400,128]{1,0:T(8,128)(2,1)S(1)} %get-tuple-element.39), channel_id=1, source_target_pairs={{0,2},{2,0},{4,6},{6,4},{8,10},{10,8},{12,14},{14,12},{16,18},{18,... | collective-permute-start | bytes 307208 | tf_op jit(solution)/shard_map/ppermute | solution.py:446
  34.9 5.8 %collective-permute-start.5 = (bf16[400,128]{1,0:T(8,128)(2,1)S(1)}, bf16[400,128]{1,0:T(8,128)(2,1)S(1)}, u32[]{:S(2)}, u32[]{:S(2)}) collective-permute-start(bf16[400,128]{1,0:T(8,128)(2,1)S(1)} %get-tuple-element.40), channel_id=1, source_target_pairs={{0,8},{2,10},{4,12},{6,14},{8,0},{10,2},{12,4},{14,6},{16,24},{18,... | collective-permute-start | bytes 307208 | tf_op jit(solution)/shard_map/ppermute | solution.py:446
  34.9 9.0 %collective-permute-start.6 = (bf16[400,128]{1,0:T(8,128)(2,1)S(1)}, bf16[400,128]{1,0:T(8,128)(2,1)S(1)}, u32[]{:S(2)}, u32[]{:S(2)}) collective-permute-start(bf16[400,128]{1,0:T(8,128)(2,1)S(1)} %get-tuple-element.41), channel_id=1, source_target_pairs={{0,10},{2,8},{4,14},{6,12},{8,2},{10,0},{12,6},{14,4},{16,26},{18,... | collective-permute-start | bytes 307208 | tf_op jit(solution)/shard_map/ppermute | solution.py:446
  38.1 13.2 %collective-permute-start.7 = (bf16[400,128]{1,0:T(8,128)(2,1)S(1)}, bf16[400,128]{1,0:T(8,128)(2,1)S(1)}, u32[]{:S(2)}, u32[]{:S(2)}) collective-permute-start(bf16[400,128]{1,0:T(8,128)(2,1)S(1)} %get-tuple-element.42), channel_id=1, source_target_pairs={{0,16},{2,18},{4,20},{6,22},{8,24},{10,26},{12,28},{14,30},{16,0},... | collective-permute-start | bytes 307208 | tf_op jit(solution)/shard_map/ppermute | solution.py:446
  40.1 12.0 %collective-permute-start.8 = (bf16[400,128]{1,0:T(8,128)(2,1)S(1)}, bf16[400,128]{1,0:T(8,128)(2,1)S(1)}, u32[]{:S(2)}, u32[]{:S(2)}) collective-permute-start(bf16[400,128]{1,0:T(8,128)(2,1)S(1)} %get-tuple-element.43), channel_id=1, source_target_pairs={{0,18},{2,16},{4,22},{6,20},{8,26},{10,24},{12,30},{14,28},{16,2},... | collective-permute-start | bytes 307208 | tf_op jit(solution)/shard_map/ppermute | solution.py:446
  40.7 11.4 %collective-permute-start.9 = (bf16[400,128]{1,0:T(8,128)(2,1)S(1)}, bf16[400,128]{1,0:T(8,128)(2,1)S(1)}, u32[]{:S(2)}, u32[]{:S(2)}) collective-permute-start(bf16[400,128]{1,0:T(8,128)(2,1)S(1)} %get-tuple-element.44), channel_id=1, source_target_pairs={{0,24},{2,26},{4,28},{6,30},{8,16},{10,18},{12,20},{14,22},{16,8},... | collective-permute-start | bytes 307208 | tf_op jit(solution)/shard_map/ppermute | solution.py:446
  54.3 41.0 %all-to-all-start = ((bf16[32,3,48,128]{3,2,1,0:T(8,128)(2,1)}), bf16[32,3,48,128]{3,2,1,0:T(8,128)(2,1)S(1)}, u32[]{:S(2)}, u32[]{:S(2)}) async-start(bf16[32,3,48,128]{3,2,1,0:T(8,128)(2,1)} %shard_map.68), calls=%async_computation | async-start | bytes 2359296 | tf_op jit(solution)/shard_map/all_to_all | solution.py:461
  60.0 21.8 %collective-permute-start.12 = (bf16[1536,128]{1,0:T(8,128)(2,1)S(1)}, bf16[1536,128]{1,0:T(8,128)(2,1)S(1)}, u32[]{:S(2)}, u32[]{:S(2)}) collective-permute-start(bf16[1536,128]{1,0:T(8,128)(2,1)S(1)} %get-tuple-element.48.refs_0_), channel_id=1, source_target_pairs={{0,1},{1,0},{2,3},{3,2},{4,5},{5,4},{6,7},{7,6},{8,9},{9,8},{10,11... | collective-permute-start | bytes 1179656 | tf_op jit(solution)/shard_map/ppermute | solution.py:442
  61.9 30.5 %collective-permute-start.13 = (bf16[1536,128]{1,0:T(8,128)(2,1)S(1)}, bf16[1536,128]{1,0:T(8,128)(2,1)S(1)}, u32[]{:S(2)}, u32[]{:S(2)}) collective-permute-start(bf16[1536,128]{1,0:T(8,128)(2,1)S(1)} %collective-permute-done.11.refs_1_), channel_id=1, source_target_pairs={{0,1},{1,0},{2,3},{3,2},{4,5},{5,4},{6,7},{7,6},{8,9},{9,8},{10,11... | collective-permute-start | bytes 1179656 | tf_op jit(solution)/shard_map/ppermute | solution.py:442
  62.1 33.2 %copy-start.6 = (s32[6]{0:T(128)S(1)}, s32[6]{0:T(128)}, u32[]{:S(2)}) copy-start(s32[6]{0:T(128)} %get-tuple-element.28.sel_ref) | copy-start | bytes 76
  62.1 33.2 %copy-start.8 = (s32[12]{0:T(128)S(1)}, s32[12]{0:T(128)}, u32[]{:S(2)}) copy-start(s32[12]{0:T(128)} %query_block_ref.1) | copy-start | bytes 148
  62.1 33.2 %copy-start.9 = (s32[12]{0:T(128)S(1)}, s32[12]{0:T(128)}, u32[]{:S(2)}) copy-start(s32[12]{0:T(128)} %valid_ref.1) | copy-start | bytes 148
  81.8 0.7 copy-start.1
  92.4 0.8 copy-start.3
  93.2 1.0 copy-start.2
  94.1 1.0 copy-start.4
  95.1 0.7 copy-start.7
  95.8 0.6 copy-start.10
  96.4 0.6 copy-start.11
  97.1 0.6 copy-start.12
  109.0 4.6 %collective-permute-start.14 = (f32[12,12,12]{2,1,0:T(8,128)S(1)}, f32[12,12,12]{2,1,0:T(8,128)S(1)}, u32[]{:S(2)}, u32[]{:S(2)}) collective-permute-start(f32[12,12,12]{2,1,0:T(8,128)S(1)} %shard_map.70), channel_id=1, source_target_pairs={{0,1},{1,0},{2,3},{3,2},{4,5},{5,4},{6,7},{7,6},{8,9},{9,8},{10,11... | collective-permute-start | bytes 20744 | tf_op jit(solution)/shard_map/ppermute | solution.py:466

commit v5 on v4

--- a/solution.py
+++ b/solution.py
@@ -13,6 +13,8 @@
 EXP2_SCALE = SHARPNESS * math.log2(math.e)
 COLS = 256
 CHUNK = 4
+LINE = 32
+SPREAD = (0, 4, 6, 5, 7, 2, 3, 1)
 SMEM = pltpu.SMEM
 VMEM = pltpu.VMEM
 
@@ -21,42 +23,55 @@
     return pltpu.CompilerParams(vmem_limit_bytes=mib * 2**20)
 
 
-def plan_kernel(pairs, cand_ref, sel_ref, first_ref, second_ref, slot_ref):
+def plan_kernel(pairs, slots, places_ref, cand_ref, query_block_ref, valid_ref, lengths_ref, sel_ref, table_ref, *scratch):
+    first_ref, second_ref, slot_ref = scratch
+    owner, side, blocks = places_ref[0], places_ref[1], places_ref[2]
+
     def step(k, count):
         block = cand_ref[k]
         found = lax.fori_loop(
             0, k, lambda e, f: jnp.where(cand_ref[e] == block, slot_ref[e], f), jnp.int32(-1)
         )
         new = found < 0
-        slot = jnp.where(new, count, found)
-        slot = jnp.minimum(slot, pairs // 2 - 1)
+        slot = jnp.minimum(jnp.where(new, count, found), pairs // 2 - 1)
         slot_ref[k] = slot
 
         @pl.when(new)
         def _():
             sel_ref[slot] = block
             first_ref[slot] = k
-            second_ref[slot] = k
-
-        @pl.when(jnp.logical_not(new))
-        def _():
-            second_ref[slot] = k
-
+
+        second_ref[slot] = k
         return count + new.astype(jnp.int32)
 
     lax.fori_loop(0, pairs, step, jnp.int32(0))
 
-
-def plan(cand_block):
+    def line(i, carry):
+        k = i // 2
+        slot = side * slots + k
+        pair = jnp.where(i - 2 * k == 0, first_ref[slot], second_ref[slot])
+        query = query_block_ref[pair]
+        table_ref[i * LINE] = pair
+        table_ref[i * LINE + 1] = query
+        table_ref[i * LINE + 2] = valid_ref[pair]
+        for a in range(BLK):
+            table_ref[i * LINE + 3 + a] = lengths_ref[sel_ref[slot] * BLK + a]
+            table_ref[i * LINE + 3 + BLK + a] = lengths_ref[(owner * blocks + query) * BLK + a]
+        return carry
+
+    lax.fori_loop(0, 2 * slots, line, 0)
+
+
+def plan(places, cand_block, query_block, valid, lengths, slots):
     pairs = cand_block.shape[0]
-    out = jax.ShapeDtypeStruct((pairs // 2,), jnp.int32)
-    return pl.pallas_call(
-        functools.partial(plan_kernel, pairs),
-        out_shape=(out, out, out),
-        in_specs=[pl.BlockSpec(memory_space=SMEM)],
-        out_specs=[pl.BlockSpec(memory_space=SMEM)] * 3,
-        scratch_shapes=[SMEM((pairs,), jnp.int32)],
-    )(cand_block)
+    shapes = (pairs // 2, 2 * slots * LINE)
+    return pl.pallas_call(
+        functools.partial(plan_kernel, pairs, slots),
+        out_shape=[jax.ShapeDtypeStruct((n,), jnp.int32) for n in shapes],
+        in_specs=[pl.BlockSpec(memory_space=SMEM)] * 5,
+        out_specs=[pl.BlockSpec(memory_space=SMEM)] * 2,
+        scratch_shapes=[SMEM((pairs,), jnp.int32)] * 3,
+    )(places, cand_block, query_block, valid, lengths)
 
 
 def project_kernel(me_ref, states_ref, weight_ref, out_ref):
@@ -152,14 +167,28 @@
     )(asked, pieces)
 
 
-def score_kernel(
-    length, where_ref, sel_ref, first_ref, second_ref, query_block_ref, lengths_ref, valid_ref,
-    query_ref, cand_ref, out_ref, totals_ref, *block_refs,
-):
-    owner, side = where_ref[0], where_ref[1]
+def query_rows(parts, out_ref):
+    _, x, _, side = place()
+    size = out_ref.shape[1] // 32
+    blocks = out_ref.shape[0]
+    for rel, ref in enumerate(parts):
+        base = (side ^ (rel // 2)) * (16 * size) + (x ^ (rel % 2)) * (2 * size)
+        for z in range(4):
+            for c in range(2):
+                target = pl.multiple_of(base + z * 4 * size + c * size, 16)
+                for b in range(blocks):
+                    begin = ((z * 2 + c) * blocks + b) * size
+                    out_ref[b, pl.ds(target, size)] = ref[begin : begin + size]
+
+
+def score_kernel(length, parts, table_ref, *refs):
+    if parts:
+        cand_ref, out_ref, totals_ref, block_ref, query_ref = refs[parts:]
+        query_rows(refs[:parts], query_ref)
+    else:
+        query_ref, cand_ref, out_ref, totals_ref = refs
     rows = query_ref.shape[1]
     slots = cand_ref.shape[-3]
-    blocks = query_ref.shape[0]
     out_ref[...] = jnp.zeros_like(out_ref)
     totals_ref[...] = jnp.ones_like(totals_ref)
     upper = lax.broadcasted_iota(jnp.int32, (length // 2, COLS), 0) + length // 2
@@ -167,57 +196,58 @@
 
     def pair_step(i, carry):
         k = i // 2
-        slot = side * slots + k
-        block = sel_ref[slot]
-        pair = jnp.where(i - 2 * k == 0, first_ref[slot], second_ref[slot])
-        query = query_block_ref[pair]
-        if block_refs:
+        line = i * LINE
+        pair, query = table_ref[line], table_ref[line + 1]
+        if parts:
             pieces, _, size, _ = cand_ref.shape
             for piece in range(pieces):
-                block_refs[0][piece * size : (piece + 1) * size] = cand_ref[piece, k]
+                block_ref[piece * size : (piece + 1) * size] = cand_ref[piece, k]
         for start in range(0, rows, COLS):
             sim = lax.dot_general(
-                block_refs[0][...] if block_refs else cand_ref[k],
+                block_ref[...] if parts else cand_ref[k],
                 query_ref[query, start : start + COLS],
                 (((1,), (1,)), ((), ())),
                 preferred_element_type=jnp.float32,
             )
             for b in range(BLK):
-                live = lengths_ref[block * BLK + b]
+                live = table_ref[line + 3 + b]
                 low = jnp.exp2(sim[b * length : b * length + length // 2] * EXP2_SCALE)
                 high = jnp.exp2(sim[b * length + length // 2 : (b + 1) * length] * EXP2_SCALE)
                 both = low + jnp.where(upper < live, high, 0.0)
                 totals_ref[b : b + 1, start : start + COLS] = jnp.sum(both, axis=0, keepdims=True)
         score = jnp.zeros((16, length), jnp.float32)
         for a in range(BLK):
-            live = lengths_ref[(owner * blocks + query) * BLK + a]
+            live = table_ref[line + 3 + BLK + a]
             logs = jnp.log(totals_ref[:, a * length : (a + 1) * length])
             summed = jnp.sum(jnp.where(lane < live, logs, 0.0), axis=1, keepdims=True)
             score = jnp.where(lane == a, summed, score)
-        keep = valid_ref[pair].astype(jnp.float32) / (SHARPNESS * length)
+        keep = table_ref[line + 2].astype(jnp.float32) / (SHARPNESS * length)
         out_ref[pair] = score[:BLK, :BLK] * keep
         return carry
 
     lax.fori_loop(0, 2 * slots, pair_step, 0)
 
 
-def score(where, sel, first, second, query_block, lengths, valid, query, cand, length):
-    pairs = query_block.shape[0]
+def score(table, query, cand, pairs, blocks, length):
     slots, width = cand.shape[-3], cand.shape[-1]
-    rows = query.shape[1]
+    rows = BLK * length
+    parts = len(query) if isinstance(query, list) else 0
     count = 2 * slots * rows * rows
-    block = [VMEM((rows, width), jnp.bfloat16)] if cand.ndim == 4 else []
-    return pl.pallas_call(
-        functools.partial(score_kernel, length),
+    scratch = [VMEM((16, rows), jnp.float32)]
+    if parts:
+        scratch += [VMEM((rows, width), jnp.bfloat16), VMEM((blocks, rows, width), jnp.bfloat16)]
+    return pl.pallas_call(
+        functools.partial(score_kernel, length, parts),
         out_shape=jax.ShapeDtypeStruct((pairs, BLK, BLK), jnp.float32),
-        in_specs=[pl.BlockSpec(memory_space=SMEM)] * 7 + [pl.BlockSpec(memory_space=VMEM)] * 2,
+        in_specs=[pl.BlockSpec(memory_space=SMEM)]
+        + [pl.BlockSpec(memory_space=VMEM)] * (max(parts, 1) + 1),
         out_specs=pl.BlockSpec(memory_space=VMEM),
-        scratch_shapes=[VMEM((16, rows), jnp.float32)] + block,
-        compiler_params=vmem_params(24),
+        scratch_shapes=scratch,
+        compiler_params=vmem_params(28),
         cost_estimate=pl.CostEstimate(
             flops=2 * count * width, bytes_accessed=4 * rows * width, transcendentals=count
         ),
-    )(where, sel, first, second, query_block, lengths, valid, query, cand)
+    )(table, *(query if parts else [query]), cand)
 
 
 def local_general(states, proj_weight, lengths, query_block, cand_block, pair_valid):
@@ -235,7 +265,9 @@
     def shift(d):
         return [(i, (i + d) % shares) for i in range(shares)]
 
-    sel, first, second = plan(cand_block)
+    slots = cand_block.shape[0] // 2 // shares
+    places = jnp.stack([owner, side, jnp.int32(blocks)])
+    sel, table = plan(places, cand_block, query_block, pair_valid, lengths, slots)
     sent = project(me, flat, proj_weight, shares, 1, shares - 1, jnp.bfloat16)
     received = [lax.ppermute(sent[d - 1], "narrow", shift(d)) for d in range(1, shares)]
     asked = lax.all_to_all(
@@ -254,9 +286,7 @@
     outgoing = route(asked, spread.reshape(owners * blocks, size, width), owners, shares)
     incoming = lax.all_to_all(outgoing, ("narrow", "wide"), 0, 0, tiled=True)
     cand = incoming.transpose(1, 0, 2, 3).reshape(-1, rows, width)
-    part = score(
-        jnp.stack([owner, side]), sel, first, second, query_block, lengths, pair_valid, query, cand, length
-    )
+    part = score(table, query, cand, cand_block.shape[0], blocks, length)
     out = part
     for d in range(1, shares):
         out = out + lax.ppermute(part, "narrow", shift(d))
@@ -320,7 +350,7 @@
     )(states, weight)
 
 
-def gather_unit_kernel(size, sel_ref, sel_x_ref, own_ref, x_ref, y_ref, xy_ref, *outs):
+def gather_unit_kernel(size, sel_ref, sel_x_ref, y_ref, xy_ref, own_ref, x_ref, *outs):
     z, _, c, _ = place()
     sends, query = outs[:8], outs[8:]
     span = CHUNK * size
@@ -343,7 +373,7 @@
         send_ref[2 * span :] = asked
 
 
-def gather_unit(sel, sel_x, own, x, y, xy, size):
+def gather_unit(sel, sel_x, y, xy, own, x, size):
     rows, width = own.shape
     send = jax.ShapeDtypeStruct((2 * CHUNK * size + 16, width), jnp.bfloat16)
     query = jax.ShapeDtypeStruct((rows, width), jnp.bfloat16)
@@ -353,7 +383,7 @@
         in_specs=[pl.BlockSpec(memory_space=SMEM)] * 2 + [pl.BlockSpec(memory_space=VMEM)] * 4,
         out_specs=[pl.BlockSpec(memory_space=VMEM)] * 10,
         compiler_params=vmem_params(12),
-    )(sel, sel_x, own, x, y, xy)
+    )(sel, sel_x, y, xy, own, x)
 
 
 def cube_route_kernel(size, slots, parts, *refs):
@@ -361,16 +391,14 @@
     z, x, c, _ = place()
     blocks = pieces_ref.shape[0] // 16
     span = CHUNK * size
-    for i, ref in enumerate(spread):
-        first, rel = i // 8 * CHUNK, i % 8
+    for rel, ref in zip(SPREAD, spread):
         for dx in range(2):
             owner = (z ^ (rel // 2)) * 4 + (x ^ dx) * 2 + (c ^ (rel % 2))
             for b in range(CHUNK):
                 begin = dx * span + b * size
-                pieces_ref[owner * blocks + first + b] = ref[begin : begin + size]
-            if ref.shape[0] > 2 * span:
-                row = ref[2 * span :].astype(jnp.float32)[dx : dx + 1]
-                rows_ref[pl.ds(owner, 1)] = row.astype(jnp.int32)
+                pieces_ref[owner * blocks + b] = ref[begin : begin + size]
+            row = ref[2 * span :].astype(jnp.float32)[dx : dx + 1]
+            rows_ref[pl.ds(owner, 1)] = row.astype(jnp.int32)
     copy = pltpu.make_async_copy(rows_ref, asked_ref, sem)
     copy.start()
     copy.wait()
@@ -401,31 +429,6 @@
     )(*spread)
 
 
-def queries_kernel(size, *refs):
-    parts, out_ref = refs[:-1], refs[-1]
-    _, x, _, side = place()
-    for rel, ref in enumerate(parts):
-        base = (side ^ (rel // 2)) * (16 * size) + (x ^ (rel % 2)) * (2 * size)
-        for first in range(0, out_ref.shape[0], CHUNK):
-            for z in range(4):
-                for c in range(2):
-                    target = pl.multiple_of(base + z * 4 * size + c * size, 16)
-                    for b in range(CHUNK):
-                        begin = (8 * first + (z * 2 + c) * CHUNK + b) * size
-                        out_ref[first + b, pl.ds(target, size)] = ref[begin : begin + size]
-
-
-def queries(parts, size, blocks):
-    width = parts[0].shape[1]
-    return pl.pallas_call(
-        functools.partial(queries_kernel, size),
-        out_shape=jax.ShapeDtypeStruct((blocks, 32 * size, width), jnp.bfloat16),
-        in_specs=[pl.BlockSpec(memory_space=VMEM)] * len(parts),
-        out_specs=pl.BlockSpec(memory_space=VMEM),
-        compiler_params=vmem_params(12),
-    )(*parts)
-
-
 def local_cube(states, proj_weight, lengths, query_block, cand_block, pair_valid):
     side = lax.axis_index("narrow").astype(jnp.int32)
     owner = lax.axis_index("wide").astype(jnp.int32)
@@ -445,24 +448,22 @@
         flip = rel // 2 * 4 + rel % 2
         return lax.ppermute(array, "wide", [(i, i ^ flip) for i in range(16)])
 
-    sel, first, second = plan(cand_block)
+    places = jnp.stack([owner, side, jnp.int32(blocks)])
+    sel, table = plan(places, cand_block, query_block, pair_valid, lengths, slots)
     sel_x = near(sel, 1)
     far = split(1, flat, proj_weight, 0)
     weight, *far = lax.optimization_barrier((proj_weight, *far))
     y, xy = near(far[0], 2), near(far[1], 3)
     own, aside = split(0, flat, weight, 0)
     x = near(aside, 1)
-    *sends, own, other = gather_unit(sel, sel_x, own, x, y, xy, size)
-    moved = {rel: along(sends[rel], rel) for rel in (4, 5, 6, 7, 2, 3, 1)}
-    other = near(other, 1)
-    spread = [sends[0]] + [moved[rel] for rel in range(1, 8)]
+    *sends, own, other = gather_unit(sel, sel_x, y, xy, own, x, size)
+    spread = [along(sends[rel], rel) if rel else sends[rel] for rel in SPREAD]
+    own_y, other = near(own, 2), near(other, 1)
     outgoing = cube_route(spread, size, slots, blocks)
-    outgoing, own, other = lax.optimization_barrier((outgoing, own, other))
+    outgoing, own_y, other = lax.optimization_barrier((outgoing, own_y, other))
     incoming = lax.all_to_all(outgoing, ("narrow", "wide"), 0, 0, tiled=True)
-    query = queries([own, other, near(own, 2), near(other, 2)], size, blocks)
-    part = score(
-        jnp.stack([owner, side]), sel, first, second, query_block, lengths, pair_valid, query, incoming, length
-    )
+    query = [own, other, own_y, near(other, 2)]
+    part = score(table, query, incoming, cand_block.shape[0], blocks, length)
     return part + lax.ppermute(part, "narrow", [(0, 1), (1, 0)])
 
 

time: 115 us -> 105 us (0.913)
  local copies, waits for them, and re-layouts: 7.38 us -> 1.51 us
  starting transfers between devices: 25.8 us -> 23.3 us
  waiting for transfers between devices: 58 us -> 56.5 us
    ppermute x7, waiting for transfers between devices: 42.6 us -> 29 us  [near(): lax.ppermute(array, ('wide', 'narrow'), [(i, i ^ flip) for i in range(32)])]
    all_to_all x1, waiting for transfers between devices: 0.01 us -> 9.2 us  [local_cube(): incoming = lax.all_to_all(outgoing, ('narrow', 'wide'), 0, 0, tiled=True)]
    unnamed x26 -> x6, local copies, waits for them, and re-layouts: 7.38 us -> 1.51 us
    ppermute x7, waiting for transfers between devices: 11.1 us -> 14.7 us  [along(): return lax.ppermute(array, 'wide', [(i, i ^ flip) for i in range(16)])]
    all_to_all x1, starting transfers between devices: 5.68 us -> 2.67 us  [local_cube(): incoming = lax.all_to_all(outgoing, ('narrow', 'wide'), 0, 0, tiled=True)]
    ppermute x7, starting transfers between devices: 9.79 us -> 8.09 us  [along(): return lax.ppermute(array, 'wide', [(i, i ^ flip) for i in range(16)])]
    ppermute x7, starting transfers between devices: 9.95 us -> 11.6 us  [near(): lax.ppermute(array, ('wide', 'narrow'), [(i, i ^ flip) for i in range(32)])]
    pallas_call x3 -> x2, Pallas kernels: 13.2 us -> 13.5 us  [the longest x1 11.3 us: score(): pl.pallas_call(functools.partial(score_kernel, length, parts), out_shape=...]
  transfers between devices with their start and end apart: 16 -> 16, of which waited for: 10 -> 8; matrix products, arithmetic and copies ran while one was open for 1% -> 1% of each run, Pallas kernels for 4% -> 7%
where the time goes in v5:
time: 105 us
  waiting for transfers between devices  56.5 us (54%)
  starting transfers between devices  23.3 us (22%)
  Pallas kernels  22 us (21%)
  local copies, waits for them, and re-layouts  1.51 us (1%)
  other arithmetic  1.3 us (1%)
    ppermute x7, waiting for transfers between devices, near(): lax.ppermute(array, ('wide', 'narrow'), [(i, i ^ flip) for i in range(32)])  29 us
    ppermute x7, waiting for transfers between devices, along(): return lax.ppermute(array, 'wide', [(i, i ^ flip) for i in range(16)])  14.7 us
    ppermute x7, starting transfers between devices, near(): lax.ppermute(array, ('wide', 'narrow'), [(i, i ^ flip) for i in range(32)])  11.6 us
    pallas_call x1, Pallas kernels, score(): pl.pallas_call(functools.partial(score_kernel, length, parts), out_shape=...  11.3 us
    all_to_all x1, waiting for transfers between devices, local_cube(): incoming = lax.all_to_all(outgoing, ('narrow', 'wide'), 0, 0, tiled=True)  9.2 us
    ppermute x7, starting transfers between devices, along(): return lax.ppermute(array, 'wide', [(i, i ^ flip) for i in range(16)])  8.09 us
    pallas_call x2, Pallas kernels, split(): pl.pallas_call(functools.partial(split_kernel, first, over), out_shape=(j...  5.26 us
    ppermute x1, waiting for transfers between devices, local_cube(): return part + lax.ppermute(part, 'narrow', [(0, 1), (1, 0)])  3.65 us
  transfers between devices with their start and end apart: 16, of which 8 were waited for; matrix products, arithmetic and copies ran while one was open for 1% of the time, Pallas kernels for 7%

profile of v5, /device:TPU:0, one launch (start us, length us, event | category | flops | bytes accessed | tf_op | source)
XLA Modules:
  0.0 104.7 jit_solution(12326834124151679651)
XLA Ops:
  0.0 0.9 copy-done
  0.9 2.6 %shard_map.65 = (bf16[1536,128]{1,0:T(8,128)(2,1)S(1)}, bf16[1536,128]{1,0:T(8,128)(2,1)S(1)}) custom-call(bf16[4,1536,512]{2,1,0:T(8,128)(2,1)} %bitcast.3, bf16[512,128]{1,0:T(8,128)(2,1)S(1)} %copy-done), custom_call_target="tpu_custom_call" | custom-call | flops 402653184 | bytes 3145728 | tf_op jit(solution)/shard_map/pallas_call | solution.py:335
  3.5 3.0 %collective-permute-start.1 = (bf16[1536,128]{1,0:T(8,128)(2,1)S(1)}, bf16[1536,128]{1,0:T(8,128)(2,1)S(1)}, u32[]{:S(2)}, u32[]{:S(2)}) collective-permute-start(bf16[1536,128]{1,0:T(8,128)(2,1)S(1)} %get-tuple-element.31), channel_id=1, source_target_pairs={{0,1},{1,0},{2,3},{3,2},{4,5},{5,4},{6,7},{7,6},{8,9},{9,8},{10,11... | collective-permute-start | bytes 1179656 | tf_op jit(solution)/shard_map/ppermute | solution.py:445
  6.6 1.4 %collective-permute-start.2 = (bf16[1536,128]{1,0:T(8,128)(2,1)S(1)}, bf16[1536,128]{1,0:T(8,128)(2,1)S(1)}, u32[]{:S(2)}, u32[]{:S(2)}) collective-permute-start(bf16[1536,128]{1,0:T(8,128)(2,1)S(1)} %get-tuple-element.32), channel_id=1, source_target_pairs={{0,5},{1,4},{2,7},{3,6},{4,1},{5,0},{6,3},{7,2},{8,13},{9,12},{10,... | collective-permute-start | bytes 1179656 | tf_op jit(solution)/shard_map/ppermute | solution.py:445
  8.0 2.6 %shard_map.66 = (bf16[1536,128]{1,0:T(8,128)(2,1)S(1)}, bf16[1536,128]{1,0:T(8,128)(2,1)S(1)}) custom-call(bf16[4,1536,512]{2,1,0:T(8,128)(2,1)} %bitcast.4, bf16[512,128]{1,0:T(8,128)(2,1)S(1)} %copy-done), custom_call_target="tpu_custom_call" | custom-call | flops 402653184 | bytes 3145728 | tf_op jit(solution)/shard_map/pallas_call | solution.py:335
  10.6 0.2 collective-permute-start.3
  10.8 0.7 pad_add_fusion.places_ref
  11.5 2.1 %shard_map.64 = (s32[6]{0:T(128)}, s32[192]{0:T(256)}) custom-call(s32[3]{0:T(128)} %pad_add_fusion.places_ref, s32[12]{0:T(128)} %cand_ref.1, s32[12]{0:T(128)} %query_block_ref.1, s32[12]{0:T(128)} %valid_ref.1, s32[768]{0:T(1024)} %lengths_ref.1), custom_call_target="tpu_custom_call" | custom-call | tf_op jit(solution)/shard_map/pallas_call | solution.py:68
  13.6 2.0 %collective-permute-start = (s32[6]{0:T(128)}, s32[6]{0:T(128)S(1)}, u32[]{:S(2)}, u32[]{:S(2)}) collective-permute-start(s32[6]{0:T(128)} %get-tuple-element.28.sel_ref), channel_id=1, source_target_pairs={{0,4},{1,5},{2,6},{3,7},{4,0},{5,1},{6,2},{7,3},{8,12},{9,13},{10,... | collective-permute-start | bytes 80 | tf_op jit(solution)/shard_map/ppermute | solution.py:445
  15.6 9.9 %collective-permute-done.sel_x_ref = s32[6]{0:T(128)S(1)} collective-permute-done((s32[6]{0:T(128)}, s32[6]{0:T(128)S(1)}, u32[]{:S(2)}, u32[]{:S(2)}) %collective-permute-start) | collective-permute-done | bytes 56 | tf_op jit(solution)/shard_map/ppermute | solution.py:445
  25.5 0.6 copy-done.1
  26.1 1.0 %shard_map.67 = (bf16[400,128]{1,0:T(8,128)(2,1)S(1)}, bf16[400,128]{1,0:T(8,128)(2,1)S(1)}, bf16[400,128]{1,0:T(8,128)(2,1)S(1)}, bf16[400,128]{1,0:T(8,128)(2,...) custom-call(s32[6]{0:T(128)S(1)} %copy-done.1, ...), custom_call_target="tpu_custom_call" | custom-call | tf_op jit(solution)/shard_map/pallas_call | solution.py:380
  27.2 1.7 %collective-permute-start.12 = (bf16[1536,128]{1,0:T(8,128)(2,1)S(1)}, bf16[1536,128]{1,0:T(8,128)(2,1)S(1)}, u32[]{:S(2)}, u32[]{:S(2)}) collective-permute-start(bf16[1536,128]{1,0:T(8,128)(2,1)S(1)} %get-tuple-element.45), channel_id=1, source_target_pairs={{0,4},{1,5},{2,6},{3,7},{4,0},{5,1},{6,2},{7,3},{8,12},{9,13},{10,... | collective-permute-start | bytes 1179656 | tf_op jit(solution)/shard_map/ppermute | solution.py:445
  28.9 1.5 %collective-permute-start.11 = (bf16[1536,128]{1,0:T(8,128)(2,1)S(1)}, bf16[1536,128]{1,0:T(8,128)(2,1)S(1)}, u32[]{:S(2)}, u32[]{:S(2)}) collective-permute-start(bf16[1536,128]{1,0:T(8,128)(2,1)S(1)} %get-tuple-element.36.refs_0_), channel_id=1, source_target_pairs={{0,1},{1,0},{2,3},{3,2},{4,5},{5,4},{6,7},{7,6},{8,9},{9,8},{10,11... | collective-permute-start | bytes 1179656 | tf_op jit(solution)/shard_map/ppermute | solution.py:445
  30.4 2.6 %collective-permute-start.4 = (bf16[400,128]{1,0:T(8,128)(2,1)S(1)}, bf16[400,128]{1,0:T(8,128)(2,1)S(1)}, u32[]{:S(2)}, u32[]{:S(2)}) collective-permute-start(bf16[400,128]{1,0:T(8,128)(2,1)S(1)} %get-tuple-element.38), channel_id=1, source_target_pairs={{0,16},{2,18},{4,20},{6,22},{8,24},{10,26},{12,28},{14,30},{16,0},... | collective-permute-start | bytes 307208 | tf_op jit(solution)/shard_map/ppermute | solution.py:449
  33.0 1.4 %collective-permute-start.5 = (bf16[400,128]{1,0:T(8,128)(2,1)S(1)}, bf16[400,128]{1,0:T(8,128)(2,1)S(1)}, u32[]{:S(2)}, u32[]{:S(2)}) collective-permute-start(bf16[400,128]{1,0:T(8,128)(2,1)S(1)} %get-tuple-element.39), channel_id=1, source_target_pairs={{0,24},{2,26},{4,28},{6,30},{8,16},{10,18},{12,20},{14,22},{16,8},... | collective-permute-start | bytes 307208 | tf_op jit(solution)/shard_map/ppermute | solution.py:449
  34.3 8.1 %collective-permute-done.4.refs_1_ = bf16[400,128]{1,0:T(8,128)(2,1)S(1)} collective-permute-done((bf16[400,128]{1,0:T(8,128)(2,1)S(1)}, bf16[400,128]{1,0:T(8,128)(2,1)S(1)}, u32[]{:S(2)}, u32[]{:S(2)}) %collective-permute-start.4) | collective-permute-done | bytes 102432 | tf_op jit(solution)/shard_map/ppermute | solution.py:449
  42.4 0.6 collective-permute-start.7
  43.0 1.8 %collective-permute-start.8 = (bf16[400,128]{1,0:T(8,128)(2,1)S(1)}, bf16[400,128]{1,0:T(8,128)(2,1)S(1)}, u32[]{:S(2)}, u32[]{:S(2)}) collective-permute-start(bf16[400,128]{1,0:T(8,128)(2,1)S(1)} %get-tuple-element.42), channel_id=1, source_target_pairs={{0,8},{2,10},{4,12},{6,14},{8,0},{10,2},{12,4},{14,6},{16,24},{18,... | collective-permute-start | bytes 307208 | tf_op jit(solution)/shard_map/ppermute | solution.py:449
  44.8 1.8 %collective-permute-start.9 = (bf16[400,128]{1,0:T(8,128)(2,1)S(1)}, bf16[400,128]{1,0:T(8,128)(2,1)S(1)}, u32[]{:S(2)}, u32[]{:S(2)}) collective-permute-start(bf16[400,128]{1,0:T(8,128)(2,1)S(1)} %get-tuple-element.43), channel_id=1, source_target_pairs={{0,10},{2,8},{4,14},{6,12},{8,2},{10,0},{12,6},{14,4},{16,26},{18,... | collective-permute-start | bytes 307208 | tf_op jit(solution)/shard_map/ppermute | solution.py:449
  46.6 2.4 %collective-permute-done.7.refs_4_ = bf16[400,128]{1,0:T(8,128)(2,1)S(1)} collective-permute-done((bf16[400,128]{1,0:T(8,128)(2,1)S(1)}, bf16[400,128]{1,0:T(8,128)(2,1)S(1)}, u32[]{:S(2)}, u32[]{:S(2)}) %collective-permute-start.7) | collective-permute-done | bytes 102432 | tf_op jit(solution)/shard_map/ppermute | solution.py:449
  49.0 1.8 %collective-permute-done.8.refs_5_ = bf16[400,128]{1,0:T(8,128)(2,1)S(1)} collective-permute-done((bf16[400,128]{1,0:T(8,128)(2,1)S(1)}, bf16[400,128]{1,0:T(8,128)(2,1)S(1)}, u32[]{:S(2)}, u32[]{:S(2)}) %collective-permute-start.8) | collective-permute-done | bytes 102432 | tf_op jit(solution)/shard_map/ppermute | solution.py:449
  50.8 2.4 %collective-permute-done.9.refs_6_ = bf16[400,128]{1,0:T(8,128)(2,1)S(1)} collective-permute-done((bf16[400,128]{1,0:T(8,128)(2,1)S(1)}, bf16[400,128]{1,0:T(8,128)(2,1)S(1)}, u32[]{:S(2)}, u32[]{:S(2)}) %collective-permute-start.9) | collective-permute-done | bytes 102432 | tf_op jit(solution)/shard_map/ppermute | solution.py:449
  53.2 2.2 %shard_map.68 = bf16[32,3,48,128]{3,2,1,0:T(8,128)(2,1)} custom-call(bf16[400,128]{1,0:T(8,128)(2,1)S(1)} %get-tuple-element.37.refs_0_, bf16[400,128]{1,0:T(8,128)(2,1)S(1)} %collective-permute-done.4.refs_1_, bf16[400,128]{1,0:T(8,128)(2,1)S(1)} %collective-permute-done.5.refs_2_, bf16[400,128]{1,0:T(8,128)(2,1)S(1)} %collective-permute-done.6.refs_3_, ...), custom_call_target="tpu_custom_call" | custom-call | tf_op jit(solution)/shard_map/pallas_call | solution.py:417
  55.4 2.7 %all-to-all-start = ((bf16[32,3,48,128]{3,2,1,0:T(8,128)(2,1)}), bf16[32,3,48,128]{3,2,1,0:T(8,128)(2,1)S(1)}, u32[]{:S(2)}, u32[]{:S(2)}) async-start(bf16[32,3,48,128]{3,2,1,0:T(8,128)(2,1)} %shard_map.68), calls=%async_computation | async-start | bytes 2359296 | tf_op jit(solution)/shard_map/all_to_all | solution.py:464
  58.1 1.7 %collective-permute-start.13 = (bf16[1536,128]{1,0:T(8,128)(2,1)S(1)}, bf16[1536,128]{1,0:T(8,128)(2,1)S(1)}, u32[]{:S(2)}, u32[]{:S(2)}) collective-permute-start(bf16[1536,128]{1,0:T(8,128)(2,1)S(1)} %collective-permute-done.12.refs_1_), channel_id=1, source_target_pairs={{0,1},{1,0},{2,3},{3,2},{4,5},{5,4},{6,7},{7,6},{8,9},{9,8},{10,11... | collective-permute-start | bytes 1179656 | tf_op jit(solution)/shard_map/ppermute | solution.py:445
  59.8 19.1 %collective-permute-done.13.refs_3_ = bf16[1536,128]{1,0:T(8,128)(2,1)S(1)} collective-permute-done((bf16[1536,128]{1,0:T(8,128)(2,1)S(1)}, bf16[1536,128]{1,0:T(8,128)(2,1)S(1)}, u32[]{:S(2)}, u32[]{:S(2)}) %collective-permute-start.13) | collective-permute-done | bytes 393248 | tf_op jit(solution)/shard_map/ppermute | solution.py:445
  78.9 9.2 %all-to-all-done.refs_4_ = bf16[32,3,48,128]{3,2,1,0:T(8,128)(2,1)S(1)} async-done(((bf16[32,3,48,128]{3,2,1,0:T(8,128)(2,1)}), bf16[32,3,48,128]{3,2,1,0:T(8,128)(2,1)S(1)}, u32[]{:S(2)}, u32[]{:S(2)}) %all-to-all-start) | async-done | bytes 1179680 | tf_op jit(solution)/shard_map/all_to_all | solution.py:464
  88.1 11.3 %shard_map.69 = f32[12,12,12]{2,1,0:T(8,128)S(1)} custom-call(s32[192]{0:T(256)S(1)} %copy-done.2, bf16[1536,128]{1,0:T(8,128)(2,1)S(1)} %get-tuple-element.36.refs_0_, bf16[1536,128]{1,0:T(8,128)(2,1)S(1)} %collective-permute-done.12.refs_1_, bf16[1536,128]{1,0:T(8,128)(2,1)S(1)} %collective-permute-done.11.refs_2_, ...), custom_call_target="tpu_custom_call" | custom-call | flops 3623878656 | bytes 786432 | tf_op jit(solution)/shard_map/pallas_call | solution.py:239
  99.4 1.0 collective-permute-start.14
  100.4 3.7 %collective-permute-done.14 = f32[12,12,12]{2,1,0:T(8,128)S(1)} collective-permute-done((f32[12,12,12]{2,1,0:T(8,128)S(1)}, f32[12,12,12]{2,1,0:T(8,128)S(1)}, u32[]{:S(2)}, u32[]{:S(2)}) %collective-permute-start.14) | collective-permute-done | bytes 6944 | tf_op jit(solution)/shard_map/ppermute | solution.py:467
  104.1 0.7 add.3
  (14 shorter events, 0.0 us)
Async XLA Ops:
  0.0 0.9 copy-start
  3.5 21.9 %collective-permute-start.1 = (bf16[1536,128]{1,0:T(8,128)(2,1)S(1)}, bf16[1536,128]{1,0:T(8,128)(2,1)S(1)}, u32[]{:S(2)}, u32[]{:S(2)}) collective-permute-start(bf16[1536,128]{1,0:T(8,128)(2,1)S(1)} %get-tuple-element.31), channel_id=1, source_target_pairs={{0,1},{1,0},{2,3},{3,2},{4,5},{5,4},{6,7},{7,6},{8,9},{9,8},{10,11... | collective-permute-start | bytes 1179656 | tf_op jit(solution)/shard_map/ppermute | solution.py:445
  6.6 18.9 %collective-permute-start.2 = (bf16[1536,128]{1,0:T(8,128)(2,1)S(1)}, bf16[1536,128]{1,0:T(8,128)(2,1)S(1)}, u32[]{:S(2)}, u32[]{:S(2)}) collective-permute-start(bf16[1536,128]{1,0:T(8,128)(2,1)S(1)} %get-tuple-element.32), channel_id=1, source_target_pairs={{0,5},{1,4},{2,7},{3,6},{4,1},{5,0},{6,3},{7,2},{8,13},{9,12},{10,... | collective-permute-start | bytes 1179656 | tf_op jit(solution)/shard_map/ppermute | solution.py:445
  10.6 14.8 %collective-permute-start.3 = (bf16[1536,128]{1,0:T(8,128)(2,1)S(1)}, bf16[1536,128]{1,0:T(8,128)(2,1)S(1)}, u32[]{:S(2)}, u32[]{:S(2)}) collective-permute-start(bf16[1536,128]{1,0:T(8,128)(2,1)S(1)} %get-tuple-element.35), channel_id=1, source_target_pairs={{0,4},{1,5},{2,6},{3,7},{4,0},{5,1},{6,2},{7,3},{8,12},{9,13},{10,... | collective-permute-start | bytes 1179656 | tf_op jit(solution)/shard_map/ppermute | solution.py:445
  13.6 11.9 %collective-permute-start = (s32[6]{0:T(128)}, s32[6]{0:T(128)S(1)}, u32[]{:S(2)}, u32[]{:S(2)}) collective-permute-start(s32[6]{0:T(128)} %get-tuple-element.28.sel_ref), channel_id=1, source_target_pairs={{0,4},{1,5},{2,6},{3,7},{4,0},{5,1},{6,2},{7,3},{8,12},{9,13},{10,... | collective-permute-start | bytes 80 | tf_op jit(solution)/shard_map/ppermute | solution.py:445
  25.5 0.6 copy-start.1
  27.2 28.3 %collective-permute-start.12 = (bf16[1536,128]{1,0:T(8,128)(2,1)S(1)}, bf16[1536,128]{1,0:T(8,128)(2,1)S(1)}, u32[]{:S(2)}, u32[]{:S(2)}) collective-permute-start(bf16[1536,128]{1,0:T(8,128)(2,1)S(1)} %get-tuple-element.45), channel_id=1, source_target_pairs={{0,4},{1,5},{2,6},{3,7},{4,0},{5,1},{6,2},{7,3},{8,12},{9,13},{10,... | collective-permute-start | bytes 1179656 | tf_op jit(solution)/shard_map/ppermute | solution.py:445
  28.9 26.6 %collective-permute-start.11 = (bf16[1536,128]{1,0:T(8,128)(2,1)S(1)}, bf16[1536,128]{1,0:T(8,128)(2,1)S(1)}, u32[]{:S(2)}, u32[]{:S(2)}) collective-permute-start(bf16[1536,128]{1,0:T(8,128)(2,1)S(1)} %get-tuple-element.36.refs_0_), channel_id=1, source_target_pairs={{0,1},{1,0},{2,3},{3,2},{4,5},{5,4},{6,7},{7,6},{8,9},{9,8},{10,11... | collective-permute-start | bytes 1179656 | tf_op jit(solution)/shard_map/ppermute | solution.py:445
  30.4 12.1 %collective-permute-start.4 = (bf16[400,128]{1,0:T(8,128)(2,1)S(1)}, bf16[400,128]{1,0:T(8,128)(2,1)S(1)}, u32[]{:S(2)}, u32[]{:S(2)}) collective-permute-start(bf16[400,128]{1,0:T(8,128)(2,1)S(1)} %get-tuple-element.38), channel_id=1, source_target_pairs={{0,16},{2,18},{4,20},{6,22},{8,24},{10,26},{12,28},{14,30},{16,0},... | collective-permute-start | bytes 307208 | tf_op jit(solution)/shard_map/ppermute | solution.py:449
  33.0 10.1 %collective-permute-start.5 = (bf16[400,128]{1,0:T(8,128)(2,1)S(1)}, bf16[400,128]{1,0:T(8,128)(2,1)S(1)}, u32[]{:S(2)}, u32[]{:S(2)}) collective-permute-start(bf16[400,128]{1,0:T(8,128)(2,1)S(1)} %get-tuple-element.39), channel_id=1, source_target_pairs={{0,24},{2,26},{4,28},{6,30},{8,16},{10,18},{12,20},{14,22},{16,8},... | collective-permute-start | bytes 307208 | tf_op jit(solution)/shard_map/ppermute | solution.py:449
  34.3 10.5 %collective-permute-start.6 = (bf16[400,128]{1,0:T(8,128)(2,1)S(1)}, bf16[400,128]{1,0:T(8,128)(2,1)S(1)}, u32[]{:S(2)}, u32[]{:S(2)}) collective-permute-start(bf16[400,128]{1,0:T(8,128)(2,1)S(1)} %get-tuple-element.40), channel_id=1, source_target_pairs={{0,18},{2,16},{4,22},{6,20},{8,26},{10,24},{12,30},{14,28},{16,2},... | collective-permute-start | bytes 307208 | tf_op jit(solution)/shard_map/ppermute | solution.py:449
  42.4 6.5 %collective-permute-start.7 = (bf16[400,128]{1,0:T(8,128)(2,1)S(1)}, bf16[400,128]{1,0:T(8,128)(2,1)S(1)}, u32[]{:S(2)}, u32[]{:S(2)}) collective-permute-start(bf16[400,128]{1,0:T(8,128)(2,1)S(1)} %get-tuple-element.41), channel_id=1, source_target_pairs={{0,26},{2,24},{4,30},{6,28},{8,18},{10,16},{12,22},{14,20},{16,10}... | collective-permute-start | bytes 307208 | tf_op jit(solution)/shard_map/ppermute | solution.py:449
  43.0 7.8 %collective-permute-start.8 = (bf16[400,128]{1,0:T(8,128)(2,1)S(1)}, bf16[400,128]{1,0:T(8,128)(2,1)S(1)}, u32[]{:S(2)}, u32[]{:S(2)}) collective-permute-start(bf16[400,128]{1,0:T(8,128)(2,1)S(1)} %get-tuple-element.42), channel_id=1, source_target_pairs={{0,8},{2,10},{4,12},{6,14},{8,0},{10,2},{12,4},{14,6},{16,24},{18,... | collective-permute-start | bytes 307208 | tf_op jit(solution)/shard_map/ppermute | solution.py:449
  44.8 8.4 %collective-permute-start.9 = (bf16[400,128]{1,0:T(8,128)(2,1)S(1)}, bf16[400,128]{1,0:T(8,128)(2,1)S(1)}, u32[]{:S(2)}, u32[]{:S(2)}) collective-permute-start(bf16[400,128]{1,0:T(8,128)(2,1)S(1)} %get-tuple-element.43), channel_id=1, source_target_pairs={{0,10},{2,8},{4,14},{6,12},{8,2},{10,0},{12,6},{14,4},{16,26},{18,... | collective-permute-start | bytes 307208 | tf_op jit(solution)/shard_map/ppermute | solution.py:449
  49.0 4.2 %collective-permute-start.10 = (bf16[400,128]{1,0:T(8,128)(2,1)S(1)}, bf16[400,128]{1,0:T(8,128)(2,1)S(1)}, u32[]{:S(2)}, u32[]{:S(2)}) collective-permute-start(bf16[400,128]{1,0:T(8,128)(2,1)S(1)} %get-tuple-element.44), channel_id=1, source_target_pairs={{0,2},{2,0},{4,6},{6,4},{8,10},{10,8},{12,14},{14,12},{16,18},{18,... | collective-permute-start | bytes 307208 | tf_op jit(solution)/shard_map/ppermute | solution.py:449
  55.4 32.7 %copy-start.2 = (s32[192]{0:T(256)S(1)}, s32[192]{0:T(256)}, u32[]{:S(2)}) copy-start(s32[192]{0:T(256)} %get-tuple-element.27.table_ref) | copy-start | bytes 2308
  55.4 32.7 %all-to-all-start = ((bf16[32,3,48,128]{3,2,1,0:T(8,128)(2,1)}), bf16[32,3,48,128]{3,2,1,0:T(8,128)(2,1)S(1)}, u32[]{:S(2)}, u32[]{:S(2)}) async-start(bf16[32,3,48,128]{3,2,1,0:T(8,128)(2,1)} %shard_map.68), calls=%async_computation | async-start | bytes 2359296 | tf_op jit(solution)/shard_map/all_to_all | solution.py:464
  58.1 20.8 %collective-permute-start.13 = (bf16[1536,128]{1,0:T(8,128)(2,1)S(1)}, bf16[1536,128]{1,0:T(8,128)(2,1)S(1)}, u32[]{:S(2)}, u32[]{:S(2)}) collective-permute-start(bf16[1536,128]{1,0:T(8,128)(2,1)S(1)} %collective-permute-done.12.refs_1_), channel_id=1, source_target_pairs={{0,1},{1,0},{2,3},{3,2},{4,5},{5,4},{6,7},{7,6},{8,9},{9,8},{10,11... | collective-permute-start | bytes 1179656 | tf_op jit(solution)/shard_map/ppermute | solution.py:445
  99.4 4.6 %collective-permute-start.14 = (f32[12,12,12]{2,1,0:T(8,128)S(1)}, f32[12,12,12]{2,1,0:T(8,128)S(1)}, u32[]{:S(2)}, u32[]{:S(2)}) collective-permute-start(f32[12,12,12]{2,1,0:T(8,128)S(1)} %shard_map.69), channel_id=1, source_target_pairs={{0,1},{1,0},{2,3},{3,2},{4,5},{5,4},{6,7},{7,6},{8,9},{9,8},{10,11... | collective-permute-start | bytes 20744 | tf_op jit(solution)/shard_map/ppermute | solution.py:467

commit v6 on v5

--- a/solution.py
+++ b/solution.py
@@ -14,7 +14,7 @@
 COLS = 256
 CHUNK = 4
 LINE = 32
-SPREAD = (0, 4, 6, 5, 7, 2, 3, 1)
+SPREAD = (0, 1, 2, 4, 3, 6, 5, 7)
 SMEM = pltpu.SMEM
 VMEM = pltpu.VMEM
 
@@ -168,16 +168,16 @@
 
 
 def query_rows(parts, out_ref):
-    _, x, _, side = place()
+    _, _, core, side = place()
     size = out_ref.shape[1] // 32
     blocks = out_ref.shape[0]
     for rel, ref in enumerate(parts):
-        base = (side ^ (rel // 2)) * (16 * size) + (x ^ (rel % 2)) * (2 * size)
+        base = (side ^ (rel // 2)) * (16 * size) + (core ^ (rel % 2)) * (2 * size)
         for z in range(4):
-            for c in range(2):
-                target = pl.multiple_of(base + z * 4 * size + c * size, 16)
+            for x in range(2):
+                target = pl.multiple_of(base + z * 4 * size + x * size, 16)
                 for b in range(blocks):
-                    begin = ((z * 2 + c) * blocks + b) * size
+                    begin = ((z * 2 + x) * blocks + b) * size
                     out_ref[b, pl.ds(target, size)] = ref[begin : begin + size]
 
 
@@ -201,7 +201,8 @@
         if parts:
             pieces, _, size, _ = cand_ref.shape
             for piece in range(pieces):
-                block_ref[piece * size : (piece + 1) * size] = cand_ref[piece, k]
+                begin = (piece // 4 * 4 + piece % 2 * 2 + piece // 2 % 2) * size
+                block_ref[begin : begin + size] = cand_ref[piece, k]
         for start in range(0, rows, COLS):
             sim = lax.dot_general(
                 block_ref[...] if parts else cand_ref[k],
@@ -300,7 +301,7 @@
 
 def split_kernel(first, over, states_ref, weight_ref, *refs):
     *outs, rows_ref, sems = refs
-    _, x, _, side = place()
+    _, _, core, side = place()
     blocks, part, _ = rows_ref.shape
     size = part // 16
     start = pl.multiple_of((side ^ over) * part, part)
@@ -315,16 +316,16 @@
     for b in range(blocks):
         load(b).wait()
         for z in range(4):
-            for dx in range(2):
-                source = pl.multiple_of((x ^ dx) * (2 * size) + z * 4 * size, 16)
+            for flip in range(2):
+                source = pl.multiple_of((core ^ flip) * (2 * size) + z * 4 * size, 16)
                 both = jnp.dot(
                     rows_ref[b, pl.ds(source, 2 * size)],
                     weight_ref[...],
                     preferred_element_type=jnp.float32,
                 ).astype(jnp.bfloat16)
-                for c in range(2):
-                    target = ((z * 2 + c) * blocks + b) * size
-                    outs[dx][target : target + size] = both[c * size : (c + 1) * size]
+                for x in range(2):
+                    target = ((z * 2 + x) * blocks + b) * size
+                    outs[flip][target : target + size] = both[x * size : (x + 1) * size]
 
 
 def split(over, states, weight, first):
@@ -350,30 +351,30 @@
     )(states, weight)
 
 
-def gather_unit_kernel(size, sel_ref, sel_x_ref, y_ref, xy_ref, own_ref, x_ref, *outs):
-    z, _, c, _ = place()
+def gather_unit_kernel(size, sel_ref, sel_near_ref, y_ref, cy_ref, own_ref, c_ref, *outs):
+    z, x, _, _ = place()
     sends, query = outs[:8], outs[8:]
     span = CHUNK * size
     shape = (16, own_ref.shape[1])
     row, lane = (lax.broadcasted_iota(jnp.int32, shape, axis) for axis in range(2))
     asked = jnp.zeros(shape, jnp.int32)
-    for dx, ids_ref in enumerate((sel_ref, sel_x_ref)):
+    for flip, ids_ref in enumerate((sel_ref, sel_near_ref)):
         for k in range(ids_ref.shape[0]):
-            asked = jnp.where((row == dx) & (lane == k), ids_ref[k], asked)
+            asked = jnp.where((row == flip) & (lane == k), ids_ref[k], asked)
     asked = asked.astype(jnp.float32).astype(jnp.bfloat16)
-    for rel, send_ref in enumerate(sends):
-        source = pl.multiple_of(((z ^ (rel // 2)) * 2 + (c ^ (rel % 2))) * span, 16)
-        for dx, (one_ref, two_ref) in enumerate(((own_ref, y_ref), (x_ref, xy_ref))):
+    for rel, send_ref in zip(SPREAD, sends):
+        source = pl.multiple_of(((z ^ (rel // 2)) * 2 + (x ^ (rel % 2))) * span, 16)
+        for flip, (one_ref, two_ref) in enumerate(((own_ref, y_ref), (c_ref, cy_ref))):
             total = one_ref[pl.ds(source, span)].astype(jnp.float32)
             total = total + two_ref[pl.ds(source, span)].astype(jnp.float32)
             norm = jnp.sum(total * total, axis=-1, keepdims=True)
             unit = (total * lax.rsqrt(norm + 1e-06)).astype(jnp.bfloat16)
-            send_ref[dx * span : (dx + 1) * span] = unit
-            query[dx][pl.ds(source, span)] = unit
+            send_ref[flip * span : (flip + 1) * span] = unit
+            query[flip][pl.ds(source, span)] = unit
         send_ref[2 * span :] = asked
 
 
-def gather_unit(sel, sel_x, y, xy, own, x, size):
+def gather_unit(sel, sel_near, y, cy, own, c, size):
     rows, width = own.shape
     send = jax.ShapeDtypeStruct((2 * CHUNK * size + 16, width), jnp.bfloat16)
     query = jax.ShapeDtypeStruct((rows, width), jnp.bfloat16)
@@ -383,21 +384,21 @@
         in_specs=[pl.BlockSpec(memory_space=SMEM)] * 2 + [pl.BlockSpec(memory_space=VMEM)] * 4,
         out_specs=[pl.BlockSpec(memory_space=VMEM)] * 10,
         compiler_params=vmem_params(12),
-    )(sel, sel_x, y, xy, own, x)
+    )(sel, sel_near, y, cy, own, c)
 
 
 def cube_route_kernel(size, slots, parts, *refs):
     spread, out_ref, pieces_ref, rows_ref, asked_ref, sem = refs[:parts], *refs[parts:]
-    z, x, c, _ = place()
+    z, x, core, _ = place()
     blocks = pieces_ref.shape[0] // 16
     span = CHUNK * size
     for rel, ref in zip(SPREAD, spread):
-        for dx in range(2):
-            owner = (z ^ (rel // 2)) * 4 + (x ^ dx) * 2 + (c ^ (rel % 2))
+        for flip in range(2):
+            owner = (z ^ (rel // 2)) * 4 + (x ^ (rel % 2)) * 2 + (core ^ flip)
             for b in range(CHUNK):
-                begin = dx * span + b * size
+                begin = flip * span + b * size
                 pieces_ref[owner * blocks + b] = ref[begin : begin + size]
-            row = ref[2 * span :].astype(jnp.float32)[dx : dx + 1]
+            row = ref[2 * span :].astype(jnp.float32)[flip : flip + 1]
             rows_ref[pl.ds(owner, 1)] = row.astype(jnp.int32)
     copy = pltpu.make_async_copy(rows_ref, asked_ref, sem)
     copy.start()
@@ -441,24 +442,26 @@
     flat = states.reshape(blocks, rows, width_part)
 
     def near(array, rel):
-        flip = rel % 2 * 4 + rel // 2
+        flip = rel % 2 * 2 + rel // 2
         return lax.ppermute(array, ("wide", "narrow"), [(i, i ^ flip) for i in range(32)])
 
     def along(array, rel):
-        flip = rel // 2 * 4 + rel % 2
+        flip = rel * 2
         return lax.ppermute(array, "wide", [(i, i ^ flip) for i in range(16)])
 
     places = jnp.stack([owner, side, jnp.int32(blocks)])
     sel, table = plan(places, cand_block, query_block, pair_valid, lengths, slots)
-    sel_x = near(sel, 1)
+    sel_near = near(sel, 1)
     far = split(1, flat, proj_weight, 0)
     weight, *far = lax.optimization_barrier((proj_weight, *far))
-    y, xy = near(far[0], 2), near(far[1], 3)
+    y, cy = near(far[0], 2), near(far[1], 3)
     own, aside = split(0, flat, weight, 0)
-    x = near(aside, 1)
-    *sends, own, other = gather_unit(sel, sel_x, y, xy, own, x, size)
-    spread = [along(sends[rel], rel) if rel else sends[rel] for rel in SPREAD]
-    own_y, other = near(own, 2), near(other, 1)
+    c = near(aside, 1)
+    *sends, own, other = gather_unit(sel, sel_near, y, cy, own, c, size)
+    other = near(other, 1)
+    sends[4], other = lax.optimization_barrier((sends[4], other))
+    spread = [along(send, rel) if rel else send for rel, send in zip(SPREAD, sends)]
+    own_y = near(own, 2)
     outgoing = cube_route(spread, size, slots, blocks)
     outgoing, own_y, other = lax.optimization_barrier((outgoing, own_y, other))
     incoming = lax.all_to_all(outgoing, ("narrow", "wide"), 0, 0, tiled=True)

time: 105 us -> 103 us (0.981)
    ppermute x7, starting transfers between devices: 11.6 us -> 7.88 us  [near(): lax.ppermute(array, ('wide', 'narrow'), [(i, i ^ flip) for i in range(32)])]
    ppermute x7, starting transfers between devices: 8.09 us -> 10.5 us  [along(): return lax.ppermute(array, 'wide', [(i, i ^ flip) for i in range(16)])]
    ppermute x7, waiting for transfers between devices: 14.7 us -> 13 us  [along(): return lax.ppermute(array, 'wide', [(i, i ^ flip) for i in range(16)])]
  transfers between devices with their start and end apart: 16 -> 16, of which waited for: 8 -> 9; matrix products, arithmetic and copies ran while one was open for 1% -> 1% of each run, Pallas kernels for 7% -> 7%
where the time goes in v6:
time: 103 us
  waiting for transfers between devices  55.6 us (54%)
  starting transfers between devices  22.7 us (22%)
  Pallas kernels  22 us (21%)
  local copies, waits for them, and re-layouts  1.52 us (1%)
  other arithmetic  1.3 us (1%)
    ppermute x7, waiting for transfers between devices, near(): lax.ppermute(array, ('wide', 'narrow'), [(i, i ^ flip) for i in range(32)])  29.9 us
    ppermute x7, waiting for transfers between devices, along(): return lax.ppermute(array, 'wide', [(i, i ^ flip) for i in range(16)])  13 us
    pallas_call x1, Pallas kernels, score(): pl.pallas_call(functools.partial(score_kernel, length, parts), out_shape=...  11.3 us
    ppermute x7, starting transfers between devices, along(): return lax.ppermute(array, 'wide', [(i, i ^ flip) for i in range(16)])  10.5 us
    all_to_all x1, waiting for transfers between devices, local_cube(): incoming = lax.all_to_all(outgoing, ('narrow', 'wide'), 0, 0, tiled=True)  8.97 us
    ppermute x7, starting transfers between devices, near(): lax.ppermute(array, ('wide', 'narrow'), [(i, i ^ flip) for i in range(32)])  7.88 us
    pallas_call x2, Pallas kernels, split(): pl.pallas_call(functools.partial(split_kernel, first, over), out_shape=(j...  5.26 us
    ppermute x1, waiting for transfers between devices, local_cube(): return part + lax.ppermute(part, 'narrow', [(0, 1), (1, 0)])  3.65 us
  transfers between devices with their start and end apart: 16, of which 9 were waited for; matrix products, arithmetic and copies ran while one was open for 1% of the time, Pallas kernels for 7%

profile of v6, /device:TPU:0, one launch (start us, length us, event | category | flops | bytes accessed | tf_op | source)
XLA Modules:
  0.0 103.2 jit_solution(3461153167454311789)
XLA Ops:
  0.0 0.9 copy-done
  0.9 2.6 %shard_map.65 = (bf16[1536,128]{1,0:T(8,128)(2,1)S(1)}, bf16[1536,128]{1,0:T(8,128)(2,1)S(1)}) custom-call(bf16[4,1536,512]{2,1,0:T(8,128)(2,1)} %bitcast.3, bf16[512,128]{1,0:T(8,128)(2,1)S(1)} %copy-done), custom_call_target="tpu_custom_call" | custom-call | flops 402653184 | bytes 3145728 | tf_op jit(solution)/shard_map/pallas_call | solution.py:336
  3.5 3.0 %collective-permute-start.1 = (bf16[1536,128]{1,0:T(8,128)(2,1)S(1)}, bf16[1536,128]{1,0:T(8,128)(2,1)S(1)}, u32[]{:S(2)}, u32[]{:S(2)}) collective-permute-start(bf16[1536,128]{1,0:T(8,128)(2,1)S(1)} %get-tuple-element.33), channel_id=1, source_target_pairs={{0,1},{1,0},{2,3},{3,2},{4,5},{5,4},{6,7},{7,6},{8,9},{9,8},{10,11... | collective-permute-start | bytes 1179656 | tf_op jit(solution)/shard_map/ppermute | solution.py:446
  6.6 2.6 %shard_map.66 = (bf16[1536,128]{1,0:T(8,128)(2,1)S(1)}, bf16[1536,128]{1,0:T(8,128)(2,1)S(1)}) custom-call(bf16[4,1536,512]{2,1,0:T(8,128)(2,1)} %bitcast.4, bf16[512,128]{1,0:T(8,128)(2,1)S(1)} %copy-done), custom_call_target="tpu_custom_call" | custom-call | flops 402653184 | bytes 3145728 | tf_op jit(solution)/shard_map/pallas_call | solution.py:336
  9.2 0.3 collective-permute-start.3
  9.5 0.7 pad_add_fusion.places_ref
  10.1 2.1 %shard_map.64 = (s32[6]{0:T(128)}, s32[192]{0:T(256)}) custom-call(s32[3]{0:T(128)} %pad_add_fusion.places_ref, s32[12]{0:T(128)} %cand_ref.1, s32[12]{0:T(128)} %query_block_ref.1, s32[12]{0:T(128)} %valid_ref.1, s32[768]{0:T(1024)} %lengths_ref.1), custom_call_target="tpu_custom_call" | custom-call | tf_op jit(solution)/shard_map/pallas_call | solution.py:68
  12.3 0.4 collective-permute-start
  12.7 1.0 collective-permute-done.sel_near_ref
  13.7 2.8 %collective-permute-done.1.y_ref = bf16[1536,128]{1,0:T(8,128)(2,1)S(1)} collective-permute-done((bf16[1536,128]{1,0:T(8,128)(2,1)S(1)}, bf16[1536,128]{1,0:T(8,128)(2,1)S(1)}, u32[]{:S(2)}, u32[]{:S(2)}) %collective-permute-start.1) | collective-permute-done | bytes 393248 | tf_op jit(solution)/shard_map/ppermute | solution.py:446
  16.5 6.9 %collective-permute-done.2.cy_ref = bf16[1536,128]{1,0:T(8,128)(2,1)S(1)} collective-permute-done((bf16[1536,128]{1,0:T(8,128)(2,1)S(1)}, bf16[1536,128]{1,0:T(8,128)(2,1)S(1)}, u32[]{:S(2)}, u32[]{:S(2)}) %collective-permute-start.2) | collective-permute-done | bytes 393248 | tf_op jit(solution)/shard_map/ppermute | solution.py:446
  23.4 0.6 copy-done.1
  24.0 1.1 %shard_map.67 = (bf16[400,128]{1,0:T(8,128)(2,1)S(1)}, bf16[400,128]{1,0:T(8,128)(2,1)S(1)}, bf16[400,128]{1,0:T(8,128)(2,1)S(1)}, bf16[400,128]{1,0:T(8,128)(2,...) custom-call(s32[6]{0:T(128)S(1)} %copy-done.1, ...), custom_call_target="tpu_custom_call" | custom-call | tf_op jit(solution)/shard_map/pallas_call | solution.py:381
  25.0 0.6 collective-permute-start.7
  25.7 1.7 %collective-permute-start.12 = (bf16[1536,128]{1,0:T(8,128)(2,1)S(1)}, bf16[1536,128]{1,0:T(8,128)(2,1)S(1)}, u32[]{:S(2)}, u32[]{:S(2)}) collective-permute-start(bf16[1536,128]{1,0:T(8,128)(2,1)S(1)} %get-tuple-element.38.refs_0_), channel_id=1, source_target_pairs={{0,1},{1,0},{2,3},{3,2},{4,5},{5,4},{6,7},{7,6},{8,9},{9,8},{10,11... | collective-permute-start | bytes 1179656 | tf_op jit(solution)/shard_map/ppermute | solution.py:446
  27.4 1.5 %collective-permute-start.4 = (bf16[400,128]{1,0:T(8,128)(2,1)S(1)}, bf16[400,128]{1,0:T(8,128)(2,1)S(1)}, u32[]{:S(2)}, u32[]{:S(2)}) collective-permute-start(bf16[400,128]{1,0:T(8,128)(2,1)S(1)} %get-tuple-element.40), channel_id=1, source_target_pairs={{0,4},{2,6},{4,0},{6,2},{8,12},{10,14},{12,8},{14,10},{16,20},{18,... | collective-permute-start | bytes 307208 | tf_op jit(solution)/shard_map/ppermute | solution.py:450
  28.9 1.6 %collective-permute-start.5 = (bf16[400,128]{1,0:T(8,128)(2,1)S(1)}, bf16[400,128]{1,0:T(8,128)(2,1)S(1)}, u32[]{:S(2)}, u32[]{:S(2)}) collective-permute-start(bf16[400,128]{1,0:T(8,128)(2,1)S(1)} %get-tuple-element.41), channel_id=1, source_target_pairs={{0,8},{2,10},{4,12},{6,14},{8,0},{10,2},{12,4},{14,6},{16,24},{18,... | collective-permute-start | bytes 307208 | tf_op jit(solution)/shard_map/ppermute | solution.py:450
  30.5 2.6 %collective-permute-start.6 = (bf16[400,128]{1,0:T(8,128)(2,1)S(1)}, bf16[400,128]{1,0:T(8,128)(2,1)S(1)}, u32[]{:S(2)}, u32[]{:S(2)}) collective-permute-start(bf16[400,128]{1,0:T(8,128)(2,1)S(1)} %get-tuple-element.42), channel_id=1, source_target_pairs={{0,16},{2,18},{4,20},{6,22},{8,24},{10,26},{12,28},{14,30},{16,0},... | collective-permute-start | bytes 307208 | tf_op jit(solution)/shard_map/ppermute | solution.py:450
  33.3 2.3 %collective-permute-start.10 = (bf16[400,128]{1,0:T(8,128)(2,1)S(1)}, bf16[400,128]{1,0:T(8,128)(2,1)S(1)}, u32[]{:S(2)}, u32[]{:S(2)}) collective-permute-start(bf16[400,128]{1,0:T(8,128)(2,1)S(1)} %get-tuple-element.47), channel_id=1, source_target_pairs={{0,20},{2,22},{4,16},{6,18},{8,28},{10,30},{12,24},{14,26},{16,4},... | collective-permute-start | bytes 307208 | tf_op jit(solution)/shard_map/ppermute | solution.py:450
  35.6 2.3 %collective-permute-start.11 = (bf16[400,128]{1,0:T(8,128)(2,1)S(1)}, bf16[400,128]{1,0:T(8,128)(2,1)S(1)}, u32[]{:S(2)}, u32[]{:S(2)}) collective-permute-start(bf16[400,128]{1,0:T(8,128)(2,1)S(1)} %get-tuple-element.48), channel_id=1, source_target_pairs={{0,28},{2,30},{4,24},{6,26},{8,20},{10,22},{12,16},{14,18},{16,12}... | collective-permute-start | bytes 307208 | tf_op jit(solution)/shard_map/ppermute | solution.py:450
  37.9 7.5 %collective-permute-done.6.refs_3_ = bf16[400,128]{1,0:T(8,128)(2,1)S(1)} collective-permute-done((bf16[400,128]{1,0:T(8,128)(2,1)S(1)}, bf16[400,128]{1,0:T(8,128)(2,1)S(1)}, u32[]{:S(2)}, u32[]{:S(2)}) %collective-permute-start.6) | collective-permute-done | bytes 102432 | tf_op jit(solution)/shard_map/ppermute | solution.py:450
  45.4 4.3 %collective-permute-done.10.refs_6_ = bf16[400,128]{1,0:T(8,128)(2,1)S(1)} collective-permute-done((bf16[400,128]{1,0:T(8,128)(2,1)S(1)}, bf16[400,128]{1,0:T(8,128)(2,1)S(1)}, u32[]{:S(2)}, u32[]{:S(2)}) %collective-permute-start.10) | collective-permute-done | bytes 102432 | tf_op jit(solution)/shard_map/ppermute | solution.py:450
  49.6 1.3 %collective-permute-done.8.refs_4_ = bf16[400,128]{1,0:T(8,128)(2,1)S(1)} collective-permute-done((bf16[400,128]{1,0:T(8,128)(2,1)S(1)}, bf16[400,128]{1,0:T(8,128)(2,1)S(1)}, u32[]{:S(2)}, u32[]{:S(2)}) %collective-permute-start.8) | collective-permute-done | bytes 102432 | tf_op jit(solution)/shard_map/ppermute | solution.py:450
  50.9 2.2 %shard_map.68 = bf16[32,3,48,128]{3,2,1,0:T(8,128)(2,1)} custom-call(bf16[400,128]{1,0:T(8,128)(2,1)S(1)} %get-tuple-element.39.refs_0_, bf16[400,128]{1,0:T(8,128)(2,1)S(1)} %collective-permute-done.4.refs_1_, bf16[400,128]{1,0:T(8,128)(2,1)S(1)} %collective-permute-done.5.refs_2_, bf16[400,128]{1,0:T(8,128)(2,1)S(1)} %collective-permute-done.6.refs_3_, ...), custom_call_target="tpu_custom_call" | custom-call | tf_op jit(solution)/shard_map/pallas_call | solution.py:418
  53.2 3.4 %all-to-all-start = ((bf16[32,3,48,128]{3,2,1,0:T(8,128)(2,1)}), bf16[32,3,48,128]{3,2,1,0:T(8,128)(2,1)S(1)}, u32[]{:S(2)}, u32[]{:S(2)}) async-start(bf16[32,3,48,128]{3,2,1,0:T(8,128)(2,1)} %shard_map.68), calls=%async_computation | async-start | bytes 2359296 | tf_op jit(solution)/shard_map/all_to_all | solution.py:467
  56.6 1.8 %collective-permute-start.13 = (bf16[1536,128]{1,0:T(8,128)(2,1)S(1)}, bf16[1536,128]{1,0:T(8,128)(2,1)S(1)}, u32[]{:S(2)}, u32[]{:S(2)}) collective-permute-start(bf16[1536,128]{1,0:T(8,128)(2,1)S(1)} %collective-permute-done.7.refs_1_), channel_id=1, source_target_pairs={{0,1},{1,0},{2,3},{3,2},{4,5},{5,4},{6,7},{7,6},{8,9},{9,8},{10,11... | collective-permute-start | bytes 1179656 | tf_op jit(solution)/shard_map/ppermute | solution.py:446
  58.4 19.2 %collective-permute-done.13.refs_3_ = bf16[1536,128]{1,0:T(8,128)(2,1)S(1)} collective-permute-done((bf16[1536,128]{1,0:T(8,128)(2,1)S(1)}, bf16[1536,128]{1,0:T(8,128)(2,1)S(1)}, u32[]{:S(2)}, u32[]{:S(2)}) %collective-permute-start.13) | collective-permute-done | bytes 393248 | tf_op jit(solution)/shard_map/ppermute | solution.py:446
  77.6 9.0 %all-to-all-done.refs_4_ = bf16[32,3,48,128]{3,2,1,0:T(8,128)(2,1)S(1)} async-done(((bf16[32,3,48,128]{3,2,1,0:T(8,128)(2,1)}), bf16[32,3,48,128]{3,2,1,0:T(8,128)(2,1)S(1)}, u32[]{:S(2)}, u32[]{:S(2)}) %all-to-all-start) | async-done | bytes 1179680 | tf_op jit(solution)/shard_map/all_to_all | solution.py:467
  86.6 11.3 %shard_map.69 = f32[12,12,12]{2,1,0:T(8,128)S(1)} custom-call(s32[192]{0:T(256)S(1)} %copy-done.2, bf16[1536,128]{1,0:T(8,128)(2,1)S(1)} %get-tuple-element.38.refs_0_, bf16[1536,128]{1,0:T(8,128)(2,1)S(1)} %collective-permute-done.7.refs_1_, bf16[1536,128]{1,0:T(8,128)(2,1)S(1)} %collective-permute-done.12.refs_2_, ...), custom_call_target="tpu_custom_call" | custom-call | flops 3623878656 | bytes 786432 | tf_op jit(solution)/shard_map/pallas_call | solution.py:240
  97.9 1.0 collective-permute-start.14
  98.9 3.7 %collective-permute-done.14 = f32[12,12,12]{2,1,0:T(8,128)S(1)} collective-permute-done((f32[12,12,12]{2,1,0:T(8,128)S(1)}, f32[12,12,12]{2,1,0:T(8,128)S(1)}, u32[]{:S(2)}, u32[]{:S(2)}) %collective-permute-start.14) | collective-permute-done | bytes 6944 | tf_op jit(solution)/shard_map/ppermute | solution.py:470
  102.5 0.7 add.3
  (14 shorter events, 0.3 us)
Async XLA Ops:
  0.0 0.9 copy-start
  3.5 13.0 %collective-permute-start.1 = (bf16[1536,128]{1,0:T(8,128)(2,1)S(1)}, bf16[1536,128]{1,0:T(8,128)(2,1)S(1)}, u32[]{:S(2)}, u32[]{:S(2)}) collective-permute-start(bf16[1536,128]{1,0:T(8,128)(2,1)S(1)} %get-tuple-element.33), channel_id=1, source_target_pairs={{0,1},{1,0},{2,3},{3,2},{4,5},{5,4},{6,7},{7,6},{8,9},{9,8},{10,11... | collective-permute-start | bytes 1179656 | tf_op jit(solution)/shard_map/ppermute | solution.py:446
  6.6 16.8 %collective-permute-start.2 = (bf16[1536,128]{1,0:T(8,128)(2,1)S(1)}, bf16[1536,128]{1,0:T(8,128)(2,1)S(1)}, u32[]{:S(2)}, u32[]{:S(2)}) collective-permute-start(bf16[1536,128]{1,0:T(8,128)(2,1)S(1)} %get-tuple-element.34), channel_id=1, source_target_pairs={{0,3},{1,2},{2,1},{3,0},{4,7},{5,6},{6,5},{7,4},{8,11},{9,10},{10,... | collective-permute-start | bytes 1179656 | tf_op jit(solution)/shard_map/ppermute | solution.py:446
  9.2 14.2 %collective-permute-start.3 = (bf16[1536,128]{1,0:T(8,128)(2,1)S(1)}, bf16[1536,128]{1,0:T(8,128)(2,1)S(1)}, u32[]{:S(2)}, u32[]{:S(2)}) collective-permute-start(bf16[1536,128]{1,0:T(8,128)(2,1)S(1)} %get-tuple-element.37), channel_id=1, source_target_pairs={{0,2},{1,3},{2,0},{3,1},{4,6},{5,7},{6,4},{7,5},{8,10},{9,11},{10,... | collective-permute-start | bytes 1179656 | tf_op jit(solution)/shard_map/ppermute | solution.py:446
  12.3 1.4 %collective-permute-start = (s32[6]{0:T(128)}, s32[6]{0:T(128)S(1)}, u32[]{:S(2)}, u32[]{:S(2)}) collective-permute-start(s32[6]{0:T(128)} %get-tuple-element.30.sel_ref), channel_id=1, source_target_pairs={{0,2},{1,3},{2,0},{3,1},{4,6},{5,7},{6,4},{7,5},{8,10},{9,11},{10,... | collective-permute-start | bytes 80 | tf_op jit(solution)/shard_map/ppermute | solution.py:446
  23.4 0.6 copy-start.1
  25.0 8.0 %collective-permute-start.7 = (bf16[1536,128]{1,0:T(8,128)(2,1)S(1)}, bf16[1536,128]{1,0:T(8,128)(2,1)S(1)}, u32[]{:S(2)}, u32[]{:S(2)}) collective-permute-start(bf16[1536,128]{1,0:T(8,128)(2,1)S(1)} %get-tuple-element.44), channel_id=1, source_target_pairs={{0,2},{1,3},{2,0},{3,1},{4,6},{5,7},{6,4},{7,5},{8,10},{9,11},{10,... | collective-permute-start | bytes 1179656 | tf_op jit(solution)/shard_map/ppermute | solution.py:446
  25.7 27.5 %collective-permute-start.12 = (bf16[1536,128]{1,0:T(8,128)(2,1)S(1)}, bf16[1536,128]{1,0:T(8,128)(2,1)S(1)}, u32[]{:S(2)}, u32[]{:S(2)}) collective-permute-start(bf16[1536,128]{1,0:T(8,128)(2,1)S(1)} %get-tuple-element.38.refs_0_), channel_id=1, source_target_pairs={{0,1},{1,0},{2,3},{3,2},{4,5},{5,4},{6,7},{7,6},{8,9},{9,8},{10,11... | collective-permute-start | bytes 1179656 | tf_op jit(solution)/shard_map/ppermute | solution.py:446
  27.4 5.9 %collective-permute-start.4 = (bf16[400,128]{1,0:T(8,128)(2,1)S(1)}, bf16[400,128]{1,0:T(8,128)(2,1)S(1)}, u32[]{:S(2)}, u32[]{:S(2)}) collective-permute-start(bf16[400,128]{1,0:T(8,128)(2,1)S(1)} %get-tuple-element.40), channel_id=1, source_target_pairs={{0,4},{2,6},{4,0},{6,2},{8,12},{10,14},{12,8},{14,10},{16,20},{18,... | collective-permute-start | bytes 307208 | tf_op jit(solution)/shard_map/ppermute | solution.py:450
  28.9 6.7 %collective-permute-start.5 = (bf16[400,128]{1,0:T(8,128)(2,1)S(1)}, bf16[400,128]{1,0:T(8,128)(2,1)S(1)}, u32[]{:S(2)}, u32[]{:S(2)}) collective-permute-start(bf16[400,128]{1,0:T(8,128)(2,1)S(1)} %get-tuple-element.41), channel_id=1, source_target_pairs={{0,8},{2,10},{4,12},{6,14},{8,0},{10,2},{12,4},{14,6},{16,24},{18,... | collective-permute-start | bytes 307208 | tf_op jit(solution)/shard_map/ppermute | solution.py:450
  30.5 14.9 %collective-permute-start.6 = (bf16[400,128]{1,0:T(8,128)(2,1)S(1)}, bf16[400,128]{1,0:T(8,128)(2,1)S(1)}, u32[]{:S(2)}, u32[]{:S(2)}) collective-permute-start(bf16[400,128]{1,0:T(8,128)(2,1)S(1)} %get-tuple-element.42), channel_id=1, source_target_pairs={{0,16},{2,18},{4,20},{6,22},{8,24},{10,26},{12,28},{14,30},{16,0},... | collective-permute-start | bytes 307208 | tf_op jit(solution)/shard_map/ppermute | solution.py:450
  33.1 12.3 %collective-permute-start.9 = (bf16[400,128]{1,0:T(8,128)(2,1)S(1)}, bf16[400,128]{1,0:T(8,128)(2,1)S(1)}, u32[]{:S(2)}, u32[]{:S(2)}) collective-permute-start(bf16[400,128]{1,0:T(8,128)(2,1)S(1)} %get-tuple-element.46), channel_id=1, source_target_pairs={{0,24},{2,26},{4,28},{6,30},{8,16},{10,18},{12,20},{14,22},{16,8},... | collective-permute-start | bytes 307208 | tf_op jit(solution)/shard_map/ppermute | solution.py:450
  33.3 16.3 %collective-permute-start.10 = (bf16[400,128]{1,0:T(8,128)(2,1)S(1)}, bf16[400,128]{1,0:T(8,128)(2,1)S(1)}, u32[]{:S(2)}, u32[]{:S(2)}) collective-permute-start(bf16[400,128]{1,0:T(8,128)(2,1)S(1)} %get-tuple-element.47), channel_id=1, source_target_pairs={{0,20},{2,22},{4,16},{6,18},{8,28},{10,30},{12,24},{14,26},{16,4},... | collective-permute-start | bytes 307208 | tf_op jit(solution)/shard_map/ppermute | solution.py:450
  35.6 14.1 %collective-permute-start.11 = (bf16[400,128]{1,0:T(8,128)(2,1)S(1)}, bf16[400,128]{1,0:T(8,128)(2,1)S(1)}, u32[]{:S(2)}, u32[]{:S(2)}) collective-permute-start(bf16[400,128]{1,0:T(8,128)(2,1)S(1)} %get-tuple-element.48), channel_id=1, source_target_pairs={{0,28},{2,30},{4,24},{6,26},{8,20},{10,22},{12,16},{14,18},{16,12}... | collective-permute-start | bytes 307208 | tf_op jit(solution)/shard_map/ppermute | solution.py:450
  45.4 5.6 %collective-permute-start.8 = (bf16[400,128]{1,0:T(8,128)(2,1)S(1)}, bf16[400,128]{1,0:T(8,128)(2,1)S(1)}, u32[]{:S(2)}, u32[]{:S(2)}) collective-permute-start(bf16[400,128]{1,0:T(8,128)(2,1)S(1)} %get-tuple-element.45), channel_id=1, source_target_pairs={{0,12},{2,14},{4,8},{6,10},{8,4},{10,6},{12,0},{14,2},{16,28},{18,... | collective-permute-start | bytes 307208 | tf_op jit(solution)/shard_map/ppermute | solution.py:450
  53.2 33.4 %copy-start.2 = (s32[192]{0:T(256)S(1)}, s32[192]{0:T(256)}, u32[]{:S(2)}) copy-start(s32[192]{0:T(256)} %get-tuple-element.29.table_ref) | copy-start | bytes 2308
  53.2 33.4 %all-to-all-start = ((bf16[32,3,48,128]{3,2,1,0:T(8,128)(2,1)}), bf16[32,3,48,128]{3,2,1,0:T(8,128)(2,1)S(1)}, u32[]{:S(2)}, u32[]{:S(2)}) async-start(bf16[32,3,48,128]{3,2,1,0:T(8,128)(2,1)} %shard_map.68), calls=%async_computation | async-start | bytes 2359296 | tf_op jit(solution)/shard_map/all_to_all | solution.py:467
  56.6 21.0 %collective-permute-start.13 = (bf16[1536,128]{1,0:T(8,128)(2,1)S(1)}, bf16[1536,128]{1,0:T(8,128)(2,1)S(1)}, u32[]{:S(2)}, u32[]{:S(2)}) collective-permute-start(bf16[1536,128]{1,0:T(8,128)(2,1)S(1)} %collective-permute-done.7.refs_1_), channel_id=1, source_target_pairs={{0,1},{1,0},{2,3},{3,2},{4,5},{5,4},{6,7},{7,6},{8,9},{9,8},{10,11... | collective-permute-start | bytes 1179656 | tf_op jit(solution)/shard_map/ppermute | solution.py:446
  97.9 4.6 %collective-permute-start.14 = (f32[12,12,12]{2,1,0:T(8,128)S(1)}, f32[12,12,12]{2,1,0:T(8,128)S(1)}, u32[]{:S(2)}, u32[]{:S(2)}) collective-permute-start(f32[12,12,12]{2,1,0:T(8,128)S(1)} %shard_map.69), channel_id=1, source_target_pairs={{0,1},{1,0},{2,3},{3,2},{4,5},{5,4},{6,7},{7,6},{8,9},{9,8},{10,11... | collective-permute-start | bytes 20744 | tf_op jit(solution)/shard_map/ppermute | solution.py:470

commit v7 on v6

--- a/solution.py
+++ b/solution.py
@@ -14,7 +14,8 @@
 COLS = 256
 CHUNK = 4
 LINE = 32
-SPREAD = (0, 1, 2, 4, 3, 6, 5, 7)
+PACK = 6
+SPREAD = (0, 2, 4, 6, 5, 7, 1, 3)
 SMEM = pltpu.SMEM
 VMEM = pltpu.VMEM
 
@@ -23,7 +24,7 @@
     return pltpu.CompilerParams(vmem_limit_bytes=mib * 2**20)
 
 
-def plan_kernel(pairs, slots, places_ref, cand_ref, query_block_ref, valid_ref, lengths_ref, sel_ref, table_ref, *scratch):
+def plan_kernel(pairs, slots, places_ref, cand_ref, query_block_ref, valid_ref, lengths_ref, sel_ref, table_ref, pairs_ref, *scratch):
     first_ref, second_ref, slot_ref = scratch
     owner, side, blocks = places_ref[0], places_ref[1], places_ref[2]
 
@@ -51,7 +52,6 @@
         slot = side * slots + k
         pair = jnp.where(i - 2 * k == 0, first_ref[slot], second_ref[slot])
         query = query_block_ref[pair]
-        table_ref[i * LINE] = pair
         table_ref[i * LINE + 1] = query
         table_ref[i * LINE + 2] = valid_ref[pair]
         for a in range(BLK):
@@ -61,15 +61,22 @@
 
     lax.fori_loop(0, 2 * slots, line, 0)
 
+    def both(slot, carry):
+        pairs_ref[2 * slot] = first_ref[slot]
+        pairs_ref[2 * slot + 1] = second_ref[slot]
+        return carry
+
+    lax.fori_loop(0, pairs // 2, both, 0)
+
 
 def plan(places, cand_block, query_block, valid, lengths, slots):
     pairs = cand_block.shape[0]
-    shapes = (pairs // 2, 2 * slots * LINE)
+    shapes = (pairs // 2, 2 * slots * LINE, pairs)
     return pl.pallas_call(
         functools.partial(plan_kernel, pairs, slots),
         out_shape=[jax.ShapeDtypeStruct((n,), jnp.int32) for n in shapes],
         in_specs=[pl.BlockSpec(memory_space=SMEM)] * 5,
-        out_specs=[pl.BlockSpec(memory_space=SMEM)] * 2,
+        out_specs=[pl.BlockSpec(memory_space=SMEM)] * 3,
         scratch_shapes=[SMEM((pairs,), jnp.int32)] * 3,
     )(places, cand_block, query_block, valid, lengths)
 
@@ -197,7 +204,7 @@
     def pair_step(i, carry):
         k = i // 2
         line = i * LINE
-        pair, query = table_ref[line], table_ref[line + 1]
+        query = table_ref[line + 1]
         if parts:
             pieces, _, size, _ = cand_ref.shape
             for piece in range(pieces):
@@ -216,20 +223,20 @@
                 high = jnp.exp2(sim[b * length + length // 2 : (b + 1) * length] * EXP2_SCALE)
                 both = low + jnp.where(upper < live, high, 0.0)
                 totals_ref[b : b + 1, start : start + COLS] = jnp.sum(both, axis=0, keepdims=True)
-        score = jnp.zeros((16, length), jnp.float32)
+        keep = table_ref[line + 2].astype(jnp.float32) / (SHARPNESS * length)
+        score = out_ref[i // PACK]
         for a in range(BLK):
             live = table_ref[line + 3 + BLK + a]
             logs = jnp.log(totals_ref[:, a * length : (a + 1) * length])
             summed = jnp.sum(jnp.where(lane < live, logs, 0.0), axis=1, keepdims=True)
-            score = jnp.where(lane == a, summed, score)
-        keep = table_ref[line + 2].astype(jnp.float32) / (SHARPNESS * length)
-        out_ref[pair] = score[:BLK, :BLK] * keep
+            score = jnp.where(lane == lax.rem(i, PACK) * BLK + a, summed * keep, score)
+        out_ref[i // PACK] = score
         return carry
 
     lax.fori_loop(0, 2 * slots, pair_step, 0)
 
 
-def score(table, query, cand, pairs, blocks, length):
+def score(table, query, cand, blocks, length):
     slots, width = cand.shape[-3], cand.shape[-1]
     rows = BLK * length
     parts = len(query) if isinstance(query, list) else 0
@@ -239,7 +246,7 @@
         scratch += [VMEM((rows, width), jnp.bfloat16), VMEM((blocks, rows, width), jnp.bfloat16)]
     return pl.pallas_call(
         functools.partial(score_kernel, length, parts),
-        out_shape=jax.ShapeDtypeStruct((pairs, BLK, BLK), jnp.float32),
+        out_shape=jax.ShapeDtypeStruct((-(-2 * slots // PACK), 16, length), jnp.float32),
         in_specs=[pl.BlockSpec(memory_space=SMEM)]
         + [pl.BlockSpec(memory_space=VMEM)] * (max(parts, 1) + 1),
         out_specs=pl.BlockSpec(memory_space=VMEM),
@@ -249,6 +256,28 @@
             flops=2 * count * width, bytes_accessed=4 * rows * width, transcendentals=count
         ),
     )(table, *(query if parts else [query]), cand)
+
+
+def place_kernel(shares, count, where_ref, pairs_ref, *refs):
+    parts, out_ref = refs[:-1], refs[-1]
+    for d, ref in enumerate(parts):
+        side = lax.rem(where_ref[1] - d + shares, shares)
+        for i in range(count):
+            tile = ref[i // PACK]
+            if i % PACK:
+                tile = pltpu.roll(tile, tile.shape[1] - i % PACK * BLK, 1)
+            out_ref[pairs_ref[side * count + i]] = tile[:BLK, :BLK]
+
+
+def place_scores(where, pair_of, parts, pairs):
+    shares = len(parts)
+    return pl.pallas_call(
+        functools.partial(place_kernel, shares, pairs // shares),
+        out_shape=jax.ShapeDtypeStruct((pairs, BLK, BLK), jnp.float32),
+        in_specs=[pl.BlockSpec(memory_space=SMEM)] * 2 + [pl.BlockSpec(memory_space=VMEM)] * shares,
+        out_specs=pl.BlockSpec(memory_space=VMEM),
+        compiler_params=vmem_params(4),
+    )(where, pair_of, *parts)
 
 
 def local_general(states, proj_weight, lengths, query_block, cand_block, pair_valid):
@@ -268,7 +297,7 @@
 
     slots = cand_block.shape[0] // 2 // shares
     places = jnp.stack([owner, side, jnp.int32(blocks)])
-    sel, table = plan(places, cand_block, query_block, pair_valid, lengths, slots)
+    sel, table, pair_of = plan(places, cand_block, query_block, pair_valid, lengths, slots)
     sent = project(me, flat, proj_weight, shares, 1, shares - 1, jnp.bfloat16)
     received = [lax.ppermute(sent[d - 1], "narrow", shift(d)) for d in range(1, shares)]
     asked = lax.all_to_all(
@@ -287,11 +316,9 @@
     outgoing = route(asked, spread.reshape(owners * blocks, size, width), owners, shares)
     incoming = lax.all_to_all(outgoing, ("narrow", "wide"), 0, 0, tiled=True)
     cand = incoming.transpose(1, 0, 2, 3).reshape(-1, rows, width)
-    part = score(table, query, cand, cand_block.shape[0], blocks, length)
-    out = part
-    for d in range(1, shares):
-        out = out + lax.ppermute(part, "narrow", shift(d))
-    return out
+    part = score(table, query, cand, blocks, length)
+    parts = [part] + [lax.ppermute(part, "narrow", shift(d)) for d in range(1, shares)]
+    return place_scores(places, pair_of, parts, cand_block.shape[0])
 
 
 def place():
@@ -299,59 +326,57 @@
     return owner // 4, owner // 2 % 2, owner % 2, lax.axis_index("narrow")
 
 
-def split_kernel(first, over, states_ref, weight_ref, *refs):
-    *outs, rows_ref, sems = refs
+def split_kernel(over, states_ref, weight_ref, *refs):
+    flips, blocks = len(over), states_ref.shape[0]
+    outs, rows_ref, sems = refs[:flips], refs[flips], refs[flips + 1]
     _, _, core, side = place()
-    blocks, part, _ = rows_ref.shape
-    size = part // 16
-    start = pl.multiple_of((side ^ over) * part, part)
-
-    def load(b):
+    _, _, _, zs, double, _ = rows_ref.shape
+    size = double // 2
+
+    def load(i, b):
+        dn, dc = over[i]
         return pltpu.make_async_copy(
-            states_ref.at[first + b, pl.ds(start, part)], rows_ref.at[b], sems.at[b]
+            states_ref.at[b, side ^ dn, :, core ^ dc], rows_ref.at[i, b, 0], sems.at[i, b]
         )
 
-    for b in range(blocks):
-        load(b).start()
-    for b in range(blocks):
-        load(b).wait()
-        for z in range(4):
-            for flip in range(2):
-                source = pl.multiple_of((core ^ flip) * (2 * size) + z * 4 * size, 16)
+    for i in range(flips):
+        for b in range(blocks):
+            load(i, b).start()
+    for i in range(flips):
+        for b in range(blocks):
+            load(i, b).wait()
+            for z in range(zs):
                 both = jnp.dot(
-                    rows_ref[b, pl.ds(source, 2 * size)],
-                    weight_ref[...],
-                    preferred_element_type=jnp.float32,
+                    rows_ref[i, b, 0, z], weight_ref[...], preferred_element_type=jnp.float32
                 ).astype(jnp.bfloat16)
                 for x in range(2):
                     target = ((z * 2 + x) * blocks + b) * size
-                    outs[flip][target : target + size] = both[x * size : (x + 1) * size]
-
-
-def split(over, states, weight, first):
-    _, rows, width = states.shape
+                    outs[i][target : target + size] = both[x * size : (x + 1) * size]
+
+
+def split(over, states, weight):
+    blocks, _, zs, _, double, width = states.shape
     out_width = weight.shape[1]
-    part = rows // 2
-    out_rows = 8 * CHUNK * (part // 16)
-    return pl.pallas_call(
-        functools.partial(split_kernel, first, over),
-        out_shape=(jax.ShapeDtypeStruct((out_rows, out_width), jnp.bfloat16),) * 2,
+    out_rows = blocks * zs * double
+    return pl.pallas_call(
+        functools.partial(split_kernel, over),
+        out_shape=(jax.ShapeDtypeStruct((out_rows, out_width), jnp.bfloat16),) * len(over),
         in_specs=[pl.BlockSpec(memory_space=pltpu.HBM), pl.BlockSpec(memory_space=VMEM)],
-        out_specs=[pl.BlockSpec(memory_space=VMEM)] * 2,
+        out_specs=[pl.BlockSpec(memory_space=VMEM)] * len(over),
         scratch_shapes=[
-            VMEM((CHUNK, part, width), jnp.bfloat16),
-            pltpu.SemaphoreType.DMA((CHUNK,)),
+            VMEM((len(over), blocks, 1, zs, double, width), jnp.bfloat16),
+            pltpu.SemaphoreType.DMA((len(over), blocks)),
         ],
         compiler_params=vmem_params(50),
         cost_estimate=pl.CostEstimate(
-            flops=2 * CHUNK * part * width * out_width,
-            bytes_accessed=2 * CHUNK * part * width,
+            flops=2 * len(over) * out_rows * width * out_width,
+            bytes_accessed=2 * len(over) * out_rows * width,
             transcendentals=0,
         ),
     )(states, weight)
 
 
-def gather_unit_kernel(size, sel_ref, sel_near_ref, y_ref, cy_ref, own_ref, c_ref, *outs):
+def gather_unit_kernel(size, sel_ref, sel_near_ref, cy_ref, y_ref, own_ref, c_ref, *outs):
     z, x, _, _ = place()
     sends, query = outs[:8], outs[8:]
     span = CHUNK * size
@@ -374,7 +399,7 @@
         send_ref[2 * span :] = asked
 
 
-def gather_unit(sel, sel_near, y, cy, own, c, size):
+def gather_unit(sel, sel_near, cy, y, own, c, size):
     rows, width = own.shape
     send = jax.ShapeDtypeStruct((2 * CHUNK * size + 16, width), jnp.bfloat16)
     query = jax.ShapeDtypeStruct((rows, width), jnp.bfloat16)
@@ -384,7 +409,7 @@
         in_specs=[pl.BlockSpec(memory_space=SMEM)] * 2 + [pl.BlockSpec(memory_space=VMEM)] * 4,
         out_specs=[pl.BlockSpec(memory_space=VMEM)] * 10,
         compiler_params=vmem_params(12),
-    )(sel, sel_near, y, cy, own, c)
+    )(sel, sel_near, cy, y, own, c)
 
 
 def cube_route_kernel(size, slots, parts, *refs):
@@ -450,24 +475,29 @@
         return lax.ppermute(array, "wide", [(i, i ^ flip) for i in range(16)])
 
     places = jnp.stack([owner, side, jnp.int32(blocks)])
-    sel, table = plan(places, cand_block, query_block, pair_valid, lengths, slots)
+    sel, table, pair_of = plan(places, cand_block, query_block, pair_valid, lengths, slots)
     sel_near = near(sel, 1)
-    far = split(1, flat, proj_weight, 0)
-    weight, *far = lax.optimization_barrier((proj_weight, *far))
-    y, cy = near(far[0], 2), near(far[1], 3)
-    own, aside = split(0, flat, weight, 0)
+    view = flat.reshape(blocks, 2, 4, 2, 2 * size, width_part)
+    (far,) = split([(1, 0)], view, proj_weight)
+    weight, far = lax.optimization_barrier((proj_weight, far))
+    (far_aside,) = split([(1, 1)], view, weight)
+    weight, far_aside = lax.optimization_barrier((weight, far_aside))
+    y, cy = near(far, 2), near(far_aside, 3)
+    own, aside = split([(0, 0), (0, 1)], view, weight)
     c = near(aside, 1)
-    *sends, own, other = gather_unit(sel, sel_near, y, cy, own, c, size)
+    *sends, own, other = gather_unit(sel, sel_near, cy, y, own, c, size)
+    sends = dict(zip(SPREAD, sends))
     other = near(other, 1)
-    sends[4], other = lax.optimization_barrier((sends[4], other))
-    spread = [along(send, rel) if rel else send for rel, send in zip(SPREAD, sends)]
+    sends[3], other = lax.optimization_barrier((sends[3], other))
+    moved = {rel: along(sends[rel], rel) if rel else sends[rel] for rel in SPREAD}
     own_y = near(own, 2)
-    outgoing = cube_route(spread, size, slots, blocks)
+    outgoing = cube_route([moved[rel] for rel in SPREAD], size, slots, blocks)
     outgoing, own_y, other = lax.optimization_barrier((outgoing, own_y, other))
     incoming = lax.all_to_all(outgoing, ("narrow", "wide"), 0, 0, tiled=True)
     query = [own, other, own_y, near(other, 2)]
-    part = score(table, query, incoming, cand_block.shape[0], blocks, length)
-    return part + lax.ppermute(part, "narrow", [(0, 1), (1, 0)])
+    part = score(table, query, incoming, blocks, length)
+    parts = [part, lax.ppermute(part, "narrow", [(0, 1), (1, 0)])]
+    return place_scores(places, pair_of, parts, cand_block.shape[0])
 
 
 def solution(mesh):

time: 103 us -> 106 us (1.029)
  starting transfers between devices: 22.7 us -> 26.6 us
  waiting for transfers between devices: 55.6 us -> 51.8 us
  Pallas kernels: 22 us -> 25.3 us
    ppermute x7, starting transfers between devices: 10.5 us -> 14.2 us  [along(): return lax.ppermute(array, 'wide', [(i, i ^ flip) for i in range(16)])]
    pallas_call x2 -> x4, Pallas kernels: 5.26 us -> 8.58 us  [the longest x3 7.31 us: split(): pl.pallas_call(functools.partial(split_kernel, over), out_shape=(jax.Shap...]
    ppermute x7, waiting for transfers between devices: 13 us -> 10.1 us  [along(): return lax.ppermute(array, 'wide', [(i, i ^ flip) for i in range(16)])]
where the time goes in v7:
time: 106 us
  waiting for transfers between devices  51.8 us (49%)
  starting transfers between devices  26.6 us (25%)
  Pallas kernels  25.3 us (24%)
  local copies, waits for them, and re-layouts  1.53 us (1%)
    ppermute x7, waiting for transfers between devices, near(): lax.ppermute(array, ('wide', 'narrow'), [(i, i ^ flip) for i in range(32)])  30 us
    ppermute x7, starting transfers between devices, along(): return lax.ppermute(array, 'wide', [(i, i ^ flip) for i in range(16)])  14.2 us
    pallas_call x1, Pallas kernels, score(): pl.pallas_call(functools.partial(score_kernel, length, parts), out_shape=...  11.3 us
    ppermute x7, waiting for transfers between devices, along(): return lax.ppermute(array, 'wide', [(i, i ^ flip) for i in range(16)])  10.1 us
    all_to_all x1, waiting for transfers between devices, local_cube(): incoming = lax.all_to_all(outgoing, ('narrow', 'wide'), 0, 0, tiled=True)  8.97 us
    ppermute x7, starting transfers between devices, near(): lax.ppermute(array, ('wide', 'narrow'), [(i, i ^ flip) for i in range(32)])  8.03 us
    pallas_call x3, Pallas kernels, split(): pl.pallas_call(functools.partial(split_kernel, over), out_shape=(jax.Shap...  7.31 us
    all_to_all x1, starting transfers between devices, local_cube(): incoming = lax.all_to_all(outgoing, ('narrow', 'wide'), 0, 0, tiled=True)  3.34 us
  transfers between devices with their start and end apart: 16, of which 9 were waited for; matrix products, arithmetic and copies ran while one was open for 1% of the time, Pallas kernels for 7%

profile of v7, /device:TPU:0, one launch (start us, length us, event | category | flops | bytes accessed | tf_op | source)
XLA Modules:
  0.0 106.0 jit_solution(9160648035173236382)
XLA Ops:
  0.0 0.9 copy-done
  0.9 2.1 %shard_map.65 = bf16[1536,128]{1,0:T(8,128)(2,1)S(1)} custom-call(bf16[4,2,4,2,96,512]{5,4,3,2,1,0:T(8,128)(2,1)} %bitcast.3, bf16[512,128]{1,0:T(8,128)(2,1)S(1)} %copy-done), custom_call_target="tpu_custom_call" | custom-call | flops 201326592 | bytes 1572864 | tf_op jit(solution)/shard_map/pallas_call | solution.py:361
  3.0 2.1 %shard_map.66 = bf16[1536,128]{1,0:T(8,128)(2,1)S(1)} custom-call(bf16[4,2,4,2,96,512]{5,4,3,2,1,0:T(8,128)(2,1)} %bitcast.4, bf16[512,128]{1,0:T(8,128)(2,1)S(1)} %copy-done), custom_call_target="tpu_custom_call" | custom-call | flops 201326592 | bytes 1572864 | tf_op jit(solution)/shard_map/pallas_call | solution.py:361
  5.1 2.5 %collective-permute-start.1 = (bf16[1536,128]{1,0:T(8,128)(2,1)S(1)}, bf16[1536,128]{1,0:T(8,128)(2,1)S(1)}, u32[]{:S(2)}, u32[]{:S(2)}) collective-permute-start(bf16[1536,128]{1,0:T(8,128)(2,1)S(1)} %shard_map.66), channel_id=1, source_target_pairs={{0,3},{1,2},{2,1},{3,0},{4,7},{5,6},{6,5},{7,4},{8,11},{9,10},{10,... | collective-permute-start | bytes 1179656 | tf_op jit(solution)/shard_map/ppermute | solution.py:471
  7.6 0.6 collective-permute-start.2
  8.2 3.2 %shard_map.67 = (bf16[1536,128]{1,0:T(8,128)(2,1)S(1)}, bf16[1536,128]{1,0:T(8,128)(2,1)S(1)}) custom-call(bf16[4,2,4,2,96,512]{5,4,3,2,1,0:T(8,128)(2,1)} %bitcast.5, bf16[512,128]{1,0:T(8,128)(2,1)S(1)} %copy-done), custom_call_target="tpu_custom_call" | custom-call | flops 402653184 | bytes 3145728 | tf_op jit(solution)/shard_map/pallas_call | solution.py:361
  11.5 0.7 pad_add_fusion.places_ref.where_ref
  12.1 2.2 %shard_map.64 = (s32[6]{0:T(128)}, s32[192]{0:T(256)}, s32[12]{0:T(128)}) custom-call(s32[3]{0:T(128)} %pad_add_fusion.places_ref.where_ref, s32[12]{0:T(128)} %cand_ref.1, s32[12]{0:T(128)} %query_block_ref.1, s32[12]{0:T(128)} %valid_ref.1, s32[768]{0:T(1024)} %lengths_ref.1), custom_call_target="tpu_custom_call" | custom-call | tf_op jit(solution)/shard_map/pallas_call | solution.py:75
  14.8 1.0 collective-permute-done.sel_near_ref
  15.9 1.2 %collective-permute-done.1.cy_ref = bf16[1536,128]{1,0:T(8,128)(2,1)S(1)} collective-permute-done((bf16[1536,128]{1,0:T(8,128)(2,1)S(1)}, bf16[1536,128]{1,0:T(8,128)(2,1)S(1)}, u32[]{:S(2)}, u32[]{:S(2)}) %collective-permute-start.1) | collective-permute-done | bytes 393248 | tf_op jit(solution)/shard_map/ppermute | solution.py:471
  17.1 8.6 %collective-permute-done.2.y_ref = bf16[1536,128]{1,0:T(8,128)(2,1)S(1)} collective-permute-done((bf16[1536,128]{1,0:T(8,128)(2,1)S(1)}, bf16[1536,128]{1,0:T(8,128)(2,1)S(1)}, u32[]{:S(2)}, u32[]{:S(2)}) %collective-permute-start.2) | collective-permute-done | bytes 393248 | tf_op jit(solution)/shard_map/ppermute | solution.py:471
  25.7 0.6 copy-done.3
  26.3 1.1 shard_map.68
  27.4 2.4 %collective-permute-start.12 = (bf16[1536,128]{1,0:T(8,128)(2,1)S(1)}, bf16[1536,128]{1,0:T(8,128)(2,1)S(1)}, u32[]{:S(2)}, u32[]{:S(2)}) collective-permute-start(bf16[1536,128]{1,0:T(8,128)(2,1)S(1)} %get-tuple-element.38.refs_0_), channel_id=1, source_target_pairs={{0,1},{1,0},{2,3},{3,2},{4,5},{5,4},{6,7},{7,6},{8,9},{9,8},{10,11... | collective-permute-start | bytes 1179656 | tf_op jit(solution)/shard_map/ppermute | solution.py:471
  29.8 1.6 %collective-permute-start.4 = (bf16[400,128]{1,0:T(8,128)(2,1)S(1)}, bf16[400,128]{1,0:T(8,128)(2,1)S(1)}, u32[]{:S(2)}, u32[]{:S(2)}) collective-permute-start(bf16[400,128]{1,0:T(8,128)(2,1)S(1)} %get-tuple-element.40), channel_id=1, source_target_pairs={{0,8},{2,10},{4,12},{6,14},{8,0},{10,2},{12,4},{14,6},{16,24},{18,... | collective-permute-start | bytes 307208 | tf_op jit(solution)/shard_map/ppermute | solution.py:475
  31.4 2.6 %collective-permute-start.5 = (bf16[400,128]{1,0:T(8,128)(2,1)S(1)}, bf16[400,128]{1,0:T(8,128)(2,1)S(1)}, u32[]{:S(2)}, u32[]{:S(2)}) collective-permute-start(bf16[400,128]{1,0:T(8,128)(2,1)S(1)} %get-tuple-element.41), channel_id=1, source_target_pairs={{0,16},{2,18},{4,20},{6,22},{8,24},{10,26},{12,28},{14,30},{16,0},... | collective-permute-start | bytes 307208 | tf_op jit(solution)/shard_map/ppermute | solution.py:475
  34.2 2.6 %collective-permute-start.7 = (bf16[400,128]{1,0:T(8,128)(2,1)S(1)}, bf16[400,128]{1,0:T(8,128)(2,1)S(1)}, u32[]{:S(2)}, u32[]{:S(2)}) collective-permute-start(bf16[400,128]{1,0:T(8,128)(2,1)S(1)} %get-tuple-element.43), channel_id=1, source_target_pairs={{0,20},{2,22},{4,16},{6,18},{8,28},{10,30},{12,24},{14,26},{16,4},... | collective-permute-start | bytes 307208 | tf_op jit(solution)/shard_map/ppermute | solution.py:475
  36.8 3.5 %collective-permute-start.8 = (bf16[400,128]{1,0:T(8,128)(2,1)S(1)}, bf16[400,128]{1,0:T(8,128)(2,1)S(1)}, u32[]{:S(2)}, u32[]{:S(2)}) collective-permute-start(bf16[400,128]{1,0:T(8,128)(2,1)S(1)} %get-tuple-element.44), channel_id=1, source_target_pairs={{0,28},{2,30},{4,24},{6,26},{8,20},{10,22},{12,16},{14,18},{16,12}... | collective-permute-start | bytes 307208 | tf_op jit(solution)/shard_map/ppermute | solution.py:475
  40.3 6.3 %collective-permute-done.5.refs_2_ = bf16[400,128]{1,0:T(8,128)(2,1)S(1)} collective-permute-done((bf16[400,128]{1,0:T(8,128)(2,1)S(1)}, bf16[400,128]{1,0:T(8,128)(2,1)S(1)}, u32[]{:S(2)}, u32[]{:S(2)}) %collective-permute-start.5) | collective-permute-done | bytes 102432 | tf_op jit(solution)/shard_map/ppermute | solution.py:475
  46.6 1.5 %collective-permute-start.9 = (bf16[400,128]{1,0:T(8,128)(2,1)S(1)}, bf16[400,128]{1,0:T(8,128)(2,1)S(1)}, u32[]{:S(2)}, u32[]{:S(2)}) collective-permute-start(bf16[400,128]{1,0:T(8,128)(2,1)S(1)} %get-tuple-element.45), channel_id=1, source_target_pairs={{0,4},{2,6},{4,0},{6,2},{8,12},{10,14},{12,8},{14,10},{16,20},{18,... | collective-permute-start | bytes 307208 | tf_op jit(solution)/shard_map/ppermute | solution.py:475
  48.1 2.2 %collective-permute-start.11 = (bf16[400,128]{1,0:T(8,128)(2,1)S(1)}, bf16[400,128]{1,0:T(8,128)(2,1)S(1)}, u32[]{:S(2)}, u32[]{:S(2)}) collective-permute-start(bf16[400,128]{1,0:T(8,128)(2,1)S(1)} %get-tuple-element.48), channel_id=1, source_target_pairs={{0,12},{2,14},{4,8},{6,10},{8,4},{10,6},{12,0},{14,2},{16,28},{18,... | collective-permute-start | bytes 307208 | tf_op jit(solution)/shard_map/ppermute | solution.py:475
  50.3 1.7 %collective-permute-done.7.refs_4_ = bf16[400,128]{1,0:T(8,128)(2,1)S(1)} collective-permute-done((bf16[400,128]{1,0:T(8,128)(2,1)S(1)}, bf16[400,128]{1,0:T(8,128)(2,1)S(1)}, u32[]{:S(2)}, u32[]{:S(2)}) %collective-permute-start.7) | collective-permute-done | bytes 102432 | tf_op jit(solution)/shard_map/ppermute | solution.py:475
  52.0 2.1 %collective-permute-done.9.refs_6_ = bf16[400,128]{1,0:T(8,128)(2,1)S(1)} collective-permute-done((bf16[400,128]{1,0:T(8,128)(2,1)S(1)}, bf16[400,128]{1,0:T(8,128)(2,1)S(1)}, u32[]{:S(2)}, u32[]{:S(2)}) %collective-permute-start.9) | collective-permute-done | bytes 102432 | tf_op jit(solution)/shard_map/ppermute | solution.py:475
  54.1 2.2 %shard_map.69 = bf16[32,3,48,128]{3,2,1,0:T(8,128)(2,1)} custom-call(bf16[400,128]{1,0:T(8,128)(2,1)S(1)} %get-tuple-element.39.refs_0_, bf16[400,128]{1,0:T(8,128)(2,1)S(1)} %collective-permute-done.4.refs_1_, bf16[400,128]{1,0:T(8,128)(2,1)S(1)} %collective-permute-done.5.refs_2_, bf16[400,128]{1,0:T(8,128)(2,1)S(1)} %collective-permute-done.6.refs_3_, ...), custom_call_target="tpu_custom_call" | custom-call | tf_op jit(solution)/shard_map/pallas_call | solution.py:443
  56.4 3.3 %all-to-all-start = ((bf16[32,3,48,128]{3,2,1,0:T(8,128)(2,1)}), bf16[32,3,48,128]{3,2,1,0:T(8,128)(2,1)S(1)}, u32[]{:S(2)}, u32[]{:S(2)}) async-start(bf16[32,3,48,128]{3,2,1,0:T(8,128)(2,1)} %shard_map.69), calls=%async_computation | async-start | bytes 2359296 | tf_op jit(solution)/shard_map/all_to_all | solution.py:496
  59.7 1.8 %collective-permute-start.13 = (bf16[1536,128]{1,0:T(8,128)(2,1)S(1)}, bf16[1536,128]{1,0:T(8,128)(2,1)S(1)}, u32[]{:S(2)}, u32[]{:S(2)}) collective-permute-start(bf16[1536,128]{1,0:T(8,128)(2,1)S(1)} %collective-permute-done.10.refs_1_), channel_id=1, source_target_pairs={{0,1},{1,0},{2,3},{3,2},{4,5},{5,4},{6,7},{7,6},{8,9},{9,8},{10,11... | collective-permute-start | bytes 1179656 | tf_op jit(solution)/shard_map/ppermute | solution.py:471
  61.6 19.2 %collective-permute-done.13.refs_3_ = bf16[1536,128]{1,0:T(8,128)(2,1)S(1)} collective-permute-done((bf16[1536,128]{1,0:T(8,128)(2,1)S(1)}, bf16[1536,128]{1,0:T(8,128)(2,1)S(1)}, u32[]{:S(2)}, u32[]{:S(2)}) %collective-permute-start.13) | collective-permute-done | bytes 393248 | tf_op jit(solution)/shard_map/ppermute | solution.py:471
  80.8 9.0 %all-to-all-done.refs_4_ = bf16[32,3,48,128]{3,2,1,0:T(8,128)(2,1)S(1)} async-done(((bf16[32,3,48,128]{3,2,1,0:T(8,128)(2,1)}), bf16[32,3,48,128]{3,2,1,0:T(8,128)(2,1)S(1)}, u32[]{:S(2)}, u32[]{:S(2)}) %all-to-all-start) | async-done | bytes 1179680 | tf_op jit(solution)/shard_map/all_to_all | solution.py:496
  89.7 11.3 %shard_map.70.refs_0_ = f32[1,16,128]{2,1,0:T(8,128)S(1)} custom-call(s32[192]{0:T(256)S(1)} %copy-done.4, bf16[1536,128]{1,0:T(8,128)(2,1)S(1)} %get-tuple-element.38.refs_0_, bf16[1536,128]{1,0:T(8,128)(2,1)S(1)} %collective-permute-done.10.refs_1_, bf16[1536,128]{1,0:T(8,128)(2,1)S(1)} %collective-permute-done.12.refs_2_, ...), custom_call_target="tpu_custom_call" | custom-call | flops 3623878656 | bytes 786432 | tf_op jit(solution)/shard_map/pallas_call | solution.py:247
  101.1 1.0 collective-permute-start.14
  102.0 2.7 %collective-permute-done.14.refs_1_ = f32[1,16,128]{2,1,0:T(8,128)S(1)} collective-permute-done((f32[1,16,128]{2,1,0:T(8,128)S(1)}, f32[1,16,128]{2,1,0:T(8,128)S(1)}, u32[]{:S(2)}, u32[]{:S(2)}) %collective-permute-start.14) | collective-permute-done | bytes 8224 | tf_op jit(solution)/shard_map/ppermute | solution.py:499
  104.7 1.3 %shard_map.71 = f32[12,12,12]{2,1,0:T(8,128)} custom-call(s32[3]{0:T(128)S(1)} %copy-done.1, s32[12]{0:T(128)S(1)} %copy-done.2, f32[1,16,128]{2,1,0:T(8,128)S(1)} %shard_map.70.refs_0_, f32[1,16,128]{2,1,0:T(8,128)S(1)} %collective-permute-done.14.refs_1_), custom_call_target="tpu_custom_call" | custom-call | tf_op jit(solution)/shard_map/pallas_call | solution.py:274
  (19 shorter events, 1.0 us)
Async XLA Ops:
  0.0 0.9 copy-start
  5.1 12.0 %collective-permute-start.1 = (bf16[1536,128]{1,0:T(8,128)(2,1)S(1)}, bf16[1536,128]{1,0:T(8,128)(2,1)S(1)}, u32[]{:S(2)}, u32[]{:S(2)}) collective-permute-start(bf16[1536,128]{1,0:T(8,128)(2,1)S(1)} %shard_map.66), channel_id=1, source_target_pairs={{0,3},{1,2},{2,1},{3,0},{4,7},{5,6},{6,5},{7,4},{8,11},{9,10},{10,... | collective-permute-start | bytes 1179656 | tf_op jit(solution)/shard_map/ppermute | solution.py:471
  7.6 18.1 %collective-permute-start.2 = (bf16[1536,128]{1,0:T(8,128)(2,1)S(1)}, bf16[1536,128]{1,0:T(8,128)(2,1)S(1)}, u32[]{:S(2)}, u32[]{:S(2)}) collective-permute-start(bf16[1536,128]{1,0:T(8,128)(2,1)S(1)} %shard_map.65), channel_id=1, source_target_pairs={{0,1},{1,0},{2,3},{3,2},{4,5},{5,4},{6,7},{7,6},{8,9},{9,8},{10,11... | collective-permute-start | bytes 1179656 | tf_op jit(solution)/shard_map/ppermute | solution.py:471
  11.4 14.3 %collective-permute-start.3 = (bf16[1536,128]{1,0:T(8,128)(2,1)S(1)}, bf16[1536,128]{1,0:T(8,128)(2,1)S(1)}, u32[]{:S(2)}, u32[]{:S(2)}) collective-permute-start(bf16[1536,128]{1,0:T(8,128)(2,1)S(1)} %get-tuple-element.37), channel_id=1, source_target_pairs={{0,2},{1,3},{2,0},{3,1},{4,6},{5,7},{6,4},{7,5},{8,10},{9,11},{10,... | collective-permute-start | bytes 1179656 | tf_op jit(solution)/shard_map/ppermute | solution.py:471
  14.3 1.6 %collective-permute-start = (s32[6]{0:T(128)}, s32[6]{0:T(128)S(1)}, u32[]{:S(2)}, u32[]{:S(2)}) collective-permute-start(s32[6]{0:T(128)} %get-tuple-element.31.sel_ref), channel_id=1, source_target_pairs={{0,2},{1,3},{2,0},{3,1},{4,6},{5,7},{6,4},{7,5},{8,10},{9,11},{10,... | collective-permute-start | bytes 80 | tf_op jit(solution)/shard_map/ppermute | solution.py:471
  25.7 0.6 copy-start.3
  27.3 6.8 %collective-permute-start.10 = (bf16[1536,128]{1,0:T(8,128)(2,1)S(1)}, bf16[1536,128]{1,0:T(8,128)(2,1)S(1)}, u32[]{:S(2)}, u32[]{:S(2)}) collective-permute-start(bf16[1536,128]{1,0:T(8,128)(2,1)S(1)} %get-tuple-element.47), channel_id=1, source_target_pairs={{0,2},{1,3},{2,0},{3,1},{4,6},{5,7},{6,4},{7,5},{8,10},{9,11},{10,... | collective-permute-start | bytes 1179656 | tf_op jit(solution)/shard_map/ppermute | solution.py:471
  27.4 29.0 %collective-permute-start.12 = (bf16[1536,128]{1,0:T(8,128)(2,1)S(1)}, bf16[1536,128]{1,0:T(8,128)(2,1)S(1)}, u32[]{:S(2)}, u32[]{:S(2)}) collective-permute-start(bf16[1536,128]{1,0:T(8,128)(2,1)S(1)} %get-tuple-element.38.refs_0_), channel_id=1, source_target_pairs={{0,1},{1,0},{2,3},{3,2},{4,5},{5,4},{6,7},{7,6},{8,9},{9,8},{10,11... | collective-permute-start | bytes 1179656 | tf_op jit(solution)/shard_map/ppermute | solution.py:471
  29.8 7.0 %collective-permute-start.4 = (bf16[400,128]{1,0:T(8,128)(2,1)S(1)}, bf16[400,128]{1,0:T(8,128)(2,1)S(1)}, u32[]{:S(2)}, u32[]{:S(2)}) collective-permute-start(bf16[400,128]{1,0:T(8,128)(2,1)S(1)} %get-tuple-element.40), channel_id=1, source_target_pairs={{0,8},{2,10},{4,12},{6,14},{8,0},{10,2},{12,4},{14,6},{16,24},{18,... | collective-permute-start | bytes 307208 | tf_op jit(solution)/shard_map/ppermute | solution.py:475
  31.4 15.3 %collective-permute-start.5 = (bf16[400,128]{1,0:T(8,128)(2,1)S(1)}, bf16[400,128]{1,0:T(8,128)(2,1)S(1)}, u32[]{:S(2)}, u32[]{:S(2)}) collective-permute-start(bf16[400,128]{1,0:T(8,128)(2,1)S(1)} %get-tuple-element.41), channel_id=1, source_target_pairs={{0,16},{2,18},{4,20},{6,22},{8,24},{10,26},{12,28},{14,30},{16,0},... | collective-permute-start | bytes 307208 | tf_op jit(solution)/shard_map/ppermute | solution.py:475
  34.0 14.2 %collective-permute-start.6 = (bf16[400,128]{1,0:T(8,128)(2,1)S(1)}, bf16[400,128]{1,0:T(8,128)(2,1)S(1)}, u32[]{:S(2)}, u32[]{:S(2)}) collective-permute-start(bf16[400,128]{1,0:T(8,128)(2,1)S(1)} %get-tuple-element.42), channel_id=1, source_target_pairs={{0,24},{2,26},{4,28},{6,30},{8,16},{10,18},{12,20},{14,22},{16,8},... | collective-permute-start | bytes 307208 | tf_op jit(solution)/shard_map/ppermute | solution.py:475
  34.2 17.9 %collective-permute-start.7 = (bf16[400,128]{1,0:T(8,128)(2,1)S(1)}, bf16[400,128]{1,0:T(8,128)(2,1)S(1)}, u32[]{:S(2)}, u32[]{:S(2)}) collective-permute-start(bf16[400,128]{1,0:T(8,128)(2,1)S(1)} %get-tuple-element.43), channel_id=1, source_target_pairs={{0,20},{2,22},{4,16},{6,18},{8,28},{10,30},{12,24},{14,26},{16,4},... | collective-permute-start | bytes 307208 | tf_op jit(solution)/shard_map/ppermute | solution.py:475
  36.8 15.2 %collective-permute-start.8 = (bf16[400,128]{1,0:T(8,128)(2,1)S(1)}, bf16[400,128]{1,0:T(8,128)(2,1)S(1)}, u32[]{:S(2)}, u32[]{:S(2)}) collective-permute-start(bf16[400,128]{1,0:T(8,128)(2,1)S(1)} %get-tuple-element.44), channel_id=1, source_target_pairs={{0,28},{2,30},{4,24},{6,26},{8,20},{10,22},{12,16},{14,18},{16,12}... | collective-permute-start | bytes 307208 | tf_op jit(solution)/shard_map/ppermute | solution.py:475
  46.6 7.5 %collective-permute-start.9 = (bf16[400,128]{1,0:T(8,128)(2,1)S(1)}, bf16[400,128]{1,0:T(8,128)(2,1)S(1)}, u32[]{:S(2)}, u32[]{:S(2)}) collective-permute-start(bf16[400,128]{1,0:T(8,128)(2,1)S(1)} %get-tuple-element.45), channel_id=1, source_target_pairs={{0,4},{2,6},{4,0},{6,2},{8,12},{10,14},{12,8},{14,10},{16,20},{18,... | collective-permute-start | bytes 307208 | tf_op jit(solution)/shard_map/ppermute | solution.py:475
  48.1 6.0 %collective-permute-start.11 = (bf16[400,128]{1,0:T(8,128)(2,1)S(1)}, bf16[400,128]{1,0:T(8,128)(2,1)S(1)}, u32[]{:S(2)}, u32[]{:S(2)}) collective-permute-start(bf16[400,128]{1,0:T(8,128)(2,1)S(1)} %get-tuple-element.48), channel_id=1, source_target_pairs={{0,12},{2,14},{4,8},{6,10},{8,4},{10,6},{12,0},{14,2},{16,28},{18,... | collective-permute-start | bytes 307208 | tf_op jit(solution)/shard_map/ppermute | solution.py:475
  56.4 33.4 %copy-start.4 = (s32[192]{0:T(256)S(1)}, s32[192]{0:T(256)}, u32[]{:S(2)}) copy-start(s32[192]{0:T(256)} %get-tuple-element.30.table_ref) | copy-start | bytes 2308
  56.4 33.3 %all-to-all-start = ((bf16[32,3,48,128]{3,2,1,0:T(8,128)(2,1)}), bf16[32,3,48,128]{3,2,1,0:T(8,128)(2,1)S(1)}, u32[]{:S(2)}, u32[]{:S(2)}) async-start(bf16[32,3,48,128]{3,2,1,0:T(8,128)(2,1)} %shard_map.69), calls=%async_computation | async-start | bytes 2359296 | tf_op jit(solution)/shard_map/all_to_all | solution.py:496
  59.7 21.0 %collective-permute-start.13 = (bf16[1536,128]{1,0:T(8,128)(2,1)S(1)}, bf16[1536,128]{1,0:T(8,128)(2,1)S(1)}, u32[]{:S(2)}, u32[]{:S(2)}) collective-permute-start(bf16[1536,128]{1,0:T(8,128)(2,1)S(1)} %collective-permute-done.10.refs_1_), channel_id=1, source_target_pairs={{0,1},{1,0},{2,3},{3,2},{4,5},{5,4},{6,7},{7,6},{8,9},{9,8},{10,11... | collective-permute-start | bytes 1179656 | tf_op jit(solution)/shard_map/ppermute | solution.py:471
  89.7 15.0 %copy-start.1 = (s32[3]{0:T(128)S(1)}, s32[3]{0:T(128)}, u32[]{:S(2)}) copy-start(s32[3]{0:T(128)} %pad_add_fusion.places_ref.where_ref) | copy-start | bytes 40
  89.7 15.0 %copy-start.2 = (s32[12]{0:T(128)S(1)}, s32[12]{0:T(128)}, u32[]{:S(2)}) copy-start(s32[12]{0:T(128)} %get-tuple-element.29.pairs_ref) | copy-start | bytes 148
  101.1 3.7 %collective-permute-start.14 = (f32[1,16,128]{2,1,0:T(8,128)S(1)}, f32[1,16,128]{2,1,0:T(8,128)S(1)}, u32[]{:S(2)}, u32[]{:S(2)}) collective-permute-start(f32[1,16,128]{2,1,0:T(8,128)S(1)} %shard_map.70.refs_0_), channel_id=1, source_target_pairs={{0,1},{1,0},{2,3},{3,2},{4,5},{5,4},{6,7},{7,6},{8,9},{9,8},{10,11... | collective-permute-start | bytes 24584 | tf_op jit(solution)/shard_map/ppermute | solution.py:499

commit v8 on v6

--- a/solution.py
+++ b/solution.py
@@ -11,10 +11,11 @@
 BLK = 12
 SHARPNESS = 20.0
 EXP2_SCALE = SHARPNESS * math.log2(math.e)
-COLS = 256
+COLS = 512
 CHUNK = 4
 LINE = 32
-SPREAD = (0, 1, 2, 4, 3, 6, 5, 7)
+PACK = 6
+FAR = (4, 6, 5, 7)
 SMEM = pltpu.SMEM
 VMEM = pltpu.VMEM
 
@@ -23,7 +24,7 @@
     return pltpu.CompilerParams(vmem_limit_bytes=mib * 2**20)
 
 
-def plan_kernel(pairs, slots, places_ref, cand_ref, query_block_ref, valid_ref, lengths_ref, sel_ref, table_ref, *scratch):
+def plan_kernel(pairs, slots, places_ref, cand_ref, query_block_ref, valid_ref, lengths_ref, sel_ref, table_ref, pairs_ref, *scratch):
     first_ref, second_ref, slot_ref = scratch
     owner, side, blocks = places_ref[0], places_ref[1], places_ref[2]
 
@@ -51,7 +52,6 @@
         slot = side * slots + k
         pair = jnp.where(i - 2 * k == 0, first_ref[slot], second_ref[slot])
         query = query_block_ref[pair]
-        table_ref[i * LINE] = pair
         table_ref[i * LINE + 1] = query
         table_ref[i * LINE + 2] = valid_ref[pair]
         for a in range(BLK):
@@ -61,15 +61,22 @@
 
     lax.fori_loop(0, 2 * slots, line, 0)
 
+    def both(slot, carry):
+        pairs_ref[2 * slot] = first_ref[slot]
+        pairs_ref[2 * slot + 1] = second_ref[slot]
+        return carry
+
+    lax.fori_loop(0, pairs // 2, both, 0)
+
 
 def plan(places, cand_block, query_block, valid, lengths, slots):
     pairs = cand_block.shape[0]
-    shapes = (pairs // 2, 2 * slots * LINE)
+    shapes = (pairs // 2, 2 * slots * LINE, pairs)
     return pl.pallas_call(
         functools.partial(plan_kernel, pairs, slots),
         out_shape=[jax.ShapeDtypeStruct((n,), jnp.int32) for n in shapes],
         in_specs=[pl.BlockSpec(memory_space=SMEM)] * 5,
-        out_specs=[pl.BlockSpec(memory_space=SMEM)] * 2,
+        out_specs=[pl.BlockSpec(memory_space=SMEM)] * 3,
         scratch_shapes=[SMEM((pairs,), jnp.int32)] * 3,
     )(places, cand_block, query_block, valid, lengths)
 
@@ -189,57 +196,61 @@
         query_ref, cand_ref, out_ref, totals_ref = refs
     rows = query_ref.shape[1]
     slots = cand_ref.shape[-3]
-    out_ref[...] = jnp.zeros_like(out_ref)
     totals_ref[...] = jnp.ones_like(totals_ref)
     upper = lax.broadcasted_iota(jnp.int32, (length // 2, COLS), 0) + length // 2
     lane = lax.broadcasted_iota(jnp.int32, (16, length), 1)
 
-    def pair_step(i, carry):
-        k = i // 2
-        line = i * LINE
-        pair, query = table_ref[line], table_ref[line + 1]
+    def slot_step(k, carry):
         if parts:
             pieces, _, size, _ = cand_ref.shape
             for piece in range(pieces):
                 begin = (piece // 4 * 4 + piece % 2 * 2 + piece // 2 % 2) * size
                 block_ref[begin : begin + size] = cand_ref[piece, k]
-        for start in range(0, rows, COLS):
-            sim = lax.dot_general(
-                block_ref[...] if parts else cand_ref[k],
-                query_ref[query, start : start + COLS],
-                (((1,), (1,)), ((), ())),
-                preferred_element_type=jnp.float32,
-            )
-            for b in range(BLK):
-                live = table_ref[line + 3 + b]
-                low = jnp.exp2(sim[b * length : b * length + length // 2] * EXP2_SCALE)
-                high = jnp.exp2(sim[b * length + length // 2 : (b + 1) * length] * EXP2_SCALE)
-                both = low + jnp.where(upper < live, high, 0.0)
-                totals_ref[b : b + 1, start : start + COLS] = jnp.sum(both, axis=0, keepdims=True)
+        for i in range(2):
+            line = (2 * k + i) * LINE
+            query = table_ref[line + 1]
+            for start in range(0, rows, COLS):
+                sim = lax.dot_general(
+                    block_ref[...] if parts else cand_ref[k],
+                    query_ref[query, start : start + COLS],
+                    (((1,), (1,)), ((), ())),
+                    preferred_element_type=jnp.float32,
+                )
+                for b in range(BLK):
+                    live = table_ref[line + 3 + b]
+                    low = jnp.exp2(sim[b * length : b * length + length // 2] * EXP2_SCALE)
+                    high = jnp.exp2(sim[b * length + length // 2 : (b + 1) * length] * EXP2_SCALE)
+                    both = low + jnp.where(upper < live, high, 0.0)
+                    totals_ref[2 * k + i, b : b + 1, start : start + COLS] = jnp.sum(
+                        both, axis=0, keepdims=True
+                    )
+        return carry
+
+    lax.fori_loop(0, slots, slot_step, 0)
+    for tile in range(out_ref.shape[0]):
         score = jnp.zeros((16, length), jnp.float32)
-        for a in range(BLK):
-            live = table_ref[line + 3 + BLK + a]
-            logs = jnp.log(totals_ref[:, a * length : (a + 1) * length])
-            summed = jnp.sum(jnp.where(lane < live, logs, 0.0), axis=1, keepdims=True)
-            score = jnp.where(lane == a, summed, score)
-        keep = table_ref[line + 2].astype(jnp.float32) / (SHARPNESS * length)
-        out_ref[pair] = score[:BLK, :BLK] * keep
-        return carry
-
-    lax.fori_loop(0, 2 * slots, pair_step, 0)
-
-
-def score(table, query, cand, pairs, blocks, length):
+        for i in range(tile * PACK, min((tile + 1) * PACK, 2 * slots)):
+            line = i * LINE
+            keep = table_ref[line + 2].astype(jnp.float32) / (SHARPNESS * length)
+            for a in range(BLK):
+                live = table_ref[line + 3 + BLK + a]
+                logs = jnp.log(totals_ref[i, :, a * length : (a + 1) * length])
+                summed = jnp.sum(jnp.where(lane < live, logs, 0.0), axis=1, keepdims=True)
+                score = jnp.where(lane == i % PACK * BLK + a, summed * keep, score)
+        out_ref[tile] = score
+
+
+def score(table, query, cand, blocks, length):
     slots, width = cand.shape[-3], cand.shape[-1]
     rows = BLK * length
     parts = len(query) if isinstance(query, list) else 0
     count = 2 * slots * rows * rows
-    scratch = [VMEM((16, rows), jnp.float32)]
+    scratch = [VMEM((2 * slots, 16, rows), jnp.float32)]
     if parts:
         scratch += [VMEM((rows, width), jnp.bfloat16), VMEM((blocks, rows, width), jnp.bfloat16)]
     return pl.pallas_call(
         functools.partial(score_kernel, length, parts),
-        out_shape=jax.ShapeDtypeStruct((pairs, BLK, BLK), jnp.float32),
+        out_shape=jax.ShapeDtypeStruct((-(-2 * slots // PACK), 16, length), jnp.float32),
         in_specs=[pl.BlockSpec(memory_space=SMEM)]
         + [pl.BlockSpec(memory_space=VMEM)] * (max(parts, 1) + 1),
         out_specs=pl.BlockSpec(memory_space=VMEM),
@@ -249,6 +260,28 @@
             flops=2 * count * width, bytes_accessed=4 * rows * width, transcendentals=count
         ),
     )(table, *(query if parts else [query]), cand)
+
+
+def place_kernel(shares, count, where_ref, pairs_ref, *refs):
+    parts, out_ref = refs[:-1], refs[-1]
+    for d, ref in enumerate(parts):
+        side = lax.rem(where_ref[1] - d + shares, shares)
+        for i in range(count):
+            tile = ref[i // PACK]
+            if i % PACK:
+                tile = pltpu.roll(tile, tile.shape[1] - i % PACK * BLK, 1)
+            out_ref[pairs_ref[side * count + i]] = tile[:BLK, :BLK]
+
+
+def place_scores(where, pair_of, parts, pairs):
+    shares = len(parts)
+    return pl.pallas_call(
+        functools.partial(place_kernel, shares, pairs // shares),
+        out_shape=jax.ShapeDtypeStruct((pairs, BLK, BLK), jnp.float32),
+        in_specs=[pl.BlockSpec(memory_space=SMEM)] * 2 + [pl.BlockSpec(memory_space=VMEM)] * shares,
+        out_specs=pl.BlockSpec(memory_space=VMEM),
+        compiler_params=vmem_params(4),
+    )(where, pair_of, *parts)
 
 
 def local_general(states, proj_weight, lengths, query_block, cand_block, pair_valid):
@@ -268,7 +301,7 @@
 
     slots = cand_block.shape[0] // 2 // shares
     places = jnp.stack([owner, side, jnp.int32(blocks)])
-    sel, table = plan(places, cand_block, query_block, pair_valid, lengths, slots)
+    sel, table, pair_of = plan(places, cand_block, query_block, pair_valid, lengths, slots)
     sent = project(me, flat, proj_weight, shares, 1, shares - 1, jnp.bfloat16)
     received = [lax.ppermute(sent[d - 1], "narrow", shift(d)) for d in range(1, shares)]
     asked = lax.all_to_all(
@@ -287,11 +320,9 @@
     outgoing = route(asked, spread.reshape(owners * blocks, size, width), owners, shares)
     incoming = lax.all_to_all(outgoing, ("narrow", "wide"), 0, 0, tiled=True)
     cand = incoming.transpose(1, 0, 2, 3).reshape(-1, rows, width)
-    part = score(table, query, cand, cand_block.shape[0], blocks, length)
-    out = part
-    for d in range(1, shares):
-        out = out + lax.ppermute(part, "narrow", shift(d))
-    return out
+    part = score(table, query, cand, blocks, length)
+    parts = [part] + [lax.ppermute(part, "narrow", shift(d)) for d in range(1, shares)]
+    return place_scores(places, pair_of, parts, cand_block.shape[0])
 
 
 def place():
@@ -353,7 +384,7 @@
 
 def gather_unit_kernel(size, sel_ref, sel_near_ref, y_ref, cy_ref, own_ref, c_ref, *outs):
     z, x, _, _ = place()
-    sends, query = outs[:8], outs[8:]
+    sends, query = outs[:5], outs[5:]
     span = CHUNK * size
     shape = (16, own_ref.shape[1])
     row, lane = (lax.broadcasted_iota(jnp.int32, shape, axis) for axis in range(2))
@@ -362,46 +393,59 @@
         for k in range(ids_ref.shape[0]):
             asked = jnp.where((row == flip) & (lane == k), ids_ref[k], asked)
     asked = asked.astype(jnp.float32).astype(jnp.bfloat16)
-    for rel, send_ref in zip(SPREAD, sends):
+    near_ref, far_refs = sends[0], sends[1:]
+    rows = 2 * span + 16
+    here = z % 2 * 2 + x
+    for rel in (*FAR, 0, 1, 2, 3):
+        if rel < 4:
+            send_ref, begin = near_ref, (here ^ rel) * rows
+        else:
+            send_ref, begin = far_refs[FAR.index(rel)], 0
         source = pl.multiple_of(((z ^ (rel // 2)) * 2 + (x ^ (rel % 2))) * span, 16)
         for flip, (one_ref, two_ref) in enumerate(((own_ref, y_ref), (c_ref, cy_ref))):
             total = one_ref[pl.ds(source, span)].astype(jnp.float32)
             total = total + two_ref[pl.ds(source, span)].astype(jnp.float32)
             norm = jnp.sum(total * total, axis=-1, keepdims=True)
             unit = (total * lax.rsqrt(norm + 1e-06)).astype(jnp.bfloat16)
-            send_ref[flip * span : (flip + 1) * span] = unit
+            send_ref[pl.ds(pl.multiple_of(begin + flip * span, 16), span)] = unit
             query[flip][pl.ds(source, span)] = unit
-        send_ref[2 * span :] = asked
+        send_ref[pl.ds(pl.multiple_of(begin + 2 * span, 16), 16)] = asked
 
 
 def gather_unit(sel, sel_near, y, cy, own, c, size):
     rows, width = own.shape
-    send = jax.ShapeDtypeStruct((2 * CHUNK * size + 16, width), jnp.bfloat16)
+    piece = 2 * CHUNK * size + 16
+    near, far = (jax.ShapeDtypeStruct((n * piece, width), jnp.bfloat16) for n in (4, 1))
     query = jax.ShapeDtypeStruct((rows, width), jnp.bfloat16)
     return pl.pallas_call(
         functools.partial(gather_unit_kernel, size),
-        out_shape=(send,) * 8 + (query,) * 2,
+        out_shape=(near,) + (far,) * 4 + (query,) * 2,
         in_specs=[pl.BlockSpec(memory_space=SMEM)] * 2 + [pl.BlockSpec(memory_space=VMEM)] * 4,
-        out_specs=[pl.BlockSpec(memory_space=VMEM)] * 10,
+        out_specs=[pl.BlockSpec(memory_space=VMEM)] * 7,
         compiler_params=vmem_params(12),
     )(sel, sel_near, y, cy, own, c)
 
 
-def cube_route_kernel(size, slots, parts, *refs):
-    spread, out_ref, pieces_ref, rows_ref, asked_ref, sem = refs[:parts], *refs[parts:]
+def cube_route_kernel(size, slots, near_ref, *refs):
+    far, out_ref, pieces_ref, rows_ref, asked_ref, sem = refs[:4], *refs[4:]
     z, x, core, _ = place()
     blocks = pieces_ref.shape[0] // 16
     span = CHUNK * size
-    for rel, ref in zip(SPREAD, spread):
+    rows = 2 * span + 16
+    parts = [(near_ref, i * rows, z // 2 * 4 + i) for i in range(4)]
+    parts += [(ref, 0, (z ^ (rel // 2)) * 2 + (x ^ (rel % 2))) for ref, rel in zip(far, FAR)]
+    for ref, begin, chip in parts:
+        ids = ref[begin + 2 * span : begin + rows].astype(jnp.float32)
         for flip in range(2):
-            owner = (z ^ (rel // 2)) * 4 + (x ^ (rel % 2)) * 2 + (core ^ flip)
-            for b in range(CHUNK):
-                begin = flip * span + b * size
-                pieces_ref[owner * blocks + b] = ref[begin : begin + size]
-            row = ref[2 * span :].astype(jnp.float32)[flip : flip + 1]
-            rows_ref[pl.ds(owner, 1)] = row.astype(jnp.int32)
+            rows_ref[pl.ds(chip * 2 + (core ^ flip), 1)] = ids[flip : flip + 1].astype(jnp.int32)
     copy = pltpu.make_async_copy(rows_ref, asked_ref, sem)
     copy.start()
+    for ref, begin, chip in parts:
+        for flip in range(2):
+            owner = chip * 2 + (core ^ flip)
+            for b in range(blocks):
+                row = begin + flip * span + b * size
+                pieces_ref[owner * blocks + b] = ref[row : row + size]
     copy.wait()
 
     def step(d, carry):
@@ -416,7 +460,7 @@
 def cube_route(spread, size, slots, blocks):
     width = spread[0].shape[1]
     return pl.pallas_call(
-        functools.partial(cube_route_kernel, size, slots, len(spread)),
+        functools.partial(cube_route_kernel, size, slots),
         out_shape=jax.ShapeDtypeStruct((32, slots, size, width), jnp.bfloat16),
         in_specs=[pl.BlockSpec(memory_space=VMEM)] * len(spread),
         out_specs=pl.BlockSpec(memory_space=VMEM),
@@ -450,24 +494,26 @@
         return lax.ppermute(array, "wide", [(i, i ^ flip) for i in range(16)])
 
     places = jnp.stack([owner, side, jnp.int32(blocks)])
-    sel, table = plan(places, cand_block, query_block, pair_valid, lengths, slots)
+    sel, table, pair_of = plan(places, cand_block, query_block, pair_valid, lengths, slots)
     sel_near = near(sel, 1)
     far = split(1, flat, proj_weight, 0)
     weight, *far = lax.optimization_barrier((proj_weight, *far))
     y, cy = near(far[0], 2), near(far[1], 3)
     own, aside = split(0, flat, weight, 0)
     c = near(aside, 1)
-    *sends, own, other = gather_unit(sel, sel_near, y, cy, own, c, size)
+    close, *sends, own, other = gather_unit(sel, sel_near, y, cy, own, c, size)
+    own_y = near(own, 2)
+    moved = [along(send, rel) for rel, send in zip(FAR, sends)]
+    groups = [[z * 4 + x * 2 + core for z in (high, high + 1) for x in (0, 1)] for high in (0, 2) for core in (0, 1)]
+    close = lax.all_to_all(close, "wide", 0, 0, tiled=True, axis_index_groups=groups)
+    outgoing = cube_route([close, *moved], size, slots, blocks)
+    outgoing, other, own_y = lax.optimization_barrier((outgoing, other, own_y))
+    incoming = lax.all_to_all(outgoing, ("narrow", "wide"), 0, 0, tiled=True)
     other = near(other, 1)
-    sends[4], other = lax.optimization_barrier((sends[4], other))
-    spread = [along(send, rel) if rel else send for rel, send in zip(SPREAD, sends)]
-    own_y = near(own, 2)
-    outgoing = cube_route(spread, size, slots, blocks)
-    outgoing, own_y, other = lax.optimization_barrier((outgoing, own_y, other))
-    incoming = lax.all_to_all(outgoing, ("narrow", "wide"), 0, 0, tiled=True)
     query = [own, other, own_y, near(other, 2)]
-    part = score(table, query, incoming, cand_block.shape[0], blocks, length)
-    return part + lax.ppermute(part, "narrow", [(0, 1), (1, 0)])
+    part = score(table, query, incoming, blocks, length)
+    parts = [part, lax.ppermute(part, "narrow", [(0, 1), (1, 0)])]
+    return place_scores(places, pair_of, parts, cand_block.shape[0])
 
 
 def solution(mesh):

time: 103 us -> 104 us (level)
    all_to_all x0 -> x1, starting transfers between devices: none -> 3.77 us  [local_cube(): lax.all_to_all(close, 'wide', 0, 0, tiled=True, axis_index_groups=groups)]
    ppermute x7 -> x4, starting transfers between devices: 10.5 us -> 7.88 us  [along(): return lax.ppermute(array, 'wide', [(i, i ^ flip) for i in range(16)])]
    pallas_call x2 -> x3, Pallas kernels: 3.27 us -> 5.27 us  [the longest x1 2.19 us: cube_route(): pl.pallas_call(functools.partial(cube_route_kernel, size, slots), out_sha...]
    pallas_call x1, Pallas kernels: 11.3 us -> 10.2 us  [score(): pl.pallas_call(functools.partial(score_kernel, length, parts), out_shape=...]
    ppermute x7 -> x4, waiting for transfers between devices: 13 us -> 13.8 us  [along(): return lax.ppermute(array, 'wide', [(i, i ^ flip) for i in range(16)])]
  transfers between devices with their start and end apart: 16 -> 14, of which waited for: 9 -> 9; matrix products, arithmetic and copies ran while one was open for 1% -> 1% of each run, Pallas kernels for 7% -> 7%
where the time goes in v8:
time: 104 us
  waiting for transfers between devices  55.1 us (53%)
  starting transfers between devices  23.7 us (23%)
  Pallas kernels  22.9 us (22%)
  local copies, waits for them, and re-layouts  1.53 us (1%)
    ppermute x7, waiting for transfers between devices, near(): lax.ppermute(array, ('wide', 'narrow'), [(i, i ^ flip) for i in range(32)])  29.6 us
    ppermute x4, waiting for transfers between devices, along(): return lax.ppermute(array, 'wide', [(i, i ^ flip) for i in range(16)])  13.8 us
    pallas_call x1, Pallas kernels, score(): pl.pallas_call(functools.partial(score_kernel, length, parts), out_shape=...  10.2 us
    all_to_all x1, waiting for transfers between devices, local_cube(): incoming = lax.all_to_all(outgoing, ('narrow', 'wide'), 0, 0, tiled=True)  8.97 us
    ppermute x4, starting transfers between devices, along(): return lax.ppermute(array, 'wide', [(i, i ^ flip) for i in range(16)])  7.88 us
    ppermute x7, starting transfers between devices, near(): lax.ppermute(array, ('wide', 'narrow'), [(i, i ^ flip) for i in range(32)])  7.08 us
    pallas_call x2, Pallas kernels, split(): pl.pallas_call(functools.partial(split_kernel, first, over), out_shape=(j...  5.26 us
    all_to_all x1, starting transfers between devices, local_cube(): incoming = lax.all_to_all(outgoing, ('narrow', 'wide'), 0, 0, tiled=True)  3.94 us
  transfers between devices with their start and end apart: 14, of which 9 were waited for; matrix products, arithmetic and copies ran while one was open for 1% of the time, Pallas kernels for 7%

profile of v8, /device:TPU:0, one launch (start us, length us, event | category | flops | bytes accessed | tf_op | source)
XLA Modules:
  0.0 104.0 jit_solution(13626225258060334961)
XLA Ops:
  0.0 0.9 copy-done
  0.9 2.6 %shard_map.65 = (bf16[1536,128]{1,0:T(8,128)(2,1)S(1)}, bf16[1536,128]{1,0:T(8,128)(2,1)S(1)}) custom-call(bf16[4,1536,512]{2,1,0:T(8,128)(2,1)} %bitcast.6, bf16[512,128]{1,0:T(8,128)(2,1)S(1)} %copy-done), custom_call_target="tpu_custom_call" | custom-call | flops 402653184 | bytes 3145728 | tf_op jit(solution)/shard_map/pallas_call | solution.py:367
  3.5 3.0 %collective-permute-start.1 = (bf16[1536,128]{1,0:T(8,128)(2,1)S(1)}, bf16[1536,128]{1,0:T(8,128)(2,1)S(1)}, u32[]{:S(2)}, u32[]{:S(2)}) collective-permute-start(bf16[1536,128]{1,0:T(8,128)(2,1)S(1)} %get-tuple-element.30), channel_id=1, source_target_pairs={{0,1},{1,0},{2,3},{3,2},{4,5},{5,4},{6,7},{7,6},{8,9},{9,8},{10,11... | collective-permute-start | bytes 1179656 | tf_op jit(solution)/shard_map/ppermute | solution.py:490
  6.6 2.6 %shard_map.66 = (bf16[1536,128]{1,0:T(8,128)(2,1)S(1)}, bf16[1536,128]{1,0:T(8,128)(2,1)S(1)}) custom-call(bf16[4,1536,512]{2,1,0:T(8,128)(2,1)} %bitcast.7, bf16[512,128]{1,0:T(8,128)(2,1)S(1)} %copy-done), custom_call_target="tpu_custom_call" | custom-call | flops 402653184 | bytes 3145728 | tf_op jit(solution)/shard_map/pallas_call | solution.py:367
  9.2 0.3 collective-permute-start.3
  9.5 0.7 pad_add_fusion.places_ref.where_ref
  10.1 2.2 %shard_map.64 = (s32[6]{0:T(128)}, s32[192]{0:T(256)}, s32[12]{0:T(128)}) custom-call(s32[3]{0:T(128)} %pad_add_fusion.places_ref.where_ref, s32[12]{0:T(128)} %cand_ref.1, s32[12]{0:T(128)} %query_block_ref.1, s32[12]{0:T(128)} %valid_ref.1, s32[768]{0:T(1024)} %lengths_ref.1), custom_call_target="tpu_custom_call" | custom-call | tf_op jit(solution)/shard_map/pallas_call | solution.py:75
  12.3 0.4 collective-permute-start
  12.7 1.0 collective-permute-done.sel_near_ref
  13.7 2.8 %collective-permute-done.1.y_ref = bf16[1536,128]{1,0:T(8,128)(2,1)S(1)} collective-permute-done((bf16[1536,128]{1,0:T(8,128)(2,1)S(1)}, bf16[1536,128]{1,0:T(8,128)(2,1)S(1)}, u32[]{:S(2)}, u32[]{:S(2)}) %collective-permute-start.1) | collective-permute-done | bytes 393248 | tf_op jit(solution)/shard_map/ppermute | solution.py:490
  16.5 6.9 %collective-permute-done.2.cy_ref = bf16[1536,128]{1,0:T(8,128)(2,1)S(1)} collective-permute-done((bf16[1536,128]{1,0:T(8,128)(2,1)S(1)}, bf16[1536,128]{1,0:T(8,128)(2,1)S(1)}, u32[]{:S(2)}, u32[]{:S(2)}) %collective-permute-start.2) | collective-permute-done | bytes 393248 | tf_op jit(solution)/shard_map/ppermute | solution.py:490
  23.4 0.6 copy-done.3
  24.0 1.8 %shard_map.67 = (bf16[1600,128]{1,0:T(8,128)(2,1)}, bf16[400,128]{1,0:T(8,128)(2,1)S(1)}, bf16[400,128]{1,0:T(8,128)(2,1)S(1)}, bf16[400,128]{1,0:T(8,128)(2,1)S...) custom-call(s32[6]{0:T(128)S(1)} %copy-done.3, ...), custom_call_target="tpu_custom_call" | custom-call | tf_op jit(solution)/shard_map/pallas_call | solution.py:420
  25.8 3.8 %all-to-all-start = ((bf16[4,400,128]{2,1,0:T(8,128)(2,1)}), bf16[4,400,128]{2,1,0:T(8,128)(2,1)S(1)}, u32[]{:S(2)}, u32[]{:S(2)}) async-start(bf16[4,400,128]{2,1,0:T(8,128)(2,1)} %bitcast.3), calls=%async_computation | async-start | bytes 819200 | tf_op jit(solution)/shard_map/all_to_all | solution.py:508
  29.6 1.3 %collective-permute-start.8 = (bf16[1536,128]{1,0:T(8,128)(2,1)S(1)}, bf16[1536,128]{1,0:T(8,128)(2,1)S(1)}, u32[]{:S(2)}, u32[]{:S(2)}) collective-permute-start(bf16[1536,128]{1,0:T(8,128)(2,1)S(1)} %get-tuple-element.35.refs_0_), channel_id=1, source_target_pairs={{0,1},{1,0},{2,3},{3,2},{4,5},{5,4},{6,7},{7,6},{8,9},{9,8},{10,11... | collective-permute-start | bytes 1179656 | tf_op jit(solution)/shard_map/ppermute | solution.py:490
  30.9 2.6 %collective-permute-start.4 = (bf16[400,128]{1,0:T(8,128)(2,1)S(1)}, bf16[400,128]{1,0:T(8,128)(2,1)S(1)}, u32[]{:S(2)}, u32[]{:S(2)}) collective-permute-start(bf16[400,128]{1,0:T(8,128)(2,1)S(1)} %get-tuple-element.37), channel_id=1, source_target_pairs={{0,16},{2,18},{4,20},{6,22},{8,24},{10,26},{12,28},{14,30},{16,0},... | collective-permute-start | bytes 307208 | tf_op jit(solution)/shard_map/ppermute | solution.py:494
  33.5 1.8 %collective-permute-start.5 = (bf16[400,128]{1,0:T(8,128)(2,1)S(1)}, bf16[400,128]{1,0:T(8,128)(2,1)S(1)}, u32[]{:S(2)}, u32[]{:S(2)}) collective-permute-start(bf16[400,128]{1,0:T(8,128)(2,1)S(1)} %get-tuple-element.38), channel_id=1, source_target_pairs={{0,24},{2,26},{4,28},{6,30},{8,16},{10,18},{12,20},{14,22},{16,8},... | collective-permute-start | bytes 307208 | tf_op jit(solution)/shard_map/ppermute | solution.py:494
  35.3 2.6 %collective-permute-start.6 = (bf16[400,128]{1,0:T(8,128)(2,1)S(1)}, bf16[400,128]{1,0:T(8,128)(2,1)S(1)}, u32[]{:S(2)}, u32[]{:S(2)}) collective-permute-start(bf16[400,128]{1,0:T(8,128)(2,1)S(1)} %get-tuple-element.39), channel_id=1, source_target_pairs={{0,20},{2,22},{4,16},{6,18},{8,28},{10,30},{12,24},{14,26},{16,4},... | collective-permute-start | bytes 307208 | tf_op jit(solution)/shard_map/ppermute | solution.py:494
  37.9 0.9 collective-permute-start.7
  38.8 5.4 %collective-permute-done.5.refs_1_ = bf16[400,128]{1,0:T(8,128)(2,1)S(1)} collective-permute-done((bf16[400,128]{1,0:T(8,128)(2,1)S(1)}, bf16[400,128]{1,0:T(8,128)(2,1)S(1)}, u32[]{:S(2)}, u32[]{:S(2)}) %collective-permute-start.5) | collective-permute-done | bytes 102432 | tf_op jit(solution)/shard_map/ppermute | solution.py:494
  44.2 8.4 %collective-permute-done.6.refs_2_ = bf16[400,128]{1,0:T(8,128)(2,1)S(1)} collective-permute-done((bf16[400,128]{1,0:T(8,128)(2,1)S(1)}, bf16[400,128]{1,0:T(8,128)(2,1)S(1)}, u32[]{:S(2)}, u32[]{:S(2)}) %collective-permute-start.6) | collective-permute-done | bytes 102432 | tf_op jit(solution)/shard_map/ppermute | solution.py:494
  52.6 2.2 %shard_map.68 = bf16[32,3,48,128]{3,2,1,0:T(8,128)(2,1)} custom-call(bf16[1600,128]{1,0:T(8,128)(2,1)S(1)} %bitcast.5, bf16[400,128]{1,0:T(8,128)(2,1)S(1)} %collective-permute-done.4.refs_0_, bf16[400,128]{1,0:T(8,128)(2,1)S(1)} %collective-permute-done.5.refs_1_, bf16[400,128]{1,0:T(8,128)(2,1)S(1)} %collective-permute-done.6.refs_2_, ...), custom_call_target="tpu_custom_call" | custom-call | tf_op jit(solution)/shard_map/pallas_call | solution.py:462
  54.8 3.9 %all-to-all-start.1 = ((bf16[32,3,48,128]{3,2,1,0:T(8,128)(2,1)}), bf16[32,3,48,128]{3,2,1,0:T(8,128)(2,1)S(1)}, u32[]{:S(2)}, u32[]{:S(2)}) async-start(bf16[32,3,48,128]{3,2,1,0:T(8,128)(2,1)} %shard_map.68), calls=%async_computation.1 | async-start | bytes 2359296 | tf_op jit(solution)/shard_map/all_to_all | solution.py:511
  58.8 0.3 collective-permute-start.9
  59.1 1.5 %collective-permute-done.9.refs_1_ = bf16[1536,128]{1,0:T(8,128)(2,1)S(1)} collective-permute-done((bf16[1536,128]{1,0:T(8,128)(2,1)S(1)}, bf16[1536,128]{1,0:T(8,128)(2,1)S(1)}, u32[]{:S(2)}, u32[]{:S(2)}) %collective-permute-start.9) | collective-permute-done | bytes 393248 | tf_op jit(solution)/shard_map/ppermute | solution.py:490
  60.5 1.8 %collective-permute-start.10 = (bf16[1536,128]{1,0:T(8,128)(2,1)S(1)}, bf16[1536,128]{1,0:T(8,128)(2,1)S(1)}, u32[]{:S(2)}, u32[]{:S(2)}) collective-permute-start(bf16[1536,128]{1,0:T(8,128)(2,1)S(1)} %collective-permute-done.9.refs_1_), channel_id=1, source_target_pairs={{0,1},{1,0},{2,3},{3,2},{4,5},{5,4},{6,7},{7,6},{8,9},{9,8},{10,11... | collective-permute-start | bytes 1179656 | tf_op jit(solution)/shard_map/ppermute | solution.py:490
  62.3 17.5 %collective-permute-done.10.refs_3_ = bf16[1536,128]{1,0:T(8,128)(2,1)S(1)} collective-permute-done((bf16[1536,128]{1,0:T(8,128)(2,1)S(1)}, bf16[1536,128]{1,0:T(8,128)(2,1)S(1)}, u32[]{:S(2)}, u32[]{:S(2)}) %collective-permute-start.10) | collective-permute-done | bytes 393248 | tf_op jit(solution)/shard_map/ppermute | solution.py:490
  79.8 9.0 %all-to-all-done.1.refs_4_ = bf16[32,3,48,128]{3,2,1,0:T(8,128)(2,1)S(1)} async-done(((bf16[32,3,48,128]{3,2,1,0:T(8,128)(2,1)}), bf16[32,3,48,128]{3,2,1,0:T(8,128)(2,1)S(1)}, u32[]{:S(2)}, u32[]{:S(2)}) %all-to-all-start.1) | async-done | bytes 1179680 | tf_op jit(solution)/shard_map/all_to_all | solution.py:511
  88.8 10.2 %shard_map.69.refs_0_ = f32[1,16,128]{2,1,0:T(8,128)S(1)} custom-call(s32[192]{0:T(256)S(1)} %copy-done.4, bf16[1536,128]{1,0:T(8,128)(2,1)S(1)} %get-tuple-element.35.refs_0_, bf16[1536,128]{1,0:T(8,128)(2,1)S(1)} %collective-permute-done.9.refs_1_, bf16[1536,128]{1,0:T(8,128)(2,1)S(1)} %collective-permute-done.8.refs_2_, ...), custom_call_target="tpu_custom_call" | custom-call | flops 3623878656 | bytes 786432 | tf_op jit(solution)/shard_map/pallas_call | solution.py:251
  99.0 1.0 collective-permute-start.11
  100.0 2.7 %collective-permute-done.11.refs_1_ = f32[1,16,128]{2,1,0:T(8,128)S(1)} collective-permute-done((f32[1,16,128]{2,1,0:T(8,128)S(1)}, f32[1,16,128]{2,1,0:T(8,128)S(1)}, u32[]{:S(2)}, u32[]{:S(2)}) %collective-permute-start.11) | collective-permute-done | bytes 8224 | tf_op jit(solution)/shard_map/ppermute | solution.py:515
  102.7 1.3 %shard_map.70 = f32[12,12,12]{2,1,0:T(8,128)} custom-call(s32[3]{0:T(128)S(1)} %copy-done.1, s32[12]{0:T(128)S(1)} %copy-done.2, f32[1,16,128]{2,1,0:T(8,128)S(1)} %shard_map.69.refs_0_, f32[1,16,128]{2,1,0:T(8,128)S(1)} %collective-permute-done.11.refs_1_), custom_call_target="tpu_custom_call" | custom-call | tf_op jit(solution)/shard_map/pallas_call | solution.py:278
  (14 shorter events, 0.0 us)
Async XLA Ops:
  0.0 0.9 copy-start
  3.5 13.0 %collective-permute-start.1 = (bf16[1536,128]{1,0:T(8,128)(2,1)S(1)}, bf16[1536,128]{1,0:T(8,128)(2,1)S(1)}, u32[]{:S(2)}, u32[]{:S(2)}) collective-permute-start(bf16[1536,128]{1,0:T(8,128)(2,1)S(1)} %get-tuple-element.30), channel_id=1, source_target_pairs={{0,1},{1,0},{2,3},{3,2},{4,5},{5,4},{6,7},{7,6},{8,9},{9,8},{10,11... | collective-permute-start | bytes 1179656 | tf_op jit(solution)/shard_map/ppermute | solution.py:490
  6.6 16.8 %collective-permute-start.2 = (bf16[1536,128]{1,0:T(8,128)(2,1)S(1)}, bf16[1536,128]{1,0:T(8,128)(2,1)S(1)}, u32[]{:S(2)}, u32[]{:S(2)}) collective-permute-start(bf16[1536,128]{1,0:T(8,128)(2,1)S(1)} %get-tuple-element.31), channel_id=1, source_target_pairs={{0,3},{1,2},{2,1},{3,0},{4,7},{5,6},{6,5},{7,4},{8,11},{9,10},{10,... | collective-permute-start | bytes 1179656 | tf_op jit(solution)/shard_map/ppermute | solution.py:490
  9.2 14.2 %collective-permute-start.3 = (bf16[1536,128]{1,0:T(8,128)(2,1)S(1)}, bf16[1536,128]{1,0:T(8,128)(2,1)S(1)}, u32[]{:S(2)}, u32[]{:S(2)}) collective-permute-start(bf16[1536,128]{1,0:T(8,128)(2,1)S(1)} %get-tuple-element.34), channel_id=1, source_target_pairs={{0,2},{1,3},{2,0},{3,1},{4,6},{5,7},{6,4},{7,5},{8,10},{9,11},{10,... | collective-permute-start | bytes 1179656 | tf_op jit(solution)/shard_map/ppermute | solution.py:490
  12.3 1.4 %collective-permute-start = (s32[6]{0:T(128)}, s32[6]{0:T(128)S(1)}, u32[]{:S(2)}, u32[]{:S(2)}) collective-permute-start(s32[6]{0:T(128)} %get-tuple-element.27.sel_ref), channel_id=1, source_target_pairs={{0,2},{1,3},{2,0},{3,1},{4,6},{5,7},{6,4},{7,5},{8,10},{9,11},{10,... | collective-permute-start | bytes 80 | tf_op jit(solution)/shard_map/ppermute | solution.py:490
  23.4 0.6 copy-start.3
  25.8 26.8 %all-to-all-start = ((bf16[4,400,128]{2,1,0:T(8,128)(2,1)}), bf16[4,400,128]{2,1,0:T(8,128)(2,1)S(1)}, u32[]{:S(2)}, u32[]{:S(2)}) async-start(bf16[4,400,128]{2,1,0:T(8,128)(2,1)} %bitcast.3), calls=%async_computation | async-start | bytes 819200 | tf_op jit(solution)/shard_map/all_to_all | solution.py:508
  29.6 25.2 %collective-permute-start.8 = (bf16[1536,128]{1,0:T(8,128)(2,1)S(1)}, bf16[1536,128]{1,0:T(8,128)(2,1)S(1)}, u32[]{:S(2)}, u32[]{:S(2)}) collective-permute-start(bf16[1536,128]{1,0:T(8,128)(2,1)S(1)} %get-tuple-element.35.refs_0_), channel_id=1, source_target_pairs={{0,1},{1,0},{2,3},{3,2},{4,5},{5,4},{6,7},{7,6},{8,9},{9,8},{10,11... | collective-permute-start | bytes 1179656 | tf_op jit(solution)/shard_map/ppermute | solution.py:490
  30.9 7.9 %collective-permute-start.4 = (bf16[400,128]{1,0:T(8,128)(2,1)S(1)}, bf16[400,128]{1,0:T(8,128)(2,1)S(1)}, u32[]{:S(2)}, u32[]{:S(2)}) collective-permute-start(bf16[400,128]{1,0:T(8,128)(2,1)S(1)} %get-tuple-element.37), channel_id=1, source_target_pairs={{0,16},{2,18},{4,20},{6,22},{8,24},{10,26},{12,28},{14,30},{16,0},... | collective-permute-start | bytes 307208 | tf_op jit(solution)/shard_map/ppermute | solution.py:494
  33.5 10.7 %collective-permute-start.5 = (bf16[400,128]{1,0:T(8,128)(2,1)S(1)}, bf16[400,128]{1,0:T(8,128)(2,1)S(1)}, u32[]{:S(2)}, u32[]{:S(2)}) collective-permute-start(bf16[400,128]{1,0:T(8,128)(2,1)S(1)} %get-tuple-element.38), channel_id=1, source_target_pairs={{0,24},{2,26},{4,28},{6,30},{8,16},{10,18},{12,20},{14,22},{16,8},... | collective-permute-start | bytes 307208 | tf_op jit(solution)/shard_map/ppermute | solution.py:494
  35.3 17.3 %collective-permute-start.6 = (bf16[400,128]{1,0:T(8,128)(2,1)S(1)}, bf16[400,128]{1,0:T(8,128)(2,1)S(1)}, u32[]{:S(2)}, u32[]{:S(2)}) collective-permute-start(bf16[400,128]{1,0:T(8,128)(2,1)S(1)} %get-tuple-element.39), channel_id=1, source_target_pairs={{0,20},{2,22},{4,16},{6,18},{8,28},{10,30},{12,24},{14,26},{16,4},... | collective-permute-start | bytes 307208 | tf_op jit(solution)/shard_map/ppermute | solution.py:494
  37.9 14.7 %collective-permute-start.7 = (bf16[400,128]{1,0:T(8,128)(2,1)S(1)}, bf16[400,128]{1,0:T(8,128)(2,1)S(1)}, u32[]{:S(2)}, u32[]{:S(2)}) collective-permute-start(bf16[400,128]{1,0:T(8,128)(2,1)S(1)} %get-tuple-element.40), channel_id=1, source_target_pairs={{0,28},{2,30},{4,24},{6,26},{8,20},{10,22},{12,16},{14,18},{16,12}... | collective-permute-start | bytes 307208 | tf_op jit(solution)/shard_map/ppermute | solution.py:494
  54.8 34.0 %copy-start.4 = (s32[192]{0:T(256)S(1)}, s32[192]{0:T(256)}, u32[]{:S(2)}) copy-start(s32[192]{0:T(256)} %get-tuple-element.26.table_ref) | copy-start | bytes 2308
  54.8 33.9 %all-to-all-start.1 = ((bf16[32,3,48,128]{3,2,1,0:T(8,128)(2,1)}), bf16[32,3,48,128]{3,2,1,0:T(8,128)(2,1)S(1)}, u32[]{:S(2)}, u32[]{:S(2)}) async-start(bf16[32,3,48,128]{3,2,1,0:T(8,128)(2,1)} %shard_map.68), calls=%async_computation.1 | async-start | bytes 2359296 | tf_op jit(solution)/shard_map/all_to_all | solution.py:511
  58.8 1.8 %collective-permute-start.9 = (bf16[1536,128]{1,0:T(8,128)(2,1)S(1)}, bf16[1536,128]{1,0:T(8,128)(2,1)S(1)}, u32[]{:S(2)}, u32[]{:S(2)}) collective-permute-start(bf16[1536,128]{1,0:T(8,128)(2,1)S(1)} %get-tuple-element.42), channel_id=1, source_target_pairs={{0,2},{1,3},{2,0},{3,1},{4,6},{5,7},{6,4},{7,5},{8,10},{9,11},{10,... | collective-permute-start | bytes 1179656 | tf_op jit(solution)/shard_map/ppermute | solution.py:490
  60.5 19.2 %collective-permute-start.10 = (bf16[1536,128]{1,0:T(8,128)(2,1)S(1)}, bf16[1536,128]{1,0:T(8,128)(2,1)S(1)}, u32[]{:S(2)}, u32[]{:S(2)}) collective-permute-start(bf16[1536,128]{1,0:T(8,128)(2,1)S(1)} %collective-permute-done.9.refs_1_), channel_id=1, source_target_pairs={{0,1},{1,0},{2,3},{3,2},{4,5},{5,4},{6,7},{7,6},{8,9},{9,8},{10,11... | collective-permute-start | bytes 1179656 | tf_op jit(solution)/shard_map/ppermute | solution.py:490
  88.8 13.9 %copy-start.1 = (s32[3]{0:T(128)S(1)}, s32[3]{0:T(128)}, u32[]{:S(2)}) copy-start(s32[3]{0:T(128)} %pad_add_fusion.places_ref.where_ref) | copy-start | bytes 40
  88.8 13.9 %copy-start.2 = (s32[12]{0:T(128)S(1)}, s32[12]{0:T(128)}, u32[]{:S(2)}) copy-start(s32[12]{0:T(128)} %get-tuple-element.25.pairs_ref) | copy-start | bytes 148
  99.0 3.7 %collective-permute-start.11 = (f32[1,16,128]{2,1,0:T(8,128)S(1)}, f32[1,16,128]{2,1,0:T(8,128)S(1)}, u32[]{:S(2)}, u32[]{:S(2)}) collective-permute-start(f32[1,16,128]{2,1,0:T(8,128)S(1)} %shard_map.69.refs_0_), channel_id=1, source_target_pairs={{0,1},{1,0},{2,3},{3,2},{4,5},{5,4},{6,7},{7,6},{8,9},{9,8},{10,11... | collective-permute-start | bytes 24584 | tf_op jit(solution)/shard_map/ppermute | solution.py:515

commit v9 on v8

--- a/solution.py
+++ b/solution.py
@@ -15,7 +15,7 @@
 CHUNK = 4
 LINE = 32
 PACK = 6
-FAR = (4, 6, 5, 7)
+SPREAD = (0, 1, 4, 6, 5, 7, 2, 3)
 SMEM = pltpu.SMEM
 VMEM = pltpu.VMEM
 
@@ -384,7 +384,7 @@
 
 def gather_unit_kernel(size, sel_ref, sel_near_ref, y_ref, cy_ref, own_ref, c_ref, *outs):
     z, x, _, _ = place()
-    sends, query = outs[:5], outs[5:]
+    sends, query = outs[:8], outs[8:]
     span = CHUNK * size
     shape = (16, own_ref.shape[1])
     row, lane = (lax.broadcasted_iota(jnp.int32, shape, axis) for axis in range(2))
@@ -393,58 +393,48 @@
         for k in range(ids_ref.shape[0]):
             asked = jnp.where((row == flip) & (lane == k), ids_ref[k], asked)
     asked = asked.astype(jnp.float32).astype(jnp.bfloat16)
-    near_ref, far_refs = sends[0], sends[1:]
-    rows = 2 * span + 16
-    here = z % 2 * 2 + x
-    for rel in (*FAR, 0, 1, 2, 3):
-        if rel < 4:
-            send_ref, begin = near_ref, (here ^ rel) * rows
-        else:
-            send_ref, begin = far_refs[FAR.index(rel)], 0
+    for rel, send_ref in zip(SPREAD, sends):
         source = pl.multiple_of(((z ^ (rel // 2)) * 2 + (x ^ (rel % 2))) * span, 16)
         for flip, (one_ref, two_ref) in enumerate(((own_ref, y_ref), (c_ref, cy_ref))):
             total = one_ref[pl.ds(source, span)].astype(jnp.float32)
             total = total + two_ref[pl.ds(source, span)].astype(jnp.float32)
             norm = jnp.sum(total * total, axis=-1, keepdims=True)
             unit = (total * lax.rsqrt(norm + 1e-06)).astype(jnp.bfloat16)
-            send_ref[pl.ds(pl.multiple_of(begin + flip * span, 16), span)] = unit
+            send_ref[flip * span : (flip + 1) * span] = unit
             query[flip][pl.ds(source, span)] = unit
-        send_ref[pl.ds(pl.multiple_of(begin + 2 * span, 16), 16)] = asked
+        send_ref[2 * span :] = asked
 
 
 def gather_unit(sel, sel_near, y, cy, own, c, size):
     rows, width = own.shape
-    piece = 2 * CHUNK * size + 16
-    near, far = (jax.ShapeDtypeStruct((n * piece, width), jnp.bfloat16) for n in (4, 1))
+    send = jax.ShapeDtypeStruct((2 * CHUNK * size + 16, width), jnp.bfloat16)
     query = jax.ShapeDtypeStruct((rows, width), jnp.bfloat16)
     return pl.pallas_call(
         functools.partial(gather_unit_kernel, size),
-        out_shape=(near,) + (far,) * 4 + (query,) * 2,
+        out_shape=(send,) * 8 + (query,) * 2,
         in_specs=[pl.BlockSpec(memory_space=SMEM)] * 2 + [pl.BlockSpec(memory_space=VMEM)] * 4,
-        out_specs=[pl.BlockSpec(memory_space=VMEM)] * 7,
+        out_specs=[pl.BlockSpec(memory_space=VMEM)] * 10,
         compiler_params=vmem_params(12),
     )(sel, sel_near, y, cy, own, c)
 
 
-def cube_route_kernel(size, slots, near_ref, *refs):
-    far, out_ref, pieces_ref, rows_ref, asked_ref, sem = refs[:4], *refs[4:]
+def cube_route_kernel(size, slots, *refs):
+    spread, out_ref, pieces_ref, rows_ref, asked_ref, sem = refs[:8], *refs[8:]
     z, x, core, _ = place()
     blocks = pieces_ref.shape[0] // 16
     span = CHUNK * size
-    rows = 2 * span + 16
-    parts = [(near_ref, i * rows, z // 2 * 4 + i) for i in range(4)]
-    parts += [(ref, 0, (z ^ (rel // 2)) * 2 + (x ^ (rel % 2))) for ref, rel in zip(far, FAR)]
-    for ref, begin, chip in parts:
-        ids = ref[begin + 2 * span : begin + rows].astype(jnp.float32)
+    chips = [(z ^ (rel // 2)) * 2 + (x ^ (rel % 2)) for rel in SPREAD]
+    for ref, chip in zip(spread, chips):
+        ids = ref[2 * span :].astype(jnp.float32)
         for flip in range(2):
             rows_ref[pl.ds(chip * 2 + (core ^ flip), 1)] = ids[flip : flip + 1].astype(jnp.int32)
     copy = pltpu.make_async_copy(rows_ref, asked_ref, sem)
     copy.start()
-    for ref, begin, chip in parts:
+    for ref, chip in zip(spread, chips):
         for flip in range(2):
             owner = chip * 2 + (core ^ flip)
             for b in range(blocks):
-                row = begin + flip * span + b * size
+                row = flip * span + b * size
                 pieces_ref[owner * blocks + b] = ref[row : row + size]
     copy.wait()
 
@@ -501,12 +491,10 @@
     y, cy = near(far[0], 2), near(far[1], 3)
     own, aside = split(0, flat, weight, 0)
     c = near(aside, 1)
-    close, *sends, own, other = gather_unit(sel, sel_near, y, cy, own, c, size)
+    *sends, own, other = gather_unit(sel, sel_near, y, cy, own, c, size)
     own_y = near(own, 2)
-    moved = [along(send, rel) for rel, send in zip(FAR, sends)]
-    groups = [[z * 4 + x * 2 + core for z in (high, high + 1) for x in (0, 1)] for high in (0, 2) for core in (0, 1)]
-    close = lax.all_to_all(close, "wide", 0, 0, tiled=True, axis_index_groups=groups)
-    outgoing = cube_route([close, *moved], size, slots, blocks)
+    spread = [along(send, rel) if rel else send for rel, send in zip(SPREAD, sends)]
+    outgoing = cube_route(spread, size, slots, blocks)
     outgoing, other, own_y = lax.optimization_barrier((outgoing, other, own_y))
     incoming = lax.all_to_all(outgoing, ("narrow", "wide"), 0, 0, tiled=True)
     other = near(other, 1)

time: 104 us -> 104 us (level)
  starting transfers between devices: 23.7 us -> 25.9 us
  waiting for transfers between devices: 55.1 us -> 53.5 us
    ppermute x4 -> x7, starting transfers between devices: 7.88 us -> 12.7 us  [along(): return lax.ppermute(array, 'wide', [(i, i ^ flip) for i in range(16)])]
    all_to_all x1 -> x0, starting transfers between devices: 3.77 us -> none  [local_cube(): lax.all_to_all(close, 'wide', 0, 0, tiled=True, axis_index_groups=groups)]
    ppermute x4 -> x7, waiting for transfers between devices: 13.8 us -> 12.2 us  [along(): return lax.ppermute(array, 'wide', [(i, i ^ flip) for i in range(16)])]
    all_to_all x1, starting transfers between devices: 3.94 us -> 5.01 us  [local_cube(): incoming = lax.all_to_all(outgoing, ('narrow', 'wide'), 0, 0, tiled=True)]
  transfers between devices with their start and end apart: 14 -> 16, of which waited for: 9 -> 11; matrix products, arithmetic and copies ran while one was open for 1% -> 1% of each run, Pallas kernels for 7% -> 7%
where the time goes in v9:
time: 104 us
  waiting for transfers between devices  53.5 us (51%)
  starting transfers between devices  25.9 us (25%)
  Pallas kernels  22.2 us (21%)
  local copies, waits for them, and re-layouts  1.6 us (2%)
    ppermute x7, waiting for transfers between devices, near(): lax.ppermute(array, ('wide', 'narrow'), [(i, i ^ flip) for i in range(32)])  29.7 us
    ppermute x7, starting transfers between devices, along(): return lax.ppermute(array, 'wide', [(i, i ^ flip) for i in range(16)])  12.7 us
    ppermute x7, waiting for transfers between devices, along(): return lax.ppermute(array, 'wide', [(i, i ^ flip) for i in range(16)])  12.2 us
    pallas_call x1, Pallas kernels, score(): pl.pallas_call(functools.partial(score_kernel, length, parts), out_shape=...  10.2 us
    all_to_all x1, waiting for transfers between devices, local_cube(): incoming = lax.all_to_all(outgoing, ('narrow', 'wide'), 0, 0, tiled=True)  8.97 us
    ppermute x7, starting transfers between devices, near(): lax.ppermute(array, ('wide', 'narrow'), [(i, i ^ flip) for i in range(32)])  7.15 us
    pallas_call x2, Pallas kernels, split(): pl.pallas_call(functools.partial(split_kernel, first, over), out_shape=(j...  5.26 us
    all_to_all x1, starting transfers between devices, local_cube(): incoming = lax.all_to_all(outgoing, ('narrow', 'wide'), 0, 0, tiled=True)  5.01 us
  transfers between devices with their start and end apart: 16, of which 11 were waited for; matrix products, arithmetic and copies ran while one was open for 1% of the time, Pallas kernels for 7%

profile of v9, /device:TPU:0, one launch (start us, length us, event | category | flops | bytes accessed | tf_op | source)
XLA Modules:
  0.0 103.9 jit_solution(2432640316821869366)
XLA Ops:
  0.0 0.9 copy-done
  0.9 2.6 %shard_map.65 = (bf16[1536,128]{1,0:T(8,128)(2,1)S(1)}, bf16[1536,128]{1,0:T(8,128)(2,1)S(1)}) custom-call(bf16[4,1536,512]{2,1,0:T(8,128)(2,1)} %bitcast.3, bf16[512,128]{1,0:T(8,128)(2,1)S(1)} %copy-done), custom_call_target="tpu_custom_call" | custom-call | flops 402653184 | bytes 3145728 | tf_op jit(solution)/shard_map/pallas_call | solution.py:367
  3.5 3.0 %collective-permute-start.1 = (bf16[1536,128]{1,0:T(8,128)(2,1)S(1)}, bf16[1536,128]{1,0:T(8,128)(2,1)S(1)}, u32[]{:S(2)}, u32[]{:S(2)}) collective-permute-start(bf16[1536,128]{1,0:T(8,128)(2,1)S(1)} %get-tuple-element.33), channel_id=1, source_target_pairs={{0,1},{1,0},{2,3},{3,2},{4,5},{5,4},{6,7},{7,6},{8,9},{9,8},{10,11... | collective-permute-start | bytes 1179656 | tf_op jit(solution)/shard_map/ppermute | solution.py:480
  6.6 2.6 %shard_map.66 = (bf16[1536,128]{1,0:T(8,128)(2,1)S(1)}, bf16[1536,128]{1,0:T(8,128)(2,1)S(1)}) custom-call(bf16[4,1536,512]{2,1,0:T(8,128)(2,1)} %bitcast.4, bf16[512,128]{1,0:T(8,128)(2,1)S(1)} %copy-done), custom_call_target="tpu_custom_call" | custom-call | flops 402653184 | bytes 3145728 | tf_op jit(solution)/shard_map/pallas_call | solution.py:367
  9.5 0.6 pad_add_fusion.places_ref.where_ref
  10.1 2.2 %shard_map.64 = (s32[6]{0:T(128)}, s32[192]{0:T(256)}, s32[12]{0:T(128)}) custom-call(s32[3]{0:T(128)} %pad_add_fusion.places_ref.where_ref, s32[12]{0:T(128)} %cand_ref.1, s32[12]{0:T(128)} %query_block_ref.1, s32[12]{0:T(128)} %valid_ref.1, s32[768]{0:T(1024)} %lengths_ref.1), custom_call_target="tpu_custom_call" | custom-call | tf_op jit(solution)/shard_map/pallas_call | solution.py:75
  12.7 0.9 collective-permute-done.sel_near_ref
  13.5 3.0 %collective-permute-done.1.y_ref = bf16[1536,128]{1,0:T(8,128)(2,1)S(1)} collective-permute-done((bf16[1536,128]{1,0:T(8,128)(2,1)S(1)}, bf16[1536,128]{1,0:T(8,128)(2,1)S(1)}, u32[]{:S(2)}, u32[]{:S(2)}) %collective-permute-start.1) | collective-permute-done | bytes 393248 | tf_op jit(solution)/shard_map/ppermute | solution.py:480
  16.5 6.9 %collective-permute-done.2.cy_ref = bf16[1536,128]{1,0:T(8,128)(2,1)S(1)} collective-permute-done((bf16[1536,128]{1,0:T(8,128)(2,1)S(1)}, bf16[1536,128]{1,0:T(8,128)(2,1)S(1)}, u32[]{:S(2)}, u32[]{:S(2)}) %collective-permute-start.2) | collective-permute-done | bytes 393248 | tf_op jit(solution)/shard_map/ppermute | solution.py:480
  23.4 0.7 copy-done.3
  24.1 1.1 %shard_map.67 = (bf16[400,128]{1,0:T(8,128)(2,1)S(1)}, bf16[400,128]{1,0:T(8,128)(2,1)S(1)}, bf16[400,128]{1,0:T(8,128)(2,1)S(1)}, bf16[400,128]{1,0:T(8,128)(2,...) custom-call(s32[6]{0:T(128)S(1)} %copy-done.3, ...), custom_call_target="tpu_custom_call" | custom-call | tf_op jit(solution)/shard_map/pallas_call | solution.py:412
  25.1 1.4 %collective-permute-start.11 = (bf16[1536,128]{1,0:T(8,128)(2,1)S(1)}, bf16[1536,128]{1,0:T(8,128)(2,1)S(1)}, u32[]{:S(2)}, u32[]{:S(2)}) collective-permute-start(bf16[1536,128]{1,0:T(8,128)(2,1)S(1)} %get-tuple-element.38.refs_0_), channel_id=1, source_target_pairs={{0,1},{1,0},{2,3},{3,2},{4,5},{5,4},{6,7},{7,6},{8,9},{9,8},{10,11... | collective-permute-start | bytes 1179656 | tf_op jit(solution)/shard_map/ppermute | solution.py:480
  26.5 1.5 %collective-permute-start.4 = (bf16[400,128]{1,0:T(8,128)(2,1)S(1)}, bf16[400,128]{1,0:T(8,128)(2,1)S(1)}, u32[]{:S(2)}, u32[]{:S(2)}) collective-permute-start(bf16[400,128]{1,0:T(8,128)(2,1)S(1)} %get-tuple-element.40), channel_id=1, source_target_pairs={{0,4},{2,6},{4,0},{6,2},{8,12},{10,14},{12,8},{14,10},{16,20},{18,... | collective-permute-start | bytes 307208 | tf_op jit(solution)/shard_map/ppermute | solution.py:484
  28.0 2.6 %collective-permute-start.5 = (bf16[400,128]{1,0:T(8,128)(2,1)S(1)}, bf16[400,128]{1,0:T(8,128)(2,1)S(1)}, u32[]{:S(2)}, u32[]{:S(2)}) collective-permute-start(bf16[400,128]{1,0:T(8,128)(2,1)S(1)} %get-tuple-element.41), channel_id=1, source_target_pairs={{0,16},{2,18},{4,20},{6,22},{8,24},{10,26},{12,28},{14,30},{16,0},... | collective-permute-start | bytes 307208 | tf_op jit(solution)/shard_map/ppermute | solution.py:484
  30.6 1.3 %collective-permute-start.6 = (bf16[400,128]{1,0:T(8,128)(2,1)S(1)}, bf16[400,128]{1,0:T(8,128)(2,1)S(1)}, u32[]{:S(2)}, u32[]{:S(2)}) collective-permute-start(bf16[400,128]{1,0:T(8,128)(2,1)S(1)} %get-tuple-element.42), channel_id=1, source_target_pairs={{0,24},{2,26},{4,28},{6,30},{8,16},{10,18},{12,20},{14,22},{16,8},... | collective-permute-start | bytes 307208 | tf_op jit(solution)/shard_map/ppermute | solution.py:484
  31.9 1.7 %collective-permute-start.7 = (bf16[400,128]{1,0:T(8,128)(2,1)S(1)}, bf16[400,128]{1,0:T(8,128)(2,1)S(1)}, u32[]{:S(2)}, u32[]{:S(2)}) collective-permute-start(bf16[400,128]{1,0:T(8,128)(2,1)S(1)} %get-tuple-element.43), channel_id=1, source_target_pairs={{0,20},{2,22},{4,16},{6,18},{8,28},{10,30},{12,24},{14,26},{16,4},... | collective-permute-start | bytes 307208 | tf_op jit(solution)/shard_map/ppermute | solution.py:484
  33.6 2.9 %collective-permute-start.8 = (bf16[400,128]{1,0:T(8,128)(2,1)S(1)}, bf16[400,128]{1,0:T(8,128)(2,1)S(1)}, u32[]{:S(2)}, u32[]{:S(2)}) collective-permute-start(bf16[400,128]{1,0:T(8,128)(2,1)S(1)} %get-tuple-element.44), channel_id=1, source_target_pairs={{0,28},{2,30},{4,24},{6,26},{8,20},{10,22},{12,16},{14,18},{16,12}... | collective-permute-start | bytes 307208 | tf_op jit(solution)/shard_map/ppermute | solution.py:484
  36.5 6.8 %collective-permute-done.5.refs_2_ = bf16[400,128]{1,0:T(8,128)(2,1)S(1)} collective-permute-done((bf16[400,128]{1,0:T(8,128)(2,1)S(1)}, bf16[400,128]{1,0:T(8,128)(2,1)S(1)}, u32[]{:S(2)}, u32[]{:S(2)}) %collective-permute-start.5) | collective-permute-done | bytes 102432 | tf_op jit(solution)/shard_map/ppermute | solution.py:484
  43.6 2.5 %collective-permute-start.10 = (bf16[400,128]{1,0:T(8,128)(2,1)S(1)}, bf16[400,128]{1,0:T(8,128)(2,1)S(1)}, u32[]{:S(2)}, u32[]{:S(2)}) collective-permute-start(bf16[400,128]{1,0:T(8,128)(2,1)S(1)} %get-tuple-element.46), channel_id=1, source_target_pairs={{0,12},{2,14},{4,8},{6,10},{8,4},{10,6},{12,0},{14,2},{16,28},{18,... | collective-permute-start | bytes 307208 | tf_op jit(solution)/shard_map/ppermute | solution.py:484
  46.1 1.7 %collective-permute-done.7.refs_4_ = bf16[400,128]{1,0:T(8,128)(2,1)S(1)} collective-permute-done((bf16[400,128]{1,0:T(8,128)(2,1)S(1)}, bf16[400,128]{1,0:T(8,128)(2,1)S(1)}, u32[]{:S(2)}, u32[]{:S(2)}) %collective-permute-start.7) | collective-permute-done | bytes 102432 | tf_op jit(solution)/shard_map/ppermute | solution.py:484
  47.8 1.8 %collective-permute-done.9.refs_6_ = bf16[400,128]{1,0:T(8,128)(2,1)S(1)} collective-permute-done((bf16[400,128]{1,0:T(8,128)(2,1)S(1)}, bf16[400,128]{1,0:T(8,128)(2,1)S(1)}, u32[]{:S(2)}, u32[]{:S(2)}) %collective-permute-start.9) | collective-permute-done | bytes 102432 | tf_op jit(solution)/shard_map/ppermute | solution.py:484
  49.6 1.8 %collective-permute-done.10.refs_7_ = bf16[400,128]{1,0:T(8,128)(2,1)S(1)} collective-permute-done((bf16[400,128]{1,0:T(8,128)(2,1)S(1)}, bf16[400,128]{1,0:T(8,128)(2,1)S(1)}, u32[]{:S(2)}, u32[]{:S(2)}) %collective-permute-start.10) | collective-permute-done | bytes 102432 | tf_op jit(solution)/shard_map/ppermute | solution.py:484
  51.4 2.2 %shard_map.68 = bf16[32,3,48,128]{3,2,1,0:T(8,128)(2,1)} custom-call(bf16[400,128]{1,0:T(8,128)(2,1)S(1)} %get-tuple-element.39.refs_0_, bf16[400,128]{1,0:T(8,128)(2,1)S(1)} %collective-permute-done.4.refs_1_, bf16[400,128]{1,0:T(8,128)(2,1)S(1)} %collective-permute-done.5.refs_2_, bf16[400,128]{1,0:T(8,128)(2,1)S(1)} %collective-permute-done.6.refs_3_, ...), custom_call_target="tpu_custom_call" | custom-call | tf_op jit(solution)/shard_map/pallas_call | solution.py:452
  53.7 5.0 %all-to-all-start = ((bf16[32,3,48,128]{3,2,1,0:T(8,128)(2,1)}), bf16[32,3,48,128]{3,2,1,0:T(8,128)(2,1)S(1)}, u32[]{:S(2)}, u32[]{:S(2)}) async-start(bf16[32,3,48,128]{3,2,1,0:T(8,128)(2,1)} %shard_map.68), calls=%async_computation | async-start | bytes 2359296 | tf_op jit(solution)/shard_map/all_to_all | solution.py:499
  59.0 1.5 %collective-permute-done.12.refs_1_ = bf16[1536,128]{1,0:T(8,128)(2,1)S(1)} collective-permute-done((bf16[1536,128]{1,0:T(8,128)(2,1)S(1)}, bf16[1536,128]{1,0:T(8,128)(2,1)S(1)}, u32[]{:S(2)}, u32[]{:S(2)}) %collective-permute-start.12) | collective-permute-done | bytes 393248 | tf_op jit(solution)/shard_map/ppermute | solution.py:480
  60.5 1.8 %collective-permute-start.13 = (bf16[1536,128]{1,0:T(8,128)(2,1)S(1)}, bf16[1536,128]{1,0:T(8,128)(2,1)S(1)}, u32[]{:S(2)}, u32[]{:S(2)}) collective-permute-start(bf16[1536,128]{1,0:T(8,128)(2,1)S(1)} %collective-permute-done.12.refs_1_), channel_id=1, source_target_pairs={{0,1},{1,0},{2,3},{3,2},{4,5},{5,4},{6,7},{7,6},{8,9},{9,8},{10,11... | collective-permute-start | bytes 1179656 | tf_op jit(solution)/shard_map/ppermute | solution.py:480
  62.3 17.5 %collective-permute-done.13.refs_3_ = bf16[1536,128]{1,0:T(8,128)(2,1)S(1)} collective-permute-done((bf16[1536,128]{1,0:T(8,128)(2,1)S(1)}, bf16[1536,128]{1,0:T(8,128)(2,1)S(1)}, u32[]{:S(2)}, u32[]{:S(2)}) %collective-permute-start.13) | collective-permute-done | bytes 393248 | tf_op jit(solution)/shard_map/ppermute | solution.py:480
  79.7 9.0 %all-to-all-done.refs_4_ = bf16[32,3,48,128]{3,2,1,0:T(8,128)(2,1)S(1)} async-done(((bf16[32,3,48,128]{3,2,1,0:T(8,128)(2,1)}), bf16[32,3,48,128]{3,2,1,0:T(8,128)(2,1)S(1)}, u32[]{:S(2)}, u32[]{:S(2)}) %all-to-all-start) | async-done | bytes 1179680 | tf_op jit(solution)/shard_map/all_to_all | solution.py:499
  88.7 10.2 %shard_map.69.refs_0_ = f32[1,16,128]{2,1,0:T(8,128)S(1)} custom-call(s32[192]{0:T(256)S(1)} %copy-done.4, bf16[1536,128]{1,0:T(8,128)(2,1)S(1)} %get-tuple-element.38.refs_0_, bf16[1536,128]{1,0:T(8,128)(2,1)S(1)} %collective-permute-done.12.refs_1_, bf16[1536,128]{1,0:T(8,128)(2,1)S(1)} %collective-permute-done.11.refs_2_, ...), custom_call_target="tpu_custom_call" | custom-call | flops 3623878656 | bytes 786432 | tf_op jit(solution)/shard_map/pallas_call | solution.py:251
  98.9 1.0 collective-permute-start.14
  100.0 2.7 %collective-permute-done.14.refs_1_ = f32[1,16,128]{2,1,0:T(8,128)S(1)} collective-permute-done((f32[1,16,128]{2,1,0:T(8,128)S(1)}, f32[1,16,128]{2,1,0:T(8,128)S(1)}, u32[]{:S(2)}, u32[]{:S(2)}) %collective-permute-start.14) | collective-permute-done | bytes 8224 | tf_op jit(solution)/shard_map/ppermute | solution.py:503
  102.6 1.3 %shard_map.70 = f32[12,12,12]{2,1,0:T(8,128)} custom-call(s32[3]{0:T(128)S(1)} %copy-done.1, s32[12]{0:T(128)S(1)} %copy-done.2, f32[1,16,128]{2,1,0:T(8,128)S(1)} %shard_map.69.refs_0_, f32[1,16,128]{2,1,0:T(8,128)S(1)} %collective-permute-done.14.refs_1_), custom_call_target="tpu_custom_call" | custom-call | tf_op jit(solution)/shard_map/pallas_call | solution.py:278
  (18 shorter events, 1.2 us)
Async XLA Ops:
  0.0 0.9 copy-start
  3.5 13.0 %collective-permute-start.1 = (bf16[1536,128]{1,0:T(8,128)(2,1)S(1)}, bf16[1536,128]{1,0:T(8,128)(2,1)S(1)}, u32[]{:S(2)}, u32[]{:S(2)}) collective-permute-start(bf16[1536,128]{1,0:T(8,128)(2,1)S(1)} %get-tuple-element.33), channel_id=1, source_target_pairs={{0,1},{1,0},{2,3},{3,2},{4,5},{5,4},{6,7},{7,6},{8,9},{9,8},{10,11... | collective-permute-start | bytes 1179656 | tf_op jit(solution)/shard_map/ppermute | solution.py:480
  6.6 16.8 %collective-permute-start.2 = (bf16[1536,128]{1,0:T(8,128)(2,1)S(1)}, bf16[1536,128]{1,0:T(8,128)(2,1)S(1)}, u32[]{:S(2)}, u32[]{:S(2)}) collective-permute-start(bf16[1536,128]{1,0:T(8,128)(2,1)S(1)} %get-tuple-element.34), channel_id=1, source_target_pairs={{0,3},{1,2},{2,1},{3,0},{4,7},{5,6},{6,5},{7,4},{8,11},{9,10},{10,... | collective-permute-start | bytes 1179656 | tf_op jit(solution)/shard_map/ppermute | solution.py:480
  9.2 14.2 %collective-permute-start.3 = (bf16[1536,128]{1,0:T(8,128)(2,1)S(1)}, bf16[1536,128]{1,0:T(8,128)(2,1)S(1)}, u32[]{:S(2)}, u32[]{:S(2)}) collective-permute-start(bf16[1536,128]{1,0:T(8,128)(2,1)S(1)} %get-tuple-element.37), channel_id=1, source_target_pairs={{0,2},{1,3},{2,0},{3,1},{4,6},{5,7},{6,4},{7,5},{8,10},{9,11},{10,... | collective-permute-start | bytes 1179656 | tf_op jit(solution)/shard_map/ppermute | solution.py:480
  12.3 1.3 %collective-permute-start = (s32[6]{0:T(128)}, s32[6]{0:T(128)S(1)}, u32[]{:S(2)}, u32[]{:S(2)}) collective-permute-start(s32[6]{0:T(128)} %get-tuple-element.30.sel_ref), channel_id=1, source_target_pairs={{0,2},{1,3},{2,0},{3,1},{4,6},{5,7},{6,4},{7,5},{8,10},{9,11},{10,... | collective-permute-start | bytes 80 | tf_op jit(solution)/shard_map/ppermute | solution.py:480
  23.4 0.7 copy-start.3
  25.1 28.5 %collective-permute-start.11 = (bf16[1536,128]{1,0:T(8,128)(2,1)S(1)}, bf16[1536,128]{1,0:T(8,128)(2,1)S(1)}, u32[]{:S(2)}, u32[]{:S(2)}) collective-permute-start(bf16[1536,128]{1,0:T(8,128)(2,1)S(1)} %get-tuple-element.38.refs_0_), channel_id=1, source_target_pairs={{0,1},{1,0},{2,3},{3,2},{4,5},{5,4},{6,7},{7,6},{8,9},{9,8},{10,11... | collective-permute-start | bytes 1179656 | tf_op jit(solution)/shard_map/ppermute | solution.py:480
  26.5 7.1 %collective-permute-start.4 = (bf16[400,128]{1,0:T(8,128)(2,1)S(1)}, bf16[400,128]{1,0:T(8,128)(2,1)S(1)}, u32[]{:S(2)}, u32[]{:S(2)}) collective-permute-start(bf16[400,128]{1,0:T(8,128)(2,1)S(1)} %get-tuple-element.40), channel_id=1, source_target_pairs={{0,4},{2,6},{4,0},{6,2},{8,12},{10,14},{12,8},{14,10},{16,20},{18,... | collective-permute-start | bytes 307208 | tf_op jit(solution)/shard_map/ppermute | solution.py:484
  28.0 15.4 %collective-permute-start.5 = (bf16[400,128]{1,0:T(8,128)(2,1)S(1)}, bf16[400,128]{1,0:T(8,128)(2,1)S(1)}, u32[]{:S(2)}, u32[]{:S(2)}) collective-permute-start(bf16[400,128]{1,0:T(8,128)(2,1)S(1)} %get-tuple-element.41), channel_id=1, source_target_pairs={{0,16},{2,18},{4,20},{6,22},{8,24},{10,26},{12,28},{14,30},{16,0},... | collective-permute-start | bytes 307208 | tf_op jit(solution)/shard_map/ppermute | solution.py:484
  30.6 13.0 %collective-permute-start.6 = (bf16[400,128]{1,0:T(8,128)(2,1)S(1)}, bf16[400,128]{1,0:T(8,128)(2,1)S(1)}, u32[]{:S(2)}, u32[]{:S(2)}) collective-permute-start(bf16[400,128]{1,0:T(8,128)(2,1)S(1)} %get-tuple-element.42), channel_id=1, source_target_pairs={{0,24},{2,26},{4,28},{6,30},{8,16},{10,18},{12,20},{14,22},{16,8},... | collective-permute-start | bytes 307208 | tf_op jit(solution)/shard_map/ppermute | solution.py:484
  31.9 15.8 %collective-permute-start.7 = (bf16[400,128]{1,0:T(8,128)(2,1)S(1)}, bf16[400,128]{1,0:T(8,128)(2,1)S(1)}, u32[]{:S(2)}, u32[]{:S(2)}) collective-permute-start(bf16[400,128]{1,0:T(8,128)(2,1)S(1)} %get-tuple-element.43), channel_id=1, source_target_pairs={{0,20},{2,22},{4,16},{6,18},{8,28},{10,30},{12,24},{14,26},{16,4},... | collective-permute-start | bytes 307208 | tf_op jit(solution)/shard_map/ppermute | solution.py:484
  33.6 14.2 %collective-permute-start.8 = (bf16[400,128]{1,0:T(8,128)(2,1)S(1)}, bf16[400,128]{1,0:T(8,128)(2,1)S(1)}, u32[]{:S(2)}, u32[]{:S(2)}) collective-permute-start(bf16[400,128]{1,0:T(8,128)(2,1)S(1)} %get-tuple-element.44), channel_id=1, source_target_pairs={{0,28},{2,30},{4,24},{6,26},{8,20},{10,22},{12,16},{14,18},{16,12}... | collective-permute-start | bytes 307208 | tf_op jit(solution)/shard_map/ppermute | solution.py:484
  43.4 6.2 %collective-permute-start.9 = (bf16[400,128]{1,0:T(8,128)(2,1)S(1)}, bf16[400,128]{1,0:T(8,128)(2,1)S(1)}, u32[]{:S(2)}, u32[]{:S(2)}) collective-permute-start(bf16[400,128]{1,0:T(8,128)(2,1)S(1)} %get-tuple-element.45), channel_id=1, source_target_pairs={{0,8},{2,10},{4,12},{6,14},{8,0},{10,2},{12,4},{14,6},{16,24},{18,... | collective-permute-start | bytes 307208 | tf_op jit(solution)/shard_map/ppermute | solution.py:484
  43.6 7.8 %collective-permute-start.10 = (bf16[400,128]{1,0:T(8,128)(2,1)S(1)}, bf16[400,128]{1,0:T(8,128)(2,1)S(1)}, u32[]{:S(2)}, u32[]{:S(2)}) collective-permute-start(bf16[400,128]{1,0:T(8,128)(2,1)S(1)} %get-tuple-element.46), channel_id=1, source_target_pairs={{0,12},{2,14},{4,8},{6,10},{8,4},{10,6},{12,0},{14,2},{16,28},{18,... | collective-permute-start | bytes 307208 | tf_op jit(solution)/shard_map/ppermute | solution.py:484
  53.7 35.0 %copy-start.4 = (s32[192]{0:T(256)S(1)}, s32[192]{0:T(256)}, u32[]{:S(2)}) copy-start(s32[192]{0:T(256)} %get-tuple-element.29.table_ref) | copy-start | bytes 2308
  53.7 35.0 %all-to-all-start = ((bf16[32,3,48,128]{3,2,1,0:T(8,128)(2,1)}), bf16[32,3,48,128]{3,2,1,0:T(8,128)(2,1)S(1)}, u32[]{:S(2)}, u32[]{:S(2)}) async-start(bf16[32,3,48,128]{3,2,1,0:T(8,128)(2,1)} %shard_map.68), calls=%async_computation | async-start | bytes 2359296 | tf_op jit(solution)/shard_map/all_to_all | solution.py:499
  58.7 1.8 %collective-permute-start.12 = (bf16[1536,128]{1,0:T(8,128)(2,1)S(1)}, bf16[1536,128]{1,0:T(8,128)(2,1)S(1)}, u32[]{:S(2)}, u32[]{:S(2)}) collective-permute-start(bf16[1536,128]{1,0:T(8,128)(2,1)S(1)} %get-tuple-element.48), channel_id=1, source_target_pairs={{0,2},{1,3},{2,0},{3,1},{4,6},{5,7},{6,4},{7,5},{8,10},{9,11},{10,... | collective-permute-start | bytes 1179656 | tf_op jit(solution)/shard_map/ppermute | solution.py:480
  60.5 19.2 %collective-permute-start.13 = (bf16[1536,128]{1,0:T(8,128)(2,1)S(1)}, bf16[1536,128]{1,0:T(8,128)(2,1)S(1)}, u32[]{:S(2)}, u32[]{:S(2)}) collective-permute-start(bf16[1536,128]{1,0:T(8,128)(2,1)S(1)} %collective-permute-done.12.refs_1_), channel_id=1, source_target_pairs={{0,1},{1,0},{2,3},{3,2},{4,5},{5,4},{6,7},{7,6},{8,9},{9,8},{10,11... | collective-permute-start | bytes 1179656 | tf_op jit(solution)/shard_map/ppermute | solution.py:480
  88.7 13.9 %copy-start.1 = (s32[3]{0:T(128)S(1)}, s32[3]{0:T(128)}, u32[]{:S(2)}) copy-start(s32[3]{0:T(128)} %pad_add_fusion.places_ref.where_ref) | copy-start | bytes 40
  88.7 13.9 %copy-start.2 = (s32[12]{0:T(128)S(1)}, s32[12]{0:T(128)}, u32[]{:S(2)}) copy-start(s32[12]{0:T(128)} %get-tuple-element.28.pairs_ref) | copy-start | bytes 148
  98.9 3.7 %collective-permute-start.14 = (f32[1,16,128]{2,1,0:T(8,128)S(1)}, f32[1,16,128]{2,1,0:T(8,128)S(1)}, u32[]{:S(2)}, u32[]{:S(2)}) collective-permute-start(f32[1,16,128]{2,1,0:T(8,128)S(1)} %shard_map.69.refs_0_), channel_id=1, source_target_pairs={{0,1},{1,0},{2,3},{3,2},{4,5},{5,4},{6,7},{7,6},{8,9},{9,8},{10,11... | collective-permute-start | bytes 24584 | tf_op jit(solution)/shard_map/ppermute | solution.py:503

commit v10 on v9

--- a/solution.py
+++ b/solution.py
@@ -12,10 +12,10 @@
 SHARPNESS = 20.0
 EXP2_SCALE = SHARPNESS * math.log2(math.e)
 COLS = 512
-CHUNK = 4
+CHUNK = 2
 LINE = 32
 PACK = 6
-SPREAD = (0, 1, 4, 6, 5, 7, 2, 3)
+SPREAD = (0, 4, 6, 5, 7, 2, 3, 1)
 SMEM = pltpu.SMEM
 VMEM = pltpu.VMEM
 
@@ -177,15 +177,18 @@
 def query_rows(parts, out_ref):
     _, _, core, side = place()
     size = out_ref.shape[1] // 32
-    blocks = out_ref.shape[0]
-    for rel, ref in enumerate(parts):
-        base = (side ^ (rel // 2)) * (16 * size) + (core ^ (rel % 2)) * (2 * size)
+    half = 8 * CHUNK * size
+    early, early_far = parts[:2]
+    pieces = [(ref, flip * half, far, flip, 0) for far, ref in ((0, early), (1, early_far)) for flip in range(2)]
+    pieces += [(ref, 0, rel // 2, rel % 2, CHUNK) for rel, ref in enumerate(parts[2:])]
+    for ref, begin, far, flip, first in pieces:
+        base = (side ^ far) * (16 * size) + (core ^ flip) * (2 * size)
         for z in range(4):
             for x in range(2):
                 target = pl.multiple_of(base + z * 4 * size + x * size, 16)
-                for b in range(blocks):
-                    begin = ((z * 2 + x) * blocks + b) * size
-                    out_ref[b, pl.ds(target, size)] = ref[begin : begin + size]
+                for b in range(CHUNK):
+                    row = begin + ((z * 2 + x) * CHUNK + b) * size
+                    out_ref[first + b, pl.ds(target, size)] = ref[row : row + size]
 
 
 def score_kernel(length, parts, table_ref, *refs):
@@ -382,60 +385,92 @@
     )(states, weight)
 
 
-def gather_unit_kernel(size, sel_ref, sel_near_ref, y_ref, cy_ref, own_ref, c_ref, *outs):
+def unit_sum(one, two):
+    total = one.astype(jnp.float32) + two.astype(jnp.float32)
+    norm = jnp.sum(total * total, axis=-1, keepdims=True)
+    return (total * lax.rsqrt(norm + 1e-06)).astype(jnp.bfloat16)
+
+
+def early_unit_kernel(size, sel_ref, y_ref, y_flip_ref, own_ref, own_flip_ref, send_ref, query_ref):
+    _, _, core, _ = place()
+    span = CHUNK * size
+    rows = span + 16
+    shape = (16, own_ref.shape[1])
+    lane = lax.broadcasted_iota(jnp.int32, shape, 1)
+    asked = jnp.zeros(shape, jnp.int32)
+    for k in range(sel_ref.shape[0]):
+        asked = jnp.where(lane == k, sel_ref[k], asked)
+    asked = asked.astype(jnp.float32).astype(jnp.bfloat16)
+    for flip, (one_ref, two_ref) in enumerate(((own_ref, y_ref), (own_flip_ref, y_flip_ref))):
+        for chip in range(8):
+            source = chip * span
+            unit = unit_sum(one_ref[source : source + span], two_ref[source : source + span])
+            begin = (chip * 2 + (core ^ flip)) * rows
+            send_ref[pl.ds(pl.multiple_of(begin, 16), span)] = unit
+            send_ref[pl.ds(pl.multiple_of(begin + span, 16), 16)] = asked
+            query_ref[8 * span * flip + source : 8 * span * flip + source + span] = unit
+
+
+def early_unit(sel, y, y_flip, own, own_flip, size):
+    rows, width = own.shape
+    return pl.pallas_call(
+        functools.partial(early_unit_kernel, size),
+        out_shape=(
+            jax.ShapeDtypeStruct((16 * (CHUNK * size + 16), width), jnp.bfloat16),
+            jax.ShapeDtypeStruct((2 * rows, width), jnp.bfloat16),
+        ),
+        in_specs=[pl.BlockSpec(memory_space=SMEM)] + [pl.BlockSpec(memory_space=VMEM)] * 4,
+        out_specs=[pl.BlockSpec(memory_space=VMEM)] * 2,
+        compiler_params=vmem_params(12),
+    )(sel, y, y_flip, own, own_flip)
+
+
+def late_unit_kernel(size, y_ref, cy_ref, own_ref, c_ref, *outs):
     z, x, _, _ = place()
     sends, query = outs[:8], outs[8:]
     span = CHUNK * size
-    shape = (16, own_ref.shape[1])
-    row, lane = (lax.broadcasted_iota(jnp.int32, shape, axis) for axis in range(2))
-    asked = jnp.zeros(shape, jnp.int32)
-    for flip, ids_ref in enumerate((sel_ref, sel_near_ref)):
-        for k in range(ids_ref.shape[0]):
-            asked = jnp.where((row == flip) & (lane == k), ids_ref[k], asked)
-    asked = asked.astype(jnp.float32).astype(jnp.bfloat16)
     for rel, send_ref in zip(SPREAD, sends):
         source = pl.multiple_of(((z ^ (rel // 2)) * 2 + (x ^ (rel % 2))) * span, 16)
         for flip, (one_ref, two_ref) in enumerate(((own_ref, y_ref), (c_ref, cy_ref))):
-            total = one_ref[pl.ds(source, span)].astype(jnp.float32)
-            total = total + two_ref[pl.ds(source, span)].astype(jnp.float32)
-            norm = jnp.sum(total * total, axis=-1, keepdims=True)
-            unit = (total * lax.rsqrt(norm + 1e-06)).astype(jnp.bfloat16)
+            unit = unit_sum(one_ref[pl.ds(source, span)], two_ref[pl.ds(source, span)])
             send_ref[flip * span : (flip + 1) * span] = unit
             query[flip][pl.ds(source, span)] = unit
-        send_ref[2 * span :] = asked
-
-
-def gather_unit(sel, sel_near, y, cy, own, c, size):
+
+
+def late_unit(y, cy, own, c, size):
     rows, width = own.shape
-    send = jax.ShapeDtypeStruct((2 * CHUNK * size + 16, width), jnp.bfloat16)
+    send = jax.ShapeDtypeStruct((2 * CHUNK * size, width), jnp.bfloat16)
     query = jax.ShapeDtypeStruct((rows, width), jnp.bfloat16)
     return pl.pallas_call(
-        functools.partial(gather_unit_kernel, size),
+        functools.partial(late_unit_kernel, size),
         out_shape=(send,) * 8 + (query,) * 2,
-        in_specs=[pl.BlockSpec(memory_space=SMEM)] * 2 + [pl.BlockSpec(memory_space=VMEM)] * 4,
+        in_specs=[pl.BlockSpec(memory_space=VMEM)] * 4,
         out_specs=[pl.BlockSpec(memory_space=VMEM)] * 10,
         compiler_params=vmem_params(12),
-    )(sel, sel_near, y, cy, own, c)
-
-
-def cube_route_kernel(size, slots, *refs):
-    spread, out_ref, pieces_ref, rows_ref, asked_ref, sem = refs[:8], *refs[8:]
+    )(y, cy, own, c)
+
+
+def cube_route_kernel(size, slots, early_ref, *refs):
+    late, out_ref, pieces_ref, rows_ref, asked_ref, sem = refs[:8], *refs[8:]
     z, x, core, _ = place()
     blocks = pieces_ref.shape[0] // 16
     span = CHUNK * size
-    chips = [(z ^ (rel // 2)) * 2 + (x ^ (rel % 2)) for rel in SPREAD]
-    for ref, chip in zip(spread, chips):
-        ids = ref[2 * span :].astype(jnp.float32)
-        for flip in range(2):
-            rows_ref[pl.ds(chip * 2 + (core ^ flip), 1)] = ids[flip : flip + 1].astype(jnp.int32)
+    for owner in range(16):
+        row = owner * (span + 16) + span
+        rows_ref[owner : owner + 1] = early_ref[row : row + 16].astype(jnp.float32)[:1].astype(jnp.int32)
     copy = pltpu.make_async_copy(rows_ref, asked_ref, sem)
     copy.start()
-    for ref, chip in zip(spread, chips):
+    for owner in range(16):
+        for b in range(CHUNK):
+            row = owner * (span + 16) + b * size
+            pieces_ref[owner * blocks + b] = early_ref[row : row + size]
+    for rel, ref in zip(SPREAD, late):
+        chip = (z ^ (rel // 2)) * 2 + (x ^ (rel % 2))
         for flip in range(2):
             owner = chip * 2 + (core ^ flip)
-            for b in range(blocks):
+            for b in range(CHUNK):
                 row = flip * span + b * size
-                pieces_ref[owner * blocks + b] = ref[row : row + size]
+                pieces_ref[owner * blocks + CHUNK + b] = ref[row : row + size]
     copy.wait()
 
     def step(d, carry):
@@ -485,20 +520,26 @@
 
     places = jnp.stack([owner, side, jnp.int32(blocks)])
     sel, table, pair_of = plan(places, cand_block, query_block, pair_valid, lengths, slots)
-    sel_near = near(sel, 1)
     far = split(1, flat, proj_weight, 0)
     weight, *far = lax.optimization_barrier((proj_weight, *far))
-    y, cy = near(far[0], 2), near(far[1], 3)
-    own, aside = split(0, flat, weight, 0)
-    c = near(aside, 1)
-    *sends, own, other = gather_unit(sel, sel_near, y, cy, own, c, size)
-    own_y = near(own, 2)
+    crossed = [near(part, 2) for part in far]
+    far = split(1, flat, weight, CHUNK)
+    weight, sel, *far = lax.optimization_barrier((weight, sel, *far))
+    early = split(0, flat, weight, 0)
+    own, aside = split(0, flat, weight, CHUNK)
+    *early, own, aside = lax.optimization_barrier((*early, own, aside))
+    send, early_query = early_unit(sel, *crossed, *early, size)
+    y, cy, c = near(far[0], 2), near(far[1], 3), near(aside, 1)
+    early_spread = lax.all_to_all(send, "wide", 0, 0, tiled=True)
+    *sends, own, other = late_unit(y, cy, own, c, size)
+    early_query, sends[0] = lax.optimization_barrier((early_query, sends[0]))
+    early_far = near(early_query, 2)
     spread = [along(send, rel) if rel else send for rel, send in zip(SPREAD, sends)]
-    outgoing = cube_route(spread, size, slots, blocks)
-    outgoing, other, own_y = lax.optimization_barrier((outgoing, other, own_y))
+    outgoing = cube_route([early_spread, *spread], size, slots, blocks)
+    outgoing, own, other, early_far = lax.optimization_barrier((outgoing, own, other, early_far))
     incoming = lax.all_to_all(outgoing, ("narrow", "wide"), 0, 0, tiled=True)
     other = near(other, 1)
-    query = [own, other, own_y, near(other, 2)]
+    query = [early_query, early_far, own, other, near(own, 2), near(other, 2)]
     part = score(table, query, incoming, blocks, length)
     parts = [part, lax.ppermute(part, "narrow", [(0, 1), (1, 0)])]
     return place_scores(places, pair_of, parts, cand_block.shape[0])

time: 104 us -> 103 us (level)
  waiting for transfers between devices: 53.5 us -> 43.7 us
  starting transfers between devices: 25.9 us -> 32 us
  Pallas kernels: 22.2 us -> 25.3 us
    ppermute x7, waiting for transfers between devices: 12.2 us -> 5.17 us  [along(): return lax.ppermute(array, 'wide', [(i, i ^ flip) for i in range(16)])]
    all_to_all x0 -> x1, starting transfers between devices: none -> 6.13 us  [local_cube(): early_spread = lax.all_to_all(send, 'wide', 0, 0, tiled=True)]
    ppermute x7 -> x9, starting transfers between devices: 7.15 us -> 10.2 us  [near(): lax.ppermute(array, ('wide', 'narrow'), [(i, i ^ flip) for i in range(32)])]
    ppermute x7 -> x9, waiting for transfers between devices: 29.7 us -> 26.9 us  [near(): lax.ppermute(array, ('wide', 'narrow'), [(i, i ^ flip) for i in range(32)])]
    pallas_call x2 -> x4, Pallas kernels: 5.26 us -> 7.6 us  [split(): pl.pallas_call(functools.partial(split_kernel, first, over), out_shape=(j...]
    all_to_all x1, starting transfers between devices: 5.01 us -> 3.43 us  [local_cube(): incoming = lax.all_to_all(outgoing, ('narrow', 'wide'), 0, 0, tiled=True)]
    ppermute x7, starting transfers between devices: 12.7 us -> 11.3 us  [along(): return lax.ppermute(array, 'wide', [(i, i ^ flip) for i in range(16)])]
  transfers between devices with their start and end apart: 16 -> 19, of which waited for: 11 -> 12; matrix products, arithmetic and copies ran while one was open for 1% -> 1% of each run, Pallas kernels for 7% -> 10%
where the time goes in v10:
time: 103 us
  waiting for transfers between devices  43.7 us (42%)
  starting transfers between devices  32 us (31%)
  Pallas kernels  25.3 us (25%)
    ppermute x9, waiting for transfers between devices, near(): lax.ppermute(array, ('wide', 'narrow'), [(i, i ^ flip) for i in range(32)])  26.9 us
    ppermute x7, starting transfers between devices, along(): return lax.ppermute(array, 'wide', [(i, i ^ flip) for i in range(16)])  11.3 us
    pallas_call x1, Pallas kernels, score(): pl.pallas_call(functools.partial(score_kernel, length, parts), out_shape=...  10.2 us
    ppermute x9, starting transfers between devices, near(): lax.ppermute(array, ('wide', 'narrow'), [(i, i ^ flip) for i in range(32)])  10.2 us
    all_to_all x1, waiting for transfers between devices, local_cube(): incoming = lax.all_to_all(outgoing, ('narrow', 'wide'), 0, 0, tiled=True)  8.97 us
    pallas_call x4, Pallas kernels, split(): pl.pallas_call(functools.partial(split_kernel, first, over), out_shape=(j...  7.6 us
    all_to_all x1, starting transfers between devices, local_cube(): early_spread = lax.all_to_all(send, 'wide', 0, 0, tiled=True)  6.13 us
    ppermute x7, waiting for transfers between devices, along(): return lax.ppermute(array, 'wide', [(i, i ^ flip) for i in range(16)])  5.17 us
  transfers between devices with their start and end apart: 19, of which 12 were waited for; matrix products, arithmetic and copies ran while one was open for 1% of the time, Pallas kernels for 10%

profile of v10, /device:TPU:0, one launch (start us, length us, event | category | flops | bytes accessed | tf_op | source)
XLA Modules:
  0.0 102.8 jit_solution(2684884531324166596)
XLA Ops:
  0.0 0.9 copy-done
  0.9 1.9 %shard_map.65 = (bf16[768,128]{1,0:T(8,128)(2,1)S(1)}, bf16[768,128]{1,0:T(8,128)(2,1)S(1)}) custom-call(bf16[4,1536,512]{2,1,0:T(8,128)(2,1)} %bitcast.6, bf16[512,128]{1,0:T(8,128)(2,1)S(1)} %copy-done), custom_call_target="tpu_custom_call" | custom-call | flops 201326592 | bytes 1572864 | tf_op jit(solution)/shard_map/pallas_call | solution.py:370
  2.8 3.0 %collective-permute-start = (bf16[768,128]{1,0:T(8,128)(2,1)S(1)}, bf16[768,128]{1,0:T(8,128)(2,1)S(1)}, u32[]{:S(2)}, u32[]{:S(2)}) collective-permute-start(bf16[768,128]{1,0:T(8,128)(2,1)S(1)} %get-tuple-element.54), channel_id=1, source_target_pairs={{0,1},{1,0},{2,3},{3,2},{4,5},{5,4},{6,7},{7,6},{8,9},{9,8},{10,11... | collective-permute-start | bytes 589832 | tf_op jit(solution)/shard_map/ppermute | solution.py:515
  6.6 2.2 %shard_map.64 = (s32[6]{0:T(128)}, s32[192]{0:T(256)}, s32[12]{0:T(128)}) custom-call(s32[3]{0:T(128)} %pad_add_fusion.places_ref.where_ref, s32[12]{0:T(128)} %cand_ref.1, s32[12]{0:T(128)} %query_block_ref.1, s32[12]{0:T(128)} %valid_ref.1, s32[768]{0:T(1024)} %lengths_ref.1), custom_call_target="tpu_custom_call" | custom-call | tf_op jit(solution)/shard_map/pallas_call | solution.py:75
  8.8 1.9 %shard_map.66 = (bf16[768,128]{1,0:T(8,128)(2,1)S(1)}, bf16[768,128]{1,0:T(8,128)(2,1)S(1)}) custom-call(bf16[4,1536,512]{2,1,0:T(8,128)(2,1)} %bitcast.7, bf16[512,128]{1,0:T(8,128)(2,1)S(1)} %copy-done.1), custom_call_target="tpu_custom_call" | custom-call | flops 201326592 | bytes 1572864 | tf_op jit(solution)/shard_map/pallas_call | solution.py:370
  10.7 1.9 %shard_map.68 = (bf16[768,128]{1,0:T(8,128)(2,1)S(1)}, bf16[768,128]{1,0:T(8,128)(2,1)S(1)}) custom-call(bf16[4,1536,512]{2,1,0:T(8,128)(2,1)} %bitcast.8, bf16[512,128]{1,0:T(8,128)(2,1)S(1)} %copy-done.1), custom_call_target="tpu_custom_call" | custom-call | flops 201326592 | bytes 1572864 | tf_op jit(solution)/shard_map/pallas_call | solution.py:370
  12.6 1.9 %shard_map.67 = (bf16[768,128]{1,0:T(8,128)(2,1)S(1)}, bf16[768,128]{1,0:T(8,128)(2,1)S(1)}) custom-call(bf16[4,1536,512]{2,1,0:T(8,128)(2,1)} %bitcast.9, bf16[512,128]{1,0:T(8,128)(2,1)S(1)} %copy-done.1), custom_call_target="tpu_custom_call" | custom-call | flops 201326592 | bytes 1572864 | tf_op jit(solution)/shard_map/pallas_call | solution.py:370
  15.0 1.6 %shard_map.69 = (bf16[1792,128]{1,0:T(8,128)(2,1)}, bf16[1536,128]{1,0:T(8,128)(2,1)S(1)}) custom-call(s32[6]{0:T(128)S(1)} %copy-done.4, bf16[768,128]{1,0:T(8,128)(2,1)S(1)} %collective-permute-done.y_ref, bf16[768,128]{1,0:T(8,128)(2,1)S(1)} %collective-permute-done.1.y_flip_ref, bf16[768,128]{1,0:T(8,128)(2,1)S(1)} %get-tuple-element.61.own_ref, ...), custom_call_target="tpu_custom_call" | custom-call | tf_op jit(solution)/shard_map/pallas_call | solution.py:416
  16.6 6.1 %all-to-all-start = ((bf16[16,112,128]{2,1,0:T(8,128)(2,1)}), bf16[16,112,128]{2,1,0:T(8,128)(2,1)S(1)}, u32[]{:S(2)}, u32[]{:S(2)}) async-start(bf16[16,112,128]{2,1,0:T(8,128)(2,1)} %bitcast.3), calls=%async_computation | async-start | bytes 917504 | tf_op jit(solution)/shard_map/all_to_all | solution.py:533
  22.7 1.6 %collective-permute-start.2 = (bf16[768,128]{1,0:T(8,128)(2,1)S(1)}, bf16[768,128]{1,0:T(8,128)(2,1)S(1)}, u32[]{:S(2)}, u32[]{:S(2)}) collective-permute-start(bf16[768,128]{1,0:T(8,128)(2,1)S(1)} %get-tuple-element.64), channel_id=1, source_target_pairs={{0,1},{1,0},{2,3},{3,2},{4,5},{5,4},{6,7},{7,6},{8,9},{9,8},{10,11... | collective-permute-start | bytes 589832 | tf_op jit(solution)/shard_map/ppermute | solution.py:515
  24.9 5.6 %collective-permute-done.2.y_ref = bf16[768,128]{1,0:T(8,128)(2,1)S(1)} collective-permute-done((bf16[768,128]{1,0:T(8,128)(2,1)S(1)}, bf16[768,128]{1,0:T(8,128)(2,1)S(1)}, u32[]{:S(2)}, u32[]{:S(2)}) %collective-permute-start.2) | collective-permute-done | bytes 196640 | tf_op jit(solution)/shard_map/ppermute | solution.py:515
  30.5 3.1 %collective-permute-done.3.cy_ref = bf16[768,128]{1,0:T(8,128)(2,1)S(1)} collective-permute-done((bf16[768,128]{1,0:T(8,128)(2,1)S(1)}, bf16[768,128]{1,0:T(8,128)(2,1)S(1)}, u32[]{:S(2)}, u32[]{:S(2)}) %collective-permute-start.3) | collective-permute-done | bytes 196640 | tf_op jit(solution)/shard_map/ppermute | solution.py:515
  33.9 1.6 %collective-permute-start.12 = (bf16[1536,128]{1,0:T(8,128)(2,1)S(1)}, bf16[1536,128]{1,0:T(8,128)(2,1)S(1)}, u32[]{:S(2)}, u32[]{:S(2)}) collective-permute-start(bf16[1536,128]{1,0:T(8,128)(2,1)S(1)} %get-tuple-element.69.refs_0_), channel_id=1, source_target_pairs={{0,1},{1,0},{2,3},{3,2},{4,5},{5,4},{6,7},{7,6},{8,9},{9,8},{10,11... | collective-permute-start | bytes 1179656 | tf_op jit(solution)/shard_map/ppermute | solution.py:515
  35.5 2.3 %collective-permute-start.5 = (bf16[192,128]{1,0:T(8,128)(2,1)S(1)}, bf16[192,128]{1,0:T(8,128)(2,1)S(1)}, u32[]{:S(2)}, u32[]{:S(2)}) collective-permute-start(bf16[192,128]{1,0:T(8,128)(2,1)S(1)} %get-tuple-element.72), channel_id=1, source_target_pairs={{0,16},{2,18},{4,20},{6,22},{8,24},{10,26},{12,28},{14,30},{16,0},... | collective-permute-start | bytes 147464 | tf_op jit(solution)/shard_map/ppermute | solution.py:519
  37.8 1.5 %collective-permute-start.6 = (bf16[192,128]{1,0:T(8,128)(2,1)S(1)}, bf16[192,128]{1,0:T(8,128)(2,1)S(1)}, u32[]{:S(2)}, u32[]{:S(2)}) collective-permute-start(bf16[192,128]{1,0:T(8,128)(2,1)S(1)} %get-tuple-element.73), channel_id=1, source_target_pairs={{0,24},{2,26},{4,28},{6,30},{8,16},{10,18},{12,20},{14,22},{16,8},... | collective-permute-start | bytes 147464 | tf_op jit(solution)/shard_map/ppermute | solution.py:519
  39.3 2.4 %collective-permute-start.7 = (bf16[192,128]{1,0:T(8,128)(2,1)S(1)}, bf16[192,128]{1,0:T(8,128)(2,1)S(1)}, u32[]{:S(2)}, u32[]{:S(2)}) collective-permute-start(bf16[192,128]{1,0:T(8,128)(2,1)S(1)} %get-tuple-element.74), channel_id=1, source_target_pairs={{0,20},{2,22},{4,16},{6,18},{8,28},{10,30},{12,24},{14,26},{16,4},... | collective-permute-start | bytes 147464 | tf_op jit(solution)/shard_map/ppermute | solution.py:519
  42.5 1.1 %collective-permute-start.9 = (bf16[192,128]{1,0:T(8,128)(2,1)S(1)}, bf16[192,128]{1,0:T(8,128)(2,1)S(1)}, u32[]{:S(2)}, u32[]{:S(2)}) collective-permute-start(bf16[192,128]{1,0:T(8,128)(2,1)S(1)} %get-tuple-element.76), channel_id=1, source_target_pairs={{0,8},{2,10},{4,12},{6,14},{8,0},{10,2},{12,4},{14,6},{16,24},{18,... | collective-permute-start | bytes 147464 | tf_op jit(solution)/shard_map/ppermute | solution.py:519
  44.0 2.9 %collective-permute-start.10 = (bf16[192,128]{1,0:T(8,128)(2,1)S(1)}, bf16[192,128]{1,0:T(8,128)(2,1)S(1)}, u32[]{:S(2)}, u32[]{:S(2)}) collective-permute-start(bf16[192,128]{1,0:T(8,128)(2,1)S(1)} %get-tuple-element.77), channel_id=1, source_target_pairs={{0,12},{2,14},{4,8},{6,10},{8,4},{10,6},{12,0},{14,2},{16,28},{18,... | collective-permute-start | bytes 147464 | tf_op jit(solution)/shard_map/ppermute | solution.py:519
  46.8 1.0 collective-permute-done.7.refs_3_
  48.5 1.4 %collective-permute-done.10.refs_6_ = bf16[192,128]{1,0:T(8,128)(2,1)S(1)} collective-permute-done((bf16[192,128]{1,0:T(8,128)(2,1)S(1)}, bf16[192,128]{1,0:T(8,128)(2,1)S(1)}, u32[]{:S(2)}, u32[]{:S(2)}) %collective-permute-start.10) | collective-permute-done | bytes 49184 | tf_op jit(solution)/shard_map/ppermute | solution.py:519
  49.9 2.1 %collective-permute-done.11.refs_7_ = bf16[192,128]{1,0:T(8,128)(2,1)S(1)} collective-permute-done((bf16[192,128]{1,0:T(8,128)(2,1)S(1)}, bf16[192,128]{1,0:T(8,128)(2,1)S(1)}, u32[]{:S(2)}, u32[]{:S(2)}) %collective-permute-start.11) | collective-permute-done | bytes 49184 | tf_op jit(solution)/shard_map/ppermute | solution.py:519
  51.9 2.2 %shard_map.71 = bf16[32,3,48,128]{3,2,1,0:T(8,128)(2,1)} custom-call(bf16[1792,128]{1,0:T(8,128)(2,1)S(1)} %bitcast.5, bf16[192,128]{1,0:T(8,128)(2,1)S(1)} %get-tuple-element.71.refs_0_, bf16[192,128]{1,0:T(8,128)(2,1)S(1)} %collective-permute-done.5.refs_1_, bf16[192,128]{1,0:T(8,128)(2,1)S(1)} %collective-permute-done.6.refs_2_, ...), custom_call_target="tpu_custom_call" | custom-call | tf_op jit(solution)/shard_map/pallas_call | solution.py:487
  54.2 3.4 %all-to-all-start.1 = ((bf16[32,3,48,128]{3,2,1,0:T(8,128)(2,1)}), bf16[32,3,48,128]{3,2,1,0:T(8,128)(2,1)S(1)}, u32[]{:S(2)}, u32[]{:S(2)}) async-start(bf16[32,3,48,128]{3,2,1,0:T(8,128)(2,1)} %shard_map.71), calls=%async_computation.1 | async-start | bytes 2359296 | tf_op jit(solution)/shard_map/all_to_all | solution.py:540
  57.9 1.7 %collective-permute-start.14 = (bf16[768,128]{1,0:T(8,128)(2,1)S(1)}, bf16[768,128]{1,0:T(8,128)(2,1)S(1)}, u32[]{:S(2)}, u32[]{:S(2)}) collective-permute-start(bf16[768,128]{1,0:T(8,128)(2,1)S(1)} %get-tuple-element.82.refs_2_), channel_id=1, source_target_pairs={{0,1},{1,0},{2,3},{3,2},{4,5},{5,4},{6,7},{7,6},{8,9},{9,8},{10,11... | collective-permute-start | bytes 589832 | tf_op jit(solution)/shard_map/ppermute | solution.py:515
  59.6 1.3 %collective-permute-start.15 = (bf16[768,128]{1,0:T(8,128)(2,1)S(1)}, bf16[768,128]{1,0:T(8,128)(2,1)S(1)}, u32[]{:S(2)}, u32[]{:S(2)}) collective-permute-start(bf16[768,128]{1,0:T(8,128)(2,1)S(1)} %collective-permute-done.13.refs_3_), channel_id=1, source_target_pairs={{0,1},{1,0},{2,3},{3,2},{4,5},{5,4},{6,7},{7,6},{8,9},{9,8},{10,11... | collective-permute-start | bytes 589832 | tf_op jit(solution)/shard_map/ppermute | solution.py:515
  60.9 12.9 %collective-permute-done.14.refs_4_ = bf16[768,128]{1,0:T(8,128)(2,1)S(1)} collective-permute-done((bf16[768,128]{1,0:T(8,128)(2,1)S(1)}, bf16[768,128]{1,0:T(8,128)(2,1)S(1)}, u32[]{:S(2)}, u32[]{:S(2)}) %collective-permute-start.14) | collective-permute-done | bytes 196640 | tf_op jit(solution)/shard_map/ppermute | solution.py:515
  73.8 4.9 %collective-permute-done.15.refs_5_ = bf16[768,128]{1,0:T(8,128)(2,1)S(1)} collective-permute-done((bf16[768,128]{1,0:T(8,128)(2,1)S(1)}, bf16[768,128]{1,0:T(8,128)(2,1)S(1)}, u32[]{:S(2)}, u32[]{:S(2)}) %collective-permute-start.15) | collective-permute-done | bytes 196640 | tf_op jit(solution)/shard_map/ppermute | solution.py:515
  78.6 9.0 %all-to-all-done.1.refs_6_ = bf16[32,3,48,128]{3,2,1,0:T(8,128)(2,1)S(1)} async-done(((bf16[32,3,48,128]{3,2,1,0:T(8,128)(2,1)}), bf16[32,3,48,128]{3,2,1,0:T(8,128)(2,1)S(1)}, u32[]{:S(2)}, u32[]{:S(2)}) %all-to-all-start.1) | async-done | bytes 1179680 | tf_op jit(solution)/shard_map/all_to_all | solution.py:540
  87.6 10.2 %shard_map.72.refs_0_ = f32[1,16,128]{2,1,0:T(8,128)S(1)} custom-call(s32[192]{0:T(256)S(1)} %copy-done.5, bf16[1536,128]{1,0:T(8,128)(2,1)S(1)} %get-tuple-element.69.refs_0_, bf16[1536,128]{1,0:T(8,128)(2,1)S(1)} %collective-permute-done.12.refs_1_, bf16[768,128]{1,0:T(8,128)(2,1)S(1)} %get-tuple-element.82.refs_2_, ...), custom_call_target="tpu_custom_call" | custom-call | flops 3623878656 | bytes 786432 | tf_op jit(solution)/shard_map/pallas_call | solution.py:254
  97.8 1.0 %collective-permute-start.16 = (f32[1,16,128]{2,1,0:T(8,128)S(1)}, f32[1,16,128]{2,1,0:T(8,128)S(1)}, u32[]{:S(2)}, u32[]{:S(2)}) collective-permute-start(f32[1,16,128]{2,1,0:T(8,128)S(1)} %shard_map.72.refs_0_), channel_id=1, source_target_pairs={{0,1},{1,0},{2,3},{3,2},{4,5},{5,4},{6,7},{7,6},{8,9},{9,8},{10,11... | collective-permute-start | bytes 24584 | tf_op jit(solution)/shard_map/ppermute | solution.py:544
  98.8 2.7 %collective-permute-done.16.refs_1_ = f32[1,16,128]{2,1,0:T(8,128)S(1)} collective-permute-done((f32[1,16,128]{2,1,0:T(8,128)S(1)}, f32[1,16,128]{2,1,0:T(8,128)S(1)}, u32[]{:S(2)}, u32[]{:S(2)}) %collective-permute-start.16) | collective-permute-done | bytes 8224 | tf_op jit(solution)/shard_map/ppermute | solution.py:544
  101.5 1.3 %shard_map.73 = f32[12,12,12]{2,1,0:T(8,128)} custom-call(s32[3]{0:T(128)S(1)} %copy-done.2, s32[12]{0:T(128)S(1)} %copy-done.3, f32[1,16,128]{2,1,0:T(8,128)S(1)} %shard_map.72.refs_0_, f32[1,16,128]{2,1,0:T(8,128)S(1)} %collective-permute-done.16.refs_1_), custom_call_target="tpu_custom_call" | custom-call | tf_op jit(solution)/shard_map/pallas_call | solution.py:281
  (29 shorter events, 4.3 us)
Async XLA Ops:
  0.0 0.9 copy-start
  0.9 7.9 %copy-start.1 = (bf16[512,128]{1,0:T(8,128)(2,1)S(1)}, bf16[512,128]{1,0:T(8,128)(2,1)}, u32[]{:S(2)}) copy-start(bf16[512,128]{1,0:T(8,128)(2,1)} %weight_ref.4) | copy-start | bytes 393220
  2.8 11.7 %collective-permute-start = (bf16[768,128]{1,0:T(8,128)(2,1)S(1)}, bf16[768,128]{1,0:T(8,128)(2,1)S(1)}, u32[]{:S(2)}, u32[]{:S(2)}) collective-permute-start(bf16[768,128]{1,0:T(8,128)(2,1)S(1)} %get-tuple-element.54), channel_id=1, source_target_pairs={{0,1},{1,0},{2,3},{3,2},{4,5},{5,4},{6,7},{7,6},{8,9},{9,8},{10,11... | collective-permute-start | bytes 589832 | tf_op jit(solution)/shard_map/ppermute | solution.py:515
  5.9 9.1 %collective-permute-start.1 = (bf16[768,128]{1,0:T(8,128)(2,1)S(1)}, bf16[768,128]{1,0:T(8,128)(2,1)S(1)}, u32[]{:S(2)}, u32[]{:S(2)}) collective-permute-start(bf16[768,128]{1,0:T(8,128)(2,1)S(1)} %get-tuple-element.55), channel_id=1, source_target_pairs={{0,1},{1,0},{2,3},{3,2},{4,5},{5,4},{6,7},{7,6},{8,9},{9,8},{10,11... | collective-permute-start | bytes 589832 | tf_op jit(solution)/shard_map/ppermute | solution.py:515
  12.6 2.4 %copy-start.4 = (s32[6]{0:T(128)S(1)}, s32[6]{0:T(128)}, u32[]{:S(2)}) copy-start(s32[6]{0:T(128)} %get-tuple-element.53.sel_ref) | copy-start | bytes 76
  16.6 35.3 %all-to-all-start = ((bf16[16,112,128]{2,1,0:T(8,128)(2,1)}), bf16[16,112,128]{2,1,0:T(8,128)(2,1)S(1)}, u32[]{:S(2)}, u32[]{:S(2)}) async-start(bf16[16,112,128]{2,1,0:T(8,128)(2,1)} %bitcast.3), calls=%async_computation | async-start | bytes 917504 | tf_op jit(solution)/shard_map/all_to_all | solution.py:533
  22.7 7.8 %collective-permute-start.2 = (bf16[768,128]{1,0:T(8,128)(2,1)S(1)}, bf16[768,128]{1,0:T(8,128)(2,1)S(1)}, u32[]{:S(2)}, u32[]{:S(2)}) collective-permute-start(bf16[768,128]{1,0:T(8,128)(2,1)S(1)} %get-tuple-element.64), channel_id=1, source_target_pairs={{0,1},{1,0},{2,3},{3,2},{4,5},{5,4},{6,7},{7,6},{8,9},{9,8},{10,11... | collective-permute-start | bytes 589832 | tf_op jit(solution)/shard_map/ppermute | solution.py:515
  24.3 9.3 %collective-permute-start.3 = (bf16[768,128]{1,0:T(8,128)(2,1)S(1)}, bf16[768,128]{1,0:T(8,128)(2,1)S(1)}, u32[]{:S(2)}, u32[]{:S(2)}) collective-permute-start(bf16[768,128]{1,0:T(8,128)(2,1)S(1)} %get-tuple-element.65), channel_id=1, source_target_pairs={{0,3},{1,2},{2,1},{3,0},{4,7},{5,6},{6,5},{7,4},{8,11},{9,10},{10,... | collective-permute-start | bytes 589832 | tf_op jit(solution)/shard_map/ppermute | solution.py:515
  24.5 9.1 %collective-permute-start.4 = (bf16[768,128]{1,0:T(8,128)(2,1)S(1)}, bf16[768,128]{1,0:T(8,128)(2,1)S(1)}, u32[]{:S(2)}, u32[]{:S(2)}) collective-permute-start(bf16[768,128]{1,0:T(8,128)(2,1)S(1)} %get-tuple-element.67), channel_id=1, source_target_pairs={{0,2},{1,3},{2,0},{3,1},{4,6},{5,7},{6,4},{7,5},{8,10},{9,11},{10,... | collective-permute-start | bytes 589832 | tf_op jit(solution)/shard_map/ppermute | solution.py:515
  33.9 20.3 %collective-permute-start.12 = (bf16[1536,128]{1,0:T(8,128)(2,1)S(1)}, bf16[1536,128]{1,0:T(8,128)(2,1)S(1)}, u32[]{:S(2)}, u32[]{:S(2)}) collective-permute-start(bf16[1536,128]{1,0:T(8,128)(2,1)S(1)} %get-tuple-element.69.refs_0_), channel_id=1, source_target_pairs={{0,1},{1,0},{2,3},{3,2},{4,5},{5,4},{6,7},{7,6},{8,9},{9,8},{10,11... | collective-permute-start | bytes 1179656 | tf_op jit(solution)/shard_map/ppermute | solution.py:515
  35.5 7.1 %collective-permute-start.5 = (bf16[192,128]{1,0:T(8,128)(2,1)S(1)}, bf16[192,128]{1,0:T(8,128)(2,1)S(1)}, u32[]{:S(2)}, u32[]{:S(2)}) collective-permute-start(bf16[192,128]{1,0:T(8,128)(2,1)S(1)} %get-tuple-element.72), channel_id=1, source_target_pairs={{0,16},{2,18},{4,20},{6,22},{8,24},{10,26},{12,28},{14,30},{16,0},... | collective-permute-start | bytes 147464 | tf_op jit(solution)/shard_map/ppermute | solution.py:519
  37.8 6.2 %collective-permute-start.6 = (bf16[192,128]{1,0:T(8,128)(2,1)S(1)}, bf16[192,128]{1,0:T(8,128)(2,1)S(1)}, u32[]{:S(2)}, u32[]{:S(2)}) collective-permute-start(bf16[192,128]{1,0:T(8,128)(2,1)S(1)} %get-tuple-element.73), channel_id=1, source_target_pairs={{0,24},{2,26},{4,28},{6,30},{8,16},{10,18},{12,20},{14,22},{16,8},... | collective-permute-start | bytes 147464 | tf_op jit(solution)/shard_map/ppermute | solution.py:519
  39.3 8.6 %collective-permute-start.7 = (bf16[192,128]{1,0:T(8,128)(2,1)S(1)}, bf16[192,128]{1,0:T(8,128)(2,1)S(1)}, u32[]{:S(2)}, u32[]{:S(2)}) collective-permute-start(bf16[192,128]{1,0:T(8,128)(2,1)S(1)} %get-tuple-element.74), channel_id=1, source_target_pairs={{0,20},{2,22},{4,16},{6,18},{8,28},{10,30},{12,24},{14,26},{16,4},... | collective-permute-start | bytes 147464 | tf_op jit(solution)/shard_map/ppermute | solution.py:519
  41.6 6.9 %collective-permute-start.8 = (bf16[192,128]{1,0:T(8,128)(2,1)S(1)}, bf16[192,128]{1,0:T(8,128)(2,1)S(1)}, u32[]{:S(2)}, u32[]{:S(2)}) collective-permute-start(bf16[192,128]{1,0:T(8,128)(2,1)S(1)} %get-tuple-element.75), channel_id=1, source_target_pairs={{0,28},{2,30},{4,24},{6,26},{8,20},{10,22},{12,16},{14,18},{16,12}... | collective-permute-start | bytes 147464 | tf_op jit(solution)/shard_map/ppermute | solution.py:519
  42.5 6.0 %collective-permute-start.9 = (bf16[192,128]{1,0:T(8,128)(2,1)S(1)}, bf16[192,128]{1,0:T(8,128)(2,1)S(1)}, u32[]{:S(2)}, u32[]{:S(2)}) collective-permute-start(bf16[192,128]{1,0:T(8,128)(2,1)S(1)} %get-tuple-element.76), channel_id=1, source_target_pairs={{0,8},{2,10},{4,12},{6,14},{8,0},{10,2},{12,4},{14,6},{16,24},{18,... | collective-permute-start | bytes 147464 | tf_op jit(solution)/shard_map/ppermute | solution.py:519
  44.0 5.9 %collective-permute-start.10 = (bf16[192,128]{1,0:T(8,128)(2,1)S(1)}, bf16[192,128]{1,0:T(8,128)(2,1)S(1)}, u32[]{:S(2)}, u32[]{:S(2)}) collective-permute-start(bf16[192,128]{1,0:T(8,128)(2,1)S(1)} %get-tuple-element.77), channel_id=1, source_target_pairs={{0,12},{2,14},{4,8},{6,10},{8,4},{10,6},{12,0},{14,2},{16,28},{18,... | collective-permute-start | bytes 147464 | tf_op jit(solution)/shard_map/ppermute | solution.py:519
  47.8 4.1 %collective-permute-start.11 = (bf16[192,128]{1,0:T(8,128)(2,1)S(1)}, bf16[192,128]{1,0:T(8,128)(2,1)S(1)}, u32[]{:S(2)}, u32[]{:S(2)}) collective-permute-start(bf16[192,128]{1,0:T(8,128)(2,1)S(1)} %get-tuple-element.78), channel_id=1, source_target_pairs={{0,4},{2,6},{4,0},{6,2},{8,12},{10,14},{12,8},{14,10},{16,20},{18,... | collective-permute-start | bytes 147464 | tf_op jit(solution)/shard_map/ppermute | solution.py:519
  54.1 33.4 %copy-start.5 = (s32[192]{0:T(256)S(1)}, s32[192]{0:T(256)}, u32[]{:S(2)}) copy-start(s32[192]{0:T(256)} %get-tuple-element.46.table_ref) | copy-start | bytes 2308
  54.2 33.4 %all-to-all-start.1 = ((bf16[32,3,48,128]{3,2,1,0:T(8,128)(2,1)}), bf16[32,3,48,128]{3,2,1,0:T(8,128)(2,1)S(1)}, u32[]{:S(2)}, u32[]{:S(2)}) async-start(bf16[32,3,48,128]{3,2,1,0:T(8,128)(2,1)} %shard_map.71), calls=%async_computation.1 | async-start | bytes 2359296 | tf_op jit(solution)/shard_map/all_to_all | solution.py:540
  57.6 2.0 %collective-permute-start.13 = (bf16[768,128]{1,0:T(8,128)(2,1)S(1)}, bf16[768,128]{1,0:T(8,128)(2,1)S(1)}, u32[]{:S(2)}, u32[]{:S(2)}) collective-permute-start(bf16[768,128]{1,0:T(8,128)(2,1)S(1)} %get-tuple-element.83), channel_id=1, source_target_pairs={{0,2},{1,3},{2,0},{3,1},{4,6},{5,7},{6,4},{7,5},{8,10},{9,11},{10,... | collective-permute-start | bytes 589832 | tf_op jit(solution)/shard_map/ppermute | solution.py:515
  57.9 15.9 %collective-permute-start.14 = (bf16[768,128]{1,0:T(8,128)(2,1)S(1)}, bf16[768,128]{1,0:T(8,128)(2,1)S(1)}, u32[]{:S(2)}, u32[]{:S(2)}) collective-permute-start(bf16[768,128]{1,0:T(8,128)(2,1)S(1)} %get-tuple-element.82.refs_2_), channel_id=1, source_target_pairs={{0,1},{1,0},{2,3},{3,2},{4,5},{5,4},{6,7},{7,6},{8,9},{9,8},{10,11... | collective-permute-start | bytes 589832 | tf_op jit(solution)/shard_map/ppermute | solution.py:515
  59.6 19.0 %collective-permute-start.15 = (bf16[768,128]{1,0:T(8,128)(2,1)S(1)}, bf16[768,128]{1,0:T(8,128)(2,1)S(1)}, u32[]{:S(2)}, u32[]{:S(2)}) collective-permute-start(bf16[768,128]{1,0:T(8,128)(2,1)S(1)} %collective-permute-done.13.refs_3_), channel_id=1, source_target_pairs={{0,1},{1,0},{2,3},{3,2},{4,5},{5,4},{6,7},{7,6},{8,9},{9,8},{10,11... | collective-permute-start | bytes 589832 | tf_op jit(solution)/shard_map/ppermute | solution.py:515
  87.6 13.9 %copy-start.2 = (s32[3]{0:T(128)S(1)}, s32[3]{0:T(128)}, u32[]{:S(2)}) copy-start(s32[3]{0:T(128)} %pad_add_fusion.places_ref.where_ref) | copy-start | bytes 40
  87.6 13.9 %copy-start.3 = (s32[12]{0:T(128)S(1)}, s32[12]{0:T(128)}, u32[]{:S(2)}) copy-start(s32[12]{0:T(128)} %get-tuple-element.45.pairs_ref) | copy-start | bytes 148
  97.8 3.7 %collective-permute-start.16 = (f32[1,16,128]{2,1,0:T(8,128)S(1)}, f32[1,16,128]{2,1,0:T(8,128)S(1)}, u32[]{:S(2)}, u32[]{:S(2)}) collective-permute-start(f32[1,16,128]{2,1,0:T(8,128)S(1)} %shard_map.72.refs_0_), channel_id=1, source_target_pairs={{0,1},{1,0},{2,3},{3,2},{4,5},{5,4},{6,7},{7,6},{8,9},{9,8},{10,11... | collective-permute-start | bytes 24584 | tf_op jit(solution)/shard_map/ppermute | solution.py:544

commit v11 on v10

--- a/solution.py
+++ b/solution.py
@@ -528,8 +528,9 @@
     early = split(0, flat, weight, 0)
     own, aside = split(0, flat, weight, CHUNK)
     *early, own, aside = lax.optimization_barrier((*early, own, aside))
+    y, cy, c = near(far[0], 2), near(far[1], 3), near(aside, 1)
+    *crossed, y, cy, c = lax.optimization_barrier((*crossed, y, cy, c))
     send, early_query = early_unit(sel, *crossed, *early, size)
-    y, cy, c = near(far[0], 2), near(far[1], 3), near(aside, 1)
     early_spread = lax.all_to_all(send, "wide", 0, 0, tiled=True)
     *sends, own, other = late_unit(y, cy, own, c, size)
     early_query, sends[0] = lax.optimization_barrier((early_query, sends[0]))

time: 103 us -> 108 us (1.049)
  waiting for transfers between devices: 43.7 us -> 49.1 us
    ppermute x7, waiting for transfers between devices: 5.17 us -> 13.8 us  [along(): return lax.ppermute(array, 'wide', [(i, i ^ flip) for i in range(16)])]
    ppermute x9, waiting for transfers between devices: 26.9 us -> 23.7 us  [near(): lax.ppermute(array, ('wide', 'narrow'), [(i, i ^ flip) for i in range(32)])]
  transfers between devices with their start and end apart: 19 -> 19, of which waited for: 12 -> 11; matrix products, arithmetic and copies ran while one was open for 1% -> 1% of each run, Pallas kernels for 10% -> 10%
where the time goes in v11:
time: 108 us
  waiting for transfers between devices  49.1 us (45%)
  starting transfers between devices  31.4 us (29%)
  Pallas kernels  25.3 us (23%)
    ppermute x9, waiting for transfers between devices, near(): lax.ppermute(array, ('wide', 'narrow'), [(i, i ^ flip) for i in range(32)])  23.7 us
    ppermute x7, waiting for transfers between devices, along(): return lax.ppermute(array, 'wide', [(i, i ^ flip) for i in range(16)])  13.8 us
    ppermute x7, starting transfers between devices, along(): return lax.ppermute(array, 'wide', [(i, i ^ flip) for i in range(16)])  11 us
    ppermute x9, starting transfers between devices, near(): lax.ppermute(array, ('wide', 'narrow'), [(i, i ^ flip) for i in range(32)])  10.3 us
    pallas_call x1, Pallas kernels, score(): pl.pallas_call(functools.partial(score_kernel, length, parts), out_shape=...  10.2 us
    all_to_all x1, waiting for transfers between devices, local_cube(): incoming = lax.all_to_all(outgoing, ('narrow', 'wide'), 0, 0, tiled=True)  8.97 us
    pallas_call x4, Pallas kernels, split(): pl.pallas_call(functools.partial(split_kernel, first, over), out_shape=(j...  7.57 us
    all_to_all x1, starting transfers between devices, local_cube(): early_spread = lax.all_to_all(send, 'wide', 0, 0, tiled=True)  6.3 us
  transfers between devices with their start and end apart: 19, of which 11 were waited for; matrix products, arithmetic and copies ran while one was open for 1% of the time, Pallas kernels for 10%

profile of v11, /device:TPU:0, one launch (start us, length us, event | category | flops | bytes accessed | tf_op | source)
XLA Modules:
  0.0 107.5 jit_solution(12429058744318761572)
XLA Ops:
  0.0 0.9 copy-done
  0.9 1.9 %shard_map.65 = (bf16[768,128]{1,0:T(8,128)(2,1)S(1)}, bf16[768,128]{1,0:T(8,128)(2,1)S(1)}) custom-call(bf16[4,1536,512]{2,1,0:T(8,128)(2,1)} %bitcast.6, bf16[512,128]{1,0:T(8,128)(2,1)S(1)} %copy-done), custom_call_target="tpu_custom_call" | custom-call | flops 201326592 | bytes 1572864 | tf_op jit(solution)/shard_map/pallas_call | solution.py:370
  2.8 3.0 %collective-permute-start = (bf16[768,128]{1,0:T(8,128)(2,1)S(1)}, bf16[768,128]{1,0:T(8,128)(2,1)S(1)}, u32[]{:S(2)}, u32[]{:S(2)}) collective-permute-start(bf16[768,128]{1,0:T(8,128)(2,1)S(1)} %get-tuple-element.59), channel_id=1, source_target_pairs={{0,1},{1,0},{2,3},{3,2},{4,5},{5,4},{6,7},{7,6},{8,9},{9,8},{10,11... | collective-permute-start | bytes 589832 | tf_op jit(solution)/shard_map/ppermute | solution.py:515
  5.9 1.9 %shard_map.66 = (bf16[768,128]{1,0:T(8,128)(2,1)S(1)}, bf16[768,128]{1,0:T(8,128)(2,1)S(1)}) custom-call(bf16[4,1536,512]{2,1,0:T(8,128)(2,1)} %bitcast.7, bf16[512,128]{1,0:T(8,128)(2,1)S(1)} %copy-done.1), custom_call_target="tpu_custom_call" | custom-call | flops 201326592 | bytes 1572864 | tf_op jit(solution)/shard_map/pallas_call | solution.py:370
  8.5 2.2 %shard_map.64 = (s32[6]{0:T(128)}, s32[192]{0:T(256)}, s32[12]{0:T(128)}) custom-call(s32[3]{0:T(128)} %pad_add_fusion.places_ref.where_ref, s32[12]{0:T(128)} %cand_ref.1, s32[12]{0:T(128)} %query_block_ref.1, s32[12]{0:T(128)} %valid_ref.1, s32[768]{0:T(1024)} %lengths_ref.1), custom_call_target="tpu_custom_call" | custom-call | tf_op jit(solution)/shard_map/pallas_call | solution.py:75
  10.7 2.0 %collective-permute-start.2 = (bf16[768,128]{1,0:T(8,128)(2,1)S(1)}, bf16[768,128]{1,0:T(8,128)(2,1)S(1)}, u32[]{:S(2)}, u32[]{:S(2)}) collective-permute-start(bf16[768,128]{1,0:T(8,128)(2,1)S(1)} %get-tuple-element.61), channel_id=1, source_target_pairs={{0,1},{1,0},{2,3},{3,2},{4,5},{5,4},{6,7},{7,6},{8,9},{9,8},{10,11... | collective-permute-start | bytes 589832 | tf_op jit(solution)/shard_map/ppermute | solution.py:515
  12.7 1.9 %shard_map.68 = (bf16[768,128]{1,0:T(8,128)(2,1)S(1)}, bf16[768,128]{1,0:T(8,128)(2,1)S(1)}) custom-call(bf16[4,1536,512]{2,1,0:T(8,128)(2,1)} %bitcast.8, bf16[512,128]{1,0:T(8,128)(2,1)S(1)} %copy-done.1), custom_call_target="tpu_custom_call" | custom-call | flops 201326592 | bytes 1572864 | tf_op jit(solution)/shard_map/pallas_call | solution.py:370
  14.6 1.9 %shard_map.67 = (bf16[768,128]{1,0:T(8,128)(2,1)S(1)}, bf16[768,128]{1,0:T(8,128)(2,1)S(1)}) custom-call(bf16[4,1536,512]{2,1,0:T(8,128)(2,1)} %bitcast.9, bf16[512,128]{1,0:T(8,128)(2,1)S(1)} %copy-done.1), custom_call_target="tpu_custom_call" | custom-call | flops 201326592 | bytes 1572864 | tf_op jit(solution)/shard_map/pallas_call | solution.py:370
  16.8 3.3 %collective-permute-done.2.y_ref = bf16[768,128]{1,0:T(8,128)(2,1)S(1)} collective-permute-done((bf16[768,128]{1,0:T(8,128)(2,1)S(1)}, bf16[768,128]{1,0:T(8,128)(2,1)S(1)}, u32[]{:S(2)}, u32[]{:S(2)}) %collective-permute-start.2) | collective-permute-done | bytes 196640 | tf_op jit(solution)/shard_map/ppermute | solution.py:515
  20.0 2.6 %collective-permute-done.3.cy_ref = bf16[768,128]{1,0:T(8,128)(2,1)S(1)} collective-permute-done((bf16[768,128]{1,0:T(8,128)(2,1)S(1)}, bf16[768,128]{1,0:T(8,128)(2,1)S(1)}, u32[]{:S(2)}, u32[]{:S(2)}) %collective-permute-start.3) | collective-permute-done | bytes 196640 | tf_op jit(solution)/shard_map/ppermute | solution.py:515
  22.7 1.6 %shard_map.69 = (bf16[1792,128]{1,0:T(8,128)(2,1)}, bf16[1536,128]{1,0:T(8,128)(2,1)S(1)}) custom-call(s32[6]{0:T(128)S(1)} %copy-done.4, bf16[768,128]{1,0:T(8,128)(2,1)S(1)} %collective-permute-done.y_ref, bf16[768,128]{1,0:T(8,128)(2,1)S(1)} %collective-permute-done.1.y_flip_ref, bf16[768,128]{1,0:T(8,128)(2,1)S(1)} %get-tuple-element.71.own_ref, ...), custom_call_target="tpu_custom_call" | custom-call | tf_op jit(solution)/shard_map/pallas_call | solution.py:416
  24.3 6.3 %all-to-all-start = ((bf16[16,112,128]{2,1,0:T(8,128)(2,1)}), bf16[16,112,128]{2,1,0:T(8,128)(2,1)S(1)}, u32[]{:S(2)}, u32[]{:S(2)}) async-start(bf16[16,112,128]{2,1,0:T(8,128)(2,1)} %bitcast.3), calls=%async_computation | async-start | bytes 917504 | tf_op jit(solution)/shard_map/all_to_all | solution.py:534
  30.9 1.6 %collective-permute-start.12 = (bf16[1536,128]{1,0:T(8,128)(2,1)S(1)}, bf16[1536,128]{1,0:T(8,128)(2,1)S(1)}, u32[]{:S(2)}, u32[]{:S(2)}) collective-permute-start(bf16[1536,128]{1,0:T(8,128)(2,1)S(1)} %get-tuple-element.79.refs_0_), channel_id=1, source_target_pairs={{0,1},{1,0},{2,3},{3,2},{4,5},{5,4},{6,7},{7,6},{8,9},{9,8},{10,11... | collective-permute-start | bytes 1179656 | tf_op jit(solution)/shard_map/ppermute | solution.py:515
  32.5 2.8 %collective-permute-start.5 = (bf16[192,128]{1,0:T(8,128)(2,1)S(1)}, bf16[192,128]{1,0:T(8,128)(2,1)S(1)}, u32[]{:S(2)}, u32[]{:S(2)}) collective-permute-start(bf16[192,128]{1,0:T(8,128)(2,1)S(1)} %get-tuple-element.82), channel_id=1, source_target_pairs={{0,16},{2,18},{4,20},{6,22},{8,24},{10,26},{12,28},{14,30},{16,0},... | collective-permute-start | bytes 147464 | tf_op jit(solution)/shard_map/ppermute | solution.py:519
  35.3 1.5 %collective-permute-start.6 = (bf16[192,128]{1,0:T(8,128)(2,1)S(1)}, bf16[192,128]{1,0:T(8,128)(2,1)S(1)}, u32[]{:S(2)}, u32[]{:S(2)}) collective-permute-start(bf16[192,128]{1,0:T(8,128)(2,1)S(1)} %get-tuple-element.83), channel_id=1, source_target_pairs={{0,24},{2,26},{4,28},{6,30},{8,16},{10,18},{12,20},{14,22},{16,8},... | collective-permute-start | bytes 147464 | tf_op jit(solution)/shard_map/ppermute | solution.py:519
  36.7 2.4 %collective-permute-start.7 = (bf16[192,128]{1,0:T(8,128)(2,1)S(1)}, bf16[192,128]{1,0:T(8,128)(2,1)S(1)}, u32[]{:S(2)}, u32[]{:S(2)}) collective-permute-start(bf16[192,128]{1,0:T(8,128)(2,1)S(1)} %get-tuple-element.84), channel_id=1, source_target_pairs={{0,20},{2,22},{4,16},{6,18},{8,28},{10,30},{12,24},{14,26},{16,4},... | collective-permute-start | bytes 147464 | tf_op jit(solution)/shard_map/ppermute | solution.py:519
  39.1 0.9 collective-permute-start.8
  40.0 10.2 %collective-permute-done.5.refs_1_ = bf16[192,128]{1,0:T(8,128)(2,1)S(1)} collective-permute-done((bf16[192,128]{1,0:T(8,128)(2,1)S(1)}, bf16[192,128]{1,0:T(8,128)(2,1)S(1)}, u32[]{:S(2)}, u32[]{:S(2)}) %collective-permute-start.5) | collective-permute-done | bytes 49184 | tf_op jit(solution)/shard_map/ppermute | solution.py:519
  50.2 2.9 %collective-permute-start.10 = (bf16[192,128]{1,0:T(8,128)(2,1)S(1)}, bf16[192,128]{1,0:T(8,128)(2,1)S(1)}, u32[]{:S(2)}, u32[]{:S(2)}) collective-permute-start(bf16[192,128]{1,0:T(8,128)(2,1)S(1)} %get-tuple-element.87), channel_id=1, source_target_pairs={{0,12},{2,14},{4,8},{6,10},{8,4},{10,6},{12,0},{14,2},{16,28},{18,... | collective-permute-start | bytes 147464 | tf_op jit(solution)/shard_map/ppermute | solution.py:519
  54.3 1.5 %collective-permute-done.10.refs_6_ = bf16[192,128]{1,0:T(8,128)(2,1)S(1)} collective-permute-done((bf16[192,128]{1,0:T(8,128)(2,1)S(1)}, bf16[192,128]{1,0:T(8,128)(2,1)S(1)}, u32[]{:S(2)}, u32[]{:S(2)}) %collective-permute-start.10) | collective-permute-done | bytes 49184 | tf_op jit(solution)/shard_map/ppermute | solution.py:519
  55.8 1.5 %collective-permute-done.11.refs_7_ = bf16[192,128]{1,0:T(8,128)(2,1)S(1)} collective-permute-done((bf16[192,128]{1,0:T(8,128)(2,1)S(1)}, bf16[192,128]{1,0:T(8,128)(2,1)S(1)}, u32[]{:S(2)}, u32[]{:S(2)}) %collective-permute-start.11) | collective-permute-done | bytes 49184 | tf_op jit(solution)/shard_map/ppermute | solution.py:519
  57.3 2.2 %shard_map.71 = bf16[32,3,48,128]{3,2,1,0:T(8,128)(2,1)} custom-call(bf16[1792,128]{1,0:T(8,128)(2,1)S(1)} %bitcast.5, bf16[192,128]{1,0:T(8,128)(2,1)S(1)} %get-tuple-element.81.refs_0_, bf16[192,128]{1,0:T(8,128)(2,1)S(1)} %collective-permute-done.5.refs_1_, bf16[192,128]{1,0:T(8,128)(2,1)S(1)} %collective-permute-done.6.refs_2_, ...), custom_call_target="tpu_custom_call" | custom-call | tf_op jit(solution)/shard_map/pallas_call | solution.py:487
  59.5 2.8 %all-to-all-start.1 = ((bf16[32,3,48,128]{3,2,1,0:T(8,128)(2,1)}), bf16[32,3,48,128]{3,2,1,0:T(8,128)(2,1)S(1)}, u32[]{:S(2)}, u32[]{:S(2)}) async-start(bf16[32,3,48,128]{3,2,1,0:T(8,128)(2,1)} %shard_map.71), calls=%async_computation.1 | async-start | bytes 2359296 | tf_op jit(solution)/shard_map/all_to_all | solution.py:541
  62.6 1.7 %collective-permute-start.14 = (bf16[768,128]{1,0:T(8,128)(2,1)S(1)}, bf16[768,128]{1,0:T(8,128)(2,1)S(1)}, u32[]{:S(2)}, u32[]{:S(2)}) collective-permute-start(bf16[768,128]{1,0:T(8,128)(2,1)S(1)} %get-tuple-element.92.refs_2_), channel_id=1, source_target_pairs={{0,1},{1,0},{2,3},{3,2},{4,5},{5,4},{6,7},{7,6},{8,9},{9,8},{10,11... | collective-permute-start | bytes 589832 | tf_op jit(solution)/shard_map/ppermute | solution.py:515
  64.3 1.3 %collective-permute-start.15 = (bf16[768,128]{1,0:T(8,128)(2,1)S(1)}, bf16[768,128]{1,0:T(8,128)(2,1)S(1)}, u32[]{:S(2)}, u32[]{:S(2)}) collective-permute-start(bf16[768,128]{1,0:T(8,128)(2,1)S(1)} %collective-permute-done.13.refs_3_), channel_id=1, source_target_pairs={{0,1},{1,0},{2,3},{3,2},{4,5},{5,4},{6,7},{7,6},{8,9},{9,8},{10,11... | collective-permute-start | bytes 589832 | tf_op jit(solution)/shard_map/ppermute | solution.py:515
  65.6 12.9 %collective-permute-done.14.refs_4_ = bf16[768,128]{1,0:T(8,128)(2,1)S(1)} collective-permute-done((bf16[768,128]{1,0:T(8,128)(2,1)S(1)}, bf16[768,128]{1,0:T(8,128)(2,1)S(1)}, u32[]{:S(2)}, u32[]{:S(2)}) %collective-permute-start.14) | collective-permute-done | bytes 196640 | tf_op jit(solution)/shard_map/ppermute | solution.py:515
  78.5 4.9 %collective-permute-done.15.refs_5_ = bf16[768,128]{1,0:T(8,128)(2,1)S(1)} collective-permute-done((bf16[768,128]{1,0:T(8,128)(2,1)S(1)}, bf16[768,128]{1,0:T(8,128)(2,1)S(1)}, u32[]{:S(2)}, u32[]{:S(2)}) %collective-permute-start.15) | collective-permute-done | bytes 196640 | tf_op jit(solution)/shard_map/ppermute | solution.py:515
  83.3 9.0 %all-to-all-done.1.refs_6_ = bf16[32,3,48,128]{3,2,1,0:T(8,128)(2,1)S(1)} async-done(((bf16[32,3,48,128]{3,2,1,0:T(8,128)(2,1)}), bf16[32,3,48,128]{3,2,1,0:T(8,128)(2,1)S(1)}, u32[]{:S(2)}, u32[]{:S(2)}) %all-to-all-start.1) | async-done | bytes 1179680 | tf_op jit(solution)/shard_map/all_to_all | solution.py:541
  92.3 10.2 %shard_map.72.refs_0_ = f32[1,16,128]{2,1,0:T(8,128)S(1)} custom-call(s32[192]{0:T(256)S(1)} %copy-done.5, bf16[1536,128]{1,0:T(8,128)(2,1)S(1)} %get-tuple-element.79.refs_0_, bf16[1536,128]{1,0:T(8,128)(2,1)S(1)} %collective-permute-done.12.refs_1_, bf16[768,128]{1,0:T(8,128)(2,1)S(1)} %get-tuple-element.92.refs_2_, ...), custom_call_target="tpu_custom_call" | custom-call | flops 3623878656 | bytes 786432 | tf_op jit(solution)/shard_map/pallas_call | solution.py:254
  102.5 1.0 collective-permute-start.16
  103.6 2.7 %collective-permute-done.16.refs_1_ = f32[1,16,128]{2,1,0:T(8,128)S(1)} collective-permute-done((f32[1,16,128]{2,1,0:T(8,128)S(1)}, f32[1,16,128]{2,1,0:T(8,128)S(1)}, u32[]{:S(2)}, u32[]{:S(2)}) %collective-permute-start.16) | collective-permute-done | bytes 8224 | tf_op jit(solution)/shard_map/ppermute | solution.py:545
  106.3 1.3 %shard_map.73 = f32[12,12,12]{2,1,0:T(8,128)} custom-call(s32[3]{0:T(128)S(1)} %copy-done.2, s32[12]{0:T(128)S(1)} %copy-done.3, f32[1,16,128]{2,1,0:T(8,128)S(1)} %shard_map.72.refs_0_, f32[1,16,128]{2,1,0:T(8,128)S(1)} %collective-permute-done.16.refs_1_), custom_call_target="tpu_custom_call" | custom-call | tf_op jit(solution)/shard_map/pallas_call | solution.py:281
  (29 shorter events, 2.8 us)
Async XLA Ops:
  0.0 0.9 copy-start
  0.9 5.0 %copy-start.1 = (bf16[512,128]{1,0:T(8,128)(2,1)S(1)}, bf16[512,128]{1,0:T(8,128)(2,1)}, u32[]{:S(2)}) copy-start(bf16[512,128]{1,0:T(8,128)(2,1)} %weight_ref.4) | copy-start | bytes 393220
  2.8 13.9 %collective-permute-start = (bf16[768,128]{1,0:T(8,128)(2,1)S(1)}, bf16[768,128]{1,0:T(8,128)(2,1)S(1)}, u32[]{:S(2)}, u32[]{:S(2)}) collective-permute-start(bf16[768,128]{1,0:T(8,128)(2,1)S(1)} %get-tuple-element.59), channel_id=1, source_target_pairs={{0,1},{1,0},{2,3},{3,2},{4,5},{5,4},{6,7},{7,6},{8,9},{9,8},{10,11... | collective-permute-start | bytes 589832 | tf_op jit(solution)/shard_map/ppermute | solution.py:515
  5.9 10.9 %collective-permute-start.1 = (bf16[768,128]{1,0:T(8,128)(2,1)S(1)}, bf16[768,128]{1,0:T(8,128)(2,1)S(1)}, u32[]{:S(2)}, u32[]{:S(2)}) collective-permute-start(bf16[768,128]{1,0:T(8,128)(2,1)S(1)} %get-tuple-element.60), channel_id=1, source_target_pairs={{0,1},{1,0},{2,3},{3,2},{4,5},{5,4},{6,7},{7,6},{8,9},{9,8},{10,11... | collective-permute-start | bytes 589832 | tf_op jit(solution)/shard_map/ppermute | solution.py:515
  10.7 9.3 %collective-permute-start.2 = (bf16[768,128]{1,0:T(8,128)(2,1)S(1)}, bf16[768,128]{1,0:T(8,128)(2,1)S(1)}, u32[]{:S(2)}, u32[]{:S(2)}) collective-permute-start(bf16[768,128]{1,0:T(8,128)(2,1)S(1)} %get-tuple-element.61), channel_id=1, source_target_pairs={{0,1},{1,0},{2,3},{3,2},{4,5},{5,4},{6,7},{7,6},{8,9},{9,8},{10,11... | collective-permute-start | bytes 589832 | tf_op jit(solution)/shard_map/ppermute | solution.py:515
  12.7 10.0 %collective-permute-start.3 = (bf16[768,128]{1,0:T(8,128)(2,1)S(1)}, bf16[768,128]{1,0:T(8,128)(2,1)S(1)}, u32[]{:S(2)}, u32[]{:S(2)}) collective-permute-start(bf16[768,128]{1,0:T(8,128)(2,1)S(1)} %get-tuple-element.62), channel_id=1, source_target_pairs={{0,3},{1,2},{2,1},{3,0},{4,7},{5,6},{6,5},{7,4},{8,11},{9,10},{10,... | collective-permute-start | bytes 589832 | tf_op jit(solution)/shard_map/ppermute | solution.py:515
  14.6 8.1 %copy-start.4 = (s32[6]{0:T(128)S(1)}, s32[6]{0:T(128)}, u32[]{:S(2)}) copy-start(s32[6]{0:T(128)} %get-tuple-element.58.sel_ref) | copy-start | bytes 76
  16.5 6.2 %collective-permute-start.4 = (bf16[768,128]{1,0:T(8,128)(2,1)S(1)}, bf16[768,128]{1,0:T(8,128)(2,1)S(1)}, u32[]{:S(2)}, u32[]{:S(2)}) collective-permute-start(bf16[768,128]{1,0:T(8,128)(2,1)S(1)} %get-tuple-element.68), channel_id=1, source_target_pairs={{0,2},{1,3},{2,0},{3,1},{4,6},{5,7},{6,4},{7,5},{8,10},{9,11},{10,... | collective-permute-start | bytes 589832 | tf_op jit(solution)/shard_map/ppermute | solution.py:515
  24.3 33.0 %all-to-all-start = ((bf16[16,112,128]{2,1,0:T(8,128)(2,1)}), bf16[16,112,128]{2,1,0:T(8,128)(2,1)S(1)}, u32[]{:S(2)}, u32[]{:S(2)}) async-start(bf16[16,112,128]{2,1,0:T(8,128)(2,1)} %bitcast.3), calls=%async_computation | async-start | bytes 917504 | tf_op jit(solution)/shard_map/all_to_all | solution.py:534
  30.9 28.6 %collective-permute-start.12 = (bf16[1536,128]{1,0:T(8,128)(2,1)S(1)}, bf16[1536,128]{1,0:T(8,128)(2,1)S(1)}, u32[]{:S(2)}, u32[]{:S(2)}) collective-permute-start(bf16[1536,128]{1,0:T(8,128)(2,1)S(1)} %get-tuple-element.79.refs_0_), channel_id=1, source_target_pairs={{0,1},{1,0},{2,3},{3,2},{4,5},{5,4},{6,7},{7,6},{8,9},{9,8},{10,11... | collective-permute-start | bytes 1179656 | tf_op jit(solution)/shard_map/ppermute | solution.py:515
  32.5 17.7 %collective-permute-start.5 = (bf16[192,128]{1,0:T(8,128)(2,1)S(1)}, bf16[192,128]{1,0:T(8,128)(2,1)S(1)}, u32[]{:S(2)}, u32[]{:S(2)}) collective-permute-start(bf16[192,128]{1,0:T(8,128)(2,1)S(1)} %get-tuple-element.82), channel_id=1, source_target_pairs={{0,16},{2,18},{4,20},{6,22},{8,24},{10,26},{12,28},{14,30},{16,0},... | collective-permute-start | bytes 147464 | tf_op jit(solution)/shard_map/ppermute | solution.py:519
  35.3 14.9 %collective-permute-start.6 = (bf16[192,128]{1,0:T(8,128)(2,1)S(1)}, bf16[192,128]{1,0:T(8,128)(2,1)S(1)}, u32[]{:S(2)}, u32[]{:S(2)}) collective-permute-start(bf16[192,128]{1,0:T(8,128)(2,1)S(1)} %get-tuple-element.83), channel_id=1, source_target_pairs={{0,24},{2,26},{4,28},{6,30},{8,16},{10,18},{12,20},{14,22},{16,8},... | collective-permute-start | bytes 147464 | tf_op jit(solution)/shard_map/ppermute | solution.py:519
  36.7 16.4 %collective-permute-start.7 = (bf16[192,128]{1,0:T(8,128)(2,1)S(1)}, bf16[192,128]{1,0:T(8,128)(2,1)S(1)}, u32[]{:S(2)}, u32[]{:S(2)}) collective-permute-start(bf16[192,128]{1,0:T(8,128)(2,1)S(1)} %get-tuple-element.84), channel_id=1, source_target_pairs={{0,20},{2,22},{4,16},{6,18},{8,28},{10,30},{12,24},{14,26},{16,4},... | collective-permute-start | bytes 147464 | tf_op jit(solution)/shard_map/ppermute | solution.py:519
  39.1 14.6 %collective-permute-start.8 = (bf16[192,128]{1,0:T(8,128)(2,1)S(1)}, bf16[192,128]{1,0:T(8,128)(2,1)S(1)}, u32[]{:S(2)}, u32[]{:S(2)}) collective-permute-start(bf16[192,128]{1,0:T(8,128)(2,1)S(1)} %get-tuple-element.85), channel_id=1, source_target_pairs={{0,28},{2,30},{4,24},{6,26},{8,20},{10,22},{12,16},{14,18},{16,12}... | collective-permute-start | bytes 147464 | tf_op jit(solution)/shard_map/ppermute | solution.py:519
  50.2 4.1 %collective-permute-start.9 = (bf16[192,128]{1,0:T(8,128)(2,1)S(1)}, bf16[192,128]{1,0:T(8,128)(2,1)S(1)}, u32[]{:S(2)}, u32[]{:S(2)}) collective-permute-start(bf16[192,128]{1,0:T(8,128)(2,1)S(1)} %get-tuple-element.86), channel_id=1, source_target_pairs={{0,8},{2,10},{4,12},{6,14},{8,0},{10,2},{12,4},{14,6},{16,24},{18,... | collective-permute-start | bytes 147464 | tf_op jit(solution)/shard_map/ppermute | solution.py:519
  50.2 5.6 %collective-permute-start.10 = (bf16[192,128]{1,0:T(8,128)(2,1)S(1)}, bf16[192,128]{1,0:T(8,128)(2,1)S(1)}, u32[]{:S(2)}, u32[]{:S(2)}) collective-permute-start(bf16[192,128]{1,0:T(8,128)(2,1)S(1)} %get-tuple-element.87), channel_id=1, source_target_pairs={{0,12},{2,14},{4,8},{6,10},{8,4},{10,6},{12,0},{14,2},{16,28},{18,... | collective-permute-start | bytes 147464 | tf_op jit(solution)/shard_map/ppermute | solution.py:519
  53.2 4.1 %collective-permute-start.11 = (bf16[192,128]{1,0:T(8,128)(2,1)S(1)}, bf16[192,128]{1,0:T(8,128)(2,1)S(1)}, u32[]{:S(2)}, u32[]{:S(2)}) collective-permute-start(bf16[192,128]{1,0:T(8,128)(2,1)S(1)} %get-tuple-element.88), channel_id=1, source_target_pairs={{0,4},{2,6},{4,0},{6,2},{8,12},{10,14},{12,8},{14,10},{16,20},{18,... | collective-permute-start | bytes 147464 | tf_op jit(solution)/shard_map/ppermute | solution.py:519
  59.5 32.8 %copy-start.5 = (s32[192]{0:T(256)S(1)}, s32[192]{0:T(256)}, u32[]{:S(2)}) copy-start(s32[192]{0:T(256)} %get-tuple-element.51.table_ref) | copy-start | bytes 2308
  59.5 32.8 %all-to-all-start.1 = ((bf16[32,3,48,128]{3,2,1,0:T(8,128)(2,1)}), bf16[32,3,48,128]{3,2,1,0:T(8,128)(2,1)S(1)}, u32[]{:S(2)}, u32[]{:S(2)}) async-start(bf16[32,3,48,128]{3,2,1,0:T(8,128)(2,1)} %shard_map.71), calls=%async_computation.1 | async-start | bytes 2359296 | tf_op jit(solution)/shard_map/all_to_all | solution.py:541
  62.3 2.0 %collective-permute-start.13 = (bf16[768,128]{1,0:T(8,128)(2,1)S(1)}, bf16[768,128]{1,0:T(8,128)(2,1)S(1)}, u32[]{:S(2)}, u32[]{:S(2)}) collective-permute-start(bf16[768,128]{1,0:T(8,128)(2,1)S(1)} %get-tuple-element.93), channel_id=1, source_target_pairs={{0,2},{1,3},{2,0},{3,1},{4,6},{5,7},{6,4},{7,5},{8,10},{9,11},{10,... | collective-permute-start | bytes 589832 | tf_op jit(solution)/shard_map/ppermute | solution.py:515
  62.6 15.9 %collective-permute-start.14 = (bf16[768,128]{1,0:T(8,128)(2,1)S(1)}, bf16[768,128]{1,0:T(8,128)(2,1)S(1)}, u32[]{:S(2)}, u32[]{:S(2)}) collective-permute-start(bf16[768,128]{1,0:T(8,128)(2,1)S(1)} %get-tuple-element.92.refs_2_), channel_id=1, source_target_pairs={{0,1},{1,0},{2,3},{3,2},{4,5},{5,4},{6,7},{7,6},{8,9},{9,8},{10,11... | collective-permute-start | bytes 589832 | tf_op jit(solution)/shard_map/ppermute | solution.py:515
  64.3 19.0 %collective-permute-start.15 = (bf16[768,128]{1,0:T(8,128)(2,1)S(1)}, bf16[768,128]{1,0:T(8,128)(2,1)S(1)}, u32[]{:S(2)}, u32[]{:S(2)}) collective-permute-start(bf16[768,128]{1,0:T(8,128)(2,1)S(1)} %collective-permute-done.13.refs_3_), channel_id=1, source_target_pairs={{0,1},{1,0},{2,3},{3,2},{4,5},{5,4},{6,7},{7,6},{8,9},{9,8},{10,11... | collective-permute-start | bytes 589832 | tf_op jit(solution)/shard_map/ppermute | solution.py:515
  92.3 13.9 %copy-start.2 = (s32[3]{0:T(128)S(1)}, s32[3]{0:T(128)}, u32[]{:S(2)}) copy-start(s32[3]{0:T(128)} %pad_add_fusion.places_ref.where_ref) | copy-start | bytes 40
  92.3 13.9 %copy-start.3 = (s32[12]{0:T(128)S(1)}, s32[12]{0:T(128)}, u32[]{:S(2)}) copy-start(s32[12]{0:T(128)} %get-tuple-element.50.pairs_ref) | copy-start | bytes 148
  102.5 3.7 %collective-permute-start.16 = (f32[1,16,128]{2,1,0:T(8,128)S(1)}, f32[1,16,128]{2,1,0:T(8,128)S(1)}, u32[]{:S(2)}, u32[]{:S(2)}) collective-permute-start(f32[1,16,128]{2,1,0:T(8,128)S(1)} %shard_map.72.refs_0_), channel_id=1, source_target_pairs={{0,1},{1,0},{2,3},{3,2},{4,5},{5,4},{6,7},{7,6},{8,9},{9,8},{10,11... | collective-permute-start | bytes 24584 | tf_op jit(solution)/shard_map/ppermute | solution.py:545

commit v12 on v9

--- a/solution.py
+++ b/solution.py
@@ -15,7 +15,7 @@
 CHUNK = 4
 LINE = 32
 PACK = 6
-SPREAD = (0, 1, 4, 6, 5, 7, 2, 3)
+SPREAD = (0, 1, 2, 4, 3, 6, 5, 7)
 SMEM = pltpu.SMEM
 VMEM = pltpu.VMEM
 
@@ -492,12 +492,13 @@
     own, aside = split(0, flat, weight, 0)
     c = near(aside, 1)
     *sends, own, other = gather_unit(sel, sel_near, y, cy, own, c, size)
+    other = near(other, 1)
+    sends[4], other = lax.optimization_barrier((sends[4], other))
+    spread = [along(send, rel) if rel else send for rel, send in zip(SPREAD, sends)]
     own_y = near(own, 2)
-    spread = [along(send, rel) if rel else send for rel, send in zip(SPREAD, sends)]
     outgoing = cube_route(spread, size, slots, blocks)
-    outgoing, other, own_y = lax.optimization_barrier((outgoing, other, own_y))
+    outgoing, own_y, other = lax.optimization_barrier((outgoing, own_y, other))
     incoming = lax.all_to_all(outgoing, ("narrow", "wide"), 0, 0, tiled=True)
-    other = near(other, 1)
     query = [own, other, own_y, near(other, 2)]
     part = score(table, query, incoming, blocks, length)
     parts = [part, lax.ppermute(part, "narrow", [(0, 1), (1, 0)])]

time: 104 us -> 102 us (0.981)
  starting transfers between devices: 25.9 us -> 22.8 us
  waiting for transfers between devices: 53.5 us -> 54.6 us
    ppermute x7, starting transfers between devices: 12.7 us -> 10.5 us  [along(): return lax.ppermute(array, 'wide', [(i, i ^ flip) for i in range(16)])]
    all_to_all x1, starting transfers between devices: 5.01 us -> 3.4 us  [local_cube(): incoming = lax.all_to_all(outgoing, ('narrow', 'wide'), 0, 0, tiled=True)]
  transfers between devices with their start and end apart: 16 -> 16, of which waited for: 11 -> 9; matrix products, arithmetic and copies ran while one was open for 1% -> 1% of each run, Pallas kernels for 7% -> 7%
where the time goes in v12:
time: 102 us
  waiting for transfers between devices  54.6 us (54%)
  starting transfers between devices  22.8 us (22%)
  Pallas kernels  22.2 us (22%)
  local copies, waits for them, and re-layouts  1.6 us (2%)
    ppermute x7, waiting for transfers between devices, near(): lax.ppermute(array, ('wide', 'narrow'), [(i, i ^ flip) for i in range(32)])  29.9 us
    ppermute x7, waiting for transfers between devices, along(): return lax.ppermute(array, 'wide', [(i, i ^ flip) for i in range(16)])  13 us
    ppermute x7, starting transfers between devices, along(): return lax.ppermute(array, 'wide', [(i, i ^ flip) for i in range(16)])  10.5 us
    pallas_call x1, Pallas kernels, score(): pl.pallas_call(functools.partial(score_kernel, length, parts), out_shape=...  10.2 us
    all_to_all x1, waiting for transfers between devices, local_cube(): incoming = lax.all_to_all(outgoing, ('narrow', 'wide'), 0, 0, tiled=True)  8.97 us
    ppermute x7, starting transfers between devices, near(): lax.ppermute(array, ('wide', 'narrow'), [(i, i ^ flip) for i in range(32)])  7.88 us
    pallas_call x2, Pallas kernels, split(): pl.pallas_call(functools.partial(split_kernel, first, over), out_shape=(j...  5.26 us
    all_to_all x1, starting transfers between devices, local_cube(): incoming = lax.all_to_all(outgoing, ('narrow', 'wide'), 0, 0, tiled=True)  3.4 us
  transfers between devices with their start and end apart: 16, of which 9 were waited for; matrix products, arithmetic and copies ran while one was open for 1% of the time, Pallas kernels for 7%

profile of v12, /device:TPU:0, one launch (start us, length us, event | category | flops | bytes accessed | tf_op | source)
XLA Modules:
  0.0 101.9 jit_solution(1122425945309734860)
XLA Ops:
  0.0 0.9 copy-done
  0.9 2.6 %shard_map.65 = (bf16[1536,128]{1,0:T(8,128)(2,1)S(1)}, bf16[1536,128]{1,0:T(8,128)(2,1)S(1)}) custom-call(bf16[4,1536,512]{2,1,0:T(8,128)(2,1)} %bitcast.3, bf16[512,128]{1,0:T(8,128)(2,1)S(1)} %copy-done), custom_call_target="tpu_custom_call" | custom-call | flops 402653184 | bytes 3145728 | tf_op jit(solution)/shard_map/pallas_call | solution.py:367
  3.5 3.0 %collective-permute-start.1 = (bf16[1536,128]{1,0:T(8,128)(2,1)S(1)}, bf16[1536,128]{1,0:T(8,128)(2,1)S(1)}, u32[]{:S(2)}, u32[]{:S(2)}) collective-permute-start(bf16[1536,128]{1,0:T(8,128)(2,1)S(1)} %get-tuple-element.35), channel_id=1, source_target_pairs={{0,1},{1,0},{2,3},{3,2},{4,5},{5,4},{6,7},{7,6},{8,9},{9,8},{10,11... | collective-permute-start | bytes 1179656 | tf_op jit(solution)/shard_map/ppermute | solution.py:480
  6.6 2.6 %shard_map.66 = (bf16[1536,128]{1,0:T(8,128)(2,1)S(1)}, bf16[1536,128]{1,0:T(8,128)(2,1)S(1)}) custom-call(bf16[4,1536,512]{2,1,0:T(8,128)(2,1)} %bitcast.4, bf16[512,128]{1,0:T(8,128)(2,1)S(1)} %copy-done), custom_call_target="tpu_custom_call" | custom-call | flops 402653184 | bytes 3145728 | tf_op jit(solution)/shard_map/pallas_call | solution.py:367
  9.2 0.3 collective-permute-start.3
  9.5 0.6 pad_add_fusion.places_ref.where_ref
  10.1 2.2 %shard_map.64 = (s32[6]{0:T(128)}, s32[192]{0:T(256)}, s32[12]{0:T(128)}) custom-call(s32[3]{0:T(128)} %pad_add_fusion.places_ref.where_ref, s32[12]{0:T(128)} %cand_ref.1, s32[12]{0:T(128)} %query_block_ref.1, s32[12]{0:T(128)} %valid_ref.1, s32[768]{0:T(1024)} %lengths_ref.1), custom_call_target="tpu_custom_call" | custom-call | tf_op jit(solution)/shard_map/pallas_call | solution.py:75
  12.3 0.4 collective-permute-start
  12.7 0.9 collective-permute-done.sel_near_ref
  13.5 3.0 %collective-permute-done.1.y_ref = bf16[1536,128]{1,0:T(8,128)(2,1)S(1)} collective-permute-done((bf16[1536,128]{1,0:T(8,128)(2,1)S(1)}, bf16[1536,128]{1,0:T(8,128)(2,1)S(1)}, u32[]{:S(2)}, u32[]{:S(2)}) %collective-permute-start.1) | collective-permute-done | bytes 393248 | tf_op jit(solution)/shard_map/ppermute | solution.py:480
  16.5 6.9 %collective-permute-done.2.cy_ref = bf16[1536,128]{1,0:T(8,128)(2,1)S(1)} collective-permute-done((bf16[1536,128]{1,0:T(8,128)(2,1)S(1)}, bf16[1536,128]{1,0:T(8,128)(2,1)S(1)}, u32[]{:S(2)}, u32[]{:S(2)}) %collective-permute-start.2) | collective-permute-done | bytes 393248 | tf_op jit(solution)/shard_map/ppermute | solution.py:480
  23.4 0.7 copy-done.3
  24.1 1.1 %shard_map.67 = (bf16[400,128]{1,0:T(8,128)(2,1)S(1)}, bf16[400,128]{1,0:T(8,128)(2,1)S(1)}, bf16[400,128]{1,0:T(8,128)(2,1)S(1)}, bf16[400,128]{1,0:T(8,128)(2,...) custom-call(s32[6]{0:T(128)S(1)} %copy-done.3, ...), custom_call_target="tpu_custom_call" | custom-call | tf_op jit(solution)/shard_map/pallas_call | solution.py:412
  25.1 0.6 collective-permute-start.7
  25.8 1.7 %collective-permute-start.12 = (bf16[1536,128]{1,0:T(8,128)(2,1)S(1)}, bf16[1536,128]{1,0:T(8,128)(2,1)S(1)}, u32[]{:S(2)}, u32[]{:S(2)}) collective-permute-start(bf16[1536,128]{1,0:T(8,128)(2,1)S(1)} %get-tuple-element.40.refs_0_), channel_id=1, source_target_pairs={{0,1},{1,0},{2,3},{3,2},{4,5},{5,4},{6,7},{7,6},{8,9},{9,8},{10,11... | collective-permute-start | bytes 1179656 | tf_op jit(solution)/shard_map/ppermute | solution.py:480
  27.5 1.5 %collective-permute-start.4 = (bf16[400,128]{1,0:T(8,128)(2,1)S(1)}, bf16[400,128]{1,0:T(8,128)(2,1)S(1)}, u32[]{:S(2)}, u32[]{:S(2)}) collective-permute-start(bf16[400,128]{1,0:T(8,128)(2,1)S(1)} %get-tuple-element.42), channel_id=1, source_target_pairs={{0,4},{2,6},{4,0},{6,2},{8,12},{10,14},{12,8},{14,10},{16,20},{18,... | collective-permute-start | bytes 307208 | tf_op jit(solution)/shard_map/ppermute | solution.py:484
  29.0 1.6 %collective-permute-start.5 = (bf16[400,128]{1,0:T(8,128)(2,1)S(1)}, bf16[400,128]{1,0:T(8,128)(2,1)S(1)}, u32[]{:S(2)}, u32[]{:S(2)}) collective-permute-start(bf16[400,128]{1,0:T(8,128)(2,1)S(1)} %get-tuple-element.43), channel_id=1, source_target_pairs={{0,8},{2,10},{4,12},{6,14},{8,0},{10,2},{12,4},{14,6},{16,24},{18,... | collective-permute-start | bytes 307208 | tf_op jit(solution)/shard_map/ppermute | solution.py:484
  30.6 2.6 %collective-permute-start.6 = (bf16[400,128]{1,0:T(8,128)(2,1)S(1)}, bf16[400,128]{1,0:T(8,128)(2,1)S(1)}, u32[]{:S(2)}, u32[]{:S(2)}) collective-permute-start(bf16[400,128]{1,0:T(8,128)(2,1)S(1)} %get-tuple-element.44), channel_id=1, source_target_pairs={{0,16},{2,18},{4,20},{6,22},{8,24},{10,26},{12,28},{14,30},{16,0},... | collective-permute-start | bytes 307208 | tf_op jit(solution)/shard_map/ppermute | solution.py:484
  33.4 2.3 %collective-permute-start.10 = (bf16[400,128]{1,0:T(8,128)(2,1)S(1)}, bf16[400,128]{1,0:T(8,128)(2,1)S(1)}, u32[]{:S(2)}, u32[]{:S(2)}) collective-permute-start(bf16[400,128]{1,0:T(8,128)(2,1)S(1)} %get-tuple-element.49), channel_id=1, source_target_pairs={{0,20},{2,22},{4,16},{6,18},{8,28},{10,30},{12,24},{14,26},{16,4},... | collective-permute-start | bytes 307208 | tf_op jit(solution)/shard_map/ppermute | solution.py:484
  35.7 2.3 %collective-permute-start.11 = (bf16[400,128]{1,0:T(8,128)(2,1)S(1)}, bf16[400,128]{1,0:T(8,128)(2,1)S(1)}, u32[]{:S(2)}, u32[]{:S(2)}) collective-permute-start(bf16[400,128]{1,0:T(8,128)(2,1)S(1)} %get-tuple-element.50), channel_id=1, source_target_pairs={{0,28},{2,30},{4,24},{6,26},{8,20},{10,22},{12,16},{14,18},{16,12}... | collective-permute-start | bytes 307208 | tf_op jit(solution)/shard_map/ppermute | solution.py:484
  38.0 7.5 %collective-permute-done.6.refs_3_ = bf16[400,128]{1,0:T(8,128)(2,1)S(1)} collective-permute-done((bf16[400,128]{1,0:T(8,128)(2,1)S(1)}, bf16[400,128]{1,0:T(8,128)(2,1)S(1)}, u32[]{:S(2)}, u32[]{:S(2)}) %collective-permute-start.6) | collective-permute-done | bytes 102432 | tf_op jit(solution)/shard_map/ppermute | solution.py:484
  45.5 4.3 %collective-permute-done.10.refs_6_ = bf16[400,128]{1,0:T(8,128)(2,1)S(1)} collective-permute-done((bf16[400,128]{1,0:T(8,128)(2,1)S(1)}, bf16[400,128]{1,0:T(8,128)(2,1)S(1)}, u32[]{:S(2)}, u32[]{:S(2)}) %collective-permute-start.10) | collective-permute-done | bytes 102432 | tf_op jit(solution)/shard_map/ppermute | solution.py:484
  49.7 1.3 %collective-permute-done.8.refs_4_ = bf16[400,128]{1,0:T(8,128)(2,1)S(1)} collective-permute-done((bf16[400,128]{1,0:T(8,128)(2,1)S(1)}, bf16[400,128]{1,0:T(8,128)(2,1)S(1)}, u32[]{:S(2)}, u32[]{:S(2)}) %collective-permute-start.8) | collective-permute-done | bytes 102432 | tf_op jit(solution)/shard_map/ppermute | solution.py:484
  51.0 2.2 %shard_map.68 = bf16[32,3,48,128]{3,2,1,0:T(8,128)(2,1)} custom-call(bf16[400,128]{1,0:T(8,128)(2,1)S(1)} %get-tuple-element.41.refs_0_, bf16[400,128]{1,0:T(8,128)(2,1)S(1)} %collective-permute-done.4.refs_1_, bf16[400,128]{1,0:T(8,128)(2,1)S(1)} %collective-permute-done.5.refs_2_, bf16[400,128]{1,0:T(8,128)(2,1)S(1)} %collective-permute-done.6.refs_3_, ...), custom_call_target="tpu_custom_call" | custom-call | tf_op jit(solution)/shard_map/pallas_call | solution.py:452
  53.3 3.4 %all-to-all-start = ((bf16[32,3,48,128]{3,2,1,0:T(8,128)(2,1)}), bf16[32,3,48,128]{3,2,1,0:T(8,128)(2,1)S(1)}, u32[]{:S(2)}, u32[]{:S(2)}) async-start(bf16[32,3,48,128]{3,2,1,0:T(8,128)(2,1)} %shard_map.68), calls=%async_computation | async-start | bytes 2359296 | tf_op jit(solution)/shard_map/all_to_all | solution.py:501
  56.7 1.8 %collective-permute-start.13 = (bf16[1536,128]{1,0:T(8,128)(2,1)S(1)}, bf16[1536,128]{1,0:T(8,128)(2,1)S(1)}, u32[]{:S(2)}, u32[]{:S(2)}) collective-permute-start(bf16[1536,128]{1,0:T(8,128)(2,1)S(1)} %collective-permute-done.7.refs_1_), channel_id=1, source_target_pairs={{0,1},{1,0},{2,3},{3,2},{4,5},{5,4},{6,7},{7,6},{8,9},{9,8},{10,11... | collective-permute-start | bytes 1179656 | tf_op jit(solution)/shard_map/ppermute | solution.py:480
  58.5 19.2 %collective-permute-done.13.refs_3_ = bf16[1536,128]{1,0:T(8,128)(2,1)S(1)} collective-permute-done((bf16[1536,128]{1,0:T(8,128)(2,1)S(1)}, bf16[1536,128]{1,0:T(8,128)(2,1)S(1)}, u32[]{:S(2)}, u32[]{:S(2)}) %collective-permute-start.13) | collective-permute-done | bytes 393248 | tf_op jit(solution)/shard_map/ppermute | solution.py:480
  77.7 9.0 %all-to-all-done.refs_4_ = bf16[32,3,48,128]{3,2,1,0:T(8,128)(2,1)S(1)} async-done(((bf16[32,3,48,128]{3,2,1,0:T(8,128)(2,1)}), bf16[32,3,48,128]{3,2,1,0:T(8,128)(2,1)S(1)}, u32[]{:S(2)}, u32[]{:S(2)}) %all-to-all-start) | async-done | bytes 1179680 | tf_op jit(solution)/shard_map/all_to_all | solution.py:501
  86.7 10.2 %shard_map.69.refs_0_ = f32[1,16,128]{2,1,0:T(8,128)S(1)} custom-call(s32[192]{0:T(256)S(1)} %copy-done.4, bf16[1536,128]{1,0:T(8,128)(2,1)S(1)} %get-tuple-element.40.refs_0_, bf16[1536,128]{1,0:T(8,128)(2,1)S(1)} %collective-permute-done.7.refs_1_, bf16[1536,128]{1,0:T(8,128)(2,1)S(1)} %collective-permute-done.12.refs_2_, ...), custom_call_target="tpu_custom_call" | custom-call | flops 3623878656 | bytes 786432 | tf_op jit(solution)/shard_map/pallas_call | solution.py:251
  96.9 1.0 %collective-permute-start.14 = (f32[1,16,128]{2,1,0:T(8,128)S(1)}, f32[1,16,128]{2,1,0:T(8,128)S(1)}, u32[]{:S(2)}, u32[]{:S(2)}) collective-permute-start(f32[1,16,128]{2,1,0:T(8,128)S(1)} %shard_map.69.refs_0_), channel_id=1, source_target_pairs={{0,1},{1,0},{2,3},{3,2},{4,5},{5,4},{6,7},{7,6},{8,9},{9,8},{10,11... | collective-permute-start | bytes 24584 | tf_op jit(solution)/shard_map/ppermute | solution.py:504
  97.9 2.7 %collective-permute-done.14.refs_1_ = f32[1,16,128]{2,1,0:T(8,128)S(1)} collective-permute-done((f32[1,16,128]{2,1,0:T(8,128)S(1)}, f32[1,16,128]{2,1,0:T(8,128)S(1)}, u32[]{:S(2)}, u32[]{:S(2)}) %collective-permute-start.14) | collective-permute-done | bytes 8224 | tf_op jit(solution)/shard_map/ppermute | solution.py:504
  100.6 1.3 %shard_map.70 = f32[12,12,12]{2,1,0:T(8,128)} custom-call(s32[3]{0:T(128)S(1)} %copy-done.1, s32[12]{0:T(128)S(1)} %copy-done.2, f32[1,16,128]{2,1,0:T(8,128)S(1)} %shard_map.69.refs_0_, f32[1,16,128]{2,1,0:T(8,128)S(1)} %collective-permute-done.14.refs_1_), custom_call_target="tpu_custom_call" | custom-call | tf_op jit(solution)/shard_map/pallas_call | solution.py:278
  (18 shorter events, 0.3 us)
Async XLA Ops:
  0.0 0.9 copy-start
  3.5 13.0 %collective-permute-start.1 = (bf16[1536,128]{1,0:T(8,128)(2,1)S(1)}, bf16[1536,128]{1,0:T(8,128)(2,1)S(1)}, u32[]{:S(2)}, u32[]{:S(2)}) collective-permute-start(bf16[1536,128]{1,0:T(8,128)(2,1)S(1)} %get-tuple-element.35), channel_id=1, source_target_pairs={{0,1},{1,0},{2,3},{3,2},{4,5},{5,4},{6,7},{7,6},{8,9},{9,8},{10,11... | collective-permute-start | bytes 1179656 | tf_op jit(solution)/shard_map/ppermute | solution.py:480
  6.6 16.8 %collective-permute-start.2 = (bf16[1536,128]{1,0:T(8,128)(2,1)S(1)}, bf16[1536,128]{1,0:T(8,128)(2,1)S(1)}, u32[]{:S(2)}, u32[]{:S(2)}) collective-permute-start(bf16[1536,128]{1,0:T(8,128)(2,1)S(1)} %get-tuple-element.36), channel_id=1, source_target_pairs={{0,3},{1,2},{2,1},{3,0},{4,7},{5,6},{6,5},{7,4},{8,11},{9,10},{10,... | collective-permute-start | bytes 1179656 | tf_op jit(solution)/shard_map/ppermute | solution.py:480
  9.2 14.2 %collective-permute-start.3 = (bf16[1536,128]{1,0:T(8,128)(2,1)S(1)}, bf16[1536,128]{1,0:T(8,128)(2,1)S(1)}, u32[]{:S(2)}, u32[]{:S(2)}) collective-permute-start(bf16[1536,128]{1,0:T(8,128)(2,1)S(1)} %get-tuple-element.39), channel_id=1, source_target_pairs={{0,2},{1,3},{2,0},{3,1},{4,6},{5,7},{6,4},{7,5},{8,10},{9,11},{10,... | collective-permute-start | bytes 1179656 | tf_op jit(solution)/shard_map/ppermute | solution.py:480
  12.3 1.3 %collective-permute-start = (s32[6]{0:T(128)}, s32[6]{0:T(128)S(1)}, u32[]{:S(2)}, u32[]{:S(2)}) collective-permute-start(s32[6]{0:T(128)} %get-tuple-element.32.sel_ref), channel_id=1, source_target_pairs={{0,2},{1,3},{2,0},{3,1},{4,6},{5,7},{6,4},{7,5},{8,10},{9,11},{10,... | collective-permute-start | bytes 80 | tf_op jit(solution)/shard_map/ppermute | solution.py:480
  23.4 0.7 copy-start.3
  25.1 8.0 %collective-permute-start.7 = (bf16[1536,128]{1,0:T(8,128)(2,1)S(1)}, bf16[1536,128]{1,0:T(8,128)(2,1)S(1)}, u32[]{:S(2)}, u32[]{:S(2)}) collective-permute-start(bf16[1536,128]{1,0:T(8,128)(2,1)S(1)} %get-tuple-element.46), channel_id=1, source_target_pairs={{0,2},{1,3},{2,0},{3,1},{4,6},{5,7},{6,4},{7,5},{8,10},{9,11},{10,... | collective-permute-start | bytes 1179656 | tf_op jit(solution)/shard_map/ppermute | solution.py:480
  25.8 27.5 %collective-permute-start.12 = (bf16[1536,128]{1,0:T(8,128)(2,1)S(1)}, bf16[1536,128]{1,0:T(8,128)(2,1)S(1)}, u32[]{:S(2)}, u32[]{:S(2)}) collective-permute-start(bf16[1536,128]{1,0:T(8,128)(2,1)S(1)} %get-tuple-element.40.refs_0_), channel_id=1, source_target_pairs={{0,1},{1,0},{2,3},{3,2},{4,5},{5,4},{6,7},{7,6},{8,9},{9,8},{10,11... | collective-permute-start | bytes 1179656 | tf_op jit(solution)/shard_map/ppermute | solution.py:480
  27.5 5.9 %collective-permute-start.4 = (bf16[400,128]{1,0:T(8,128)(2,1)S(1)}, bf16[400,128]{1,0:T(8,128)(2,1)S(1)}, u32[]{:S(2)}, u32[]{:S(2)}) collective-permute-start(bf16[400,128]{1,0:T(8,128)(2,1)S(1)} %get-tuple-element.42), channel_id=1, source_target_pairs={{0,4},{2,6},{4,0},{6,2},{8,12},{10,14},{12,8},{14,10},{16,20},{18,... | collective-permute-start | bytes 307208 | tf_op jit(solution)/shard_map/ppermute | solution.py:484
  29.0 6.7 %collective-permute-start.5 = (bf16[400,128]{1,0:T(8,128)(2,1)S(1)}, bf16[400,128]{1,0:T(8,128)(2,1)S(1)}, u32[]{:S(2)}, u32[]{:S(2)}) collective-permute-start(bf16[400,128]{1,0:T(8,128)(2,1)S(1)} %get-tuple-element.43), channel_id=1, source_target_pairs={{0,8},{2,10},{4,12},{6,14},{8,0},{10,2},{12,4},{14,6},{16,24},{18,... | collective-permute-start | bytes 307208 | tf_op jit(solution)/shard_map/ppermute | solution.py:484
  30.6 14.9 %collective-permute-start.6 = (bf16[400,128]{1,0:T(8,128)(2,1)S(1)}, bf16[400,128]{1,0:T(8,128)(2,1)S(1)}, u32[]{:S(2)}, u32[]{:S(2)}) collective-permute-start(bf16[400,128]{1,0:T(8,128)(2,1)S(1)} %get-tuple-element.44), channel_id=1, source_target_pairs={{0,16},{2,18},{4,20},{6,22},{8,24},{10,26},{12,28},{14,30},{16,0},... | collective-permute-start | bytes 307208 | tf_op jit(solution)/shard_map/ppermute | solution.py:484
  33.2 12.3 %collective-permute-start.9 = (bf16[400,128]{1,0:T(8,128)(2,1)S(1)}, bf16[400,128]{1,0:T(8,128)(2,1)S(1)}, u32[]{:S(2)}, u32[]{:S(2)}) collective-permute-start(bf16[400,128]{1,0:T(8,128)(2,1)S(1)} %get-tuple-element.48), channel_id=1, source_target_pairs={{0,24},{2,26},{4,28},{6,30},{8,16},{10,18},{12,20},{14,22},{16,8},... | collective-permute-start | bytes 307208 | tf_op jit(solution)/shard_map/ppermute | solution.py:484
  33.4 16.3 %collective-permute-start.10 = (bf16[400,128]{1,0:T(8,128)(2,1)S(1)}, bf16[400,128]{1,0:T(8,128)(2,1)S(1)}, u32[]{:S(2)}, u32[]{:S(2)}) collective-permute-start(bf16[400,128]{1,0:T(8,128)(2,1)S(1)} %get-tuple-element.49), channel_id=1, source_target_pairs={{0,20},{2,22},{4,16},{6,18},{8,28},{10,30},{12,24},{14,26},{16,4},... | collective-permute-start | bytes 307208 | tf_op jit(solution)/shard_map/ppermute | solution.py:484
  35.7 14.1 %collective-permute-start.11 = (bf16[400,128]{1,0:T(8,128)(2,1)S(1)}, bf16[400,128]{1,0:T(8,128)(2,1)S(1)}, u32[]{:S(2)}, u32[]{:S(2)}) collective-permute-start(bf16[400,128]{1,0:T(8,128)(2,1)S(1)} %get-tuple-element.50), channel_id=1, source_target_pairs={{0,28},{2,30},{4,24},{6,26},{8,20},{10,22},{12,16},{14,18},{16,12}... | collective-permute-start | bytes 307208 | tf_op jit(solution)/shard_map/ppermute | solution.py:484
  45.4 5.6 %collective-permute-start.8 = (bf16[400,128]{1,0:T(8,128)(2,1)S(1)}, bf16[400,128]{1,0:T(8,128)(2,1)S(1)}, u32[]{:S(2)}, u32[]{:S(2)}) collective-permute-start(bf16[400,128]{1,0:T(8,128)(2,1)S(1)} %get-tuple-element.47), channel_id=1, source_target_pairs={{0,12},{2,14},{4,8},{6,10},{8,4},{10,6},{12,0},{14,2},{16,28},{18,... | collective-permute-start | bytes 307208 | tf_op jit(solution)/shard_map/ppermute | solution.py:484
  53.2 33.4 %copy-start.4 = (s32[192]{0:T(256)S(1)}, s32[192]{0:T(256)}, u32[]{:S(2)}) copy-start(s32[192]{0:T(256)} %get-tuple-element.31.table_ref) | copy-start | bytes 2308
  53.3 33.4 %all-to-all-start = ((bf16[32,3,48,128]{3,2,1,0:T(8,128)(2,1)}), bf16[32,3,48,128]{3,2,1,0:T(8,128)(2,1)S(1)}, u32[]{:S(2)}, u32[]{:S(2)}) async-start(bf16[32,3,48,128]{3,2,1,0:T(8,128)(2,1)} %shard_map.68), calls=%async_computation | async-start | bytes 2359296 | tf_op jit(solution)/shard_map/all_to_all | solution.py:501
  56.7 21.0 %collective-permute-start.13 = (bf16[1536,128]{1,0:T(8,128)(2,1)S(1)}, bf16[1536,128]{1,0:T(8,128)(2,1)S(1)}, u32[]{:S(2)}, u32[]{:S(2)}) collective-permute-start(bf16[1536,128]{1,0:T(8,128)(2,1)S(1)} %collective-permute-done.7.refs_1_), channel_id=1, source_target_pairs={{0,1},{1,0},{2,3},{3,2},{4,5},{5,4},{6,7},{7,6},{8,9},{9,8},{10,11... | collective-permute-start | bytes 1179656 | tf_op jit(solution)/shard_map/ppermute | solution.py:480
  86.7 13.9 %copy-start.1 = (s32[3]{0:T(128)S(1)}, s32[3]{0:T(128)}, u32[]{:S(2)}) copy-start(s32[3]{0:T(128)} %pad_add_fusion.places_ref.where_ref) | copy-start | bytes 40
  86.7 13.9 %copy-start.2 = (s32[12]{0:T(128)S(1)}, s32[12]{0:T(128)}, u32[]{:S(2)}) copy-start(s32[12]{0:T(128)} %get-tuple-element.30.pairs_ref) | copy-start | bytes 148
  96.9 3.7 %collective-permute-start.14 = (f32[1,16,128]{2,1,0:T(8,128)S(1)}, f32[1,16,128]{2,1,0:T(8,128)S(1)}, u32[]{:S(2)}, u32[]{:S(2)}) collective-permute-start(f32[1,16,128]{2,1,0:T(8,128)S(1)} %shard_map.69.refs_0_), channel_id=1, source_target_pairs={{0,1},{1,0},{2,3},{3,2},{4,5},{5,4},{6,7},{7,6},{8,9},{9,8},{10,11... | collective-permute-start | bytes 24584 | tf_op jit(solution)/shard_map/ppermute | solution.py:504

commit v13 on v12

--- a/solution.py
+++ b/solution.py
@@ -78,6 +78,7 @@
         in_specs=[pl.BlockSpec(memory_space=SMEM)] * 5,
         out_specs=[pl.BlockSpec(memory_space=SMEM)] * 3,
         scratch_shapes=[SMEM((pairs,), jnp.int32)] * 3,
+        compiler_params=vmem_params(4),
     )(places, cand_block, query_block, valid, lengths)
 
 

time: 102 us -> 101 us (level)
  transfers between devices with their start and end apart: 16 -> 16, of which waited for: 9 -> 9; matrix products, arithmetic and copies ran while one was open for 1% -> 0% of each run, Pallas kernels for 7% -> 7%
where the time goes in v13:
time: 101 us
  waiting for transfers between devices  55.2 us (55%)
  starting transfers between devices  22.8 us (23%)
  Pallas kernels  22.1 us (22%)
    ppermute x7, waiting for transfers between devices, near(): lax.ppermute(array, ('wide', 'narrow'), [(i, i ^ flip) for i in range(32)])  30.5 us
    ppermute x7, waiting for transfers between devices, along(): return lax.ppermute(array, 'wide', [(i, i ^ flip) for i in range(16)])  13 us
    ppermute x7, starting transfers between devices, along(): return lax.ppermute(array, 'wide', [(i, i ^ flip) for i in range(16)])  10.5 us
    pallas_call x1, Pallas kernels, score(): pl.pallas_call(functools.partial(score_kernel, length, parts), out_shape=...  10.2 us
    all_to_all x1, waiting for transfers between devices, local_cube(): incoming = lax.all_to_all(outgoing, ('narrow', 'wide'), 0, 0, tiled=True)  8.97 us
    ppermute x7, starting transfers between devices, near(): lax.ppermute(array, ('wide', 'narrow'), [(i, i ^ flip) for i in range(32)])  7.88 us
    pallas_call x2, Pallas kernels, split(): pl.pallas_call(functools.partial(split_kernel, first, over), out_shape=(j...  5.26 us
    all_to_all x1, starting transfers between devices, local_cube(): incoming = lax.all_to_all(outgoing, ('narrow', 'wide'), 0, 0, tiled=True)  3.4 us
  transfers between devices with their start and end apart: 16, of which 9 were waited for; matrix products, arithmetic and copies ran while one was open for 0% of the time, Pallas kernels for 7%

profile of v13, /device:TPU:0, one launch (start us, length us, event | category | flops | bytes accessed | tf_op | source)
XLA Modules:
  0.0 101.2 jit_solution(14855047037457849326)
XLA Ops:
  0.0 0.9 copy-done
  0.9 2.6 %shard_map.65 = (bf16[1536,128]{1,0:T(8,128)(2,1)S(1)}, bf16[1536,128]{1,0:T(8,128)(2,1)S(1)}) custom-call(bf16[4,1536,512]{2,1,0:T(8,128)(2,1)} %bitcast.3, bf16[512,128]{1,0:T(8,128)(2,1)S(1)} %copy-done), custom_call_target="tpu_custom_call" | custom-call | flops 402653184 | bytes 3145728 | tf_op jit(solution)/shard_map/pallas_call | solution.py:368
  3.6 3.0 %collective-permute-start.1 = (bf16[1536,128]{1,0:T(8,128)(2,1)S(1)}, bf16[1536,128]{1,0:T(8,128)(2,1)S(1)}, u32[]{:S(2)}, u32[]{:S(2)}) collective-permute-start(bf16[1536,128]{1,0:T(8,128)(2,1)S(1)} %get-tuple-element.35), channel_id=1, source_target_pairs={{0,1},{1,0},{2,3},{3,2},{4,5},{5,4},{6,7},{7,6},{8,9},{9,8},{10,11... | collective-permute-start | bytes 1179656 | tf_op jit(solution)/shard_map/ppermute | solution.py:481
  6.6 2.6 %shard_map.66 = (bf16[1536,128]{1,0:T(8,128)(2,1)S(1)}, bf16[1536,128]{1,0:T(8,128)(2,1)S(1)}) custom-call(bf16[4,1536,512]{2,1,0:T(8,128)(2,1)} %bitcast.4, bf16[512,128]{1,0:T(8,128)(2,1)S(1)} %copy-done), custom_call_target="tpu_custom_call" | custom-call | flops 402653184 | bytes 3145728 | tf_op jit(solution)/shard_map/pallas_call | solution.py:368
  9.3 0.3 collective-permute-start.3
  9.5 0.1 pad_add_fusion.places_ref.where_ref
  9.6 2.1 %shard_map.64 = (s32[6]{0:T(128)S(1)}, s32[192]{0:T(256)S(1)}, s32[12]{0:T(128)S(1)}) custom-call(s32[3]{0:T(128)S(1)} %pad_add_fusion.places_ref.where_ref, s32[12]{0:T(128)S(1)} %copy-done.2, s32[12]{0:T(128)S(1)} %copy-done.3, s32[12]{0:T(128)S(1)} %copy-done.4, s32[768]{0:T(1024)S(1)} %copy-done.1), custom_call_target="tpu_custom_call" | custom-call | tf_op jit(solution)/shard_map/pallas_call | solution.py:75
  11.7 0.4 collective-permute-start
  12.1 0.8 collective-permute-done.sel_near_ref
  12.9 3.6 %collective-permute-done.1.y_ref = bf16[1536,128]{1,0:T(8,128)(2,1)S(1)} collective-permute-done((bf16[1536,128]{1,0:T(8,128)(2,1)S(1)}, bf16[1536,128]{1,0:T(8,128)(2,1)S(1)}, u32[]{:S(2)}, u32[]{:S(2)}) %collective-permute-start.1) | collective-permute-done | bytes 393248 | tf_op jit(solution)/shard_map/ppermute | solution.py:481
  16.6 6.9 %collective-permute-done.2.cy_ref = bf16[1536,128]{1,0:T(8,128)(2,1)S(1)} collective-permute-done((bf16[1536,128]{1,0:T(8,128)(2,1)S(1)}, bf16[1536,128]{1,0:T(8,128)(2,1)S(1)}, u32[]{:S(2)}, u32[]{:S(2)}) %collective-permute-start.2) | collective-permute-done | bytes 393248 | tf_op jit(solution)/shard_map/ppermute | solution.py:481
  23.4 1.1 %shard_map.67 = (bf16[400,128]{1,0:T(8,128)(2,1)S(1)}, bf16[400,128]{1,0:T(8,128)(2,1)S(1)}, bf16[400,128]{1,0:T(8,128)(2,1)S(1)}, bf16[400,128]{1,0:T(8,128)(2,...) custom-call(s32[6]{0:T(128)S(1)} %get-tuple-element.32.sel_ref, ...), custom_call_target="tpu_custom_call" | custom-call | tf_op jit(solution)/shard_map/pallas_call | solution.py:413
  24.5 0.6 collective-permute-start.7
  25.1 1.7 %collective-permute-start.12 = (bf16[1536,128]{1,0:T(8,128)(2,1)S(1)}, bf16[1536,128]{1,0:T(8,128)(2,1)S(1)}, u32[]{:S(2)}, u32[]{:S(2)}) collective-permute-start(bf16[1536,128]{1,0:T(8,128)(2,1)S(1)} %get-tuple-element.40.refs_0_), channel_id=1, source_target_pairs={{0,1},{1,0},{2,3},{3,2},{4,5},{5,4},{6,7},{7,6},{8,9},{9,8},{10,11... | collective-permute-start | bytes 1179656 | tf_op jit(solution)/shard_map/ppermute | solution.py:481
  26.9 1.5 %collective-permute-start.4 = (bf16[400,128]{1,0:T(8,128)(2,1)S(1)}, bf16[400,128]{1,0:T(8,128)(2,1)S(1)}, u32[]{:S(2)}, u32[]{:S(2)}) collective-permute-start(bf16[400,128]{1,0:T(8,128)(2,1)S(1)} %get-tuple-element.42), channel_id=1, source_target_pairs={{0,4},{2,6},{4,0},{6,2},{8,12},{10,14},{12,8},{14,10},{16,20},{18,... | collective-permute-start | bytes 307208 | tf_op jit(solution)/shard_map/ppermute | solution.py:485
  28.3 1.6 %collective-permute-start.5 = (bf16[400,128]{1,0:T(8,128)(2,1)S(1)}, bf16[400,128]{1,0:T(8,128)(2,1)S(1)}, u32[]{:S(2)}, u32[]{:S(2)}) collective-permute-start(bf16[400,128]{1,0:T(8,128)(2,1)S(1)} %get-tuple-element.43), channel_id=1, source_target_pairs={{0,8},{2,10},{4,12},{6,14},{8,0},{10,2},{12,4},{14,6},{16,24},{18,... | collective-permute-start | bytes 307208 | tf_op jit(solution)/shard_map/ppermute | solution.py:485
  29.9 2.6 %collective-permute-start.6 = (bf16[400,128]{1,0:T(8,128)(2,1)S(1)}, bf16[400,128]{1,0:T(8,128)(2,1)S(1)}, u32[]{:S(2)}, u32[]{:S(2)}) collective-permute-start(bf16[400,128]{1,0:T(8,128)(2,1)S(1)} %get-tuple-element.44), channel_id=1, source_target_pairs={{0,16},{2,18},{4,20},{6,22},{8,24},{10,26},{12,28},{14,30},{16,0},... | collective-permute-start | bytes 307208 | tf_op jit(solution)/shard_map/ppermute | solution.py:485
  32.5 0.2 collective-permute-start.9
  32.7 2.3 %collective-permute-start.10 = (bf16[400,128]{1,0:T(8,128)(2,1)S(1)}, bf16[400,128]{1,0:T(8,128)(2,1)S(1)}, u32[]{:S(2)}, u32[]{:S(2)}) collective-permute-start(bf16[400,128]{1,0:T(8,128)(2,1)S(1)} %get-tuple-element.49), channel_id=1, source_target_pairs={{0,20},{2,22},{4,16},{6,18},{8,28},{10,30},{12,24},{14,26},{16,4},... | collective-permute-start | bytes 307208 | tf_op jit(solution)/shard_map/ppermute | solution.py:485
  35.0 2.3 %collective-permute-start.11 = (bf16[400,128]{1,0:T(8,128)(2,1)S(1)}, bf16[400,128]{1,0:T(8,128)(2,1)S(1)}, u32[]{:S(2)}, u32[]{:S(2)}) collective-permute-start(bf16[400,128]{1,0:T(8,128)(2,1)S(1)} %get-tuple-element.50), channel_id=1, source_target_pairs={{0,28},{2,30},{4,24},{6,26},{8,20},{10,22},{12,16},{14,18},{16,12}... | collective-permute-start | bytes 307208 | tf_op jit(solution)/shard_map/ppermute | solution.py:485
  37.3 7.5 %collective-permute-done.6.refs_3_ = bf16[400,128]{1,0:T(8,128)(2,1)S(1)} collective-permute-done((bf16[400,128]{1,0:T(8,128)(2,1)S(1)}, bf16[400,128]{1,0:T(8,128)(2,1)S(1)}, u32[]{:S(2)}, u32[]{:S(2)}) %collective-permute-start.6) | collective-permute-done | bytes 102432 | tf_op jit(solution)/shard_map/ppermute | solution.py:485
  44.8 4.3 %collective-permute-done.10.refs_6_ = bf16[400,128]{1,0:T(8,128)(2,1)S(1)} collective-permute-done((bf16[400,128]{1,0:T(8,128)(2,1)S(1)}, bf16[400,128]{1,0:T(8,128)(2,1)S(1)}, u32[]{:S(2)}, u32[]{:S(2)}) %collective-permute-start.10) | collective-permute-done | bytes 102432 | tf_op jit(solution)/shard_map/ppermute | solution.py:485
  49.1 1.3 %collective-permute-done.8.refs_4_ = bf16[400,128]{1,0:T(8,128)(2,1)S(1)} collective-permute-done((bf16[400,128]{1,0:T(8,128)(2,1)S(1)}, bf16[400,128]{1,0:T(8,128)(2,1)S(1)}, u32[]{:S(2)}, u32[]{:S(2)}) %collective-permute-start.8) | collective-permute-done | bytes 102432 | tf_op jit(solution)/shard_map/ppermute | solution.py:485
  50.4 2.2 %shard_map.68 = bf16[32,3,48,128]{3,2,1,0:T(8,128)(2,1)} custom-call(bf16[400,128]{1,0:T(8,128)(2,1)S(1)} %get-tuple-element.41.refs_0_, bf16[400,128]{1,0:T(8,128)(2,1)S(1)} %collective-permute-done.4.refs_1_, bf16[400,128]{1,0:T(8,128)(2,1)S(1)} %collective-permute-done.5.refs_2_, bf16[400,128]{1,0:T(8,128)(2,1)S(1)} %collective-permute-done.6.refs_3_, ...), custom_call_target="tpu_custom_call" | custom-call | tf_op jit(solution)/shard_map/pallas_call | solution.py:453
  52.6 3.4 %all-to-all-start = ((bf16[32,3,48,128]{3,2,1,0:T(8,128)(2,1)}), bf16[32,3,48,128]{3,2,1,0:T(8,128)(2,1)S(1)}, u32[]{:S(2)}, u32[]{:S(2)}) async-start(bf16[32,3,48,128]{3,2,1,0:T(8,128)(2,1)} %shard_map.68), calls=%async_computation | async-start | bytes 2359296 | tf_op jit(solution)/shard_map/all_to_all | solution.py:502
  56.0 1.8 %collective-permute-start.13 = (bf16[1536,128]{1,0:T(8,128)(2,1)S(1)}, bf16[1536,128]{1,0:T(8,128)(2,1)S(1)}, u32[]{:S(2)}, u32[]{:S(2)}) collective-permute-start(bf16[1536,128]{1,0:T(8,128)(2,1)S(1)} %collective-permute-done.7.refs_1_), channel_id=1, source_target_pairs={{0,1},{1,0},{2,3},{3,2},{4,5},{5,4},{6,7},{7,6},{8,9},{9,8},{10,11... | collective-permute-start | bytes 1179656 | tf_op jit(solution)/shard_map/ppermute | solution.py:481
  57.9 19.2 %collective-permute-done.13.refs_3_ = bf16[1536,128]{1,0:T(8,128)(2,1)S(1)} collective-permute-done((bf16[1536,128]{1,0:T(8,128)(2,1)S(1)}, bf16[1536,128]{1,0:T(8,128)(2,1)S(1)}, u32[]{:S(2)}, u32[]{:S(2)}) %collective-permute-start.13) | collective-permute-done | bytes 393248 | tf_op jit(solution)/shard_map/ppermute | solution.py:481
  77.1 9.0 %all-to-all-done.refs_4_ = bf16[32,3,48,128]{3,2,1,0:T(8,128)(2,1)S(1)} async-done(((bf16[32,3,48,128]{3,2,1,0:T(8,128)(2,1)}), bf16[32,3,48,128]{3,2,1,0:T(8,128)(2,1)S(1)}, u32[]{:S(2)}, u32[]{:S(2)}) %all-to-all-start) | async-done | bytes 1179680 | tf_op jit(solution)/shard_map/all_to_all | solution.py:502
  86.0 10.2 %shard_map.69.refs_0_ = f32[1,16,128]{2,1,0:T(8,128)S(1)} custom-call(s32[192]{0:T(256)S(1)} %get-tuple-element.31.table_ref, bf16[1536,128]{1,0:T(8,128)(2,1)S(1)} %get-tuple-element.40.refs_0_, bf16[1536,128]{1,0:T(8,128)(2,1)S(1)} %collective-permute-done.7.refs_1_, bf16[1536,128]{1,0:T(8,128)(2,1)S(1)} %collective-permute-done.12.refs_2_, ...), custom_call_target="tpu_custom_call" | custom-call | flops 3623878656 | bytes 786432 | tf_op jit(solution)/shard_map/pallas_call | solution.py:252
  96.2 1.0 %collective-permute-start.14 = (f32[1,16,128]{2,1,0:T(8,128)S(1)}, f32[1,16,128]{2,1,0:T(8,128)S(1)}, u32[]{:S(2)}, u32[]{:S(2)}) collective-permute-start(f32[1,16,128]{2,1,0:T(8,128)S(1)} %shard_map.69.refs_0_), channel_id=1, source_target_pairs={{0,1},{1,0},{2,3},{3,2},{4,5},{5,4},{6,7},{7,6},{8,9},{9,8},{10,11... | collective-permute-start | bytes 24584 | tf_op jit(solution)/shard_map/ppermute | solution.py:505
  97.3 2.7 %collective-permute-done.14.refs_1_ = f32[1,16,128]{2,1,0:T(8,128)S(1)} collective-permute-done((f32[1,16,128]{2,1,0:T(8,128)S(1)}, f32[1,16,128]{2,1,0:T(8,128)S(1)}, u32[]{:S(2)}, u32[]{:S(2)}) %collective-permute-start.14) | collective-permute-done | bytes 8224 | tf_op jit(solution)/shard_map/ppermute | solution.py:505
  99.9 1.3 %shard_map.70 = f32[12,12,12]{2,1,0:T(8,128)} custom-call(s32[3]{0:T(128)S(1)} %pad_add_fusion.places_ref.where_ref, s32[12]{0:T(128)S(1)} %get-tuple-element.30.pairs_ref, f32[1,16,128]{2,1,0:T(8,128)S(1)} %shard_map.69.refs_0_, f32[1,16,128]{2,1,0:T(8,128)S(1)} %collective-permute-done.14.refs_1_), custom_call_target="tpu_custom_call" | custom-call | tf_op jit(solution)/shard_map/pallas_call | solution.py:279
  (18 shorter events, 0.1 us)
Async XLA Ops:
  0.0 0.9 copy-start
  3.5 6.1 %copy-start.1 = (s32[768]{0:T(1024)S(1)}, s32[768]{0:T(1024)}, u32[]{:S(2)}) copy-start(s32[768]{0:T(1024)} %lengths_ref.1) | copy-start | bytes 9220
  3.6 6.0 %copy-start.2 = (s32[12]{0:T(128)S(1)}, s32[12]{0:T(128)}, u32[]{:S(2)}) copy-start(s32[12]{0:T(128)} %cand_ref.1) | copy-start | bytes 148
  3.6 6.0 %copy-start.3 = (s32[12]{0:T(128)S(1)}, s32[12]{0:T(128)}, u32[]{:S(2)}) copy-start(s32[12]{0:T(128)} %query_block_ref.1) | copy-start | bytes 148
  3.6 6.0 %copy-start.4 = (s32[12]{0:T(128)S(1)}, s32[12]{0:T(128)}, u32[]{:S(2)}) copy-start(s32[12]{0:T(128)} %valid_ref.1) | copy-start | bytes 148
  3.6 13.0 %collective-permute-start.1 = (bf16[1536,128]{1,0:T(8,128)(2,1)S(1)}, bf16[1536,128]{1,0:T(8,128)(2,1)S(1)}, u32[]{:S(2)}, u32[]{:S(2)}) collective-permute-start(bf16[1536,128]{1,0:T(8,128)(2,1)S(1)} %get-tuple-element.35), channel_id=1, source_target_pairs={{0,1},{1,0},{2,3},{3,2},{4,5},{5,4},{6,7},{7,6},{8,9},{9,8},{10,11... | collective-permute-start | bytes 1179656 | tf_op jit(solution)/shard_map/ppermute | solution.py:481
  6.6 16.8 %collective-permute-start.2 = (bf16[1536,128]{1,0:T(8,128)(2,1)S(1)}, bf16[1536,128]{1,0:T(8,128)(2,1)S(1)}, u32[]{:S(2)}, u32[]{:S(2)}) collective-permute-start(bf16[1536,128]{1,0:T(8,128)(2,1)S(1)} %get-tuple-element.36), channel_id=1, source_target_pairs={{0,3},{1,2},{2,1},{3,0},{4,7},{5,6},{6,5},{7,4},{8,11},{9,10},{10,... | collective-permute-start | bytes 1179656 | tf_op jit(solution)/shard_map/ppermute | solution.py:481
  9.3 14.2 %collective-permute-start.3 = (bf16[1536,128]{1,0:T(8,128)(2,1)S(1)}, bf16[1536,128]{1,0:T(8,128)(2,1)S(1)}, u32[]{:S(2)}, u32[]{:S(2)}) collective-permute-start(bf16[1536,128]{1,0:T(8,128)(2,1)S(1)} %get-tuple-element.39), channel_id=1, source_target_pairs={{0,2},{1,3},{2,0},{3,1},{4,6},{5,7},{6,4},{7,5},{8,10},{9,11},{10,... | collective-permute-start | bytes 1179656 | tf_op jit(solution)/shard_map/ppermute | solution.py:481
  11.7 1.2 %collective-permute-start = (s32[6]{0:T(128)S(1)}, s32[6]{0:T(128)S(1)}, u32[]{:S(2)}, u32[]{:S(2)}) collective-permute-start(s32[6]{0:T(128)S(1)} %get-tuple-element.32.sel_ref), channel_id=1, source_target_pairs={{0,2},{1,3},{2,0},{3,1},{4,6},{5,7},{6,4},{7,5},{8,10},{9,11},{10,... | collective-permute-start | bytes 80 | tf_op jit(solution)/shard_map/ppermute | solution.py:481
  24.5 8.0 %collective-permute-start.7 = (bf16[1536,128]{1,0:T(8,128)(2,1)S(1)}, bf16[1536,128]{1,0:T(8,128)(2,1)S(1)}, u32[]{:S(2)}, u32[]{:S(2)}) collective-permute-start(bf16[1536,128]{1,0:T(8,128)(2,1)S(1)} %get-tuple-element.46), channel_id=1, source_target_pairs={{0,2},{1,3},{2,0},{3,1},{4,6},{5,7},{6,4},{7,5},{8,10},{9,11},{10,... | collective-permute-start | bytes 1179656 | tf_op jit(solution)/shard_map/ppermute | solution.py:481
  25.1 27.5 %collective-permute-start.12 = (bf16[1536,128]{1,0:T(8,128)(2,1)S(1)}, bf16[1536,128]{1,0:T(8,128)(2,1)S(1)}, u32[]{:S(2)}, u32[]{:S(2)}) collective-permute-start(bf16[1536,128]{1,0:T(8,128)(2,1)S(1)} %get-tuple-element.40.refs_0_), channel_id=1, source_target_pairs={{0,1},{1,0},{2,3},{3,2},{4,5},{5,4},{6,7},{7,6},{8,9},{9,8},{10,11... | collective-permute-start | bytes 1179656 | tf_op jit(solution)/shard_map/ppermute | solution.py:481
  26.9 5.9 %collective-permute-start.4 = (bf16[400,128]{1,0:T(8,128)(2,1)S(1)}, bf16[400,128]{1,0:T(8,128)(2,1)S(1)}, u32[]{:S(2)}, u32[]{:S(2)}) collective-permute-start(bf16[400,128]{1,0:T(8,128)(2,1)S(1)} %get-tuple-element.42), channel_id=1, source_target_pairs={{0,4},{2,6},{4,0},{6,2},{8,12},{10,14},{12,8},{14,10},{16,20},{18,... | collective-permute-start | bytes 307208 | tf_op jit(solution)/shard_map/ppermute | solution.py:485
  28.3 6.7 %collective-permute-start.5 = (bf16[400,128]{1,0:T(8,128)(2,1)S(1)}, bf16[400,128]{1,0:T(8,128)(2,1)S(1)}, u32[]{:S(2)}, u32[]{:S(2)}) collective-permute-start(bf16[400,128]{1,0:T(8,128)(2,1)S(1)} %get-tuple-element.43), channel_id=1, source_target_pairs={{0,8},{2,10},{4,12},{6,14},{8,0},{10,2},{12,4},{14,6},{16,24},{18,... | collective-permute-start | bytes 307208 | tf_op jit(solution)/shard_map/ppermute | solution.py:485
  29.9 14.9 %collective-permute-start.6 = (bf16[400,128]{1,0:T(8,128)(2,1)S(1)}, bf16[400,128]{1,0:T(8,128)(2,1)S(1)}, u32[]{:S(2)}, u32[]{:S(2)}) collective-permute-start(bf16[400,128]{1,0:T(8,128)(2,1)S(1)} %get-tuple-element.44), channel_id=1, source_target_pairs={{0,16},{2,18},{4,20},{6,22},{8,24},{10,26},{12,28},{14,30},{16,0},... | collective-permute-start | bytes 307208 | tf_op jit(solution)/shard_map/ppermute | solution.py:485
  32.5 12.3 %collective-permute-start.9 = (bf16[400,128]{1,0:T(8,128)(2,1)S(1)}, bf16[400,128]{1,0:T(8,128)(2,1)S(1)}, u32[]{:S(2)}, u32[]{:S(2)}) collective-permute-start(bf16[400,128]{1,0:T(8,128)(2,1)S(1)} %get-tuple-element.48), channel_id=1, source_target_pairs={{0,24},{2,26},{4,28},{6,30},{8,16},{10,18},{12,20},{14,22},{16,8},... | collective-permute-start | bytes 307208 | tf_op jit(solution)/shard_map/ppermute | solution.py:485
  32.7 16.3 %collective-permute-start.10 = (bf16[400,128]{1,0:T(8,128)(2,1)S(1)}, bf16[400,128]{1,0:T(8,128)(2,1)S(1)}, u32[]{:S(2)}, u32[]{:S(2)}) collective-permute-start(bf16[400,128]{1,0:T(8,128)(2,1)S(1)} %get-tuple-element.49), channel_id=1, source_target_pairs={{0,20},{2,22},{4,16},{6,18},{8,28},{10,30},{12,24},{14,26},{16,4},... | collective-permute-start | bytes 307208 | tf_op jit(solution)/shard_map/ppermute | solution.py:485
  35.0 14.1 %collective-permute-start.11 = (bf16[400,128]{1,0:T(8,128)(2,1)S(1)}, bf16[400,128]{1,0:T(8,128)(2,1)S(1)}, u32[]{:S(2)}, u32[]{:S(2)}) collective-permute-start(bf16[400,128]{1,0:T(8,128)(2,1)S(1)} %get-tuple-element.50), channel_id=1, source_target_pairs={{0,28},{2,30},{4,24},{6,26},{8,20},{10,22},{12,16},{14,18},{16,12}... | collective-permute-start | bytes 307208 | tf_op jit(solution)/shard_map/ppermute | solution.py:485
  44.8 5.6 %collective-permute-start.8 = (bf16[400,128]{1,0:T(8,128)(2,1)S(1)}, bf16[400,128]{1,0:T(8,128)(2,1)S(1)}, u32[]{:S(2)}, u32[]{:S(2)}) collective-permute-start(bf16[400,128]{1,0:T(8,128)(2,1)S(1)} %get-tuple-element.47), channel_id=1, source_target_pairs={{0,12},{2,14},{4,8},{6,10},{8,4},{10,6},{12,0},{14,2},{16,28},{18,... | collective-permute-start | bytes 307208 | tf_op jit(solution)/shard_map/ppermute | solution.py:485
  52.6 33.4 %all-to-all-start = ((bf16[32,3,48,128]{3,2,1,0:T(8,128)(2,1)}), bf16[32,3,48,128]{3,2,1,0:T(8,128)(2,1)S(1)}, u32[]{:S(2)}, u32[]{:S(2)}) async-start(bf16[32,3,48,128]{3,2,1,0:T(8,128)(2,1)} %shard_map.68), calls=%async_computation | async-start | bytes 2359296 | tf_op jit(solution)/shard_map/all_to_all | solution.py:502
  56.0 21.0 %collective-permute-start.13 = (bf16[1536,128]{1,0:T(8,128)(2,1)S(1)}, bf16[1536,128]{1,0:T(8,128)(2,1)S(1)}, u32[]{:S(2)}, u32[]{:S(2)}) collective-permute-start(bf16[1536,128]{1,0:T(8,128)(2,1)S(1)} %collective-permute-done.7.refs_1_), channel_id=1, source_target_pairs={{0,1},{1,0},{2,3},{3,2},{4,5},{5,4},{6,7},{7,6},{8,9},{9,8},{10,11... | collective-permute-start | bytes 1179656 | tf_op jit(solution)/shard_map/ppermute | solution.py:481
  96.2 3.7 %collective-permute-start.14 = (f32[1,16,128]{2,1,0:T(8,128)S(1)}, f32[1,16,128]{2,1,0:T(8,128)S(1)}, u32[]{:S(2)}, u32[]{:S(2)}) collective-permute-start(f32[1,16,128]{2,1,0:T(8,128)S(1)} %shard_map.69.refs_0_), channel_id=1, source_target_pairs={{0,1},{1,0},{2,3},{3,2},{4,5},{5,4},{6,7},{7,6},{8,9},{9,8},{10,11... | collective-permute-start | bytes 24584 | tf_op jit(solution)/shard_map/ppermute | solution.py:505

commit v14 on v13

--- a/solution.py
+++ b/solution.py
@@ -15,7 +15,7 @@
 CHUNK = 4
 LINE = 32
 PACK = 6
-SPREAD = (0, 1, 2, 4, 3, 6, 5, 7)
+SPREAD = (0, 1, 2, 5, 3, 7, 4, 6)
 SMEM = pltpu.SMEM
 VMEM = pltpu.VMEM
 

time: 101 us -> 102 us (level)
  no operation moved by 1% of the time
where the time goes in v14:
time: 102 us
  waiting for transfers between devices  55.5 us (54%)
  starting transfers between devices  22.9 us (22%)
  Pallas kernels  22.1 us (22%)
    ppermute x7, waiting for transfers between devices, near(): lax.ppermute(array, ('wide', 'narrow'), [(i, i ^ flip) for i in range(32)])  30.5 us
    ppermute x7, waiting for transfers between devices, along(): return lax.ppermute(array, 'wide', [(i, i ^ flip) for i in range(16)])  13.3 us
    ppermute x7, starting transfers between devices, along(): return lax.ppermute(array, 'wide', [(i, i ^ flip) for i in range(16)])  10.6 us
    pallas_call x1, Pallas kernels, score(): pl.pallas_call(functools.partial(score_kernel, length, parts), out_shape=...  10.2 us
    all_to_all x1, waiting for transfers between devices, local_cube(): incoming = lax.all_to_all(outgoing, ('narrow', 'wide'), 0, 0, tiled=True)  8.97 us
    ppermute x7, starting transfers between devices, near(): lax.ppermute(array, ('wide', 'narrow'), [(i, i ^ flip) for i in range(32)])  7.88 us
    pallas_call x2, Pallas kernels, split(): pl.pallas_call(functools.partial(split_kernel, first, over), out_shape=(j...  5.26 us
    all_to_all x1, starting transfers between devices, local_cube(): incoming = lax.all_to_all(outgoing, ('narrow', 'wide'), 0, 0, tiled=True)  3.44 us
  transfers between devices with their start and end apart: 16, of which 9 were waited for; matrix products, arithmetic and copies ran while one was open for 0% of the time, Pallas kernels for 7%

profile of v14, /device:TPU:0, one launch (start us, length us, event | category | flops | bytes accessed | tf_op | source)
XLA Modules:
  0.0 101.7 jit_solution(15699861847891235145)
XLA Ops:
  0.0 0.9 copy-done
  0.9 2.6 %shard_map.65 = (bf16[1536,128]{1,0:T(8,128)(2,1)S(1)}, bf16[1536,128]{1,0:T(8,128)(2,1)S(1)}) custom-call(bf16[4,1536,512]{2,1,0:T(8,128)(2,1)} %bitcast.3, bf16[512,128]{1,0:T(8,128)(2,1)S(1)} %copy-done), custom_call_target="tpu_custom_call" | custom-call | flops 402653184 | bytes 3145728 | tf_op jit(solution)/shard_map/pallas_call | solution.py:368
  3.6 3.0 %collective-permute-start.1 = (bf16[1536,128]{1,0:T(8,128)(2,1)S(1)}, bf16[1536,128]{1,0:T(8,128)(2,1)S(1)}, u32[]{:S(2)}, u32[]{:S(2)}) collective-permute-start(bf16[1536,128]{1,0:T(8,128)(2,1)S(1)} %get-tuple-element.35), channel_id=1, source_target_pairs={{0,1},{1,0},{2,3},{3,2},{4,5},{5,4},{6,7},{7,6},{8,9},{9,8},{10,11... | collective-permute-start | bytes 1179656 | tf_op jit(solution)/shard_map/ppermute | solution.py:481
  6.6 2.6 %shard_map.66 = (bf16[1536,128]{1,0:T(8,128)(2,1)S(1)}, bf16[1536,128]{1,0:T(8,128)(2,1)S(1)}) custom-call(bf16[4,1536,512]{2,1,0:T(8,128)(2,1)} %bitcast.4, bf16[512,128]{1,0:T(8,128)(2,1)S(1)} %copy-done), custom_call_target="tpu_custom_call" | custom-call | flops 402653184 | bytes 3145728 | tf_op jit(solution)/shard_map/pallas_call | solution.py:368
  9.3 0.3 collective-permute-start.3
  9.6 2.1 %shard_map.64 = (s32[6]{0:T(128)S(1)}, s32[192]{0:T(256)S(1)}, s32[12]{0:T(128)S(1)}) custom-call(s32[3]{0:T(128)S(1)} %pad_add_fusion.places_ref.where_ref, s32[12]{0:T(128)S(1)} %copy-done.2, s32[12]{0:T(128)S(1)} %copy-done.3, s32[12]{0:T(128)S(1)} %copy-done.4, s32[768]{0:T(1024)S(1)} %copy-done.1), custom_call_target="tpu_custom_call" | custom-call | tf_op jit(solution)/shard_map/pallas_call | solution.py:75
  11.7 0.4 collective-permute-start
  12.1 0.8 collective-permute-done.sel_near_ref
  12.9 3.6 %collective-permute-done.1.y_ref = bf16[1536,128]{1,0:T(8,128)(2,1)S(1)} collective-permute-done((bf16[1536,128]{1,0:T(8,128)(2,1)S(1)}, bf16[1536,128]{1,0:T(8,128)(2,1)S(1)}, u32[]{:S(2)}, u32[]{:S(2)}) %collective-permute-start.1) | collective-permute-done | bytes 393248 | tf_op jit(solution)/shard_map/ppermute | solution.py:481
  16.6 6.9 %collective-permute-done.2.cy_ref = bf16[1536,128]{1,0:T(8,128)(2,1)S(1)} collective-permute-done((bf16[1536,128]{1,0:T(8,128)(2,1)S(1)}, bf16[1536,128]{1,0:T(8,128)(2,1)S(1)}, u32[]{:S(2)}, u32[]{:S(2)}) %collective-permute-start.2) | collective-permute-done | bytes 393248 | tf_op jit(solution)/shard_map/ppermute | solution.py:481
  23.4 1.1 %shard_map.67 = (bf16[400,128]{1,0:T(8,128)(2,1)S(1)}, bf16[400,128]{1,0:T(8,128)(2,1)S(1)}, bf16[400,128]{1,0:T(8,128)(2,1)S(1)}, bf16[400,128]{1,0:T(8,128)(2,...) custom-call(s32[6]{0:T(128)S(1)} %get-tuple-element.32.sel_ref, ...), custom_call_target="tpu_custom_call" | custom-call | tf_op jit(solution)/shard_map/pallas_call | solution.py:413
  24.5 0.6 collective-permute-start.7
  25.1 1.7 %collective-permute-start.12 = (bf16[1536,128]{1,0:T(8,128)(2,1)S(1)}, bf16[1536,128]{1,0:T(8,128)(2,1)S(1)}, u32[]{:S(2)}, u32[]{:S(2)}) collective-permute-start(bf16[1536,128]{1,0:T(8,128)(2,1)S(1)} %get-tuple-element.40.refs_0_), channel_id=1, source_target_pairs={{0,1},{1,0},{2,3},{3,2},{4,5},{5,4},{6,7},{7,6},{8,9},{9,8},{10,11... | collective-permute-start | bytes 1179656 | tf_op jit(solution)/shard_map/ppermute | solution.py:481
  26.9 1.5 %collective-permute-start.4 = (bf16[400,128]{1,0:T(8,128)(2,1)S(1)}, bf16[400,128]{1,0:T(8,128)(2,1)S(1)}, u32[]{:S(2)}, u32[]{:S(2)}) collective-permute-start(bf16[400,128]{1,0:T(8,128)(2,1)S(1)} %get-tuple-element.42), channel_id=1, source_target_pairs={{0,4},{2,6},{4,0},{6,2},{8,12},{10,14},{12,8},{14,10},{16,20},{18,... | collective-permute-start | bytes 307208 | tf_op jit(solution)/shard_map/ppermute | solution.py:485
  28.3 1.6 %collective-permute-start.5 = (bf16[400,128]{1,0:T(8,128)(2,1)S(1)}, bf16[400,128]{1,0:T(8,128)(2,1)S(1)}, u32[]{:S(2)}, u32[]{:S(2)}) collective-permute-start(bf16[400,128]{1,0:T(8,128)(2,1)S(1)} %get-tuple-element.43), channel_id=1, source_target_pairs={{0,8},{2,10},{4,12},{6,14},{8,0},{10,2},{12,4},{14,6},{16,24},{18,... | collective-permute-start | bytes 307208 | tf_op jit(solution)/shard_map/ppermute | solution.py:485
  29.9 2.6 %collective-permute-start.6 = (bf16[400,128]{1,0:T(8,128)(2,1)S(1)}, bf16[400,128]{1,0:T(8,128)(2,1)S(1)}, u32[]{:S(2)}, u32[]{:S(2)}) collective-permute-start(bf16[400,128]{1,0:T(8,128)(2,1)S(1)} %get-tuple-element.44), channel_id=1, source_target_pairs={{0,20},{2,22},{4,16},{6,18},{8,28},{10,30},{12,24},{14,26},{16,4},... | collective-permute-start | bytes 307208 | tf_op jit(solution)/shard_map/ppermute | solution.py:485
  32.5 1.1 %collective-permute-start.9 = (bf16[400,128]{1,0:T(8,128)(2,1)S(1)}, bf16[400,128]{1,0:T(8,128)(2,1)S(1)}, u32[]{:S(2)}, u32[]{:S(2)}) collective-permute-start(bf16[400,128]{1,0:T(8,128)(2,1)S(1)} %get-tuple-element.48), channel_id=1, source_target_pairs={{0,28},{2,30},{4,24},{6,26},{8,20},{10,22},{12,16},{14,18},{16,12}... | collective-permute-start | bytes 307208 | tf_op jit(solution)/shard_map/ppermute | solution.py:485
  33.6 1.7 %collective-permute-start.10 = (bf16[400,128]{1,0:T(8,128)(2,1)S(1)}, bf16[400,128]{1,0:T(8,128)(2,1)S(1)}, u32[]{:S(2)}, u32[]{:S(2)}) collective-permute-start(bf16[400,128]{1,0:T(8,128)(2,1)S(1)} %get-tuple-element.49), channel_id=1, source_target_pairs={{0,16},{2,18},{4,20},{6,22},{8,24},{10,26},{12,28},{14,30},{16,0},... | collective-permute-start | bytes 307208 | tf_op jit(solution)/shard_map/ppermute | solution.py:485
  35.3 2.0 %collective-permute-start.11 = (bf16[400,128]{1,0:T(8,128)(2,1)S(1)}, bf16[400,128]{1,0:T(8,128)(2,1)S(1)}, u32[]{:S(2)}, u32[]{:S(2)}) collective-permute-start(bf16[400,128]{1,0:T(8,128)(2,1)S(1)} %get-tuple-element.50), channel_id=1, source_target_pairs={{0,24},{2,26},{4,28},{6,30},{8,16},{10,18},{12,20},{14,22},{16,8},... | collective-permute-start | bytes 307208 | tf_op jit(solution)/shard_map/ppermute | solution.py:485
  37.4 7.9 %collective-permute-done.6.refs_3_ = bf16[400,128]{1,0:T(8,128)(2,1)S(1)} collective-permute-done((bf16[400,128]{1,0:T(8,128)(2,1)S(1)}, bf16[400,128]{1,0:T(8,128)(2,1)S(1)}, u32[]{:S(2)}, u32[]{:S(2)}) %collective-permute-start.6) | collective-permute-done | bytes 102432 | tf_op jit(solution)/shard_map/ppermute | solution.py:485
  45.2 0.1 collective-permute-start.8
  45.4 3.6 %collective-permute-done.10.refs_6_ = bf16[400,128]{1,0:T(8,128)(2,1)S(1)} collective-permute-done((bf16[400,128]{1,0:T(8,128)(2,1)S(1)}, bf16[400,128]{1,0:T(8,128)(2,1)S(1)}, u32[]{:S(2)}, u32[]{:S(2)}) %collective-permute-start.10) | collective-permute-done | bytes 102432 | tf_op jit(solution)/shard_map/ppermute | solution.py:485
  48.9 1.9 %collective-permute-done.8.refs_4_ = bf16[400,128]{1,0:T(8,128)(2,1)S(1)} collective-permute-done((bf16[400,128]{1,0:T(8,128)(2,1)S(1)}, bf16[400,128]{1,0:T(8,128)(2,1)S(1)}, u32[]{:S(2)}, u32[]{:S(2)}) %collective-permute-start.8) | collective-permute-done | bytes 102432 | tf_op jit(solution)/shard_map/ppermute | solution.py:485
  50.8 2.2 %shard_map.68 = bf16[32,3,48,128]{3,2,1,0:T(8,128)(2,1)} custom-call(bf16[400,128]{1,0:T(8,128)(2,1)S(1)} %get-tuple-element.41.refs_0_, bf16[400,128]{1,0:T(8,128)(2,1)S(1)} %collective-permute-done.4.refs_1_, bf16[400,128]{1,0:T(8,128)(2,1)S(1)} %collective-permute-done.5.refs_2_, bf16[400,128]{1,0:T(8,128)(2,1)S(1)} %collective-permute-done.6.refs_3_, ...), custom_call_target="tpu_custom_call" | custom-call | tf_op jit(solution)/shard_map/pallas_call | solution.py:453
  53.0 3.4 %all-to-all-start = ((bf16[32,3,48,128]{3,2,1,0:T(8,128)(2,1)}), bf16[32,3,48,128]{3,2,1,0:T(8,128)(2,1)S(1)}, u32[]{:S(2)}, u32[]{:S(2)}) async-start(bf16[32,3,48,128]{3,2,1,0:T(8,128)(2,1)} %shard_map.68), calls=%async_computation | async-start | bytes 2359296 | tf_op jit(solution)/shard_map/all_to_all | solution.py:502
  56.5 1.8 %collective-permute-start.13 = (bf16[1536,128]{1,0:T(8,128)(2,1)S(1)}, bf16[1536,128]{1,0:T(8,128)(2,1)S(1)}, u32[]{:S(2)}, u32[]{:S(2)}) collective-permute-start(bf16[1536,128]{1,0:T(8,128)(2,1)S(1)} %collective-permute-done.7.refs_1_), channel_id=1, source_target_pairs={{0,1},{1,0},{2,3},{3,2},{4,5},{5,4},{6,7},{7,6},{8,9},{9,8},{10,11... | collective-permute-start | bytes 1179656 | tf_op jit(solution)/shard_map/ppermute | solution.py:481
  58.3 19.2 %collective-permute-done.13.refs_3_ = bf16[1536,128]{1,0:T(8,128)(2,1)S(1)} collective-permute-done((bf16[1536,128]{1,0:T(8,128)(2,1)S(1)}, bf16[1536,128]{1,0:T(8,128)(2,1)S(1)}, u32[]{:S(2)}, u32[]{:S(2)}) %collective-permute-start.13) | collective-permute-done | bytes 393248 | tf_op jit(solution)/shard_map/ppermute | solution.py:481
  77.5 9.0 %all-to-all-done.refs_4_ = bf16[32,3,48,128]{3,2,1,0:T(8,128)(2,1)S(1)} async-done(((bf16[32,3,48,128]{3,2,1,0:T(8,128)(2,1)}), bf16[32,3,48,128]{3,2,1,0:T(8,128)(2,1)S(1)}, u32[]{:S(2)}, u32[]{:S(2)}) %all-to-all-start) | async-done | bytes 1179680 | tf_op jit(solution)/shard_map/all_to_all | solution.py:502
  86.5 10.2 %shard_map.69.refs_0_ = f32[1,16,128]{2,1,0:T(8,128)S(1)} custom-call(s32[192]{0:T(256)S(1)} %get-tuple-element.31.table_ref, bf16[1536,128]{1,0:T(8,128)(2,1)S(1)} %get-tuple-element.40.refs_0_, bf16[1536,128]{1,0:T(8,128)(2,1)S(1)} %collective-permute-done.7.refs_1_, bf16[1536,128]{1,0:T(8,128)(2,1)S(1)} %collective-permute-done.12.refs_2_, ...), custom_call_target="tpu_custom_call" | custom-call | flops 3623878656 | bytes 786432 | tf_op jit(solution)/shard_map/pallas_call | solution.py:252
  96.7 1.0 %collective-permute-start.14 = (f32[1,16,128]{2,1,0:T(8,128)S(1)}, f32[1,16,128]{2,1,0:T(8,128)S(1)}, u32[]{:S(2)}, u32[]{:S(2)}) collective-permute-start(f32[1,16,128]{2,1,0:T(8,128)S(1)} %shard_map.69.refs_0_), channel_id=1, source_target_pairs={{0,1},{1,0},{2,3},{3,2},{4,5},{5,4},{6,7},{7,6},{8,9},{9,8},{10,11... | collective-permute-start | bytes 24584 | tf_op jit(solution)/shard_map/ppermute | solution.py:505
  97.7 2.7 %collective-permute-done.14.refs_1_ = f32[1,16,128]{2,1,0:T(8,128)S(1)} collective-permute-done((f32[1,16,128]{2,1,0:T(8,128)S(1)}, f32[1,16,128]{2,1,0:T(8,128)S(1)}, u32[]{:S(2)}, u32[]{:S(2)}) %collective-permute-start.14) | collective-permute-done | bytes 8224 | tf_op jit(solution)/shard_map/ppermute | solution.py:505
  100.4 1.3 %shard_map.70 = f32[12,12,12]{2,1,0:T(8,128)} custom-call(s32[3]{0:T(128)S(1)} %pad_add_fusion.places_ref.where_ref, s32[12]{0:T(128)S(1)} %get-tuple-element.30.pairs_ref, f32[1,16,128]{2,1,0:T(8,128)S(1)} %shard_map.69.refs_0_, f32[1,16,128]{2,1,0:T(8,128)S(1)} %collective-permute-done.14.refs_1_), custom_call_target="tpu_custom_call" | custom-call | tf_op jit(solution)/shard_map/pallas_call | solution.py:279
  (18 shorter events, 0.1 us)
Async XLA Ops:
  0.0 0.9 copy-start
  3.5 6.1 %copy-start.1 = (s32[768]{0:T(1024)S(1)}, s32[768]{0:T(1024)}, u32[]{:S(2)}) copy-start(s32[768]{0:T(1024)} %lengths_ref.1) | copy-start | bytes 9220
  3.6 6.0 %copy-start.2 = (s32[12]{0:T(128)S(1)}, s32[12]{0:T(128)}, u32[]{:S(2)}) copy-start(s32[12]{0:T(128)} %cand_ref.1) | copy-start | bytes 148
  3.6 6.0 %copy-start.3 = (s32[12]{0:T(128)S(1)}, s32[12]{0:T(128)}, u32[]{:S(2)}) copy-start(s32[12]{0:T(128)} %query_block_ref.1) | copy-start | bytes 148
  3.6 6.0 %copy-start.4 = (s32[12]{0:T(128)S(1)}, s32[12]{0:T(128)}, u32[]{:S(2)}) copy-start(s32[12]{0:T(128)} %valid_ref.1) | copy-start | bytes 148
  3.6 13.0 %collective-permute-start.1 = (bf16[1536,128]{1,0:T(8,128)(2,1)S(1)}, bf16[1536,128]{1,0:T(8,128)(2,1)S(1)}, u32[]{:S(2)}, u32[]{:S(2)}) collective-permute-start(bf16[1536,128]{1,0:T(8,128)(2,1)S(1)} %get-tuple-element.35), channel_id=1, source_target_pairs={{0,1},{1,0},{2,3},{3,2},{4,5},{5,4},{6,7},{7,6},{8,9},{9,8},{10,11... | collective-permute-start | bytes 1179656 | tf_op jit(solution)/shard_map/ppermute | solution.py:481
  6.6 16.8 %collective-permute-start.2 = (bf16[1536,128]{1,0:T(8,128)(2,1)S(1)}, bf16[1536,128]{1,0:T(8,128)(2,1)S(1)}, u32[]{:S(2)}, u32[]{:S(2)}) collective-permute-start(bf16[1536,128]{1,0:T(8,128)(2,1)S(1)} %get-tuple-element.36), channel_id=1, source_target_pairs={{0,3},{1,2},{2,1},{3,0},{4,7},{5,6},{6,5},{7,4},{8,11},{9,10},{10,... | collective-permute-start | bytes 1179656 | tf_op jit(solution)/shard_map/ppermute | solution.py:481
  9.3 14.2 %collective-permute-start.3 = (bf16[1536,128]{1,0:T(8,128)(2,1)S(1)}, bf16[1536,128]{1,0:T(8,128)(2,1)S(1)}, u32[]{:S(2)}, u32[]{:S(2)}) collective-permute-start(bf16[1536,128]{1,0:T(8,128)(2,1)S(1)} %get-tuple-element.39), channel_id=1, source_target_pairs={{0,2},{1,3},{2,0},{3,1},{4,6},{5,7},{6,4},{7,5},{8,10},{9,11},{10,... | collective-permute-start | bytes 1179656 | tf_op jit(solution)/shard_map/ppermute | solution.py:481
  11.7 1.2 %collective-permute-start = (s32[6]{0:T(128)S(1)}, s32[6]{0:T(128)S(1)}, u32[]{:S(2)}, u32[]{:S(2)}) collective-permute-start(s32[6]{0:T(128)S(1)} %get-tuple-element.32.sel_ref), channel_id=1, source_target_pairs={{0,2},{1,3},{2,0},{3,1},{4,6},{5,7},{6,4},{7,5},{8,10},{9,11},{10,... | collective-permute-start | bytes 80 | tf_op jit(solution)/shard_map/ppermute | solution.py:481
  24.5 8.0 %collective-permute-start.7 = (bf16[1536,128]{1,0:T(8,128)(2,1)S(1)}, bf16[1536,128]{1,0:T(8,128)(2,1)S(1)}, u32[]{:S(2)}, u32[]{:S(2)}) collective-permute-start(bf16[1536,128]{1,0:T(8,128)(2,1)S(1)} %get-tuple-element.46), channel_id=1, source_target_pairs={{0,2},{1,3},{2,0},{3,1},{4,6},{5,7},{6,4},{7,5},{8,10},{9,11},{10,... | collective-permute-start | bytes 1179656 | tf_op jit(solution)/shard_map/ppermute | solution.py:481
  25.1 27.9 %collective-permute-start.12 = (bf16[1536,128]{1,0:T(8,128)(2,1)S(1)}, bf16[1536,128]{1,0:T(8,128)(2,1)S(1)}, u32[]{:S(2)}, u32[]{:S(2)}) collective-permute-start(bf16[1536,128]{1,0:T(8,128)(2,1)S(1)} %get-tuple-element.40.refs_0_), channel_id=1, source_target_pairs={{0,1},{1,0},{2,3},{3,2},{4,5},{5,4},{6,7},{7,6},{8,9},{9,8},{10,11... | collective-permute-start | bytes 1179656 | tf_op jit(solution)/shard_map/ppermute | solution.py:481
  26.9 6.8 %collective-permute-start.4 = (bf16[400,128]{1,0:T(8,128)(2,1)S(1)}, bf16[400,128]{1,0:T(8,128)(2,1)S(1)}, u32[]{:S(2)}, u32[]{:S(2)}) collective-permute-start(bf16[400,128]{1,0:T(8,128)(2,1)S(1)} %get-tuple-element.42), channel_id=1, source_target_pairs={{0,4},{2,6},{4,0},{6,2},{8,12},{10,14},{12,8},{14,10},{16,20},{18,... | collective-permute-start | bytes 307208 | tf_op jit(solution)/shard_map/ppermute | solution.py:485
  28.3 7.0 %collective-permute-start.5 = (bf16[400,128]{1,0:T(8,128)(2,1)S(1)}, bf16[400,128]{1,0:T(8,128)(2,1)S(1)}, u32[]{:S(2)}, u32[]{:S(2)}) collective-permute-start(bf16[400,128]{1,0:T(8,128)(2,1)S(1)} %get-tuple-element.43), channel_id=1, source_target_pairs={{0,8},{2,10},{4,12},{6,14},{8,0},{10,2},{12,4},{14,6},{16,24},{18,... | collective-permute-start | bytes 307208 | tf_op jit(solution)/shard_map/ppermute | solution.py:485
  29.9 15.3 %collective-permute-start.6 = (bf16[400,128]{1,0:T(8,128)(2,1)S(1)}, bf16[400,128]{1,0:T(8,128)(2,1)S(1)}, u32[]{:S(2)}, u32[]{:S(2)}) collective-permute-start(bf16[400,128]{1,0:T(8,128)(2,1)S(1)} %get-tuple-element.44), channel_id=1, source_target_pairs={{0,20},{2,22},{4,16},{6,18},{8,28},{10,30},{12,24},{14,26},{16,4},... | collective-permute-start | bytes 307208 | tf_op jit(solution)/shard_map/ppermute | solution.py:485
  32.5 12.9 %collective-permute-start.9 = (bf16[400,128]{1,0:T(8,128)(2,1)S(1)}, bf16[400,128]{1,0:T(8,128)(2,1)S(1)}, u32[]{:S(2)}, u32[]{:S(2)}) collective-permute-start(bf16[400,128]{1,0:T(8,128)(2,1)S(1)} %get-tuple-element.48), channel_id=1, source_target_pairs={{0,28},{2,30},{4,24},{6,26},{8,20},{10,22},{12,16},{14,18},{16,12}... | collective-permute-start | bytes 307208 | tf_op jit(solution)/shard_map/ppermute | solution.py:485
  33.6 15.3 %collective-permute-start.10 = (bf16[400,128]{1,0:T(8,128)(2,1)S(1)}, bf16[400,128]{1,0:T(8,128)(2,1)S(1)}, u32[]{:S(2)}, u32[]{:S(2)}) collective-permute-start(bf16[400,128]{1,0:T(8,128)(2,1)S(1)} %get-tuple-element.49), channel_id=1, source_target_pairs={{0,16},{2,18},{4,20},{6,22},{8,24},{10,26},{12,28},{14,30},{16,0},... | collective-permute-start | bytes 307208 | tf_op jit(solution)/shard_map/ppermute | solution.py:485
  35.3 13.6 %collective-permute-start.11 = (bf16[400,128]{1,0:T(8,128)(2,1)S(1)}, bf16[400,128]{1,0:T(8,128)(2,1)S(1)}, u32[]{:S(2)}, u32[]{:S(2)}) collective-permute-start(bf16[400,128]{1,0:T(8,128)(2,1)S(1)} %get-tuple-element.50), channel_id=1, source_target_pairs={{0,24},{2,26},{4,28},{6,30},{8,16},{10,18},{12,20},{14,22},{16,8},... | collective-permute-start | bytes 307208 | tf_op jit(solution)/shard_map/ppermute | solution.py:485
  45.2 5.6 %collective-permute-start.8 = (bf16[400,128]{1,0:T(8,128)(2,1)S(1)}, bf16[400,128]{1,0:T(8,128)(2,1)S(1)}, u32[]{:S(2)}, u32[]{:S(2)}) collective-permute-start(bf16[400,128]{1,0:T(8,128)(2,1)S(1)} %get-tuple-element.47), channel_id=1, source_target_pairs={{0,12},{2,14},{4,8},{6,10},{8,4},{10,6},{12,0},{14,2},{16,28},{18,... | collective-permute-start | bytes 307208 | tf_op jit(solution)/shard_map/ppermute | solution.py:485
  53.0 33.4 %all-to-all-start = ((bf16[32,3,48,128]{3,2,1,0:T(8,128)(2,1)}), bf16[32,3,48,128]{3,2,1,0:T(8,128)(2,1)S(1)}, u32[]{:S(2)}, u32[]{:S(2)}) async-start(bf16[32,3,48,128]{3,2,1,0:T(8,128)(2,1)} %shard_map.68), calls=%async_computation | async-start | bytes 2359296 | tf_op jit(solution)/shard_map/all_to_all | solution.py:502
  56.5 21.0 %collective-permute-start.13 = (bf16[1536,128]{1,0:T(8,128)(2,1)S(1)}, bf16[1536,128]{1,0:T(8,128)(2,1)S(1)}, u32[]{:S(2)}, u32[]{:S(2)}) collective-permute-start(bf16[1536,128]{1,0:T(8,128)(2,1)S(1)} %collective-permute-done.7.refs_1_), channel_id=1, source_target_pairs={{0,1},{1,0},{2,3},{3,2},{4,5},{5,4},{6,7},{7,6},{8,9},{9,8},{10,11... | collective-permute-start | bytes 1179656 | tf_op jit(solution)/shard_map/ppermute | solution.py:481
  96.7 3.7 %collective-permute-start.14 = (f32[1,16,128]{2,1,0:T(8,128)S(1)}, f32[1,16,128]{2,1,0:T(8,128)S(1)}, u32[]{:S(2)}, u32[]{:S(2)}) collective-permute-start(f32[1,16,128]{2,1,0:T(8,128)S(1)} %shard_map.69.refs_0_), channel_id=1, source_target_pairs={{0,1},{1,0},{2,3},{3,2},{4,5},{5,4},{6,7},{7,6},{8,9},{9,8},{10,11... | collective-permute-start | bytes 24584 | tf_op jit(solution)/shard_map/ppermute | solution.py:505
